TPU v7x, 32 devices: a whole 2x2x4 slice. The times are simulated.
32 devices in a mesh: pipe: 4 (over x, core), dp: 8 (over z, y).
Axes of the slice: x: 2, y: 2, z: 4, core: 2. Of those that a mesh axis runs over, the one named last changes fastest.
Arguments:
- text_embed: bfloat16 [256, 64, 768], P(('pipe', 'dp')), may hold values from -9 to 9
- image_feats: bfloat16 [256, 145, 1024], P(('pipe', 'dp')), may hold values from -6 to 6
- caption_len: int32 [256], P(('pipe', 'dp')), may hold values from 8 to 31
- phrase_len: int32 [256, 6], P(('pipe', 'dp')), may hold values from 1 to 8
- box_count: int32 [256], P(('pipe', 'dp')), may hold values from 0 to 6
- patch_mask: int32 [256, 145], P(('pipe', 'dp')), may hold values 0 or 1
- attn_qkv: bfloat16 [1536, 2304], P('pipe', 'dp'), may hold values from -0.21875 to 0.21875
- attn_out: bfloat16 [1536, 768], P('pipe', 'dp'), may hold values from -1.25 to 1.25
- ffn_up: bfloat16 [1536, 3072], P('pipe', 'dp'), may hold values from -0.21875 to 0.21875
- ffn_down: bfloat16 [6144, 768], P('pipe', 'dp'), may hold values from -0.109375 to 0.109375
- layer_vectors: bfloat16 [24, 768], P('pipe', 'dp'), may hold values from -1.203125 to 1.3984375, as said below
- cross_query: bfloat16 [768, 768], P(('pipe', 'dp')), may hold values from -0.21875 to 0.21875
- cross_kv: bfloat16 [1024, 1536], P(('pipe', 'dp')), may hold values from -0.1875 to 0.1875
- cross_out: bfloat16 [768, 768], P(('pipe', 'dp')), may hold values from -2 to 2
- cross_vectors: bfloat16 [768, 5], P(('pipe', 'dp')), may hold values from -1.203125 to 1.3984375, as said below
- cotangent: bfloat16 [256, 64, 768], P(('pipe', 'dp')), may hold values from -6 to 6
Outputs:
- joined: float32 [256, 64, 768], P(('pipe', 'dp'))
- embed_grad: float32 [256, 64, 768], P(('pipe', 'dp'))
- grad_attn_qkv: float32 [1536, 2304], P('pipe', 'dp')
- grad_attn_out: float32 [1536, 768], P('pipe', 'dp')
- grad_ffn_up: float32 [1536, 3072], P('pipe', 'dp')
- grad_ffn_down: float32 [6144, 768], P('pipe', 'dp')
- grad_layer_vectors: float32 [24, 768], P('pipe', 'dp')
- grad_cross_query: float32 [768, 768], P(('pipe', 'dp'))
- grad_cross_kv: float32 [1024, 1536], P(('pipe', 'dp'))
- grad_cross_out: float32 [768, 768], P(('pipe', 'dp'))
- grad_cross_vectors: float32 [768, 5], P(('pipe', 'dp'))
Inputs may be any that keep to these rules, and one draw needn't show every extreme that they name: `layer_vectors`: norm gains near one and biases of the two layers. `cross_vectors`: biases and a norm gain of the cross-attention.
All inputs are finite; a program needn't handle non-finite values. No bound on the sum of `patch_mask` on one device may be relied on, other than what follows from the above.
Results may differ from a plain program's by a relative error of at most 0.035.
Values may be sent and summed in bfloat16 or wider, within the bound.
No kernel may reach another device: no remote copies, remote signals or barrier semaphores. Data moves between devices by JAX's collectives and lax.ppermute only.
A program may use at most 448 MiB of HBM per device.

v0:
```python
from functools import partial

import jax
import jax.numpy as jnp
from jax import lax
from jax.sharding import PartitionSpec as P

HEADS = 12


NORM_EPS = 1e-12
MASK_FILL = -1000000000.0


def shortened(value):
    return jax.tree.map(lambda a: a.astype(jnp.bfloat16) if a.dtype == jnp.float32 else a, value)


def partner_2(block, axis, bit):
    count = lax.axis_size(axis)
    route = []
    for low in range(count):
        high = low | 1 << bit
        if high != low and high < count:
            route += [(low, high), (high, low)]
    return lax.ppermute(block, axis, route)


def shifted(block, axis, distance):
    devices = range(lax.axis_size(axis))
    route = [(i - distance, i) for i in devices if i - distance in devices]
    return lax.ppermute(block, axis, route)


def rows_product(inputs, weight):
    flat = inputs.reshape(-1, inputs.shape[-1])
    result = jnp.dot(flat, weight, preferred_element_type=jnp.float32)
    return result.reshape(inputs.shape[:-1] + (weight.shape[1],))


def weight_grad(inputs, grads):
    flat_inputs = inputs.reshape(-1, inputs.shape[-1])
    flat_grads = grads.reshape(-1, grads.shape[-1])
    return lax.dot_general(
        flat_inputs, flat_grads, (((0,), (0,)), ((), ())), preferred_element_type=jnp.float32
    )


def input_grad(grads, weight):
    flat = grads.reshape(-1, grads.shape[-1])
    result = lax.dot_general(
        flat, weight, (((1,), (1,)), ((), ())), preferred_element_type=jnp.float32
    )
    return result.reshape(grads.shape[:-1] + (weight.shape[0],))


def row_total(grads):
    return jnp.sum(grads.reshape(-1, grads.shape[-1]).astype(jnp.float32), axis=0)


def norm_forward(summed, gain, offset):
    center = summed - jnp.mean(summed, axis=-1, keepdims=True)
    scale_row = lax.rsqrt(jnp.mean(center * center, axis=-1, keepdims=True) + NORM_EPS)
    normed = center * scale_row
    return (normed * gain + offset, (normed, scale_row))


def norm_backward(grad_output, norm_saved, gain):
    normed, scale_row = norm_saved
    flat_grad = grad_output.reshape(-1, grad_output.shape[-1])
    grad_gain = jnp.sum(flat_grad * normed.reshape(flat_grad.shape), axis=0)
    grad_offset = jnp.sum(flat_grad, axis=0)
    scaled = grad_output * gain
    grad_input = scale_row * (
        scaled
        - jnp.mean(scaled, axis=-1, keepdims=True)
        - normed * jnp.mean(scaled * normed, axis=-1, keepdims=True)
    )
    return (grad_input, grad_gain, grad_offset)


def attention_forward(queries, keys, values, key_keep, head_count):
    samples, query_rows, model_width = queries.shape
    head_size = model_width // head_count
    query_heads = queries.reshape(samples, query_rows, head_count, head_size)
    key_heads = keys.reshape(samples, keys.shape[1], head_count, head_size)
    value_heads = values.reshape(samples, values.shape[1], head_count, head_size)
    scores = jnp.einsum(
        "sqhd,skhd->shqk", query_heads, key_heads, preferred_element_type=jnp.float32
    ) * head_size ** (-0.5)
    scores = jnp.where(key_keep[:, None, None, :] > 0, scores, MASK_FILL)
    row_top = jnp.max(scores, axis=-1, keepdims=True)
    exponent = jnp.exp(scores - row_top)
    attention = exponent / jnp.sum(exponent, axis=-1, keepdims=True)
    mixed = jnp.einsum(
        "shqk,skhd->sqhd",
        attention.astype(jnp.bfloat16),
        value_heads,
        preferred_element_type=jnp.float32,
    )
    return (mixed.reshape(samples, query_rows, model_width), attention)


def attention_backward(grad_mixed, attention, queries, keys, values, head_count):
    samples, query_rows, model_width = queries.shape
    key_rows = keys.shape[1]
    head_size = model_width // head_count
    query_heads = queries.reshape(samples, query_rows, head_count, head_size)
    key_heads = keys.reshape(samples, key_rows, head_count, head_size)
    value_heads = values.reshape(samples, key_rows, head_count, head_size)
    grad_heads = grad_mixed.reshape(samples, query_rows, head_count, head_size)
    grad_values = jnp.einsum(
        "shqk,sqhd->skhd",
        attention.astype(jnp.bfloat16),
        grad_heads,
        preferred_element_type=jnp.float32,
    )
    grad_attention = jnp.einsum(
        "sqhd,skhd->shqk", grad_heads, value_heads, preferred_element_type=jnp.float32
    )
    grad_scores = attention * (
        grad_attention - jnp.sum(grad_attention * attention, axis=-1, keepdims=True)
    )
    grad_scores = grad_scores.astype(jnp.bfloat16)
    grad_queries = jnp.einsum(
        "shqk,skhd->sqhd", grad_scores, key_heads, preferred_element_type=jnp.float32
    ) * head_size ** (-0.5)
    grad_keys = jnp.einsum(
        "shqk,sqhd->skhd", grad_scores, query_heads, preferred_element_type=jnp.float32
    ) * head_size ** (-0.5)
    return (
        grad_queries.reshape(samples, query_rows, model_width),
        grad_keys.reshape(samples, key_rows, model_width),
        grad_values.reshape(samples, key_rows, model_width),
    )


def self_forward(state, key_keep, vectors, qkv_weight, out_weight, head_count):
    model_width = state.shape[-1]
    state_low = state.astype(jnp.bfloat16)
    bias_row = jnp.concatenate([vectors[0], jnp.zeros((model_width,), jnp.float32), vectors[1]])
    projected = (rows_product(state_low, qkv_weight) + bias_row).astype(jnp.bfloat16)
    mixed, attention = attention_forward(
        projected[..., :model_width],
        projected[..., model_width : 2 * model_width],
        projected[..., 2 * model_width :],
        key_keep,
        head_count,
    )
    mixed_low = mixed.astype(jnp.bfloat16)
    summed = state + (rows_product(mixed_low, out_weight) + vectors[2])
    output, norm_saved = norm_forward(summed, vectors[3], vectors[4])
    return (output, (state_low, projected, attention, mixed_low, norm_saved))


def self_backward(grad_output, saved, vectors, qkv_weight, out_weight, head_count):
    state_low, projected, attention, mixed_low, norm_saved = saved
    model_width = state_low.shape[-1]
    grad_summed, grad_gain, grad_offset = norm_backward(grad_output, norm_saved, vectors[3])
    grad_branch = grad_summed.astype(jnp.bfloat16)
    grad_out_weight = weight_grad(mixed_low, grad_branch)
    grad_out_bias = row_total(grad_branch)
    grad_mixed = input_grad(grad_branch, out_weight).astype(jnp.bfloat16)
    grad_query, grad_key, grad_value = attention_backward(
        grad_mixed,
        attention,
        projected[..., :model_width],
        projected[..., model_width : 2 * model_width],
        projected[..., 2 * model_width :],
        head_count,
    )
    grad_projected = jnp.concatenate([grad_query, grad_key, grad_value], axis=-1).astype(
        jnp.bfloat16
    )
    grad_qkv_weight = weight_grad(state_low, grad_projected)
    bias_totals = row_total(grad_projected)
    grad_state = grad_summed + input_grad(grad_projected, qkv_weight)
    vector_grads = jnp.stack(
        [
            bias_totals[:model_width],
            bias_totals[2 * model_width :],
            grad_out_bias,
            grad_gain,
            grad_offset,
        ]
    )
    return (grad_state, grad_qkv_weight, grad_out_weight, vector_grads)


def cross_forward(state, image_low, patch_keep, cross_weights, head_count):
    query_weight, kv_weight, out_weight, vector_low = cross_weights
    vectors = vector_low.astype(jnp.float32)
    model_width = state.shape[-1]
    state_low = state.astype(jnp.bfloat16)
    queries = (rows_product(state_low, query_weight) + vectors[:, 0]).astype(jnp.bfloat16)
    kv_bias = jnp.concatenate([jnp.zeros((model_width,), jnp.float32), vectors[:, 1]])
    kv_pairs = (rows_product(image_low, kv_weight) + kv_bias).astype(jnp.bfloat16)
    mixed, attention = attention_forward(
        queries, kv_pairs[..., :model_width], kv_pairs[..., model_width:], patch_keep, head_count
    )
    mixed_low = mixed.astype(jnp.bfloat16)
    summed = state + (rows_product(mixed_low, out_weight) + vectors[:, 2])
    output, norm_saved = norm_forward(summed, vectors[:, 3], vectors[:, 4])
    return (output, (state_low, queries, kv_pairs, attention, mixed_low, norm_saved))


def cross_blank(state, image_low, head_count):
    samples, text_rows, model_width = state.shape
    patch_count = image_low.shape[1]
    return (
        jnp.zeros(state.shape, jnp.bfloat16),
        jnp.zeros(state.shape, jnp.bfloat16),
        jnp.zeros((samples, patch_count, 2 * model_width), jnp.bfloat16),
        jnp.zeros((samples, head_count, text_rows, patch_count), jnp.float32),
        jnp.zeros(state.shape, jnp.bfloat16),
        (jnp.zeros(state.shape, jnp.float32), jnp.zeros((samples, text_rows, 1), jnp.float32)),
    )


def cross_backward(grad_output, saved, image_low, cross_weights, head_count):
    query_weight, kv_weight, out_weight, vector_low = cross_weights
    vectors = vector_low.astype(jnp.float32)
    state_low, queries, kv_pairs, attention, mixed_low, norm_saved = saved
    model_width = state_low.shape[-1]
    grad_summed, grad_gain, grad_offset = norm_backward(grad_output, norm_saved, vectors[:, 3])
    grad_branch = grad_summed.astype(jnp.bfloat16)
    grad_out_weight = weight_grad(mixed_low, grad_branch)
    grad_out_bias = row_total(grad_branch)
    grad_mixed = input_grad(grad_branch, out_weight).astype(jnp.bfloat16)
    grad_query, grad_key, grad_value = attention_backward(
        grad_mixed,
        attention,
        queries,
        kv_pairs[..., :model_width],
        kv_pairs[..., model_width:],
        head_count,
    )
    grad_queries = grad_query.astype(jnp.bfloat16)
    grad_pairs = jnp.concatenate([grad_key, grad_value], axis=-1).astype(jnp.bfloat16)
    grad_query_weight = weight_grad(state_low, grad_queries)
    grad_kv_weight = weight_grad(image_low, grad_pairs)
    vector_grads = jnp.stack(
        [
            row_total(grad_queries),
            row_total(grad_pairs)[model_width:],
            grad_out_bias,
            grad_gain,
            grad_offset,
        ],
        axis=1,
    )
    grad_state = grad_summed + input_grad(grad_queries, query_weight)
    return (grad_state, (grad_query_weight, grad_kv_weight, grad_out_weight, vector_grads))


def feed_forward(state, vectors, up_weight, down_weight):
    state_low = state.astype(jnp.bfloat16)
    hidden = rows_product(state_low, up_weight) + vectors[8:12].reshape(-1)
    activated = jax.nn.gelu(hidden, approximate=False).astype(jnp.bfloat16)
    summed = state + (rows_product(activated, down_weight) + vectors[5])
    output, norm_saved = norm_forward(summed, vectors[6], vectors[7])
    return (output, (state_low, hidden, activated, norm_saved))


def feed_backward(grad_output, saved, vectors, up_weight, down_weight):
    state_low, hidden, activated, norm_saved = saved
    grad_summed, grad_gain, grad_offset = norm_backward(grad_output, norm_saved, vectors[6])
    grad_branch = grad_summed.astype(jnp.bfloat16)
    grad_down = weight_grad(activated, grad_branch)
    grad_down_bias = row_total(grad_branch)
    grad_activated = input_grad(grad_branch, down_weight)
    unused_value, gelu_pull = jax.vjp(partial(jax.nn.gelu, approximate=False), hidden)
    grad_hidden = gelu_pull(grad_activated)[0].astype(jnp.bfloat16)
    grad_up = weight_grad(state_low, grad_hidden)
    grad_up_bias = row_total(grad_hidden)
    grad_state = grad_summed + input_grad(grad_hidden, up_weight)
    vector_grads = jnp.concatenate(
        [jnp.stack([grad_down_bias, grad_gain, grad_offset]), grad_up_bias.reshape(4, -1)], axis=0
    )
    return (grad_state, grad_up, grad_down, vector_grads)


def layer_forward(
    state, key_keep, image_low, patch_keep, section_weights, cross_weights, joining, head_count
):
    qkv_weight, out_weight, up_weight, down_weight, vector_low = section_weights
    vectors = vector_low.astype(jnp.float32)
    after_self, self_saved = self_forward(
        state, key_keep, vectors, qkv_weight, out_weight, head_count
    )

    def with_cross():
        return cross_forward(after_self, image_low, patch_keep, cross_weights, head_count)

    def without_cross():
        return (after_self, cross_blank(after_self, image_low, head_count))

    after_cross, cross_saved = lax.cond(joining, with_cross, without_cross)
    output, feed_saved = feed_forward(after_cross, vectors, up_weight, down_weight)
    return (output, (self_saved, cross_saved, feed_saved))


def layer_backward(
    grad_output, saved, image_low, section_weights, cross_weights, joining, head_count
):
    qkv_weight, out_weight, up_weight, down_weight, vector_low = section_weights
    vectors = vector_low.astype(jnp.float32)
    self_saved, cross_saved, feed_saved = saved
    grad_state, grad_up, grad_down, feed_vectors = feed_backward(
        grad_output, feed_saved, vectors, up_weight, down_weight
    )

    def with_cross():
        return cross_backward(grad_state, cross_saved, image_low, cross_weights, head_count)

    def without_cross():
        return (
            grad_state,
            tuple((jnp.zeros(weight.shape, jnp.float32) for weight in cross_weights)),
        )

    grad_state, cross_grads = lax.cond(joining, with_cross, without_cross)
    grad_state, grad_qkv, grad_out, self_vectors = self_backward(
        grad_state, self_saved, vectors, qkv_weight, out_weight, head_count
    )
    section_grads = (
        grad_qkv,
        grad_out,
        grad_up,
        grad_down,
        jnp.concatenate([self_vectors, feed_vectors], axis=0),
    )
    return (grad_state, section_grads, cross_grads)


def fetch_weights(section_parts, cross_parts, pipe_place, half_pipe):
    for bit_index in range(half_pipe.bit_length() - 1):
        partner = jax.tree.map(
            lambda part, own: part.astype(own.dtype),
            partner_2(shortened(section_parts), "pipe", bit_index),
            section_parts,
        )
        lower_side = pipe_place // (1 << bit_index) % 2 == 0
        section_parts = tuple(
            (
                jnp.where(
                    lower_side,
                    jnp.concatenate([own_piece, their_piece], 0),
                    jnp.concatenate([their_piece, own_piece], 0),
                )
                for own_piece, their_piece in zip(section_parts, partner)
            )
        )
    section_parts = jax.tree.map(
        lambda part, own: part.astype(own.dtype),
        lax.all_gather(shortened(section_parts), "dp", axis=1, tiled=True),
        section_parts,
    )
    cross_parts = jax.tree.map(
        lambda part, own: part.astype(own.dtype),
        lax.all_gather(shortened(cross_parts), ("pipe", "dp"), axis=0, tiled=True),
        cross_parts,
    )
    return (section_parts, cross_parts)


def reduce_rows(shards, pipe_place, half_pipe):
    for bit_index in reversed(range(half_pipe.bit_length() - 1)):
        lower_side = pipe_place // (1 << bit_index) % 2 == 0
        outgoing = tuple(
            (
                jnp.where(lower_side, piece[piece.shape[0] // 2 :], piece[: piece.shape[0] // 2])
                for piece in shards
            )
        )
        staying = tuple(
            (
                jnp.where(lower_side, piece[: piece.shape[0] // 2], piece[piece.shape[0] // 2 :])
                for piece in shards
            )
        )
        incoming = jax.tree.map(
            lambda part, own: part.astype(own.dtype),
            partner_2(shortened(outgoing), "pipe", bit_index),
            outgoing,
        )
        shards = tuple((kept_rows + came_rows for kept_rows, came_rows in zip(staying, incoming)))
    return shards


def reduce_section(section_total, pipe_place, half_pipe):
    shards = jax.tree.map(
        lambda part: part.astype(jnp.float32),
        lax.psum_scatter(shortened(section_total), "dp", scatter_dimension=1, tiled=True),
    )
    return reduce_rows(shards, pipe_place, half_pipe)


def on_device(
    text_embed,
    image_feats,
    caption_len,
    phrase_len,
    box_count,
    patch_mask,
    attn_qkv,
    attn_out,
    ffn_up,
    ffn_down,
    layer_vectors,
    cross_query,
    cross_kv,
    cross_out,
    cross_vectors,
    cotangent,
):
    head_count = HEADS
    half_pipe = lax.axis_size("pipe") // 2
    pipe_place = lax.axis_index("pipe")
    joining = pipe_place >= half_pipe
    text_rows = text_embed.shape[1]
    slot_index = jnp.arange(phrase_len.shape[1], dtype=jnp.int32)
    phrase_total = jnp.sum(
        jnp.where(slot_index[None, :] < box_count[:, None], phrase_len, 0), axis=1
    )
    lengths = jnp.minimum(caption_len + phrase_total, text_rows)
    own_keep = (jnp.arange(text_rows, dtype=jnp.int32)[None, :] < lengths[:, None]).astype(
        jnp.bfloat16
    )
    first_patch = (jnp.arange(patch_mask.shape[1], dtype=jnp.int32) == 0).astype(jnp.int32)
    own_patch = jnp.maximum(patch_mask, first_patch[None, :]).astype(jnp.bfloat16)
    down_image, down_cot, down_keep, down_patch = shifted(
        (image_feats, cotangent, own_keep, own_patch), "pipe", half_pipe
    )
    up_embed, up_keep = shifted((text_embed, own_keep), "pipe", -half_pipe)
    keep_first = jnp.where(joining, down_keep, own_keep)
    keep_second = jnp.where(joining, own_keep, up_keep)
    text_first = text_embed.astype(jnp.float32)
    text_second = up_embed.astype(jnp.float32)
    section_parts = (attn_qkv, attn_out, ffn_up, ffn_down, layer_vectors)
    cross_parts = (cross_query, cross_kv, cross_out, cross_vectors)
    section_weights, cross_weights = fetch_weights(
        section_parts, cross_parts, pipe_place, half_pipe
    )

    def run_forward(state, key_keep, image_low, patch_keep):
        return layer_forward(
            state,
            key_keep,
            image_low,
            patch_keep,
            section_weights,
            cross_weights,
            joining,
            head_count,
        )[0]

    def send_forward(values):
        return shifted(values.astype(jnp.bfloat16), "pipe", half_pipe)

    blank_state = jnp.zeros_like(text_first)
    first_out = lax.cond(
        joining,
        lambda: blank_state,
        lambda: run_forward(text_first, keep_first, down_image, down_patch),
    )
    joining_first = send_forward(first_out).astype(jnp.float32)
    middle_state = jnp.where(joining, joining_first, text_second)
    middle_out = run_forward(
        middle_state, jnp.where(joining, keep_first, keep_second), down_image, down_patch
    )
    joining_second = send_forward(middle_out).astype(jnp.float32)
    last_out = lax.cond(
        joining,
        lambda: run_forward(joining_second, keep_second, image_feats, own_patch),
        lambda: blank_state,
    )
    returned = shifted(middle_out.astype(jnp.bfloat16), "pipe", -half_pipe).astype(middle_out.dtype)
    joined = jnp.where(joining, last_out, returned)
    section_weights, cross_weights = fetch_weights(
        section_parts, cross_parts, pipe_place, half_pipe
    )

    def run_backward(state, key_keep, image_low, patch_keep, grad_output):
        unused_output, saved = layer_forward(
            state,
            key_keep,
            image_low,
            patch_keep,
            section_weights,
            cross_weights,
            joining,
            head_count,
        )
        return layer_backward(
            grad_output, saved, image_low, section_weights, cross_weights, joining, head_count
        )

    def send_backward(values):
        return shifted(values.astype(jnp.bfloat16), "pipe", -half_pipe)

    grad_blank = (
        blank_state,
        jax.tree.map(lambda weight: jnp.zeros(weight.shape, jnp.float32), section_weights),
        jax.tree.map(lambda weight: jnp.zeros(weight.shape, jnp.float32), cross_weights),
    )
    back_first = lax.cond(
        joining,
        lambda: run_backward(
            joining_first, keep_first, down_image, down_patch, down_cot.astype(jnp.float32)
        ),
        lambda: grad_blank,
    )
    arrived_first = send_backward(back_first[0]).astype(jnp.float32)
    middle_grad = jnp.where(joining, cotangent.astype(jnp.float32), arrived_first)
    back_middle = run_backward(
        jnp.where(joining, joining_second, text_first),
        jnp.where(joining, keep_second, keep_first),
        image_feats,
        own_patch,
        middle_grad,
    )
    arrived_second = send_backward(back_middle[0]).astype(jnp.float32)
    back_last = lax.cond(
        joining,
        lambda: grad_blank,
        lambda: run_backward(text_second, keep_second, image_feats, own_patch, arrived_second),
    )
    sent_down = shifted(back_last[0].astype(jnp.bfloat16), "pipe", half_pipe).astype(jnp.float32)
    embed_grad = jnp.where(joining, sent_down, back_middle[0])
    section_total = jax.tree.map(
        lambda first_term, middle_term, last_term: first_term + middle_term + last_term,
        back_first[1],
        back_middle[1],
        back_last[1],
    )
    cross_total = jax.tree.map(
        lambda first_term, middle_term, last_term: first_term + middle_term + last_term,
        back_first[2],
        back_middle[2],
        back_last[2],
    )
    section_grads = reduce_section(section_total, pipe_place, half_pipe)
    cross_grads = lax.psum_scatter(cross_total, ("pipe", "dp"), scatter_dimension=0, tiled=True)
    return (
        joined,
        embed_grad,
        section_grads[0],
        section_grads[1],
        section_grads[2],
        section_grads[3],
        section_grads[4],
        cross_grads[0],
        cross_grads[1],
        cross_grads[2],
        cross_grads[3],
    )


def solution(mesh):
    in_specs = (
        P(("pipe", "dp"), None, None),
        P(("pipe", "dp"), None, None),
        P(("pipe", "dp")),
        P(("pipe", "dp"), None),
        P(("pipe", "dp")),
        P(("pipe", "dp"), None),
        P("pipe", "dp"),
        P("pipe", "dp"),
        P("pipe", "dp"),
        P("pipe", "dp"),
        P("pipe", "dp"),
        P(("pipe", "dp"), None),
        P(("pipe", "dp"), None),
        P(("pipe", "dp"), None),
        P(("pipe", "dp"), None),
        P(("pipe", "dp"), None, None),
    )
    out_specs = (
        P(("pipe", "dp"), None, None),
        P(("pipe", "dp"), None, None),
        P("pipe", "dp"),
        P("pipe", "dp"),
        P("pipe", "dp"),
        P("pipe", "dp"),
        P("pipe", "dp"),
        P(("pipe", "dp"), None),
        P(("pipe", "dp"), None),
        P(("pipe", "dp"), None),
        P(("pipe", "dp"), None),
    )
    return jax.shard_map(
        on_device, mesh=mesh, in_specs=in_specs, out_specs=out_specs, check_vma=False
    )
```

profile of v0, /device:TPU:0, one launch (start us, length us, event | category | flops | bytes accessed | tf_op | source)
XLA Modules:
  0.0 2240.7 jit_solution(11184434593293576072)
XLA Ops:
  23.2 6.2 collective-permute-start.4
  36.9 71.9 %all-gather.1 = bf16[32,24,5]{1,2,0:T(8,128)(2,1)S(1)} all-gather(bf16[1,24,5]{1,2,0:T(8,128)(2,1)S(1)} %bitcast.745), channel_id=1, replica_groups=mesh['pipe'=4,'dp'=8] {'pipe','dp'}, dimensions={0}, use_global_device_ids=true | all-gather | bytes 7920 | tf_op jit(solution)/shard_map/all_gather | solution.py:361
  112.2 30.4 %all-gather = bf16[8,96,12]{1,2,0:T(8,128)(2,1)S(1)} all-gather(bf16[1,96,12]{1,2,0:T(8,128)(2,1)S(1)} %fusion.588), channel_id=1, replica_groups=mesh['pipe'=4,'dp'=8] {'dp'}, dimensions={0}, use_global_device_ids=true | all-gather | bytes 20736 | tf_op jit(solution)/shard_map/all_gather | solution.py:356
  143.4 23.4 %all-gather.18.cloned.1.call-done = bf16[768,768]{1,0:T(8,128)(2,1)} async-done(((bf16[24,768]{1,0:T(8,128)(2,1)}), bf16[768,768]{1,0:T(8,128)(2,1)}) %all-gather.18.cloned.1.call-update) | async-done | bytes 1179664 | tf_op jit(solution)/shard_map/all_gather | solution.py:361
  166.8 60.8 %all-gather.14.cloned.1.call-done = bf16[1024,1536]{1,0:T(8,128)(2,1)} async-done(((bf16[32,1536]{1,0:T(8,128)(2,1)}), bf16[1024,1536]{1,0:T(8,128)(2,1)}) %all-gather.14.cloned.1.call-update) | async-done | bytes 3145744 | tf_op jit(solution)/shard_map/all_gather | solution.py:361
  227.5 66.6 %all-gather.10.cloned.1.call-done = bf16[768,2304]{0,1:T(8,128)(2,1)} async-done(((bf16[768,288]{0,1:T(8,128)(2,1)}), bf16[768,2304]{0,1:T(8,128)(2,1)}) %all-gather.10.cloned.1.call-update) | async-done | bytes 3538960 | tf_op jit(solution)/shard_map/all_gather | solution.py:356
  294.2 82.0 %all-gather.20.cloned.1.call-done = bf16[768,3072]{1,0:T(8,128)(2,1)} async-done(((bf16[768,384]{1,0:T(8,128)(2,1)}), bf16[768,3072]{1,0:T(8,128)(2,1)}) %all-gather.20.cloned.1.call-update) | async-done | bytes 4718608 | tf_op jit(solution)/shard_map/all_gather | solution.py:356
  376.2 80.9 %all-gather.22.cloned.1.call-done = bf16[3072,768]{0,1:T(8,128)(2,1)} async-done(((bf16[3072,96]{0,1:T(8,128)(2,1)}), bf16[3072,768]{0,1:T(8,128)(2,1)}) %all-gather.22.cloned.1.call-update) | async-done | bytes 4718608 | tf_op jit(solution)/shard_map/all_gather | solution.py:356
  457.1 64.8 %conditional.13 = (bf16[8,64,768]{2,1,0:T(8,128)(2,1)S(1)}) conditional(s32[]{:T(128)} %convert_element_type.713, (pred[]{:T(512)}, f32[8,64,768]{2,1,0:T(8,128)S(1)}, bf16[768,2304]{0,1:T(8,128)(2,1)}, bf16[12,768]{1,0:T(8,128)(2,1)}, bf16[8,64]{1,0:T(8,128)(2,1)}, /*index=5*/bf16[768,768]{0,1:T(8,128)(2,1)}, bf16[8,145,1024]{2,0,1:T(8,128)(2,1)}, ...), branch_computations={%region_1.14_spmd, %region_14.15_spmd} | conditional | flops 12597949440 | bytes 172321344 | solution.py:462
  485.9 15.9 fusion.197
  501.8 19.0 fusion.651
  527.0 14.1 collective-permute-done.8
  566.4 8.7 fusion.546
  575.1 19.2 fusion.683
  595.9 45.4 %collective-permute-start.11 = (bf16[8,64,768]{2,1,0:T(8,128)(2,1)}, bf16[8,64,768]{2,1,0:T(8,128)(2,1)}, u32[]{:S(2)}, u32[]{:S(2)}) collective-permute-start(bf16[8,64,768]{2,1,0:T(8,128)(2,1)} %add_convert_fusion.15), channel_id=1, source_target_pairs={{0,16},{8,24},{1,17},{9,25},{2,18},{10,26},{3,19},{11,27},{4,20},{... | collective-permute-start | bytes 2359304 | tf_op jit(solution)/shard_map/ppermute | solution.py:32
  641.5 30.0 %conditional.17 = (bf16[8,64,768]{2,1,0:T(8,128)(2,1)}, f32[768,2304]{0,1:T(8,128)}, f32[768,768]{1,0:T(8,128)}, f32[768,3072]{1,0:T(8,128)}, f32[12,768]{1,0:T(...) conditional(s32[]{:T(128)} %convert_element_type.713, ...), branch_computations={%region_53.54_spmd, %region_54.90_spmd} | conditional | flops 33926027264 | bytes 639708032 | solution.py:507
  699.1 17.3 conditional.16
  716.4 6.5 fusion.547
  722.9 14.3 multiply_convert_fusion.17
  737.3 6.2 fusion.686
  743.9 259.1 %collective-permute-done.14 = bf16[8,64,768]{2,1,0:T(8,128)(2,1)} collective-permute-done((bf16[8,64,768]{2,1,0:T(8,128)(2,1)}, bf16[8,64,768]{2,1,0:T(8,128)(2,1)}, u32[]{:S(2)}, u32[]{:S(2)}) %collective-permute-start.14) | collective-permute-done | bytes 786464 | tf_op jit(solution)/shard_map/ppermute | solution.py:32
  1008.2 8.4 convert_reduce_fusion.21
  1021.1 16.3 conditional.18
  1071.8 6.4 fusion.687
  1109.2 184.8 %collective-permute-done.15 = bf16[8,64,768]{2,1,0:T(8,128)(2,1)} collective-permute-done((bf16[8,64,768]{2,1,0:T(8,128)(2,1)}, bf16[8,64,768]{2,1,0:T(8,128)(2,1)}, u32[]{:S(2)}, u32[]{:S(2)}) %collective-permute-start.15) | collective-permute-done | bytes 786464 | tf_op jit(solution)/shard_map/ppermute | solution.py:32
  1296.4 198.1 %conditional.19 = (bf16[8,64,768]{2,1,0:T(8,128)(2,1)}, f32[768,2304]{0,1:T(8,128)}, f32[768,3072]{1,0:T(8,128)}, f32[12,768]{1,0:T(8,128)}, f32[1024,1536]{0,1:...) conditional(s32[]{:T(128)} %convert_element_type.713, ...), branch_computations={%region_105.141_spmd, %region_141.142_spmd} | conditional | flops 33924847616 | bytes 599671424 | solution.py:524
  1325.3 10.1 conditional.4
  1338.0 6.5 fusion.427
  1344.5 14.3 multiply_convert_fusion.13
  1372.0 8.1 convert_reduce_fusion.17
  1384.1 14.9 conditional.5
  1450.5 8.8 convolution_bitcast_fusion.13
  1475.1 6.9 convolution_bitcast_fusion.14
  1502.4 7.0 fusion.571
  1509.3 10.0 fusion.462
  1525.4 9.6 fusion.460
  1535.0 6.6 copy.767
  1547.4 9.5 fusion.458
  1568.9 6.5 copy.697
  1575.4 11.4 add_add_fusion.14
  1593.9 10.4 collective-permute-done.12
  1606.7 90.3 %collective-permute-start.16 = (bf16[8,64,768]{2,1,0:T(8,128)(2,1)S(1)}, bf16[8,64,768]{2,1,0:T(8,128)(2,1)S(1)}, u32[]{:S(2)}, u32[]{:S(2)}) collective-permute-start(bf16[8,64,768]{2,1,0:T(8,128)(2,1)S(1)} %copy-done.250), channel_id=1, source_target_pairs={{0,16},{8,24},{1,17},{9,25},{2,18},{10,26},{3,19},{11,27},{4,20},{... | collective-permute-start | bytes 2359304 | tf_op jit(solution)/shard_map/ppermute | solution.py:32
  1697.8 52.2 %all-reduce.6 = f32[768,5]{0,1:T(8,128)S(1)} all-reduce(f32[768,5]{0,1:T(8,128)S(1)} %add_add_fusion.21), channel_id=10, replica_groups=mesh['pipe'=4,'dp'=8] {'pipe','dp'}, use_global_device_ids=true, to_apply=%region_158.159.clone | all-reduce | flops 3840 | bytes 30720
  1758.8 47.6 %reduce-scatter.26.cloned.1.call-done = bf16[384,768]{1,0:T(8,128)(2,1)} async-done(((bf16[3072,768]{1,0:T(8,128)(2,1)}), bf16[384,768]{1,0:T(8,128)(2,1)}) %reduce-scatter.26.cloned.1.call-update) | async-done | bytes 589840
  1808.0 96.9 %reduce-scatter.18.cloned.1.call-done = bf16[3072,96]{0,1:T(8,128)(2,1)} async-done(((bf16[3072,768]{0,1:T(8,128)(2,1)}), bf16[3072,96]{0,1:T(8,128)(2,1)}) %reduce-scatter.18.cloned.1.call-update) | async-done | bytes 589840 | tf_op jit(solution)/shard_map/reduce_scatter | solution.py:394
  1908.9 100.7 %reduce-scatter.24.cloned.1.call-done = f32[24,768]{1,0:T(8,128)} async-done(((f32[768,768]{1,0:T(8,128)}), f32[24,768]{1,0:T(8,128)}) %reduce-scatter.24.cloned.1.call-update) | async-done | bytes 73744 | tf_op jit(solution)/shard_map/reduce_scatter | solution.py:544
  2009.7 104.6 %reduce-scatter.20.cloned.1.call-done = f32[24,768]{1,0:T(8,128)} async-done(((f32[768,768]{1,0:T(8,128)}), f32[24,768]{1,0:T(8,128)}) %reduce-scatter.20.cloned.1.call-update) | async-done | bytes 73744 | tf_op jit(solution)/shard_map/reduce_scatter | solution.py:544
  2114.3 119.3 %reduce-scatter.22.cloned.1.call-done = f32[32,1536]{1,0:T(8,128)} async-done(((f32[1024,1536]{1,0:T(8,128)}), f32[32,1536]{1,0:T(8,128)}) %reduce-scatter.22.cloned.1.call-update) | async-done | bytes 196624 | tf_op jit(solution)/shard_map/reduce_scatter | solution.py:544
  (598 shorter events, 434.6 us)
Async XLA Ops:
  7.2 136.1 %all-gather.12.cloned.1.call-start = ((), (), s32[]{:S(2)}) async-start(), calls=%async_computation.9 | async-start | bytes 1327104 | tf_op jit(solution)/shard_map/all_gather | solution.py:356
  7.3 1.6 collective-permute-start.3
  10.6 132.7 %all-gather.16.cloned.1.call-start = ((), (), s32[]{:S(2)}) async-start(), calls=%async_computation.11 | async-start | bytes 1216512 | tf_op jit(solution)/shard_map/all_gather | solution.py:361
  11.4 155.4 %all-gather.18.cloned.1.call-start = ((), (), s32[]{:S(2)}) async-start(), calls=%async_computation.12 | async-start | bytes 1216512 | tf_op jit(solution)/shard_map/all_gather | solution.py:361
  12.1 215.4 %all-gather.14.cloned.1.call-start = ((), (), s32[]{:S(2)}) async-start(), calls=%async_computation.10 | async-start | bytes 3244032 | tf_op jit(solution)/shard_map/all_gather | solution.py:361
  12.7 281.5 %all-gather.10.cloned.1.call-start = ((), (), s32[]{:S(2)}) async-start(), calls=%async_computation.8 | async-start | bytes 3981312 | tf_op jit(solution)/shard_map/all_gather | solution.py:356
  12.7 1.8 collective-permute-start
  16.5 359.7 %all-gather.20.cloned.1.call-start = ((), (), s32[]{:S(2)}) async-start(), calls=%async_computation.13 | async-start | bytes 5308416 | tf_op jit(solution)/shard_map/all_gather | solution.py:356
  16.5 1.9 collective-permute-start.6
  20.4 436.6 %all-gather.22.cloned.1.call-start = ((), (), s32[]{:S(2)}) async-start(), calls=%async_computation.14 | async-start | bytes 5308416 | tf_op jit(solution)/shard_map/all_gather | solution.py:356
  20.5 1.6 collective-permute-start.7
  23.1 1726.9 %reduce-scatter.28.cloned.1.call-start = ((), (), s32[]{:S(2)}) async-start(), calls=%async_computation.22 | async-start | bytes 221184
  23.2 143.6 %collective-permute-start.4 = (bf16[8,145,1024]{2,0,1:T(8,128)(2,1)}, bf16[8,145,1024]{2,0,1:T(8,128)(2,1)}, u32[]{:S(2)}, u32[]{:S(2)}) collective-permute-start(bf16[8,145,1024]{2,0,1:T(8,128)(2,1)} %param.43), channel_id=1, source_target_pairs={{0,16},{8,24},{1,17},{9,25},{2,18},{10,26},{3,19},{11,27},{4,20},{... | collective-permute-start | bytes 7127048 | tf_op jit(solution)/shard_map/ppermute | solution.py:32
  29.6 80.6 %collective-permute-start.10 = (bf16[8,64]{1,0:T(8,128)(2,1)S(1)}, bf16[8,64]{1,0:T(8,128)(2,1)S(1)}, u32[]{:S(2)}, u32[]{:S(2)}) collective-permute-start(bf16[8,64]{1,0:T(8,128)(2,1)S(1)} %fusion.589), channel_id=1, source_target_pairs={{16,0},{24,8},{17,1},{25,9},{18,2},{26,10},{19,3},{27,11},{20,4},{... | collective-permute-start | bytes 3080 | tf_op jit(solution)/shard_map/ppermute | solution.py:32
  30.9 80.6 %collective-permute-start.2 = (bf16[8,64]{1,0:T(8,128)(2,1)S(1)}, bf16[8,64]{1,0:T(8,128)(2,1)S(1)}, u32[]{:S(2)}, u32[]{:S(2)}) collective-permute-start(bf16[8,64]{1,0:T(8,128)(2,1)S(1)} %fusion.589), channel_id=1, source_target_pairs={{0,16},{8,24},{1,17},{9,25},{2,18},{10,26},{3,19},{11,27},{4,20},{... | collective-permute-start | bytes 3080 | tf_op jit(solution)/shard_map/ppermute | solution.py:32
  35.5 76.7 %collective-permute-start.1 = (bf16[6,96]{1,0:T(8,128)(2,1)S(1)}, bf16[6,96]{1,0:T(8,128)(2,1)S(1)}, u32[]{:S(2)}, u32[]{:S(2)}) collective-permute-start(bf16[6,96]{1,0:T(8,128)(2,1)S(1)} %copy-done.241), channel_id=1, source_target_pairs={{0,8},{8,0},{16,24},{24,16},{1,9},{9,1},{17,25},{25,17},{2,10},{10... | collective-permute-start | bytes 3464 | tf_op jit(solution)/shard_map/ppermute | solution.py:26
  35.5 491.5 %collective-permute-start.9 = (bf16[8,64,768]{2,1,0:T(8,128)(2,1)}, bf16[8,64,768]{2,1,0:T(8,128)(2,1)}, u32[]{:S(2)}, u32[]{:S(2)}) collective-permute-start(bf16[8,64,768]{2,1,0:T(8,128)(2,1)} %param.42), channel_id=1, source_target_pairs={{16,0},{24,8},{17,1},{25,9},{18,2},{26,10},{19,3},{27,11},{20,4},{... | collective-permute-start | bytes 2359304 | tf_op jit(solution)/shard_map/ppermute | solution.py:32
  36.9 420.2 %copy-start.137 = (bf16[8,145]{1,0:T(8,128)(2,1)}, bf16[8,145]{1,0:T(8,128)(2,1)S(1)}, u32[]{:S(2)}) copy-start(bf16[8,145]{1,0:T(8,128)(2,1)S(1)} %maximum_convert_fusion) | copy-start | bytes 6964
  110.2 33.1 %collective-permute-start.5 = (bf16[8,145]{1,0:T(8,128)(2,1)S(1)}, bf16[8,145]{1,0:T(8,128)(2,1)S(1)}, u32[]{:S(2)}, u32[]{:S(2)}) collective-permute-start(bf16[8,145]{1,0:T(8,128)(2,1)S(1)} %maximum_convert_fusion), channel_id=1, source_target_pairs={{0,16},{8,24},{1,17},{9,25},{2,18},{10,26},{3,19},{11,27},{4,20},{... | collective-permute-start | bytes 6968 | tf_op jit(solution)/shard_map/ppermute | solution.py:32
  521.9 19.3 collective-permute-start.8
  523.2 118.2 %collective-permute-start.13 = (bf16[8,64,768]{2,1,0:T(8,128)(2,1)}, bf16[8,64,768]{2,1,0:T(8,128)(2,1)}, u32[]{:S(2)}, u32[]{:S(2)}) collective-permute-start(bf16[8,64,768]{2,1,0:T(8,128)(2,1)} %param.57), channel_id=1, source_target_pairs={{0,16},{8,24},{1,17},{9,25},{2,18},{10,26},{3,19},{11,27},{4,20},{... | collective-permute-start | bytes 2359304 | tf_op jit(solution)/shard_map/ppermute | solution.py:32
  526.9 48.2 %copy-start.157 = (f32[3072]{0:T(1024)}, f32[3072]{0:T(1024)S(1)}, u32[]{:S(2)}) copy-start(f32[3072]{0:T(1024)S(1)} %add.916) | copy-start | bytes 36868
  527.0 67.7 %copy-start.141 = (f32[768]{0:T(1024)}, f32[768]{0:T(1024)S(1)}, u32[]{:S(2)}) copy-start(f32[768]{0:T(1024)S(1)} %get-tuple-element.1268) | copy-start | bytes 9220
  595.9 76.9 %collective-permute-start.11 = (bf16[8,64,768]{2,1,0:T(8,128)(2,1)}, bf16[8,64,768]{2,1,0:T(8,128)(2,1)}, u32[]{:S(2)}, u32[]{:S(2)}) collective-permute-start(bf16[8,64,768]{2,1,0:T(8,128)(2,1)} %add_convert_fusion.15), channel_id=1, source_target_pairs={{0,16},{8,24},{1,17},{9,25},{2,18},{10,26},{3,19},{11,27},{4,20},{... | collective-permute-start | bytes 2359304 | tf_op jit(solution)/shard_map/ppermute | solution.py:32
  671.4 331.6 %collective-permute-start.14 = (bf16[8,64,768]{2,1,0:T(8,128)(2,1)}, bf16[8,64,768]{2,1,0:T(8,128)(2,1)}, u32[]{:S(2)}, u32[]{:S(2)}) collective-permute-start(bf16[8,64,768]{2,1,0:T(8,128)(2,1)} %get-tuple-element.521), channel_id=1, source_target_pairs={{16,0},{24,8},{17,1},{25,9},{18,2},{26,10},{19,3},{27,11},{20,4},{... | collective-permute-start | bytes 2359304 | tf_op jit(solution)/shard_map/ppermute | solution.py:32
  737.3 265.7 %copy-start.91 = (bf16[8,64,768]{2,1,0:T(8,128)(2,1)S(1)}, bf16[8,64,768]{2,1,0:T(8,128)(2,1)}, u32[]{:S(2)}) copy-start(bf16[8,64,768]{2,1,0:T(8,128)(2,1)} %param.57) | copy-start | bytes 2359300
  737.3 265.7 %copy-start.142 = (f32[768]{0:T(1024)S(1)}, f32[768]{0:T(1024)}, u32[]{:S(2)}) copy-start(f32[768]{0:T(1024)} %copy-done.141) | copy-start | bytes 9220
  1078.2 215.8 %collective-permute-start.15 = (bf16[8,64,768]{2,1,0:T(8,128)(2,1)}, bf16[8,64,768]{2,1,0:T(8,128)(2,1)}, u32[]{:S(2)}, u32[]{:S(2)}) collective-permute-start(bf16[8,64,768]{2,1,0:T(8,128)(2,1)} %get-tuple-element.1455), channel_id=1, source_target_pairs={{16,0},{24,8},{17,1},{25,9},{18,2},{26,10},{19,3},{27,11},{20,4},{... | collective-permute-start | bytes 2359304 | tf_op jit(solution)/shard_map/ppermute | solution.py:32
  1104.6 191.8 %copy-start.22 = (bf16[768,768]{0,1:T(8,128)(2,1)S(1)}, bf16[768,768]{0,1:T(8,128)(2,1)}, u32[]{:S(2)}) copy-start(bf16[768,768]{0,1:T(8,128)(2,1)} %all-gather.12.cloned.1.call-done) | copy-start | bytes 3538948
  1104.6 191.8 %copy-start.62 = (f32[8,64,768]{2,1,0:T(8,128)S(1)}, f32[8,64,768]{2,1,0:T(8,128)}, u32[]{:S(2)}) copy-start(f32[8,64,768]{2,1,0:T(8,128)} %convert_element_type.720) | copy-start | bytes 4718596
  1104.6 191.8 %copy-start.138 = (bf16[8,145]{1,0:T(8,128)(2,1)S(1)}, bf16[8,145]{1,0:T(8,128)(2,1)}, u32[]{:S(2)}) copy-start(bf16[8,145]{1,0:T(8,128)(2,1)} %copy-done.137) | copy-start | bytes 6964
  1104.6 191.8 %copy-start.177 = (bf16[8,64]{1,0:T(8,128)(2,1)S(1)}, bf16[8,64]{1,0:T(8,128)(2,1)}, u32[]{:S(2)}) copy-start(bf16[8,64]{1,0:T(8,128)(2,1)} %get-tuple-element.1307) | copy-start | bytes 3076
  1104.6 191.8 %copy-start.245 = (bf16[768,2304]{0,1:T(8,128)(2,1)S(1)}, bf16[768,2304]{0,1:T(8,128)(2,1)}, u32[]{:S(2)}) copy-start(bf16[768,2304]{0,1:T(8,128)(2,1)} %all-gather.10.cloned.1.call-done) | copy-start | bytes 10616836
  1497.8 254.9 %reduce-scatter.16.cloned.1.call-start = ((), (), s32[]{:S(2)}) async-start(), calls=%async_computation.16 | async-start | bytes 1327104 | tf_op jit(solution)/shard_map/reduce_scatter | solution.py:394
  1502.3 254.9 %reduce-scatter.14.cloned.1.call-start = ((), (), s32[]{:S(2)}) async-start(), calls=%async_computation.15 | async-start | bytes 3981312 | tf_op jit(solution)/shard_map/reduce_scatter | solution.py:394
  1519.4 287.0 %reduce-scatter.26.cloned.1.call-start = ((), (), s32[]{:S(2)}) async-start(), calls=%async_computation.21 | async-start | bytes 5308416
  1541.7 363.3 %reduce-scatter.18.cloned.1.call-start = ((), (), s32[]{:S(2)}) async-start(), calls=%async_computation.17 | async-start | bytes 5308416 | tf_op jit(solution)/shard_map/reduce_scatter | solution.py:394
  1557.0 452.7 %reduce-scatter.24.cloned.1.call-start = ((), (), s32[]{:S(2)}) async-start(), calls=%async_computation.20 | async-start | bytes 2433024 | tf_op jit(solution)/shard_map/reduce_scatter | solution.py:544
  1562.9 551.4 %reduce-scatter.20.cloned.1.call-start = ((), (), s32[]{:S(2)}) async-start(), calls=%async_computation.18 | async-start | bytes 2433024 | tf_op jit(solution)/shard_map/reduce_scatter | solution.py:544
  1568.8 664.8 %reduce-scatter.22.cloned.1.call-start = ((), (), s32[]{:S(2)}) async-start(), calls=%async_computation.19 | async-start | bytes 6488064 | tf_op jit(solution)/shard_map/reduce_scatter | solution.py:544
  1586.9 17.4 collective-permute-start.12
  1593.9 103.2 %copy-start.126 = (f32[768,5]{0,1:T(8,128)S(1)}, f32[768,5]{0,1:T(8,128)}, u32[]{:S(2)}) copy-start(f32[768,5]{0,1:T(8,128)} %get-tuple-element.552) | copy-start | bytes 46084
  1606.7 147.1 %collective-permute-start.16 = (bf16[8,64,768]{2,1,0:T(8,128)(2,1)S(1)}, bf16[8,64,768]{2,1,0:T(8,128)(2,1)S(1)}, u32[]{:S(2)}, u32[]{:S(2)}) collective-permute-start(bf16[8,64,768]{2,1,0:T(8,128)(2,1)S(1)} %copy-done.250), channel_id=1, source_target_pairs={{0,16},{8,24},{1,17},{9,25},{2,18},{10,26},{3,19},{11,27},{4,20},{... | collective-permute-start | bytes 2359304 | tf_op jit(solution)/shard_map/ppermute | solution.py:32
  1750.8 1.2 collective-permute-start.21
  1753.6 3.0 collective-permute-start.18
  1758.4 147.9 %collective-permute-start.17 = (bf16[384,288]{0,1:T(8,128)(2,1)S(1)}, bf16[384,288]{0,1:T(8,128)(2,1)S(1)}, u32[]{:S(2)}, u32[]{:S(2)}) collective-permute-start(bf16[384,288]{0,1:T(8,128)(2,1)S(1)} %select_convert_fusion.2), channel_id=1, source_target_pairs={{0,8},{8,0},{16,24},{24,16},{1,9},{9,1},{17,25},{25,17},{2,10},{10... | collective-permute-start | bytes 663560 | tf_op jit(solution)/shard_map/ppermute | solution.py:26
  1808.0 99.2 %collective-permute-start.19 = (bf16[384,384]{1,0:T(8,128)(2,1)S(1)}, bf16[384,384]{1,0:T(8,128)(2,1)S(1)}, u32[]{:S(2)}, u32[]{:S(2)}) collective-permute-start(bf16[384,384]{1,0:T(8,128)(2,1)S(1)} %select_convert_fusion.1), channel_id=1, source_target_pairs={{0,8},{8,0},{16,24},{24,16},{1,9},{9,1},{17,25},{25,17},{2,10},{10... | collective-permute-start | bytes 884744 | tf_op jit(solution)/shard_map/ppermute | solution.py:26
  1906.2 1.8 collective-permute-start.20
  (124 other events, 1035.8 us)
Sparse Core Ops, SparseCore 0:
  10.8 43.8 all-gather.11
  57.6 53.0 all-gather.15
  113.6 53.1 all-gather.17
  169.5 57.9 all-gather.13
  230.1 63.9 all-gather.9
  296.7 79.4 all-gather.19
  379.0 78.0 all-gather.21
  1497.9 60.7 reduce-scatter.27
  1562.1 62.9 reduce-scatter.15
  1628.6 78.1 reduce-scatter.13
  1710.4 95.9 reduce-scatter.25
  1809.9 94.9 reduce-scatter.17
  1910.8 98.7 reduce-scatter.23
  2016.2 98.0 reduce-scatter.19
  2120.4 113.2 reduce-scatter.21
where the time goes:
time: 2260 us; the launch traced here: 2240 us
  waiting for transfers between devices  1260 us (56%)
  matrix products  241 us (11%)
  local copies, waits for them, and re-layouts  221 us (10%)
  starting transfers between devices  161 us (7%)
  blocking collectives  154 us (7%)
  other arithmetic  152 us (7%)
  loops' own time  35.9 us (2%)
    ppermute x12, waiting for transfers between devices, shifted(): return lax.ppermute(block, axis, route)  468 us
    reduce_scatter x3, waiting for transfers between devices, on_device(): lax.psum_scatter(cross_total, ('pipe', 'dp'), scatter_dimension=0, tiled=...  325 us
    all_gather x4, waiting for transfers between devices, fetch_weights(): lax.all_gather(shortened(section_parts), 'dp', axis=1, tiled=True)  230 us
    ppermute x12, starting transfers between devices, shifted(): return lax.ppermute(block, axis, route)  158 us
    dot_general x16, matrix products, rows_product(): result = jnp.dot(flat, weight, preferred_element_type=jnp.float32)  111 us
    reduce_scatter x3, waiting for transfers between devices, reduce_section(): lax.psum_scatter(shortened(section_total), 'dp', scatter_dimension=1, til...  96.9 us
    all_gather x3, waiting for transfers between devices, fetch_weights(): lax.all_gather(shortened(cross_parts), ('pipe', 'dp'), axis=0, tiled=True)  84.2 us
    another operation x43, local copies, waits for them, and re-layouts  76.1 us
  transfers between devices with their start and end apart: 37, of which 19 were waited for; matrix products, arithmetic and copies ran while one was open for 15% of the time, Pallas kernels for 0%

commit v1 on v0

v1 whole, which is shorter than its diff:
```python
from functools import partial

import jax
import jax.numpy as jnp
import numpy as np
from jax import lax
from jax.sharding import PartitionSpec as P

HEADS = 12


NORM_EPS = 1e-12
MASK_FILL = -1000000000.0


def rows_product(inputs, weight):
    flat = inputs.reshape(-1, inputs.shape[-1])
    result = jnp.dot(flat, weight, preferred_element_type=jnp.float32)
    return result.reshape(inputs.shape[:-1] + (weight.shape[1],))


def input_grad(grads, weight):
    flat = grads.reshape(-1, grads.shape[-1])
    result = lax.dot_general(
        flat, weight, (((1,), (1,)), ((), ())), preferred_element_type=jnp.float32
    )
    return result.reshape(grads.shape[:-1] + (weight.shape[0],))


def row_total(grads):
    return jnp.sum(grads.reshape(-1, grads.shape[-1]).astype(jnp.float32), axis=0)


def norm_forward(summed, gain, offset):
    center = summed - jnp.mean(summed, axis=-1, keepdims=True)
    scale_row = lax.rsqrt(jnp.mean(center * center, axis=-1, keepdims=True) + NORM_EPS)
    normed = center * scale_row
    return (normed * gain + offset, (normed, scale_row))


def norm_backward(grad_output, norm_saved, gain):
    normed, scale_row = norm_saved
    flat_grad = grad_output.reshape(-1, grad_output.shape[-1])
    grad_gain = jnp.sum(flat_grad * normed.reshape(flat_grad.shape), axis=0)
    grad_offset = jnp.sum(flat_grad, axis=0)
    scaled = grad_output * gain
    grad_input = scale_row * (
        scaled
        - jnp.mean(scaled, axis=-1, keepdims=True)
        - normed * jnp.mean(scaled * normed, axis=-1, keepdims=True)
    )
    return (grad_input, grad_gain, grad_offset)


def attention_forward(queries, keys, values, key_keep, head_count):
    samples, query_rows, model_width = queries.shape
    head_size = model_width // head_count
    query_heads = queries.reshape(samples, query_rows, head_count, head_size)
    key_heads = keys.reshape(samples, keys.shape[1], head_count, head_size)
    value_heads = values.reshape(samples, values.shape[1], head_count, head_size)
    scores = jnp.einsum(
        "sqhd,skhd->shqk", query_heads, key_heads, preferred_element_type=jnp.float32
    ) * head_size ** (-0.5)
    scores = jnp.where(key_keep[:, None, None, :] > 0, scores, MASK_FILL)
    row_top = jnp.max(scores, axis=-1, keepdims=True)
    exponent = jnp.exp(scores - row_top)
    attention = exponent / jnp.sum(exponent, axis=-1, keepdims=True)
    mixed = jnp.einsum(
        "shqk,skhd->sqhd",
        attention.astype(jnp.bfloat16),
        value_heads,
        preferred_element_type=jnp.float32,
    )
    return (mixed.reshape(samples, query_rows, model_width), attention)


def attention_backward(grad_mixed, attention, queries, keys, values, head_count):
    samples, query_rows, model_width = queries.shape
    key_rows = keys.shape[1]
    head_size = model_width // head_count
    query_heads = queries.reshape(samples, query_rows, head_count, head_size)
    key_heads = keys.reshape(samples, key_rows, head_count, head_size)
    value_heads = values.reshape(samples, key_rows, head_count, head_size)
    grad_heads = grad_mixed.reshape(samples, query_rows, head_count, head_size)
    grad_values = jnp.einsum(
        "shqk,sqhd->skhd",
        attention.astype(jnp.bfloat16),
        grad_heads,
        preferred_element_type=jnp.float32,
    )
    grad_attention = jnp.einsum(
        "sqhd,skhd->shqk", grad_heads, value_heads, preferred_element_type=jnp.float32
    )
    grad_scores = attention * (
        grad_attention - jnp.sum(grad_attention * attention, axis=-1, keepdims=True)
    )
    grad_scores = grad_scores.astype(jnp.bfloat16)
    grad_queries = jnp.einsum(
        "shqk,skhd->sqhd", grad_scores, key_heads, preferred_element_type=jnp.float32
    ) * head_size ** (-0.5)
    grad_keys = jnp.einsum(
        "shqk,sqhd->skhd", grad_scores, query_heads, preferred_element_type=jnp.float32
    ) * head_size ** (-0.5)
    return (
        grad_queries.reshape(samples, query_rows, model_width),
        grad_keys.reshape(samples, key_rows, model_width),
        grad_values.reshape(samples, key_rows, model_width),
    )


def mm(x, wt):
    flat = x.reshape(-1, x.shape[-1])
    y = lax.dot_general(flat, wt, (((1,), (1,)), ((), ())), preferred_element_type=jnp.float32)
    return y.reshape(x.shape[:-1] + (wt.shape[0],))


def mm_back(dy, wt):
    flat = dy.reshape(-1, dy.shape[-1])
    dx = jnp.dot(flat, wt, preferred_element_type=jnp.float32)
    return dx.reshape(dy.shape[:-1] + (wt.shape[1],))


def wgrad(dy, x):
    return lax.dot_general(
        dy.reshape(-1, dy.shape[-1]),
        x.reshape(-1, x.shape[-1]),
        (((0,), (0,)), ((), ())),
        preferred_element_type=jnp.float32,
    ).astype(jnp.bfloat16)


def self_forward(state, key_keep, vec, qkv, out):
    width = state.shape[-1]
    low = state.astype(jnp.bfloat16)
    bias = jnp.concatenate([vec[0], jnp.zeros((width,), jnp.float32), vec[1]])
    proj = (mm(low, qkv) + bias).astype(jnp.bfloat16)
    mixed, attention = attention_forward(
        proj[..., :width], proj[..., width : 2 * width], proj[..., 2 * width :], key_keep, HEADS
    )
    mixed = mixed.astype(jnp.bfloat16)
    y, saved = norm_forward(state + (mm(mixed, out) + vec[2]), vec[3], vec[4])
    return y, (low, proj, attention, mixed, saved)


def self_backward(dy, saved, vec, qkv, out):
    low, proj, attention, mixed, norm_saved = saved
    width = low.shape[-1]
    du, d_gain, d_offset = norm_backward(dy, norm_saved, vec[3])
    db = du.astype(jnp.bfloat16)
    g_out = wgrad(db, mixed)
    dmixed = mm_back(db, out).astype(jnp.bfloat16)
    dq, dk, dv = attention_backward(
        dmixed, attention, proj[..., :width], proj[..., width : 2 * width], proj[..., 2 * width :], HEADS
    )
    dproj = jnp.concatenate([dq, dk, dv], axis=-1).astype(jnp.bfloat16)
    g_qkv = wgrad(dproj, low)
    totals = row_total(dproj)
    dx = du + mm_back(dproj, qkv)
    g_vec = [totals[:width], totals[2 * width :], row_total(db), d_gain, d_offset]
    return dx, g_qkv, g_out, g_vec


def cross_forward(state, image, patch_keep, vec, wq, wkv, wo):
    width = state.shape[-1]
    low = state.astype(jnp.bfloat16)
    q = (rows_product(low, wq) + vec[0]).astype(jnp.bfloat16)
    kv_bias = jnp.concatenate([jnp.zeros((width,), jnp.float32), vec[1]])
    kv = (rows_product(image, wkv) + kv_bias).astype(jnp.bfloat16)
    mixed, attention = attention_forward(q, kv[..., :width], kv[..., width:], patch_keep, HEADS)
    mixed = mixed.astype(jnp.bfloat16)
    y, saved = norm_forward(state + (rows_product(mixed, wo) + vec[2]), vec[3], vec[4])
    return y, (low, q, kv, attention, mixed, saved)


def cross_backward(dy, saved, image, vec, wq, wo):
    low, q, kv, attention, mixed, norm_saved = saved
    width = low.shape[-1]
    du, d_gain, d_offset = norm_backward(dy, norm_saved, vec[3])
    db = du.astype(jnp.bfloat16)
    g_out = wgrad(mixed, db)
    dmixed = input_grad(db, wo).astype(jnp.bfloat16)
    dq, dk, dv = attention_backward(dmixed, attention, q, kv[..., :width], kv[..., width:], HEADS)
    dq = dq.astype(jnp.bfloat16)
    dkv = jnp.concatenate([dk, dv], axis=-1).astype(jnp.bfloat16)
    g_q = wgrad(low, dq)
    g_kv = wgrad(image, dkv)
    g_vec = [row_total(dq), row_total(dkv)[width:], row_total(db), d_gain, d_offset]
    return du + input_grad(dq, wq), g_q, g_kv, g_out, g_vec


def gelu_pair(h):
    value, pull = jax.vjp(partial(jax.nn.gelu, approximate=False), h)
    return value.astype(jnp.bfloat16), pull(jnp.ones_like(h))[0].astype(jnp.bfloat16)


def feed_forward(state, vec, up, down):
    low = state.astype(jnp.bfloat16)
    act, slope = gelu_pair(mm(low, up) + vec[8:12].reshape(-1))
    y, saved = norm_forward(state + (mm(act, down) + vec[5]), vec[6], vec[7])
    return y, (low, act, slope, saved)


def feed_backward(dy, saved, vec, up, down):
    low, act, slope, norm_saved = saved
    du, d_gain, d_offset = norm_backward(dy, norm_saved, vec[6])
    db = du.astype(jnp.bfloat16)
    g_down = wgrad(db, act)
    dh = (mm_back(db, down) * slope).astype(jnp.bfloat16)
    g_up = wgrad(dh, low)
    dx = du + mm_back(dh, up)
    g_vec = [row_total(db), d_gain, d_offset, row_total(dh)]
    return dx, g_up, g_down, g_vec


def lane_slices(a, lanes):
    return jnp.concatenate([a[:, i : i + lanes] for i in range(0, a.shape[1], lanes)], axis=0)


def lane_join(a, count):
    rows = a.shape[-2] // count
    return jnp.concatenate([a[..., i * rows : (i + 1) * rows, :] for i in range(count)], axis=-1)


def pad_lanes(a, lanes):
    return jnp.pad(a, ((0, 0), (0, lanes - a.shape[1])))


def on_device(
    text_embed,
    image_feats,
    caption_len,
    phrase_len,
    box_count,
    patch_mask,
    attn_qkv,
    attn_out,
    ffn_up,
    ffn_down,
    layer_vectors,
    cross_query,
    cross_kv,
    cross_out,
    cross_vectors,
    cotangent,
):
    n_pipe, n_dp = lax.axis_size("pipe"), lax.axis_size("dp")
    half = n_pipe // 2
    width = text_embed.shape[-1]
    text_rows = text_embed.shape[1]
    lanes = attn_qkv.shape[0]
    everyone = ("pipe", "dp")
    slots = jnp.arange(phrase_len.shape[1], dtype=jnp.int32)
    phrase_total = jnp.sum(jnp.where(slots[None, :] < box_count[:, None], phrase_len, 0), axis=1)
    lengths = jnp.minimum(caption_len + phrase_total, text_rows)
    text_keep = (jnp.arange(text_rows, dtype=jnp.int32)[None, :] < lengths[:, None]).astype(jnp.float32)
    first_patch = (jnp.arange(patch_mask.shape[1], dtype=jnp.int32) == 0).astype(jnp.int32)
    patch_keep = jnp.maximum(patch_mask, first_patch[None, :]).astype(jnp.float32)

    k_down = ffn_down.shape[0] // lanes
    k_q = width // lanes
    k_kv = cross_kv.shape[1] // lanes
    parts = [
        attn_qkv.T,
        attn_out.T,
        ffn_up.T,
        lane_slices(ffn_down.T, lanes),
        lane_slices(cross_query, lanes),
        lane_slices(cross_kv, lanes),
        lane_slices(cross_out, lanes),
        pad_lanes(layer_vectors, lanes),
        pad_lanes(cross_vectors.T, lanes),
    ]
    counts = [p.shape[0] for p in parts]
    ends = np.cumsum(counts)
    pack = jnp.concatenate(parts, axis=0)
    whole = lax.all_gather(pack, everyone, axis=0, tiled=False)
    whole = whole.reshape(n_pipe, n_dp, pack.shape[0], lanes)

    def part(i):
        return whole[:, :, ends[i] - counts[i] : ends[i]]

    def section(piece, layer):
        piece = piece[layer * half : (layer + 1) * half]
        piece = jnp.moveaxis(piece, 0, 2)
        return piece.reshape(n_dp * piece.shape[1], half * piece.shape[-1])

    def section_vectors(layer):
        v = part(7)[layer * half : (layer + 1) * half, :, :, : layer_vectors.shape[1]]
        return jnp.moveaxis(v, 1, 2).reshape(12, width).astype(jnp.float32)

    layers = []
    for layer in range(2):
        layers.append(
            (
                section(part(0), layer),
                section(part(1), layer),
                section(part(2), layer),
                section(lane_join(part(3), k_down), layer),
                section_vectors(layer),
            )
        )
    wq = lane_join(part(4), k_q).reshape(width, width)
    wkv = lane_join(part(5), k_kv).reshape(-1, 2 * width)
    wo = lane_join(part(6), k_q).reshape(width, width)
    cvec = part(8)[..., : cross_vectors.shape[0]].reshape(n_pipe * n_dp, 5, -1)
    cvec = jnp.moveaxis(cvec, 1, 0).reshape(5, width).astype(jnp.float32)

    qkv, out, up, down, vec = layers[0]
    state, s_self = self_forward(text_embed.astype(jnp.float32), text_keep, vec, qkv, out)
    state, s_feed = feed_forward(state, vec, up, down)
    passed = state.astype(jnp.bfloat16).astype(jnp.float32)
    qkv2, out2, up2, down2, vec2 = layers[1]
    state, s_self2 = self_forward(passed, text_keep, vec2, qkv2, out2)
    state, s_cross = cross_forward(state, image_feats, patch_keep, cvec, wq, wkv, wo)
    joined, s_feed2 = feed_forward(state, vec2, up2, down2)

    grad = cotangent.astype(jnp.float32)
    grad, g_up2, g_down2, v_feed2 = feed_backward(grad, s_feed2, vec2, up2, down2)
    grad, g_cq, g_ckv, g_co, g_cvec = cross_backward(grad, s_cross, image_feats, cvec, wq, wo)
    grad, g_qkv2, g_out2, v_self2 = self_backward(grad, s_self2, vec2, qkv2, out2)
    grad = grad.astype(jnp.bfloat16).astype(jnp.float32)
    grad, g_up1, g_down1, v_feed1 = feed_backward(grad, s_feed, vec, up, down)
    embed_grad, g_qkv1, g_out1, v_self1 = self_backward(grad, s_self, vec, qkv, out)

    def split(first, second):
        both = jnp.stack([first, second])
        rows = both.shape[1] // n_dp
        k = both.shape[2] // (half * lanes)
        both = both.reshape(2, n_dp, rows, half, k, lanes)
        return both.transpose(0, 3, 1, 4, 2, 5).reshape(n_pipe, n_dp, k * rows, lanes)

    def split_cross(g):
        rows = g.shape[0] // (n_pipe * n_dp)
        k = g.shape[1] // lanes
        g = g.reshape(n_pipe, n_dp, rows, k, lanes)
        return jnp.moveaxis(g, 3, 2).reshape(n_pipe, n_dp, k * rows, lanes)

    def split_vectors(v_self, v_feed):
        v = jnp.concatenate([jnp.stack(v_self + v_feed[:3]), v_feed[3].reshape(4, width)], axis=0)
        v = v.reshape(half, 12 // half, n_dp, width // n_dp)
        v = jnp.moveaxis(v, 2, 1)
        return jnp.pad(v, ((0, 0), (0, 0), (0, 0), (0, lanes - v.shape[-1])))

    cv = jnp.stack(g_cvec).reshape(5, n_pipe, n_dp, width // (n_pipe * n_dp))
    cv = jnp.moveaxis(cv, 0, 2)
    cv = jnp.pad(cv, ((0, 0), (0, 0), (0, 0), (0, lanes - cv.shape[-1])))
    vs = jnp.concatenate([split_vectors(v_self1, v_feed1), split_vectors(v_self2, v_feed2)], axis=0)
    packed = jnp.concatenate(
        [
            split(g_qkv1, g_qkv2),
            split(g_out1, g_out2),
            split(g_up1, g_up2),
            split(g_down1, g_down2),
            split_cross(g_cq),
            split_cross(g_ckv),
            split_cross(g_co),
            vs.astype(jnp.bfloat16),
            cv.astype(jnp.bfloat16),
        ],
        axis=2,
    )
    mine = lax.psum_scatter(packed.reshape(-1, lanes), everyone, scatter_dimension=0, tiled=True)
    mine = mine.astype(jnp.float32)
    got = [mine[ends[i] - counts[i] : ends[i]] for i in range(len(counts))]
    return (
        joined,
        embed_grad,
        got[0].T,
        got[1].T,
        got[2].T,
        lane_join(got[3], k_down).T,
        got[7][:, : layer_vectors.shape[1]],
        lane_join(got[4], k_q),
        lane_join(got[5], k_kv),
        lane_join(got[6], k_q),
        got[8][:, : cross_vectors.shape[0]].T,
    )


def solution(mesh):
    in_specs = (
        P(("pipe", "dp"), None, None),
        P(("pipe", "dp"), None, None),
        P(("pipe", "dp")),
        P(("pipe", "dp"), None),
        P(("pipe", "dp")),
        P(("pipe", "dp"), None),
        P("pipe", "dp"),
        P("pipe", "dp"),
        P("pipe", "dp"),
        P("pipe", "dp"),
        P("pipe", "dp"),
        P(("pipe", "dp"), None),
        P(("pipe", "dp"), None),
        P(("pipe", "dp"), None),
        P(("pipe", "dp"), None),
        P(("pipe", "dp"), None, None),
    )
    out_specs = (
        P(("pipe", "dp"), None, None),
        P(("pipe", "dp"), None, None),
        P("pipe", "dp"),
        P("pipe", "dp"),
        P("pipe", "dp"),
        P("pipe", "dp"),
        P("pipe", "dp"),
        P(("pipe", "dp"), None),
        P(("pipe", "dp"), None),
        P(("pipe", "dp"), None),
        P(("pipe", "dp"), None),
    )
    return jax.shard_map(
        on_device, mesh=mesh, in_specs=in_specs, out_specs=out_specs, check_vma=False
    )
```

time: 2260 us -> 1950 us (0.86)
  waiting for transfers between devices: 1260 us -> 198 us
  blocking collectives: 154 us -> 730 us
  local copies, waits for them, and re-layouts: 221 us -> 700 us
  starting transfers between devices: 161 us -> 2.17 us
  other arithmetic: 152 us -> 92.8 us
  matrix products: 241 us -> 183 us
  loops' own time: 35.9 us -> 0 us
    unnamed x1, blocking collectives: 52.2 us -> 730 us
    ppermute x22 -> x0, waiting for transfers between devices: 474 us -> none  [the longest x12 468 us: shifted(): return lax.ppermute(block, axis, route)]
    reduce_scatter x6 -> x0, waiting for transfers between devices: 422 us -> none  [the longest x3 325 us: on_device(): lax.psum_scatter(cross_total, ('pipe', 'dp'), scatter_dimension=0, tiled=...]
    concatenate x14 -> x19, local copies, waits for them, and re-layouts: 40.3 us -> 244 us  [the longest x1 177 us: on_device(): jnp.concatenate([split(g_qkv1, g_qkv2), split(g_out1, g_out2), split(g_up...]
    ppermute x22 -> x0, starting transfers between devices: 161 us -> none  [the longest x12 158 us: shifted(): return lax.ppermute(block, axis, route)]
    reshape x2 -> x24, local copies, waits for them, and re-layouts: 0.73 us -> 136 us  [the longest x8 63 us: section(): return piece.reshape(n_dp * piece.shape[1], half * piece.shape[-1])]
    all_gather x7 -> x1, waiting for transfers between devices: 314 us -> 194 us  [on_device(): whole = lax.all_gather(pack, everyone, axis=0, tiled=False)]
    dot_general x16 -> x3, matrix products: 111 us -> 8.84 us  [rows_product(): result = jnp.dot(flat, weight, preferred_element_type=jnp.float32)]
  transfers between devices with their start and end apart: 37 -> 2, of which waited for: 19 -> 2; matrix products, arithmetic and copies ran while one was open for 15% -> 1% of each run, Pallas kernels for 0% -> 0%
where the time goes in v1:
time: 1950 us; the launch traced here: 1920 us
  blocking collectives  730 us (37%)
  local copies, waits for them, and re-layouts  700 us (36%)
  waiting for transfers between devices  198 us (10%)
  matrix products  183 us (9%)
  other arithmetic  92.8 us (5%)
    unnamed x1, blocking collectives  730 us
    all_gather x1, waiting for transfers between devices, on_device(): whole = lax.all_gather(pack, everyone, axis=0, tiled=False)  194 us
    concatenate x1, local copies, waits for them, and re-layouts, on_device(): jnp.concatenate([split(g_qkv1, g_qkv2), split(g_out1, g_out2), split(g_up...  177 us
    another operation x16, local copies, waits for them, and re-layouts, split(): both = jnp.stack([first, second])  97.8 us
    transpose x12, local copies, waits for them, and re-layouts, section(): piece = jnp.moveaxis(piece, 0, 2)  78.5 us
    reshape x8, local copies, waits for them, and re-layouts, section(): return piece.reshape(n_dp * piece.shape[1], half * piece.shape[-1])  63 us
    dot_general x11, matrix products, wgrad(): lax.dot_general(dy.reshape(-1, dy.shape[-1]), x.reshape(-1, x.shape[-1]),...  44.6 us
    dot_general x8, matrix products, mm_back(): dx = jnp.dot(flat, wt, preferred_element_type=jnp.float32)  42 us
  transfers between devices with their start and end apart: 2, of which 2 were waited for; matrix products, arithmetic and copies ran while one was open for 1% of the time, Pallas kernels for 0%

profile of v1, /device:TPU:0, one launch (start us, length us, event | category | flops | bytes accessed | tf_op | source)
XLA Modules:
  0.0 1923.3 jit_solution(3288248741076931580)
XLA Ops:
  12.4 13.9 concatenate.112
  33.0 194.3 %all-gather.4.cloned.1.call-done = bf16[32,1387,384]{2,1,0:T(8,128)(2,1)} async-done(((bf16[1,1387,384]{2,1,0:T(8,128)(2,1)}), bf16[32,1387,384]{2,1,0:T(8,128)(2,1)}) %all-gather.4.cloned.1.call-update) | async-done | bytes 34086928 | tf_op jit(solution)/shard_map/all_gather | solution.py:276
  228.8 8.9 slice_bitcast_fusion.3
  244.8 6.8 slice_bitcast_fusion.4
  255.0 6.8 fusion.115
  262.5 9.3 copy.233
  271.8 11.5 reshape.636
  286.3 5.9 convolution_bitcast_fusion
  292.3 6.9 reshape.593
  308.3 9.4 copy.217
  317.7 11.6 reshape.630
  329.3 5.6 copy.209
  372.8 9.3 copy.218
  382.1 11.8 reshape.631
  393.9 6.4 fusion.53
  400.4 15.4 multiply_convert_fusion.5
  468.3 7.2 fusion.135
  482.0 9.6 copy.234
  491.5 11.7 reshape.637
  503.3 6.4 fusion.54
  509.7 14.3 multiply_convert_fusion.4
  532.0 7.4 fusion.138
  539.3 5.8 multiply_reduce_fusion.3
  552.5 6.6 multiply_reduce_fusion
  607.3 6.4 fusion.42
  615.0 9.3 fusion.139
  710.4 7.9 stack.119
  726.5 7.9 stack.118
  750.9 10.1 stack.125
  761.0 5.4 copy.270
  766.4 10.3 stack.124
  776.7 5.3 copy.269
  782.0 9.6 stack.128
  791.6 5.3 copy.272
  797.0 9.7 stack.127
  806.6 5.4 copy.271
  825.0 9.5 fusion.21
  839.5 6.3 reshape.612
  889.4 5.6 copy.292
  895.0 6.1 concatenate.141
  904.8 6.1 concatenate.140
  923.0 5.8 pad_maximum_fusion.3
  930.5 8.4 pad_maximum_fusion.1
  938.9 8.6 pad_maximum_fusion.2
  948.4 176.7 %concatenate.143 = bf16[4,8,1387,384]{3,2,1,0:T(8,128)(2,1)} concatenate(bf16[4,8,288,384]{3,2,1,0:T(8,128)(2,1)} %bitcast.287, bf16[4,8,96,384]{3,2,1,0:T(8,128)(2,1)} %bitcast.296, bf16[4,8,384,384]{3,2,1,0:T(8,128)(2,1)} %bitcast.276, bf16[4,8,384,384]{3,2,1,0:T(8,128)(2,1)} %bitcast.277, bf16[4,8,48,384]{3,2,1,0:T(8,128)(2,1)} %bitcast.322, ...), dimensions={2} | concatenate | bytes 68173824 | tf_op jit(solution)/shard_map/concatenate | solution.py:348
  1125.1 36.9 %reshape.620 = bf16[44384,384]{1,0:T(8,128)(2,1)} reshape(bf16[4,8,1387,384]{3,2,1,0:T(8,128)(2,1)} %concatenate.143) | data formatting | bytes 68173824 | tf_op jit(solution)/shard_map/reshape | solution.py:362
  1162.0 730.5 %fusion = bf16[1408,384]{1,0:T(8,128)(2,1)S(1)} fusion(bf16[44384,384]{1,0:T(8,128)(2,1)} %reshape.620), kind=kCustom, calls=%all-reduce-scatter | all-reduce-scatter fusion | flops 17301504 | bytes 35168256
  1894.8 6.1 convolution_add_fusion.2
  (580 shorter events, 404.6 us)
Async XLA Ops:
  7.2 220.1 %all-gather.4.cloned.1.call-start = ((), (), s32[]{:S(2)}) async-start(), calls=%async_computation | async-start | bytes 35278848 | tf_op jit(solution)/shard_map/all_gather | solution.py:276
  228.1 9.6 copy-start.82
  244.1 7.5 copy-start.83
  255.0 6.8 slice-start.8
  308.3 92.1 %copy-start.88 = (f32[3072]{0:T(1024)}, f32[3072]{0:T(1024)S(1)}, u32[]{:S(2)}) copy-start(f32[3072]{0:T(1024)S(1)} %add.252) | copy-start | bytes 36868
  346.7 10.5 copy-start.23
  348.8 11.6 copy-start.25
  348.8 8.4 copy-start.154
  365.1 50.8 %copy-start.94 = (f32[8,64]{1,0:T(8,128)}, f32[8,64]{1,0:T(8,128)S(1)}, u32[]{:S(2)}) copy-start(f32[8,64]{1,0:T(8,128)S(1)} %broadcast_multiply_fusion.14) | copy-start | bytes 6148
  365.5 50.4 %copy-start.115 = (f32[8,64]{1,0:T(8,128)}, f32[8,64]{1,0:T(8,128)S(1)}, u32[]{:S(2)}) copy-start(f32[8,64]{1,0:T(8,128)S(1)} %add_rsqrt_fusion.4) | copy-start | bytes 6148
  382.1 11.8 copy-start.18
  382.1 11.8 copy-start.108
  382.1 11.8 copy-start.132
  400.4 15.5 copy-start.16
  400.4 15.5 copy-start.32
  400.4 15.5 copy-start.136
  419.9 7.6 copy-start.92
  437.9 10.3 copy-start.27
  440.0 11.5 copy-start.29
  440.0 8.2 copy-start.155
  481.6 88.0 %copy-start.6 = (f32[8,64,768]{2,1,0:T(8,128)}, f32[8,64,768]{2,1,0:T(8,128)S(1)}, u32[]{:S(2)}) copy-start(f32[8,64,768]{2,1,0:T(8,128)S(1)} %get-tuple-element.179) | copy-start | bytes 4718596
  491.5 11.7 copy-start.90
  509.7 14.4 copy-start.33
  509.7 14.4 copy-start.134
  527.2 12.1 slice-start.6
  532.0 7.4 slice-start.7
  562.9 6.8 copy-start.98
  599.2 8.0 copy-start.5
  599.2 8.0 copy-start.93
  607.3 17.0 slice-start.4
  614.9 9.3 copy-start.74
  614.9 9.3 copy-start.19
  615.0 9.3 slice-start.5
  615.0 9.3 copy-start.95
  615.0 9.3 copy-start.109
  615.0 9.3 copy-start.116
  663.4 10.8 slice-start.2
  910.9 12.1 copy-start.2
  938.9 9.4 copy-start.9
  938.9 9.4 copy-start.81
  1162.0 732.8 %copy-start.21 = (f32[8,64,768]{2,1,0:T(8,128)S(1)}, f32[8,64,768]{2,1,0:T(8,128)}, u32[]{:S(2)}) copy-start(f32[8,64,768]{2,1,0:T(8,128)} %copy-done.17) | copy-start | bytes 4718596
  1162.0 732.8 %copy-start.65 = (bf16[8,64,768]{2,1,0:T(8,128)(2,1)S(1)}, bf16[8,64,768]{2,1,0:T(8,128)(2,1)}, u32[]{:S(2)}) copy-start(bf16[8,64,768]{2,1,0:T(8,128)(2,1)} %copy.262) | copy-start | bytes 2359300
  1162.0 732.8 %copy-start.96 = (f32[8,64]{1,0:T(8,128)S(1)}, f32[8,64]{1,0:T(8,128)}, u32[]{:S(2)}) copy-start(f32[8,64]{1,0:T(8,128)} %copy-done.94) | copy-start | bytes 6148
  1162.0 732.8 %copy-start.110 = (f32[768]{0:T(1024)S(1)}, f32[768]{0:T(1024)}, u32[]{:S(2)}) copy-start(f32[768]{0:T(1024)} %get-tuple-element.78) | copy-start | bytes 9220
  1162.0 732.8 %copy-start.117 = (f32[8,64]{1,0:T(8,128)S(1)}, f32[8,64]{1,0:T(8,128)}, u32[]{:S(2)}) copy-start(f32[8,64]{1,0:T(8,128)} %copy-done.115) | copy-start | bytes 6148
  1162.0 732.8 %copy-start.119 = (f32[8,64]{1,0:T(8,128)S(1)}, f32[8,64]{1,0:T(8,128)}, u32[]{:S(2)}) copy-start(f32[8,64]{1,0:T(8,128)} %copy-done.118) | copy-start | bytes 6148
  1162.0 732.8 %copy-start.121 = (f32[8,64]{1,0:T(8,128)S(1)}, f32[8,64]{1,0:T(8,128)}, u32[]{:S(2)}) copy-start(f32[8,64]{1,0:T(8,128)} %copy-done.120) | copy-start | bytes 6148
  1892.6 11.7 collective-permute-start
  (123 other events, 420.6 us)
Sparse Core Ops, SparseCore 0:
  26.5 200.6 all-gather.3

commit v2 on v1

v2 whole, which is shorter than its diff:
```python
from functools import partial

import jax
import jax.numpy as jnp
import numpy as np
from jax import lax
from jax.experimental import pallas as pl
from jax.experimental.pallas import tpu as pltpu
from jax.sharding import PartitionSpec as P

HEADS = 12
NORM_EPS = 1e-12
MASKED = -1e30
BF = jnp.bfloat16
F32 = jnp.float32
NT = (((1,), (1,)), ((), ()))
NN = (((1,), (0,)), ((), ()))
TN = (((0,), (0,)), ((), ()))
VMEM_BYTES = 58 * 2**20
TILE = 256


def dot(a, b, dims=NN):
    return lax.dot_general(a, b, dims, preferred_element_type=F32)


def span(start, size, unit=128):
    return pl.ds(pl.multiple_of(start, unit), size)


def tiles(count, body):
    def step(i, carry):
        body(i)
        return carry

    lax.fori_loop(0, count, step, 0)


def fetch(copies, sems):
    started = [pltpu.make_async_copy(s, t, sems.at[i]) for i, (s, t) in enumerate(copies)]
    for copy in started:
        copy.start()
    return started


def settle(started):
    for copy in started:
        copy.wait()


def placed(refs, where_ref, layout, target, lanes):
    if len(refs) == 1:
        return [(refs[0], target)]
    core, z, y = where_ref[0], where_ref[1], where_ref[2]
    copies = []
    for i, ref in enumerate(refs):
        c_rel, y_rel, z_rel = i // 8, (i // 4) % 2, i % 4
        block = lax.rem(z - z_rel + 4, 4) * 2 + lax.rem(y + y_rel, 2)
        side = lax.rem(core + c_rel, 2)
        for first, rows, shift in layout:
            place = target.at[
                span(block * rows, rows, 16),
                span(side * lanes + shift * ref.shape[1], ref.shape[1]),
            ]
            copies.append((ref.at[pl.ds(first, rows)], place))
    return copies


def norm_rows(u_ref, gain, offset, y_ref, low_ref, n_ref, r_ref):
    for i in range(0, u_ref.shape[0], 128):
        rows = pl.ds(i, 128)
        u = u_ref[rows, :]
        center = u - jnp.mean(u, axis=-1, keepdims=True)
        scale = lax.rsqrt(jnp.mean(center * center, axis=-1, keepdims=True) + NORM_EPS)
        normed = center * scale
        y = normed * gain + offset
        y_ref[rows, :] = y
        low_ref[rows, :] = y.astype(BF)
        n_ref[rows, :] = normed
        r_ref[rows, :] = scale


def norm_rows_back(dy_ref, n_ref, r_ref, gain, du_ref, db_ref):
    sums = [jnp.zeros((1, dy_ref.shape[1]), F32)] * 3
    for i in range(0, dy_ref.shape[0], 128):
        rows = pl.ds(i, 128)
        dy = dy_ref[rows, :].astype(F32)
        n = n_ref[rows, :]
        s = dy * gain
        du = r_ref[rows, :] * (
            s - jnp.mean(s, axis=-1, keepdims=True) - n * jnp.mean(s * n, axis=-1, keepdims=True)
        )
        db = du.astype(BF)
        du_ref[rows, :] = du
        db_ref[rows, :] = db
        sums = [
            sums[0] + jnp.sum(dy * n, axis=0, keepdims=True),
            sums[1] + jnp.sum(dy, axis=0, keepdims=True),
            sums[2] + jnp.sum(db.astype(F32), axis=0, keepdims=True),
        ]
    return sums


def split_heads(a):
    first = lax.broadcasted_iota(jnp.int32, a.shape, 1) < a.shape[1] // 2
    zero = jnp.zeros_like(a)
    return jnp.concatenate([jnp.where(first, a, zero), jnp.where(first, zero, a)], axis=0)


def join_heads(a):
    rows = a.shape[0] // 2
    first = lax.broadcasted_iota(jnp.int32, (rows, a.shape[1]), 1) < a.shape[1] // 2
    return jnp.where(first, a[:rows], a[rows:])


def softmax(scores, valid):
    scores = jnp.where(valid, scores * 0.125, MASKED)
    e = jnp.exp(scores - jnp.max(scores, axis=-1, keepdims=True))
    return (e / jnp.sum(e, axis=-1, keepdims=True)).astype(BF)


def score_back(weights, d_weights):
    a = weights.astype(F32)
    t = a * d_weights
    return (t - a * jnp.sum(t, axis=-1, keepdims=True)).astype(BF)


def project_and_norm(x_ref, o_ref, w_ref, dims, bias, gain, offset, outs):
    y_ref, low_ref, n_ref, r_ref = outs
    width = y_ref.shape[1]

    def tile(j):
        cols = span(j * TILE, TILE)
        w = w_ref[cols, :] if dims is NT else w_ref[:, cols]
        y_ref[:, cols] = dot(o_ref[...], w, dims)

    tiles(width // TILE, tile)
    for i in range(0, y_ref.shape[0], 128):
        rows = pl.ds(i, 128)
        y_ref[rows, :] = x_ref[rows, :].astype(F32) + (y_ref[rows, :] + bias)
    norm_rows(y_ref, gain, offset, y_ref, low_ref, n_ref, r_ref)


def self_forward_kernel(count, lengths, where_ref, x_ref, vec_ref, *rest):
    refs, rest = rest[:count], rest[count:]
    p_ref, a_ref, o_ref, y_ref, low_ref, n_ref, r_ref, qkv, out, bias_ref, sems, sems2 = rest
    width = x_ref.shape[1]
    n, m = qkv.shape[0] // 8, out.shape[0] // 8
    whole = count == 2
    first = fetch(placed(refs[:1] if whole else refs, where_ref, [(0, n, 0)], qkv, width // 2), sems)
    second = fetch(placed(refs[1:] if whole else refs, where_ref, [(n, m, 0)], out, width // 2), sems2)
    bias_ref[:, :width] = vec_ref[0:1, :]
    bias_ref[:, width : 2 * width] = jnp.zeros((1, width), F32)
    bias_ref[:, 2 * width :] = vec_ref[1:2, :]
    settle(first)

    def tile(j):
        cols = span(j * TILE, TILE)
        p_ref[:, cols] = (dot(x_ref[...], qkv[cols, :], NT) + bias_ref[:, cols]).astype(BF)

    tiles(3 * width // TILE, tile)
    pairs = width // 128
    row = lax.broadcasted_iota(jnp.int32, (256, 128), 0)
    lane = lax.broadcasted_iota(jnp.int32, (256, 128), 1)
    same = ((row // 64) % 2) == (lane // 64)
    key_lane = lax.broadcasted_iota(jnp.int32, (1, 128), 1)

    def attend(i):
        s, h = i // pairs, lax.rem(i, pairs)
        rows = span(s * 128, 128)
        q = p_ref[rows, span(h * 128, 128)]
        k = p_ref[rows, span(width + h * 128, 128)]
        v = p_ref[rows, span(2 * width + h * 128, 128)]
        length = jnp.where(key_lane < 64, lengths[2 * s], lengths[2 * s + 1])
        valid = same & (lax.rem(key_lane, 64) < length)
        a = softmax(dot(split_heads(q), k, NT), valid)
        a_ref[i] = a
        o_ref[rows, span(h * 128, 128)] = join_heads(dot(a, v)).astype(BF)

    tiles(x_ref.shape[0] // 128 * pairs, attend)
    settle(second)
    project_and_norm(
        x_ref, o_ref, out, NT, vec_ref[2:3, :], vec_ref[3:4, :], vec_ref[4:5, :], (y_ref, low_ref, n_ref, r_ref)
    )


def self_backward_kernel(count, where_ref, dy_ref, x_ref, vec_ref, p_ref, a_ref, o_ref, n_ref, r_ref, *rest):
    refs, rest = rest[:count], rest[count:]
    dx_ref, gq_own, gq_other, go_own, go_other, gv_ref = rest[:6]
    qkv, out, db_ref, dmix_ref, dp_ref, rel_ref, sems, sems2 = rest[6:]
    width = x_ref.shape[1]
    half = width // 2
    n, m = qkv.shape[0] // 8, out.shape[0] // 8
    whole = count == 2
    second = fetch(placed(refs[1:] if whole else refs, where_ref, [(n, m, 0)], out, half), sems2)
    first = fetch(placed(refs[:1] if whole else refs, where_ref, [(0, n, 0)], qkv, half), sems)
    core = where_ref[0]
    g_gain, g_offset, g_bias = norm_rows_back(dy_ref, n_ref, r_ref, vec_ref[3:4, :], dx_ref, db_ref)
    settle(second)

    def mix(j):
        cols = span(j * TILE, TILE)
        dmix_ref[:, cols] = dot(db_ref[...], out[:, cols]).astype(BF)

    tiles(width // TILE, mix)
    rel_ref[:, :half] = o_ref[:, span(core * half, half)]
    rel_ref[:, half:] = o_ref[:, span((1 - core) * half, half)]

    def out_grad(j):
        rows = span(j * TILE, TILE)
        g = dot(db_ref[:, rows], rel_ref[...], TN).astype(BF)
        go_own[rows, :] = g[:, :half]
        go_other[rows, :] = g[:, half:]

    tiles(width // TILE, out_grad)
    pairs = width // 128

    def attend(i):
        s, h = i // pairs, lax.rem(i, pairs)
        rows = span(s * 128, 128)
        q2 = split_heads(p_ref[rows, span(h * 128, 128)])
        k = p_ref[rows, span(width + h * 128, 128)]
        v = p_ref[rows, span(2 * width + h * 128, 128)]
        do2 = split_heads(dmix_ref[rows, span(h * 128, 128)])
        a = a_ref[i]
        ds = score_back(a, dot(do2, v, NT))
        dp_ref[rows, span(h * 128, 128)] = (join_heads(dot(ds, k)) * 0.125).astype(BF)
        dp_ref[rows, span(width + h * 128, 128)] = (dot(ds, q2, TN) * 0.125).astype(BF)
        dp_ref[rows, span(2 * width + h * 128, 128)] = dot(a, do2, TN).astype(BF)

    tiles(x_ref.shape[0] // 128 * pairs, attend)
    settle(first)

    def back(j):
        cols = span(j * TILE, TILE)
        dx_ref[:, cols] += dot(dp_ref[...], qkv[:, cols])

    tiles(width // TILE, back)
    rel_ref[:, :half] = x_ref[:, span(core * half, half)]
    rel_ref[:, half:] = x_ref[:, span((1 - core) * half, half)]

    def qkv_grad(j):
        rows = span(j * TILE, TILE)
        g = dot(dp_ref[:, rows], rel_ref[...], TN).astype(BF)
        gq_own[rows, :] = g[:, :half]
        gq_other[rows, :] = g[:, half:]

    tiles(3 * width // TILE, qkv_grad)
    gv_ref[0:1, :] = jnp.sum(dp_ref[:, :width].astype(F32), axis=0, keepdims=True)
    gv_ref[1:2, :] = jnp.sum(dp_ref[:, 2 * width :].astype(F32), axis=0, keepdims=True)
    gv_ref[2:3, :] = g_bias
    gv_ref[3:4, :] = g_gain
    gv_ref[4:5, :] = g_offset


def cross_forward_kernel(x_ref, low_x_ref, keep_ref, kv_ref, vec_ref, wq_ref, wo_ref, *rest):
    q_ref, a_ref, o_ref, y_ref, low_ref, n_ref, r_ref = rest
    width = x_ref.shape[1]
    patches = kv_ref.shape[0] // keep_ref.shape[0]

    def tile(j):
        cols = span(j * TILE, TILE)
        q_ref[:, cols] = (dot(low_x_ref[...], wq_ref[:, cols]) + vec_ref[0:1, cols]).astype(BF)

    tiles(width // TILE, tile)
    pairs = width // 128

    def attend(i):
        s, h = i // pairs, lax.rem(i, pairs)
        rows, keys = span(s * 64, 64, 64), span(s * patches, patches, 16)
        q = q_ref[rows, span(h * 128, 128)]
        k = kv_ref[keys, span(h * 128, 128)]
        v = kv_ref[keys, span(width + h * 128, 128)]
        a = softmax(dot(split_heads(q), k, NT), keep_ref[pl.ds(s, 1), :] > 0)
        a_ref[i] = a
        o_ref[rows, span(h * 128, 128)] = join_heads(dot(a, v)).astype(BF)

    tiles(keep_ref.shape[0] * pairs, attend)
    project_and_norm(
        x_ref, o_ref, wo_ref, NN, vec_ref[2:3, :], vec_ref[3:4, :], vec_ref[4:5, :], (y_ref, low_ref, n_ref, r_ref)
    )


def cross_backward_kernel(dy_ref, low_x_ref, kv_ref, vec_ref, wq_ref, wo_ref, q_ref, a_ref, o_ref, n_ref, r_ref, *rest):
    dx_ref, dkv_ref, gq_ref, go_ref, gv_ref, db_ref, dmix_ref, dq_ref = rest
    width = low_x_ref.shape[1]
    patches = a_ref.shape[2]
    g_gain, g_offset, g_bias = norm_rows_back(dy_ref, n_ref, r_ref, vec_ref[3:4, :], dx_ref, db_ref)

    def mix(j):
        cols = span(j * TILE, TILE)
        dmix_ref[:, cols] = dot(db_ref[...], wo_ref[cols, :], NT).astype(BF)
        go_ref[cols, :] = dot(o_ref[:, cols], db_ref[...], TN).astype(BF)

    tiles(width // TILE, mix)
    pairs = width // 128

    def attend(i):
        s, h = i // pairs, lax.rem(i, pairs)
        rows, keys = span(s * 64, 64, 64), span(s * patches, patches, 16)
        q2 = split_heads(q_ref[rows, span(h * 128, 128)])
        k = kv_ref[keys, span(h * 128, 128)]
        v = kv_ref[keys, span(width + h * 128, 128)]
        do2 = split_heads(dmix_ref[rows, span(h * 128, 128)])
        a = a_ref[i]
        ds = score_back(a, dot(do2, v, NT))
        dq_ref[rows, span(h * 128, 128)] = (join_heads(dot(ds, k)) * 0.125).astype(BF)
        dkv_ref[keys, span(h * 128, 128)] = (dot(ds, q2, TN) * 0.125).astype(BF)
        dkv_ref[keys, span(width + h * 128, 128)] = dot(a, do2, TN).astype(BF)

    tiles(a_ref.shape[0], attend)

    def back(j):
        cols = span(j * TILE, TILE)
        dx_ref[:, cols] += dot(dq_ref[...], wq_ref[cols, :], NT)
        gq_ref[cols, :] = dot(low_x_ref[:, cols], dq_ref[...], TN).astype(BF)

    tiles(width // TILE, back)
    gv_ref[0:1, :] = jnp.sum(dq_ref[...].astype(F32), axis=0, keepdims=True)
    gv_ref[1:2, :] = jnp.sum(dkv_ref[:, width:].astype(F32), axis=0, keepdims=True)
    gv_ref[2:3, :] = g_bias
    gv_ref[3:4, :] = g_gain
    gv_ref[4:5, :] = g_offset


def gelu_parts(h):
    size = jnp.abs(h) * 0.7071067811865476
    t = 1.0 / (1.0 + 0.3275911 * size)
    e = jnp.exp(-size * size)
    poly = t * (0.254829592 + t * (-0.284496736 + t * (1.421413741 + t * (-1.453152027 + t * 1.061405429))))
    tail = 0.5 * poly * e
    cdf = jnp.where(h < 0, tail, 1.0 - tail)
    return h * cdf, cdf + h * (e * 0.3989422804014327)


def feed_forward_kernel(count, where_ref, x_ref, low_x_ref, vec_ref, bias_ref, *rest):
    refs, rest = rest[: 2 * count], rest[2 * count :]
    act_ref, slope_ref, y_ref, low_ref, n_ref, r_ref, up, down, sems, sems2 = rest
    width, hidden = x_ref.shape[1], up.shape[0]
    n, m = hidden // 8, width // 8
    quarter = [(m * i, m, i) for i in range(hidden // width)]
    first = fetch(placed(refs[:count], where_ref, [(0, n, 0)], up, width // 2), sems)
    second = fetch(placed(refs[count:], where_ref, quarter, down, hidden // 2), sems2)
    settle(first)

    def tile(j):
        cols = span(j * TILE, TILE)
        h = dot(low_x_ref[...], up[cols, :], NT) + bias_ref[:, cols]
        act, slope = gelu_parts(h)
        act_ref[:, cols] = act.astype(BF)
        slope_ref[:, cols] = slope.astype(BF)

    tiles(hidden // TILE, tile)
    settle(second)
    project_and_norm(
        x_ref, act_ref, down, NT, vec_ref[5:6, :], vec_ref[6:7, :], vec_ref[7:8, :], (y_ref, low_ref, n_ref, r_ref)
    )


def feed_backward_kernel(count, where_ref, dy_ref, low_x_ref, vec_ref, act_ref, slope_ref, n_ref, r_ref, *rest):
    refs, rest = rest[: 2 * count], rest[2 * count :]
    dx_ref, gu_own, gu_other, gd_own, gd_other, gv_ref, gb_ref = rest[:7]
    up, down, db_ref, dh_ref, rel_ref, sems, sems2 = rest[7:]
    width, hidden = low_x_ref.shape[1], up.shape[0]
    n, m, half = hidden // 8, width // 8, width // 2
    quarter = [(m * i, m, i) for i in range(hidden // width)]
    second = fetch(placed(refs[count:], where_ref, quarter, down, hidden // 2), sems2)
    first = fetch(placed(refs[:count], where_ref, [(0, n, 0)], up, half), sems)
    core = where_ref[0]
    g_gain, g_offset, g_bias = norm_rows_back(dy_ref, n_ref, r_ref, vec_ref[6:7, :], dx_ref, db_ref)
    settle(second)
    per_side = hidden // 2 // TILE

    def down_tile(j):
        cols = span(j * TILE, TILE)
        dh = (dot(db_ref[...], down[:, cols]) * slope_ref[:, cols].astype(F32)).astype(BF)
        dh_ref[:, cols] = dh
        gb_ref[:, cols] = jnp.sum(dh.astype(F32), axis=0, keepdims=True)

    tiles(hidden // TILE, down_tile)

    def down_grad(j):
        cols = span(j * TILE, TILE)
        own = span(core * (hidden // 2) + j * TILE, TILE)
        other = span((1 - core) * (hidden // 2) + j * TILE, TILE)
        gd_own[:, cols] = dot(db_ref[...], act_ref[:, own], TN).astype(BF)
        gd_other[:, cols] = dot(db_ref[...], act_ref[:, other], TN).astype(BF)

    tiles(per_side, down_grad)
    rel_ref[:, :half] = low_x_ref[:, span(core * half, half)]
    rel_ref[:, half:] = low_x_ref[:, span((1 - core) * half, half)]

    def up_grad(j):
        rows = span(j * TILE, TILE)
        g = dot(dh_ref[:, rows], rel_ref[...], TN).astype(BF)
        gu_own[rows, :] = g[:, :half]
        gu_other[rows, :] = g[:, half:]

    tiles(hidden // TILE, up_grad)
    settle(first)

    def back(j):
        cols = span(j * TILE, TILE)
        dx_ref[:, cols] += dot(dh_ref[...], up[:, cols])

    tiles(width // TILE, back)
    gv_ref[0:1, :] = g_bias
    gv_ref[1:2, :] = g_gain
    gv_ref[2:3, :] = g_offset


def struct(*shape, dtype=F32):
    return jax.ShapeDtypeStruct(shape, dtype)


VMEM = pl.BlockSpec(memory_space=pltpu.VMEM)
SMEM = pl.BlockSpec(memory_space=pltpu.SMEM)
ANYWHERE = pl.BlockSpec(memory_space=pl.ANY)


def call(kernel, outs, specs, scratch, flops, args):
    return pl.pallas_call(
        kernel,
        out_shape=outs,
        in_specs=specs,
        out_specs=[VMEM] * len(outs),
        scratch_shapes=scratch,
        cost_estimate=pl.CostEstimate(flops=flops, bytes_accessed=20 * 2**20, transcendentals=0),
        compiler_params=pltpu.CompilerParams(vmem_limit_bytes=VMEM_BYTES),
    )(*args)


def copy_sems(count, parts=1):
    return pltpu.SemaphoreType.DMA((max(1, (count if count > 2 else 1) * parts),))


def self_forward(x, lengths, where, vec, weights):
    rows, width = x.shape
    blocks = rows // 128 * (width // 128)
    count = len(weights)
    outs = [
        struct(rows, 3 * width, dtype=BF),
        struct(blocks, 256, 128, dtype=BF),
        struct(rows, width, dtype=BF),
        struct(rows, width),
        struct(rows, width, dtype=BF),
        struct(rows, width),
        struct(rows, 1),
    ]
    scratch = [
        pltpu.VMEM((3 * width, width), BF),
        pltpu.VMEM((width, width), BF),
        pltpu.VMEM((1, 3 * width), F32),
        copy_sems(count),
        copy_sems(count),
    ]
    p, a, o, y, low, n, r = call(
        partial(self_forward_kernel, count),
        outs,
        [SMEM, SMEM, VMEM, VMEM] + [ANYWHERE] * count,
        scratch,
        10 * rows * width * width,
        (lengths, where, x, vec, *weights),
    )
    return y, low, (x, p, a, o, n, r)


def self_backward(dy, saved, where, vec, weights):
    x, p, a, o, n, r = saved
    rows, width = x.shape
    half = width // 2
    count = len(weights)
    outs = [
        struct(rows, width),
        struct(3 * width, half, dtype=BF),
        struct(3 * width, half, dtype=BF),
        struct(width, half, dtype=BF),
        struct(width, half, dtype=BF),
        struct(8, width),
    ]
    scratch = [
        pltpu.VMEM((3 * width, width), BF),
        pltpu.VMEM((width, width), BF),
        pltpu.VMEM((rows, width), BF),
        pltpu.VMEM((rows, width), BF),
        pltpu.VMEM((rows, 3 * width), BF),
        pltpu.VMEM((rows, width), BF),
        copy_sems(count),
        copy_sems(count),
    ]
    return call(
        partial(self_backward_kernel, count),
        outs,
        [SMEM] + [VMEM] * 8 + [ANYWHERE] * count,
        scratch,
        20 * rows * width * width,
        (where, dy, x, vec, p, a, o, n, r, *weights),
    )


def cross_forward(x, low_x, keep, kv, vec, wq, wo):
    rows, width = x.shape
    samples, patches = keep.shape
    outs = [
        struct(rows, width, dtype=BF),
        struct(samples * (width // 128), 128, patches, dtype=BF),
        struct(rows, width, dtype=BF),
        struct(rows, width),
        struct(rows, width, dtype=BF),
        struct(rows, width),
        struct(rows, 1),
    ]
    q, a, o, y, low, n, r = call(
        cross_forward_kernel, outs, [VMEM] * 7, [], 8 * rows * width * width, (x, low_x, keep, kv, vec, wq, wo)
    )
    return y, low, (low_x, kv, q, a, o, n, r)


def cross_backward(dy, saved, vec, wq, wo):
    low_x, kv, q, a, o, n, r = saved
    rows, width = low_x.shape
    outs = [
        struct(rows, width),
        struct(*kv.shape, dtype=BF),
        struct(width, width, dtype=BF),
        struct(width, width, dtype=BF),
        struct(8, width),
    ]
    scratch = [pltpu.VMEM((rows, width), BF)] * 3
    return call(
        cross_backward_kernel,
        outs,
        [VMEM] * 11,
        scratch,
        16 * rows * width * width,
        (dy, low_x, kv, vec, wq, wo, q, a, o, n, r),
    )


def feed_forward(x, low_x, where, vec, bias, up, down):
    rows, width = x.shape
    hidden = bias.shape[1]
    count = len(up)
    outs = [
        struct(rows, hidden, dtype=BF),
        struct(rows, hidden, dtype=BF),
        struct(rows, width),
        struct(rows, width, dtype=BF),
        struct(rows, width),
        struct(rows, 1),
    ]
    scratch = [
        pltpu.VMEM((hidden, width), BF),
        pltpu.VMEM((width, hidden), BF),
        copy_sems(count),
        copy_sems(count, hidden // width),
    ]
    act, slope, y, low, n, r = call(
        partial(feed_forward_kernel, count),
        outs,
        [SMEM] + [VMEM] * 4 + [ANYWHERE] * (2 * count),
        scratch,
        4 * rows * width * hidden,
        (where, x, low_x, vec, bias, *up, *down),
    )
    return y, low, (low_x, act, slope, n, r)


def feed_backward(dy, saved, where, vec, up, down):
    low_x, act, slope, n, r = saved
    rows, width = low_x.shape
    hidden = act.shape[1]
    count = len(up)
    outs = [
        struct(rows, width),
        struct(hidden, width // 2, dtype=BF),
        struct(hidden, width // 2, dtype=BF),
        struct(width, hidden // 2, dtype=BF),
        struct(width, hidden // 2, dtype=BF),
        struct(8, width),
        struct(1, hidden),
    ]
    scratch = [
        pltpu.VMEM((hidden, width), BF),
        pltpu.VMEM((width, hidden), BF),
        pltpu.VMEM((rows, width), BF),
        pltpu.VMEM((rows, hidden), BF),
        pltpu.VMEM((rows, width), BF),
        copy_sems(count),
        copy_sems(count, hidden // width),
    ]
    return call(
        partial(feed_backward_kernel, count),
        outs,
        [SMEM] + [VMEM] * 7 + [ANYWHERE] * (2 * count),
        scratch,
        8 * rows * width * hidden,
        (where, dy, low_x, vec, act, slope, n, r, *up, *down),
    )


def lane_slices(a, lanes):
    return jnp.concatenate([a[:, i : i + lanes] for i in range(0, a.shape[1], lanes)], axis=0)


def lane_join(a, count):
    rows = a.shape[-2] // count
    return jnp.concatenate([a[..., i * rows : (i + 1) * rows, :] for i in range(count)], axis=-1)


def pad_to(a, rows, lanes):
    return jnp.pad(a, ((0, rows - a.shape[0]), (0, lanes - a.shape[1])))


def dynamic(a, index, axis):
    return lax.dynamic_index_in_dim(a, index, axis, keepdims=False)


class Grid:
    def __init__(self):
        pipe, dp = lax.axis_index("pipe"), lax.axis_index("dp")
        self.x, self.core = pipe // 2, pipe % 2
        self.z, self.y = dp // 2, dp % 2

    def swap_x(self, a):
        return lax.ppermute(a, "pipe", [(i, i ^ 2) for i in range(4)])

    def over_x(self, a, to):
        return lax.ppermute(a, "pipe", [(i ^ 2, i) for i in (2 * to, 2 * to + 1)])

    def swap_core(self, a):
        return lax.ppermute(a, "pipe", [(i, i ^ 1) for i in range(4)])

    def swap_y(self, a):
        return lax.ppermute(a, "dp", [(i, i ^ 1) for i in range(8)])

    def ring_z(self, a):
        return lax.ppermute(a, "dp", [(i, (i + 2) % 8) for i in range(8)])

    def gather(self, piece):
        along_z = [piece]
        for _ in range(3):
            along_z.append(self.ring_z(along_z[-1]))
        across = along_z + [self.swap_y(p) for p in along_z]
        return across + [self.swap_core(p) for p in across]

    def gather_small(self, block):
        a = block[None]
        for swap, place in ((self.swap_y, self.y), (self.swap_x, self.x), (self.swap_core, self.core)):
            other = swap(a)
            low = place == 0
            a = jnp.stack([jnp.where(low, a, other), jnp.where(low, other, a)])
        ring = [a]
        for _ in range(3):
            ring.append(self.ring_z(ring[-1]))
        order = jnp.stack([ring[0], ring[3], ring[2], ring[1]] * 2)
        a = lax.dynamic_slice_in_dim(order, (4 - self.z) % 4, 4, 0)[:, :, :, :, 0]
        return a.transpose(2, 1, 0, 3, 4, 5)

    def reduce(self, own, other):
        came = self.swap_core(other)
        rows = own.shape[0] // 8
        own = own.reshape(4, 2, rows, own.shape[1])
        came = came.reshape(own.shape)

        def both(index):
            return dynamic(own, index, 1).astype(F32) + dynamic(came, index, 1).astype(F32)

        across = self.swap_y(both(1 - self.y).astype(own.dtype))
        keep = both(self.y)

        def block(step):
            at = (self.z + 3 - step) % 4
            return dynamic(keep, at, 0) + dynamic(across, at, 0).astype(F32)

        total = block(0)
        for step in range(3):
            total = self.ring_z(total.astype(own.dtype)).astype(F32) + block(step + 1)
        return total

    def reduce_small(self, a):
        for swap, place, axis in ((self.swap_core, self.core, 1), (self.swap_x, self.x, 0), (self.swap_y, self.y, -3)):
            a = dynamic(a, place, axis) + swap(dynamic(a, 1 - place, axis))
        total = dynamic(a, (self.z + 3) % 4, 0)
        for step in range(3):
            total = self.ring_z(total) + dynamic(a, (self.z + 2 - step) % 4, 0)
        return total


def masks(caption_len, phrase_len, box_count, patch_mask, text_rows, patches):
    slots = jnp.arange(phrase_len.shape[1], dtype=jnp.int32)
    phrase_total = jnp.sum(jnp.where(slots[None, :] < box_count[:, None], phrase_len, 0), axis=1)
    lengths = jnp.minimum(caption_len + phrase_total, text_rows)
    first_patch = (jnp.arange(patch_mask.shape[1], dtype=jnp.int32) == 0).astype(jnp.int32)
    keep = jnp.maximum(patch_mask, first_patch[None, :]).astype(F32)
    return lengths, jnp.pad(keep, ((0, 0), (0, patches - keep.shape[1])))


def on_device(
    text_embed,
    image_feats,
    caption_len,
    phrase_len,
    box_count,
    patch_mask,
    attn_qkv,
    attn_out,
    ffn_up,
    ffn_down,
    layer_vectors,
    cross_query,
    cross_kv,
    cross_out,
    cross_vectors,
    cotangent,
):
    n_pipe, n_dp = lax.axis_size("pipe"), lax.axis_size("dp")
    everyone = ("pipe", "dp")
    shards, half = n_pipe * n_dp, n_pipe // 2
    samples, text_rows, width = text_embed.shape
    hidden = ffn_up.shape[1] * n_dp
    lanes = attn_qkv.shape[0]
    patches = -(-image_feats.shape[1] // 32) * 32
    direct = (n_pipe, n_dp) == (4, 8) and lanes % 128 == 0
    lengths, patch_keep = masks(caption_len, phrase_len, box_count, patch_mask, text_rows, patches)
    x = text_embed.reshape(-1, width)
    image = jnp.pad(image_feats, ((0, 0), (0, patches - image_feats.shape[1]), (0, 0)))
    image = image.reshape(samples * patches, -1)

    c_rows = cross_query.shape[0]
    kv_slices = cross_kv.shape[1] // width
    cross_pack = jnp.concatenate([cross_query, cross_out, lane_slices(cross_kv, width)], axis=0)
    cross_whole = lax.all_gather(cross_pack, everyone, axis=0, tiled=True).reshape(shards, -1, width)
    wq = cross_whole[:, :c_rows].reshape(-1, width)
    wo = cross_whole[:, c_rows : 2 * c_rows].reshape(-1, width)
    wkv = lane_join(cross_whole[:, 2 * c_rows :], kv_slices).reshape(-1, kv_slices * width)

    v_rows, v_lanes = layer_vectors.shape
    x_rows = cross_vectors.shape[1]
    small = jnp.concatenate([pad_to(layer_vectors, v_rows, 128), pad_to(cross_vectors.T, x_rows, 128)], axis=0)
    small = pad_to(small, 16, 128).astype(F32)
    packs = [
        jnp.concatenate([attn_qkv.T, attn_out.T], axis=0),
        ffn_up.T,
        lane_slices(ffn_down.T, lanes),
    ]
    if direct:
        grid = Grid()
        where = jnp.stack([grid.core, grid.z, grid.y]).astype(jnp.int32)
        vectors = grid.gather_small(small)
        vectors = vectors.reshape(n_pipe, n_dp, 16, 128)
        weights = [[], []]
        swapped = [grid.swap_x(p) for p in packs]
        for layer in range(2):
            for pack, other in zip(packs, swapped):
                weights[layer].append(grid.gather(jnp.where(grid.x == layer, pack, other)))
    else:
        where = jnp.zeros((3,), jnp.int32)
        vectors = lax.all_gather(small, everyone, axis=0, tiled=False).reshape(n_pipe, n_dp, 16, 128)
        whole = lax.all_gather(jnp.concatenate(packs, axis=0), everyone, axis=0, tiled=False)
        whole = whole.reshape(n_pipe, n_dp, -1, lanes)

        def section(piece, layer):
            piece = jnp.moveaxis(piece[layer * half : (layer + 1) * half], 0, 2)
            return piece.reshape(n_dp * piece.shape[1], half * piece.shape[-1])

        ends = np.cumsum([0, attn_qkv.shape[1], attn_out.shape[1], ffn_up.shape[1], packs[2].shape[0]])
        cut = [whole[:, :, a:b] for a, b in zip(ends[:-1], ends[1:])]
        cut[3] = lane_join(cut[3], hidden // width)
        weights = []
        for layer in range(2):
            qkv, out, up, down = (section(c, layer) for c in cut)
            weights.append([[qkv, out], [up], [down]])

    def layer_vec(layer):
        v = vectors[layer * half : (layer + 1) * half, :, :v_rows, :v_lanes]
        return jnp.moveaxis(v, 1, 2).reshape(12, width)

    vecs = [layer_vec(0), layer_vec(1)]
    biases = [v[8:12].reshape(1, hidden) for v in vecs]
    cvec = vectors.reshape(shards, 16, 128)[:, v_rows : v_rows + x_rows, :c_rows]
    cvec = jnp.moveaxis(cvec, 1, 0).reshape(x_rows, width)

    state, low, s_self = self_forward(x, lengths, where, vecs[0], weights[0][0])
    state, passed, s_feed = feed_forward(state, low, where, vecs[0], biases[0], *weights[0][1:])
    kv_bias = jnp.concatenate([jnp.zeros((width,), F32), cvec[1]])
    kv = (jnp.dot(image, wkv, preferred_element_type=F32) + kv_bias).astype(BF)
    state, low, s_self2 = self_forward(passed, lengths, where, vecs[1], weights[1][0])
    state, low, s_cross = cross_forward(state, low, patch_keep, kv, cvec, wq, wo)
    joined, _, s_feed2 = feed_forward(state, low, where, vecs[1], biases[1], *weights[1][1:])

    grad = cotangent.reshape(-1, width)
    grad, gu_own, gu_other, gd_own, gd_other, v_feed2, v_up2 = feed_backward(
        grad, s_feed2, where, vecs[1], *weights[1][1:]
    )
    halves2 = [None, None, (gu_own, gu_other), (gd_own, gd_other)]
    grad, dkv, g_cq, g_co, v_cross = cross_backward(grad, s_cross, cvec, wq, wo)
    g_ckv = dot(image, dkv, TN).astype(BF)
    grad, gq_own, gq_other, go_own, go_other, v_self2 = self_backward(
        grad, s_self2, where, vecs[1], weights[1][0]
    )
    halves2[:2] = [(gq_own, gq_other), (go_own, go_other)]
    grad, gu_own, gu_other, gd_own, gd_other, v_feed, v_up = feed_backward(
        grad.astype(BF), s_feed, where, vecs[0], *weights[0][1:]
    )
    halves = [None, None, (gu_own, gu_other), (gd_own, gd_other)]
    embed_grad, gq_own, gq_other, go_own, go_other, v_self = self_backward(
        grad, s_self, where, vecs[0], weights[0][0]
    )
    halves[:2] = [(gq_own, gq_other), (go_own, go_other)]

    def cross_rows(g):
        g = g.reshape(shards, c_rows, width)
        return g

    g_kv = g_ckv.reshape(shards, -1, kv_slices, width)
    g_kv = jnp.moveaxis(g_kv, 2, 1).reshape(shards, -1, width)
    cross_grads = jnp.concatenate([cross_rows(g_cq), cross_rows(g_co), g_kv], axis=1)
    cross_grads = lax.psum_scatter(cross_grads.reshape(-1, width), everyone, scatter_dimension=0, tiled=True)
    cross_grads = cross_grads.astype(F32)

    def vector_block(v_self, v_feed, v_up):
        v = jnp.concatenate([v_self[:5], v_feed[:3], v_up.reshape(4, width)], axis=0)
        return jnp.moveaxis(v.reshape(half, v_rows, n_dp, v_lanes), 2, 1)

    section_vec = jnp.concatenate([vector_block(v_self, v_feed, v_up), vector_block(v_self2, v_feed2, v_up2)], axis=0)
    cross_vec = jnp.moveaxis(v_cross[:x_rows].reshape(x_rows, n_pipe, n_dp, c_rows), 0, 2)

    def padded(v):
        return jnp.pad(v, ((0, 0), (0, 0), (0, 0), (0, 128 - v.shape[3])))

    small = jnp.concatenate([padded(section_vec), padded(cross_vec)], axis=2)
    small = jnp.pad(small, ((0, 0), (0, 0), (0, 16 - small.shape[2]), (0, 0)))
    if direct:
        mine = []
        for pair, pair2 in zip(halves, halves2):
            first, second = grid.reduce(*pair), grid.reduce(*pair2)
            came2 = grid.over_x(second.astype(BF), 1).astype(F32)
            came = grid.over_x(first.astype(BF), 0).astype(F32)
            mine.append(jnp.where(grid.x == 0, first + came, second + came2))
        small = grid.reduce_small(small.reshape(2, 2, 4, 2, 16, 128))
    else:

        def split(pair, pair2):
            both = jnp.stack([jnp.concatenate(pair, axis=1), jnp.concatenate(pair2, axis=1)])
            rows, k = both.shape[1] // n_dp, both.shape[2] // (half * lanes)
            both = both.reshape(2, n_dp, rows, half, k, lanes)
            return both.transpose(0, 3, 1, 4, 2, 5).reshape(n_pipe, n_dp, k * rows, lanes)

        parts = [split(pair, pair2) for pair, pair2 in zip(halves, halves2)]
        ends = np.cumsum([0] + [p.shape[2] for p in parts])
        packed = jnp.concatenate(parts, axis=2).reshape(-1, lanes)
        packed = lax.psum_scatter(packed, everyone, scatter_dimension=0, tiled=True).astype(F32)
        mine = [packed[a:b] for a, b in zip(ends[:-1], ends[1:])]
        mine[3] = lane_join(mine[3], hidden // width)
        small = lax.psum_scatter(small.reshape(-1, 128), everyone, scatter_dimension=0, tiled=True)
    return (
        joined.reshape(text_embed.shape),
        embed_grad.reshape(text_embed.shape),
        mine[0].T,
        mine[1].T,
        mine[2].T,
        mine[3].T,
        small[:v_rows, :v_lanes],
        cross_grads[:c_rows],
        lane_join(cross_grads[2 * c_rows :], kv_slices),
        cross_grads[c_rows : 2 * c_rows],
        small[v_rows : v_rows + x_rows, :c_rows].T,
    )


def solution(mesh):
    in_specs = (
        P(("pipe", "dp"), None, None),
        P(("pipe", "dp"), None, None),
        P(("pipe", "dp")),
        P(("pipe", "dp"), None),
        P(("pipe", "dp")),
        P(("pipe", "dp"), None),
        P("pipe", "dp"),
        P("pipe", "dp"),
        P("pipe", "dp"),
        P("pipe", "dp"),
        P("pipe", "dp"),
        P(("pipe", "dp"), None),
        P(("pipe", "dp"), None),
        P(("pipe", "dp"), None),
        P(("pipe", "dp"), None),
        P(("pipe", "dp"), None, None),
    )
    out_specs = (
        P(("pipe", "dp"), None, None),
        P(("pipe", "dp"), None, None),
        P("pipe", "dp"),
        P("pipe", "dp"),
        P("pipe", "dp"),
        P("pipe", "dp"),
        P("pipe", "dp"),
        P(("pipe", "dp"), None),
        P(("pipe", "dp"), None),
        P(("pipe", "dp"), None),
        P(("pipe", "dp"), None),
    )
    return jax.shard_map(
        on_device, mesh=mesh, in_specs=in_specs, out_specs=out_specs, check_vma=False
    )
```

time: 1950 us -> 858 us (0.44)
  blocking collectives: 730 us -> 0 us
  local copies, waits for them, and re-layouts: 700 us -> 33.5 us
  Pallas kernels: 0 us -> 272 us
  waiting for transfers between devices: 198 us -> 384 us
  matrix products: 183 us -> 12 us
  starting transfers between devices: 2.17 us -> 82.7 us
  other arithmetic: 92.8 us -> 48.5 us
    unnamed x1 -> x0, blocking collectives: 730 us -> none
    ppermute x0 -> x153, waiting for transfers between devices: none -> 384 us  [the longest x48 245 us: ring_z(): return lax.ppermute(a, 'dp', [(i, (i + 2) % 8) for i in range(8)])]
    pallas_call x0 -> x10, Pallas kernels: none -> 272 us  [call(): pl.pallas_call(kernel, out_shape=outs, in_specs=specs, out_specs=[VMEM] *...]
    concatenate x19 -> x1, local copies, waits for them, and re-layouts: 244 us -> 0.01 us  [on_device(): kv_bias = jnp.concatenate([jnp.zeros((width,), F32), cvec[1]])]
    all_gather x1, waiting for transfers between devices: 194 us -> 0.01 us  [on_device(): lax.all_gather(cross_pack, everyone, axis=0, tiled=True)]
    dot_general x47 -> x2, matrix products: 170 us -> 12 us  [the longest x1 6.17 us: on_device(): kv = (jnp.dot(image, wkv, preferred_element_type=F32) + kv_bias).astype(BF)]
    another operation x51 -> x1, local copies, waits for them, and re-layouts: 146 us -> 0.01 us  [gather_small(): order = jnp.stack([ring[0], ring[3], ring[2], ring[1]] * 2)]
    reshape x33 -> x11, local copies, waits for them, and re-layouts: 153 us -> 8.76 us  [the longest x2 6.98 us: on_device(): g_kv = g_ckv.reshape(shards, -1, kv_slices, width)]
  transfers between devices with their start and end apart: 2 -> 155, of which waited for: 2 -> 68; matrix products, arithmetic and copies ran while one was open for 1% -> 9% of each run, Pallas kernels for 0% -> 12%
where the time goes in v2:
time: 858 us; the launch traced here: 850 us
  waiting for transfers between devices  384 us (45%)
  Pallas kernels  272 us (32%)
  starting transfers between devices  82.7 us (10%)
  other arithmetic  48.5 us (6%)
  local copies, waits for them, and re-layouts  33.5 us (4%)
  between operations  16.8 us (2%)
  matrix products  12 us (1%)
    pallas_call x10, Pallas kernels, call(): pl.pallas_call(kernel, out_shape=outs, in_specs=specs, out_specs=[VMEM] *...  272 us
    ppermute x48, waiting for transfers between devices, ring_z(): return lax.ppermute(a, 'dp', [(i, (i + 2) % 8) for i in range(8)])  245 us
    ppermute x34, waiting for transfers between devices, swap_y(): return lax.ppermute(a, 'dp', [(i, i ^ 1) for i in range(8)])  122 us
    ppermute x34, starting transfers between devices, swap_y(): return lax.ppermute(a, 'dp', [(i, i ^ 1) for i in range(8)])  40.4 us
    ppermute x8, starting transfers between devices, over_x(): return lax.ppermute(a, 'pipe', [(i ^ 2, i) for i in (2 * to, 2 * to + 1)])  19.6 us
  transfers between devices with their start and end apart: 155, of which 68 were waited for; matrix products, arithmetic and copies ran while one was open for 9% of the time, Pallas kernels for 12%

profile of v2, /device:TPU:0, one launch (start us, length us, event | category | flops | bytes accessed | tf_op | source)
XLA Modules:
  0.0 850.1 jit_solution(18153686619261864123)
XLA Ops:
  25.6 4.7 collective-permute-done.3
  31.9 4.7 collective-permute-done.4
  38.5 5.0 collective-permute-done.5
  47.5 7.7 collective-permute-done.7.rest_1_
  56.7 5.5 collective-permute-done.23.rest_1_
  63.6 6.2 collective-permute-done.39.rest_17_
  71.0 11.5 %collective-permute-done.54.rest_1_ = bf16[384,384]{1,0:T(8,128)(2,1)S(1)} collective-permute-done((bf16[384,384]{1,0:T(8,128)(2,1)S(1)}, bf16[384,384]{1,0:T(8,128)(2,1)S(1)}, u32[]{:S(2)}, u32[]{:S(2)}) %collective-permute-start.54) | collective-permute-done | bytes 294944 | tf_op jit(solution)/shard_map/ppermute | solution.py:638
  83.6 9.4 %collective-permute-done.69.rest_1_ = bf16[384,384]{1,0:T(8,128)(2,1)S(1)} collective-permute-done((bf16[384,384]{1,0:T(8,128)(2,1)S(1)}, bf16[384,384]{1,0:T(8,128)(2,1)S(1)}, u32[]{:S(2)}, u32[]{:S(2)}) %collective-permute-start.69) | collective-permute-done | bytes 294944 | tf_op jit(solution)/shard_map/ppermute | solution.py:638
  94.5 7.4 collective-permute-done.84.rest_17_
  103.3 5.0 collective-permute-done.8.rest_2_
  118.4 9.2 %collective-permute-done.40.rest_18_ = bf16[384,384]{1,0:T(8,128)(2,1)S(1)} collective-permute-done((bf16[384,384]{1,0:T(8,128)(2,1)S(1)}, bf16[384,384]{1,0:T(8,128)(2,1)S(1)}, u32[]{:S(2)}, u32[]{:S(2)}) %collective-permute-start.40) | collective-permute-done | bytes 294944 | tf_op jit(solution)/shard_map/ppermute | solution.py:638
  149.9 4.8 collective-permute-done.41.rest_19_
  178.5 4.8 collective-permute-done.45.rest_23_
  183.9 4.6 collective-permute-done.60.rest_7_
  191.3 23.6 %shard_map.239 = (bf16[512,2304]{1,0:T(8,128)(2,1)}, bf16[24,256,128]{2,1,0:T(8,128)(2,1)}, bf16[512,768]{1,0:T(8,128)(2,1)}, f32[512,768]{1,0:T(8,128)}, bf16[5...) custom-call(s32[8]{0:T(128)} %add_minimum_fusion.lengths, s32[3]{0:T(128)} %pad_add_fusion.where_ref, ...), custom_call_target="tpu_custom_call" | custom-call | flops 3019898880 | bytes 20971520 | tf_op jit(solution)/shard_map/pallas_call | solution.py:422
  217.4 21.8 %shard_map.240 = (bf16[512,3072]{1,0:T(8,128)(2,1)}, bf16[512,3072]{1,0:T(8,128)(2,1)}, f32[512,768]{1,0:T(8,128)}, bf16[512,768]{1,0:T(8,128)(2,1)}, f32[512,768]{1,0:T(8,128)}, /*index=5*/f32[512,1]{1,0:T(8,128)}) custom-call(s32[3]{0:T(128)} %pad_add_fusion.where_ref, f32[512,768]{1,0:T(8,128)} %get-tuple-element.73.x_ref, ...), custom_call_target="tpu_custom_call" | custom-call | flops 4831838208 | bytes 20971520 | tf_op jit(solution)/shard_map/pallas_call | solution.py:422
  239.2 23.6 %shard_map.241 = (bf16[512,2304]{1,0:T(8,128)(2,1)}, bf16[24,256,128]{2,1,0:T(8,128)(2,1)}, bf16[512,768]{1,0:T(8,128)(2,1)}, f32[512,768]{1,0:T(8,128)}, bf16[5...) custom-call(s32[8]{0:T(128)} %add_minimum_fusion.lengths, s32[3]{0:T(128)} %pad_add_fusion.where_ref, ...), custom_call_target="tpu_custom_call" | custom-call | flops 3019898880 | bytes 20971520 | tf_op jit(solution)/shard_map/pallas_call | solution.py:422
  267.0 7.5 collective-permute-done.85.rest_18_
  290.4 6.2 fusion.kv_ref
  304.7 32.4 %shard_map.242 = (bf16[512,768]{1,0:T(8,128)(2,1)}, bf16[48,128,160]{2,1,0:T(8,128)(2,1)}, bf16[512,768]{1,0:T(8,128)(2,1)}, f32[512,768]{1,0:T(8,128)}, bf16[51...) custom-call(f32[512,768]{1,0:T(8,128)} %get-tuple-element.76.x_ref, ...), custom_call_target="tpu_custom_call" | custom-call | flops 2415919104 | bytes 20971520 | tf_op jit(solution)/shard_map/pallas_call | solution.py:422
  338.2 21.8 %shard_map.243 = (bf16[512,3072]{1,0:T(8,128)(2,1)}, bf16[512,3072]{1,0:T(8,128)(2,1)}, f32[512,768]{1,0:T(8,128)}, bf16[512,768]{1,0:T(8,128)(2,1)}, f32[512,768]{1,0:T(8,128)}, /*index=5*/f32[512,1]{1,0:T(8,128)}) custom-call(s32[3]{0:T(128)} %pad_add_fusion.where_ref, f32[512,768]{1,0:T(8,128)} %get-tuple-element.78.x_ref, ...), custom_call_target="tpu_custom_call" | custom-call | flops 4831838208 | bytes 20971520 | tf_op jit(solution)/shard_map/pallas_call | solution.py:422
  360.0 28.5 %shard_map.244 = (f32[512,768]{1,0:T(8,128)}, bf16[3072,384]{1,0:T(8,128)(2,1)}, bf16[3072,384]{1,0:T(8,128)(2,1)}, bf16[768,1536]{1,0:T(8,128)(2,1)}, bf16[768,...) custom-call(s32[3]{0:T(128)} %pad_add_fusion.where_ref, bf16[512,768]{1,0:T(8,128)(2,1)} %bitcast.560, ...), custom_call_target="tpu_custom_call" | custom-call | flops 9663676416 | bytes 20971520 | tf_op jit(solution)/shard_map/pallas_call | solution.py:422
  388.5 35.0 %shard_map.245 = (f32[512,768]{1,0:T(8,128)}, bf16[1280,1536]{1,0:T(8,128)(2,1)}, bf16[768,768]{1,0:T(8,128)(2,1)}, bf16[768,768]{1,0:T(8,128)(2,1)}, f32[8,768]{1,0:T(8,128)}) custom-call(f32[512,768]{1,0:T(8,128)} %get-tuple-element.85.dy_ref, bf16[512,768]{1,0:T(8,128)(2,1)} %get-tuple-element.77.low_x_ref, bf16[1280,1536]{1,0:T(8,128)(2,1)} %fusion.kv_ref, ...), custom_call_target="tpu_custom_call" | custom-call | flops 4831838208 | bytes 20971520 | tf_op jit(solution)/shard_map/pallas_call | solution.py:422
  423.5 28.6 %shard_map.246 = (f32[512,768]{1,0:T(8,128)}, bf16[2304,384]{1,0:T(8,128)(2,1)}, bf16[2304,384]{1,0:T(8,128)(2,1)}, bf16[768,384]{1,0:T(8,128)(2,1)}, bf16[768,384]{1,0:T(8,128)(2,1)}, /*index=5*/f32[8,768]{1,0:T(8,128)}) custom-call(s32[3]{0:T(128)} %pad_add_fusion.where_ref, f32[512,768]{1,0:T(8,128)} %get-tuple-element.91.dy_ref, ...), custom_call_target="tpu_custom_call" | custom-call | flops 6039797760 | bytes 20971520 | tf_op jit(solution)/shard_map/pallas_call | solution.py:422
  456.0 28.5 %shard_map.247 = (f32[512,768]{1,0:T(8,128)}, bf16[3072,384]{1,0:T(8,128)(2,1)}, bf16[3072,384]{1,0:T(8,128)(2,1)}, bf16[768,1536]{1,0:T(8,128)(2,1)}, bf16[768,...) custom-call(s32[3]{0:T(128)} %pad_add_fusion.where_ref, bf16[512,768]{1,0:T(8,128)(2,1)} %convert_element_type.562.dy_ref, ...), custom_call_target="tpu_custom_call" | custom-call | flops 9663676416 | bytes 20971520 | tf_op jit(solution)/shard_map/pallas_call | solution.py:422
  486.7 28.6 %shard_map.248 = (f32[512,768]{1,0:T(8,128)}, bf16[2304,384]{1,0:T(8,128)(2,1)}, bf16[2304,384]{1,0:T(8,128)(2,1)}, bf16[768,384]{1,0:T(8,128)(2,1)}, bf16[768,384]{1,0:T(8,128)(2,1)}, /*index=5*/f32[8,768]{1,0:T(8,128)}) custom-call(s32[3]{0:T(128)} %pad_add_fusion.where_ref, f32[512,768]{1,0:T(8,128)} %get-tuple-element.102.dy_ref, ...), custom_call_target="tpu_custom_call" | custom-call | flops 6039797760 | bytes 20971520 | tf_op jit(solution)/shard_map/pallas_call | solution.py:422
  530.1 5.3 collective-permute-done.150
  569.8 5.4 collective-permute-done.152
  576.1 5.8 convolution_convert_fusion
  582.0 6.3 reshape.356
  621.7 17.3 %collective-permute-done.100 = bf16[4,288,384]{2,1,0:T(8,128)(2,1)S(1)} collective-permute-done((bf16[4,288,384]{2,1,0:T(8,128)(2,1)S(1)}, bf16[4,288,384]{2,1,0:T(8,128)(2,1)S(1)}, u32[]{:S(2)}, u32[]{:S(2)}) %collective-permute-start.100) | collective-permute-done | bytes 884768 | tf_op jit(solution)/shard_map/ppermute | solution.py:635
  639.9 13.4 %collective-permute-done.101 = bf16[288,384]{1,0:T(8,128)(2,1)S(1)} collective-permute-done((bf16[288,384]{1,0:T(8,128)(2,1)S(1)}, bf16[288,384]{1,0:T(8,128)(2,1)S(1)}, u32[]{:S(2)}, u32[]{:S(2)}) %collective-permute-start.101) | collective-permute-done | bytes 221216 | tf_op jit(solution)/shard_map/ppermute | solution.py:638
  653.5 10.0 %collective-permute-done.108 = bf16[288,384]{1,0:T(8,128)(2,1)S(1)} collective-permute-done((bf16[288,384]{1,0:T(8,128)(2,1)S(1)}, bf16[288,384]{1,0:T(8,128)(2,1)S(1)}, u32[]{:S(2)}, u32[]{:S(2)}) %collective-permute-start.108) | collective-permute-done | bytes 221216 | tf_op jit(solution)/shard_map/ppermute | solution.py:638
  663.5 14.3 %collective-permute-done.102 = bf16[288,384]{1,0:T(8,128)(2,1)S(1)} collective-permute-done((bf16[288,384]{1,0:T(8,128)(2,1)S(1)}, bf16[288,384]{1,0:T(8,128)(2,1)S(1)}, u32[]{:S(2)}, u32[]{:S(2)}) %collective-permute-start.102) | collective-permute-done | bytes 221216 | tf_op jit(solution)/shard_map/ppermute | solution.py:638
  677.9 10.7 %collective-permute-done.109 = bf16[288,384]{1,0:T(8,128)(2,1)S(1)} collective-permute-done((bf16[288,384]{1,0:T(8,128)(2,1)S(1)}, bf16[288,384]{1,0:T(8,128)(2,1)S(1)}, u32[]{:S(2)}, u32[]{:S(2)}) %collective-permute-start.109) | collective-permute-done | bytes 221216 | tf_op jit(solution)/shard_map/ppermute | solution.py:638
  688.7 8.3 collective-permute-done.103
  704.4 26.4 %collective-permute-done.142 = bf16[4,96,1536]{2,1,0:T(8,128)(2,1)S(1)} collective-permute-done((bf16[4,96,1536]{2,1,0:T(8,128)(2,1)S(1)}, bf16[4,96,1536]{2,1,0:T(8,128)(2,1)S(1)}, u32[]{:S(2)}, u32[]{:S(2)}) %collective-permute-start.142) | collective-permute-done | bytes 1179680 | tf_op jit(solution)/shard_map/ppermute | solution.py:635
  730.9 24.3 %collective-permute-done.136 = bf16[4,96,1536]{2,1,0:T(8,128)(2,1)S(1)} collective-permute-done((bf16[4,96,1536]{2,1,0:T(8,128)(2,1)S(1)}, bf16[4,96,1536]{2,1,0:T(8,128)(2,1)S(1)}, u32[]{:S(2)}, u32[]{:S(2)}) %collective-permute-start.136) | collective-permute-done | bytes 1179680 | tf_op jit(solution)/shard_map/ppermute | solution.py:635
  756.4 10.5 %collective-permute-done.143 = bf16[96,1536]{1,0:T(8,128)(2,1)S(1)} collective-permute-done((bf16[96,1536]{1,0:T(8,128)(2,1)S(1)}, bf16[96,1536]{1,0:T(8,128)(2,1)S(1)}, u32[]{:S(2)}, u32[]{:S(2)}) %collective-permute-start.143) | collective-permute-done | bytes 294944 | tf_op jit(solution)/shard_map/ppermute | solution.py:638
  767.0 6.2 collective-permute-done.137
  773.3 6.2 collective-permute-done.132
  779.7 6.2 collective-permute-done.126
  786.0 6.2 collective-permute-done.144
  792.3 6.2 collective-permute-done.138
  798.6 6.2 collective-permute-done.133
  804.9 6.2 collective-permute-done.127
  822.0 5.3 collective-permute-start.146
  831.8 5.5 collective-permute-done.140
  (636 shorter events, 244.5 us)
Async XLA Ops:
  7.2 257.7 %all-gather.2.cloned.1.call-start = ((), (), s32[]{:S(2)}) async-start(), calls=%async_computation.1 | async-start | bytes 5677056 | tf_op jit(solution)/shard_map/all_gather | solution.py:733
  9.7 830.1 %reduce-scatter.2.cloned.1.call-start = ((), (), s32[]{:S(2)}) async-start(), calls=%async_computation.2 | async-start | bytes 5677056 | tf_op jit(solution)/shard_map/reduce_scatter | solution.py:819
  62.2 20.2 %collective-permute-start.54 = (bf16[384,384]{1,0:T(8,128)(2,1)S(1)}, bf16[384,384]{1,0:T(8,128)(2,1)S(1)}, u32[]{:S(2)}, u32[]{:S(2)}) collective-permute-start(bf16[384,384]{1,0:T(8,128)(2,1)S(1)} %get-tuple-element.176.rest_0_), channel_id=1, source_target_pairs={{0,2},{1,3},{2,4},{3,5},{4,6},{5,7},{6,0},{7,1},{8,10},{9,11},{10,... | collective-permute-start | bytes 884744 | tf_op jit(solution)/shard_map/ppermute | solution.py:638
  62.3 20.2 %collective-permute-start.57 = (bf16[384,384]{1,0:T(8,128)(2,1)S(1)}, bf16[384,384]{1,0:T(8,128)(2,1)S(1)}, u32[]{:S(2)}, u32[]{:S(2)}) collective-permute-start(bf16[384,384]{1,0:T(8,128)(2,1)S(1)} %get-tuple-element.176.rest_0_), channel_id=1, source_target_pairs={{0,1},{1,0},{2,3},{3,2},{4,5},{5,4},{6,7},{7,6},{8,9},{9,8},{10,11... | collective-permute-start | bytes 884744 | tf_op jit(solution)/shard_map/ppermute | solution.py:635
  69.8 23.1 %collective-permute-start.69 = (bf16[384,384]{1,0:T(8,128)(2,1)S(1)}, bf16[384,384]{1,0:T(8,128)(2,1)S(1)}, u32[]{:S(2)}, u32[]{:S(2)}) collective-permute-start(bf16[384,384]{1,0:T(8,128)(2,1)S(1)} %get-tuple-element.174.rest_0_), channel_id=1, source_target_pairs={{0,2},{1,3},{2,4},{3,5},{4,6},{5,7},{6,0},{7,1},{8,10},{9,11},{10,... | collective-permute-start | bytes 884744 | tf_op jit(solution)/shard_map/ppermute | solution.py:638
  69.9 23.1 %collective-permute-start.72 = (bf16[384,384]{1,0:T(8,128)(2,1)S(1)}, bf16[384,384]{1,0:T(8,128)(2,1)}, u32[]{:S(2)}, u32[]{:S(2)}) collective-permute-start(bf16[384,384]{1,0:T(8,128)(2,1)S(1)} %get-tuple-element.174.rest_0_), channel_id=1, source_target_pairs={{0,1},{1,0},{2,3},{3,2},{4,5},{5,4},{6,7},{7,6},{8,9},{9,8},{10,11... | collective-permute-start | bytes 884744 | tf_op jit(solution)/shard_map/ppermute | solution.py:635
  82.5 19.5 %collective-permute-start.84 = (bf16[384,384]{1,0:T(8,128)(2,1)S(1)}, bf16[384,384]{1,0:T(8,128)(2,1)S(1)}, u32[]{:S(2)}, u32[]{:S(2)}) collective-permute-start(bf16[384,384]{1,0:T(8,128)(2,1)S(1)} %get-tuple-element.172.rest_16_), channel_id=1, source_target_pairs={{0,2},{1,3},{2,4},{3,5},{4,6},{5,7},{6,0},{7,1},{8,10},{9,11},{10,... | collective-permute-start | bytes 884744 | tf_op jit(solution)/shard_map/ppermute | solution.py:638
  82.6 19.4 %collective-permute-start.87 = (bf16[384,384]{1,0:T(8,128)(2,1)S(1)}, bf16[384,384]{1,0:T(8,128)(2,1)S(1)}, u32[]{:S(2)}, u32[]{:S(2)}) collective-permute-start(bf16[384,384]{1,0:T(8,128)(2,1)S(1)} %get-tuple-element.172.rest_16_), channel_id=1, source_target_pairs={{0,1},{1,0},{2,3},{3,2},{4,5},{5,4},{6,7},{7,6},{8,9},{9,8},{10,11... | collective-permute-start | bytes 884744 | tf_op jit(solution)/shard_map/ppermute | solution.py:635
  183.3 31.7 %collective-permute-start.64 = (bf16[384,384]{1,0:T(8,128)(2,1)}, bf16[384,384]{1,0:T(8,128)(2,1)}, u32[]{:S(2)}, u32[]{:S(2)}) collective-permute-start(bf16[384,384]{1,0:T(8,128)(2,1)} %copy-done.76), channel_id=1, source_target_pairs={{0,8},{8,0},{16,24},{24,16},{1,9},{9,1},{17,25},{25,17},{2,10},{10... | collective-permute-start | bytes 884744 | tf_op jit(solution)/shard_map/ppermute | solution.py:632
  183.3 32.2 %collective-permute-start.67 = (bf16[384,384]{1,0:T(8,128)(2,1)}, bf16[384,384]{1,0:T(8,128)(2,1)}, u32[]{:S(2)}, u32[]{:S(2)}) collective-permute-start(bf16[384,384]{1,0:T(8,128)(2,1)} %copy-done.78), channel_id=1, source_target_pairs={{0,8},{8,0},{16,24},{24,16},{1,9},{9,1},{17,25},{25,17},{2,10},{10... | collective-permute-start | bytes 884744 | tf_op jit(solution)/shard_map/ppermute | solution.py:632
  183.9 31.7 %collective-permute-start.37 = (bf16[384,384]{1,0:T(8,128)(2,1)}, bf16[384,384]{1,0:T(8,128)(2,1)}, u32[]{:S(2)}, u32[]{:S(2)}) collective-permute-start(bf16[384,384]{1,0:T(8,128)(2,1)} %collective-permute-done.29.rest_7_), channel_id=1, source_target_pairs={{0,8},{8,0},{16,24},{24,16},{1,9},{9,1},{17,25},{25,17},{2,10},{10... | collective-permute-start | bytes 884744 | tf_op jit(solution)/shard_map/ppermute | solution.py:632
  188.5 28.3 %collective-permute-start.53 = (bf16[384,384]{1,0:T(8,128)(2,1)}, bf16[384,384]{1,0:T(8,128)(2,1)}, u32[]{:S(2)}, u32[]{:S(2)}) collective-permute-start(bf16[384,384]{1,0:T(8,128)(2,1)} %collective-permute-done.45.rest_23_), channel_id=1, source_target_pairs={{0,8},{8,0},{16,24},{24,16},{1,9},{9,1},{17,25},{25,17},{2,10},{10... | collective-permute-start | bytes 884744 | tf_op jit(solution)/shard_map/ppermute | solution.py:632
  188.6 28.3 %collective-permute-start.68 = (bf16[384,384]{1,0:T(8,128)(2,1)}, bf16[384,384]{1,0:T(8,128)(2,1)}, u32[]{:S(2)}, u32[]{:S(2)}) collective-permute-start(bf16[384,384]{1,0:T(8,128)(2,1)} %collective-permute-done.60.rest_7_), channel_id=1, source_target_pairs={{0,8},{8,0},{16,24},{24,16},{1,9},{9,1},{17,25},{25,17},{2,10},{10... | collective-permute-start | bytes 884744 | tf_op jit(solution)/shard_map/ppermute | solution.py:632
  215.0 47.8 %collective-permute-start.91 = (bf16[384,384]{1,0:T(8,128)(2,1)S(1)}, bf16[384,384]{1,0:T(8,128)(2,1)S(1)}, u32[]{:S(2)}, u32[]{:S(2)}) collective-permute-start(bf16[384,384]{1,0:T(8,128)(2,1)S(1)} %copy-done.26), channel_id=1, source_target_pairs={{0,8},{8,0},{16,24},{24,16},{1,9},{9,1},{17,25},{25,17},{2,10},{10... | collective-permute-start | bytes 884744 | tf_op jit(solution)/shard_map/ppermute | solution.py:632
  215.6 47.3 %collective-permute-start.70 = (bf16[384,384]{1,0:T(8,128)(2,1)S(1)}, bf16[384,384]{1,0:T(8,128)(2,1)}, u32[]{:S(2)}, u32[]{:S(2)}) collective-permute-start(bf16[384,384]{1,0:T(8,128)(2,1)S(1)} %copy-done.51), channel_id=1, source_target_pairs={{0,2},{1,3},{2,4},{3,5},{4,6},{5,7},{6,0},{7,1},{8,10},{9,11},{10,... | collective-permute-start | bytes 884744 | tf_op jit(solution)/shard_map/ppermute | solution.py:638
  215.6 48.2 %collective-permute-start.73 = (bf16[384,384]{1,0:T(8,128)(2,1)S(1)}, bf16[384,384]{1,0:T(8,128)(2,1)}, u32[]{:S(2)}, u32[]{:S(2)}) collective-permute-start(bf16[384,384]{1,0:T(8,128)(2,1)S(1)} %copy-done.51), channel_id=1, source_target_pairs={{0,1},{1,0},{2,3},{3,2},{4,5},{5,4},{6,7},{7,6},{8,9},{9,8},{10,11... | collective-permute-start | bytes 884744 | tf_op jit(solution)/shard_map/ppermute | solution.py:635
  216.9 46.9 %collective-permute-start.77 = (bf16[384,384]{1,0:T(8,128)(2,1)S(1)}, bf16[384,384]{1,0:T(8,128)(2,1)S(1)}, u32[]{:S(2)}, u32[]{:S(2)}) collective-permute-start(bf16[384,384]{1,0:T(8,128)(2,1)S(1)} %copy-done.51), channel_id=1, source_target_pairs={{0,8},{8,0},{16,24},{24,16},{1,9},{9,1},{17,25},{25,17},{2,10},{10... | collective-permute-start | bytes 884744 | tf_op jit(solution)/shard_map/ppermute | solution.py:632
  216.9 47.5 %collective-permute-start.80 = (bf16[384,384]{1,0:T(8,128)(2,1)}, bf16[384,384]{1,0:T(8,128)(2,1)S(1)}, u32[]{:S(2)}, u32[]{:S(2)}) collective-permute-start(bf16[384,384]{1,0:T(8,128)(2,1)} %collective-permute-done.72.rest_4_), channel_id=1, source_target_pairs={{0,8},{8,0},{16,24},{24,16},{1,9},{9,1},{17,25},{25,17},{2,10},{10... | collective-permute-start | bytes 884744 | tf_op jit(solution)/shard_map/ppermute | solution.py:632
  296.6 40.5 %collective-permute-start.94 = (bf16[384,384]{1,0:T(8,128)(2,1)S(1)}, bf16[384,384]{1,0:T(8,128)(2,1)S(1)}, u32[]{:S(2)}, u32[]{:S(2)}) collective-permute-start(bf16[384,384]{1,0:T(8,128)(2,1)S(1)} %collective-permute-done.86.rest_19_), channel_id=1, source_target_pairs={{0,8},{8,0},{16,24},{24,16},{1,9},{9,1},{17,25},{25,17},{2,10},{10... | collective-permute-start | bytes 884744 | tf_op jit(solution)/shard_map/ppermute | solution.py:632
  296.7 40.4 %collective-permute-start.82 = (bf16[384,384]{1,0:T(8,128)(2,1)S(1)}, bf16[384,384]{1,0:T(8,128)(2,1)S(1)}, u32[]{:S(2)}, u32[]{:S(2)}) collective-permute-start(bf16[384,384]{1,0:T(8,128)(2,1)S(1)} %collective-permute-done.74.rest_6_), channel_id=1, source_target_pairs={{0,8},{8,0},{16,24},{24,16},{1,9},{9,1},{17,25},{25,17},{2,10},{10... | collective-permute-start | bytes 884744 | tf_op jit(solution)/shard_map/ppermute | solution.py:632
  297.3 39.9 %collective-permute-start.97 = (bf16[384,384]{1,0:T(8,128)(2,1)S(1)}, bf16[384,384]{1,0:T(8,128)(2,1)S(1)}, u32[]{:S(2)}, u32[]{:S(2)}) collective-permute-start(bf16[384,384]{1,0:T(8,128)(2,1)S(1)} %collective-permute-done.89.rest_22_), channel_id=1, source_target_pairs={{0,8},{8,0},{16,24},{24,16},{1,9},{9,1},{17,25},{25,17},{2,10},{10... | collective-permute-start | bytes 884744 | tf_op jit(solution)/shard_map/ppermute | solution.py:632
  297.4 39.8 %collective-permute-start.83 = (bf16[384,384]{1,0:T(8,128)(2,1)S(1)}, bf16[384,384]{1,0:T(8,128)(2,1)S(1)}, u32[]{:S(2)}, u32[]{:S(2)}) collective-permute-start(bf16[384,384]{1,0:T(8,128)(2,1)S(1)} %collective-permute-done.75.rest_7_), channel_id=1, source_target_pairs={{0,8},{8,0},{16,24},{24,16},{1,9},{9,1},{17,25},{25,17},{2,10},{10... | collective-permute-start | bytes 884744 | tf_op jit(solution)/shard_map/ppermute | solution.py:632
  301.5 35.7 %collective-permute-start.98 = (bf16[384,384]{1,0:T(8,128)(2,1)}, bf16[384,384]{1,0:T(8,128)(2,1)S(1)}, u32[]{:S(2)}, u32[]{:S(2)}) collective-permute-start(bf16[384,384]{1,0:T(8,128)(2,1)} %collective-permute-done.90.rest_23_), channel_id=1, source_target_pairs={{0,8},{8,0},{16,24},{24,16},{1,9},{9,1},{17,25},{25,17},{2,10},{10... | collective-permute-start | bytes 884744 | tf_op jit(solution)/shard_map/ppermute | solution.py:632
  530.0 45.7 %collective-permute-start.105 = (bf16[2304,384]{1,0:T(8,128)(2,1)}, bf16[2304,384]{1,0:T(8,128)(2,1)}, u32[]{:S(2)}, u32[]{:S(2)}) collective-permute-start(bf16[2304,384]{1,0:T(8,128)(2,1)} %get-tuple-element.112), channel_id=1, source_target_pairs={{0,8},{8,0},{16,24},{24,16},{1,9},{9,1},{17,25},{25,17},{2,10},{10... | collective-permute-start | bytes 5308424 | tf_op jit(solution)/shard_map/ppermute | solution.py:632
  535.4 34.2 %collective-permute-start.151 = (f32[16,128]{1,0:T(8,128)S(1)}, f32[16,128]{1,0:T(8,128)S(1)}, u32[]{:S(2)}, u32[]{:S(2)}) collective-permute-start(f32[16,128]{1,0:T(8,128)S(1)} %fusion.53), channel_id=1, source_target_pairs={{0,2},{1,3},{2,4},{3,5},{4,6},{5,7},{6,0},{7,1},{8,10},{9,11},{10,... | collective-permute-start | bytes 24584 | tf_op jit(solution)/shard_map/ppermute | solution.py:638
  569.7 27.8 %collective-permute-start.99 = (bf16[2304,384]{1,0:T(8,128)(2,1)}, bf16[2304,384]{1,0:T(8,128)(2,1)}, u32[]{:S(2)}, u32[]{:S(2)}) collective-permute-start(bf16[2304,384]{1,0:T(8,128)(2,1)} %get-tuple-element.110), channel_id=1, source_target_pairs={{0,8},{8,0},{16,24},{24,16},{1,9},{9,1},{17,25},{25,17},{2,10},{10... | collective-permute-start | bytes 5308424 | tf_op jit(solution)/shard_map/ppermute | solution.py:632
  575.1 27.5 %collective-permute-start.129 = (bf16[3072,384]{1,0:T(8,128)(2,1)}, bf16[3072,384]{1,0:T(8,128)(2,1)}, u32[]{:S(2)}, u32[]{:S(2)}) collective-permute-start(bf16[3072,384]{1,0:T(8,128)(2,1)} %get-tuple-element.120), channel_id=1, source_target_pairs={{0,8},{8,0},{16,24},{24,16},{1,9},{9,1},{17,25},{25,17},{2,10},{10... | collective-permute-start | bytes 7077896 | tf_op jit(solution)/shard_map/ppermute | solution.py:632
  575.1 30.6 %collective-permute-start.123 = (bf16[3072,384]{1,0:T(8,128)(2,1)}, bf16[3072,384]{1,0:T(8,128)(2,1)}, u32[]{:S(2)}, u32[]{:S(2)}) collective-permute-start(bf16[3072,384]{1,0:T(8,128)(2,1)} %get-tuple-element.118), channel_id=1, source_target_pairs={{0,8},{8,0},{16,24},{24,16},{1,9},{9,1},{17,25},{25,17},{2,10},{10... | collective-permute-start | bytes 7077896 | tf_op jit(solution)/shard_map/ppermute | solution.py:632
  575.6 34.2 %collective-permute-start.141 = (bf16[768,1536]{1,0:T(8,128)(2,1)}, bf16[768,1536]{1,0:T(8,128)(2,1)}, u32[]{:S(2)}, u32[]{:S(2)}) collective-permute-start(bf16[768,1536]{1,0:T(8,128)(2,1)} %get-tuple-element.124), channel_id=1, source_target_pairs={{0,8},{8,0},{16,24},{24,16},{1,9},{9,1},{17,25},{25,17},{2,10},{10... | collective-permute-start | bytes 7077896 | tf_op jit(solution)/shard_map/ppermute | solution.py:632
  575.7 37.1 %collective-permute-start.135 = (bf16[768,1536]{1,0:T(8,128)(2,1)}, bf16[768,1536]{1,0:T(8,128)(2,1)}, u32[]{:S(2)}, u32[]{:S(2)}) collective-permute-start(bf16[768,1536]{1,0:T(8,128)(2,1)} %get-tuple-element.122), channel_id=1, source_target_pairs={{0,8},{8,0},{16,24},{24,16},{1,9},{9,1},{17,25},{25,17},{2,10},{10... | collective-permute-start | bytes 7077896 | tf_op jit(solution)/shard_map/ppermute | solution.py:632
  597.5 22.6 %collective-permute-start.106 = (bf16[4,288,384]{2,1,0:T(8,128)(2,1)S(1)}, bf16[4,288,384]{2,1,0:T(8,128)(2,1)S(1)}, u32[]{:S(2)}, u32[]{:S(2)}) collective-permute-start(bf16[4,288,384]{2,1,0:T(8,128)(2,1)S(1)} %fusion.6), channel_id=1, source_target_pairs={{0,1},{1,0},{2,3},{3,2},{4,5},{5,4},{6,7},{7,6},{8,9},{9,8},{10,11... | collective-permute-start | bytes 2654216 | tf_op jit(solution)/shard_map/ppermute | solution.py:635
  602.7 36.3 %collective-permute-start.100 = (bf16[4,288,384]{2,1,0:T(8,128)(2,1)S(1)}, bf16[4,288,384]{2,1,0:T(8,128)(2,1)S(1)}, u32[]{:S(2)}, u32[]{:S(2)}) collective-permute-start(bf16[4,288,384]{2,1,0:T(8,128)(2,1)S(1)} %fusion.5), channel_id=1, source_target_pairs={{0,1},{1,0},{2,3},{3,2},{4,5},{5,4},{6,7},{7,6},{8,9},{9,8},{10,11... | collective-permute-start | bytes 2654216 | tf_op jit(solution)/shard_map/ppermute | solution.py:635
  605.7 92.7 %collective-permute-start.130 = (bf16[4,384,384]{2,1,0:T(8,128)(2,1)S(1)}, bf16[4,384,384]{2,1,0:T(8,128)(2,1)S(1)}, u32[]{:S(2)}, u32[]{:S(2)}) collective-permute-start(bf16[4,384,384]{2,1,0:T(8,128)(2,1)S(1)} %fusion.2), channel_id=1, source_target_pairs={{0,1},{1,0},{2,3},{3,2},{4,5},{5,4},{6,7},{7,6},{8,9},{9,8},{10,11... | collective-permute-start | bytes 3538952 | tf_op jit(solution)/shard_map/ppermute | solution.py:635
  609.8 94.5 %collective-permute-start.124 = (bf16[4,384,384]{2,1,0:T(8,128)(2,1)S(1)}, bf16[4,384,384]{2,1,0:T(8,128)(2,1)S(1)}, u32[]{:S(2)}, u32[]{:S(2)}) collective-permute-start(bf16[4,384,384]{2,1,0:T(8,128)(2,1)S(1)} %fusion.1), channel_id=1, source_target_pairs={{0,1},{1,0},{2,3},{3,2},{4,5},{5,4},{6,7},{7,6},{8,9},{9,8},{10,11... | collective-permute-start | bytes 3538952 | tf_op jit(solution)/shard_map/ppermute | solution.py:635
  612.8 118.0 %collective-permute-start.142 = (bf16[4,96,1536]{2,1,0:T(8,128)(2,1)S(1)}, bf16[4,96,1536]{2,1,0:T(8,128)(2,1)S(1)}, u32[]{:S(2)}, u32[]{:S(2)}) collective-permute-start(bf16[4,96,1536]{2,1,0:T(8,128)(2,1)S(1)} %fusion.4), channel_id=1, source_target_pairs={{0,1},{1,0},{2,3},{3,2},{4,5},{5,4},{6,7},{7,6},{8,9},{9,8},{10,11... | collective-permute-start | bytes 3538952 | tf_op jit(solution)/shard_map/ppermute | solution.py:635
  620.1 19.7 %collective-permute-start.107 = (bf16[288,384]{1,0:T(8,128)(2,1)S(1)}, bf16[288,384]{1,0:T(8,128)(2,1)S(1)}, u32[]{:S(2)}, u32[]{:S(2)}) collective-permute-start(bf16[288,384]{1,0:T(8,128)(2,1)S(1)} %fusion.32), channel_id=1, source_target_pairs={{0,2},{1,3},{2,4},{3,5},{4,6},{5,7},{6,0},{7,1},{8,10},{9,11},{10,... | collective-permute-start | bytes 663560 | tf_op jit(solution)/shard_map/ppermute | solution.py:638
  639.0 116.2 %collective-permute-start.136 = (bf16[4,96,1536]{2,1,0:T(8,128)(2,1)S(1)}, bf16[4,96,1536]{2,1,0:T(8,128)(2,1)S(1)}, u32[]{:S(2)}, u32[]{:S(2)}) collective-permute-start(bf16[4,96,1536]{2,1,0:T(8,128)(2,1)S(1)} %fusion.3), channel_id=1, source_target_pairs={{0,1},{1,0},{2,3},{3,2},{4,5},{5,4},{6,7},{7,6},{8,9},{9,8},{10,11... | collective-permute-start | bytes 3538952 | tf_op jit(solution)/shard_map/ppermute | solution.py:635
  697.0 131.2 %collective-permute-start.110 = (bf16[288,384]{1,0:T(8,128)(2,1)S(1)}, bf16[288,384]{1,0:T(8,128)(2,1)S(1)}, u32[]{:S(2)}, u32[]{:S(2)}) collective-permute-start(bf16[288,384]{1,0:T(8,128)(2,1)S(1)} %fusion.44), channel_id=1, source_target_pairs={{0,16},{8,24},{1,17},{9,25},{2,18},{10,26},{3,19},{11,27},{4,20},{... | collective-permute-start | bytes 663560 | tf_op jit(solution)/shard_map/ppermute | solution.py:629
  698.4 131.1 %collective-permute-start.104 = (bf16[288,384]{1,0:T(8,128)(2,1)S(1)}, bf16[288,384]{1,0:T(8,128)(2,1)S(1)}, u32[]{:S(2)}, u32[]{:S(2)}) collective-permute-start(bf16[288,384]{1,0:T(8,128)(2,1)S(1)} %fusion.43), channel_id=1, source_target_pairs={{16,0},{24,8},{17,1},{25,9},{18,2},{26,10},{19,3},{27,11},{20,4},{... | collective-permute-start | bytes 663560 | tf_op jit(solution)/shard_map/ppermute | solution.py:629
  704.3 50.9 %collective-permute-start.131 = (bf16[384,384]{1,0:T(8,128)(2,1)S(1)}, bf16[384,384]{1,0:T(8,128)(2,1)S(1)}, u32[]{:S(2)}, u32[]{:S(2)}) collective-permute-start(bf16[384,384]{1,0:T(8,128)(2,1)S(1)} %fusion.28), channel_id=1, source_target_pairs={{0,2},{1,3},{2,4},{3,5},{4,6},{5,7},{6,0},{7,1},{8,10},{9,11},{10,... | collective-permute-start | bytes 884744 | tf_op jit(solution)/shard_map/ppermute | solution.py:638
  730.8 24.6 %collective-permute-start.125 = (bf16[384,384]{1,0:T(8,128)(2,1)S(1)}, bf16[384,384]{1,0:T(8,128)(2,1)S(1)}, u32[]{:S(2)}, u32[]{:S(2)}) collective-permute-start(bf16[384,384]{1,0:T(8,128)(2,1)S(1)} %fusion.27), channel_id=1, source_target_pairs={{0,2},{1,3},{2,4},{3,5},{4,6},{5,7},{6,0},{7,1},{8,10},{9,11},{10,... | collective-permute-start | bytes 884744 | tf_op jit(solution)/shard_map/ppermute | solution.py:638
  755.4 24.1 %collective-permute-start.132 = (bf16[384,384]{1,0:T(8,128)(2,1)S(1)}, bf16[384,384]{1,0:T(8,128)(2,1)S(1)}, u32[]{:S(2)}, u32[]{:S(2)}) collective-permute-start(bf16[384,384]{1,0:T(8,128)(2,1)S(1)} %fusion.14), channel_id=1, source_target_pairs={{0,2},{1,3},{2,4},{3,5},{4,6},{5,7},{6,0},{7,1},{8,10},{9,11},{10,... | collective-permute-start | bytes 884744 | tf_op jit(solution)/shard_map/ppermute | solution.py:638
  766.9 19.0 %collective-permute-start.126 = (bf16[384,384]{1,0:T(8,128)(2,1)S(1)}, bf16[384,384]{1,0:T(8,128)(2,1)S(1)}, u32[]{:S(2)}, u32[]{:S(2)}) collective-permute-start(bf16[384,384]{1,0:T(8,128)(2,1)S(1)} %fusion.17), channel_id=1, source_target_pairs={{0,2},{1,3},{2,4},{3,5},{4,6},{5,7},{6,0},{7,1},{8,10},{9,11},{10,... | collective-permute-start | bytes 884744 | tf_op jit(solution)/shard_map/ppermute | solution.py:638
  773.2 19.0 %collective-permute-start.144 = (bf16[96,1536]{1,0:T(8,128)(2,1)S(1)}, bf16[96,1536]{1,0:T(8,128)(2,1)S(1)}, u32[]{:S(2)}, u32[]{:S(2)}) collective-permute-start(bf16[96,1536]{1,0:T(8,128)(2,1)S(1)} %fusion.8), channel_id=1, source_target_pairs={{0,2},{1,3},{2,4},{3,5},{4,6},{5,7},{6,0},{7,1},{8,10},{9,11},{10,... | collective-permute-start | bytes 884744 | tf_op jit(solution)/shard_map/ppermute | solution.py:638
  779.6 19.0 %collective-permute-start.138 = (bf16[96,1536]{1,0:T(8,128)(2,1)S(1)}, bf16[96,1536]{1,0:T(8,128)(2,1)S(1)}, u32[]{:S(2)}, u32[]{:S(2)}) collective-permute-start(bf16[96,1536]{1,0:T(8,128)(2,1)S(1)} %fusion.11), channel_id=1, source_target_pairs={{0,2},{1,3},{2,4},{3,5},{4,6},{5,7},{6,0},{7,1},{8,10},{9,11},{10,... | collective-permute-start | bytes 884744 | tf_op jit(solution)/shard_map/ppermute | solution.py:638
  785.9 19.0 %collective-permute-start.133 = (bf16[384,384]{1,0:T(8,128)(2,1)S(1)}, bf16[384,384]{1,0:T(8,128)(2,1)S(1)}, u32[]{:S(2)}, u32[]{:S(2)}) collective-permute-start(bf16[384,384]{1,0:T(8,128)(2,1)S(1)} %fusion.13), channel_id=1, source_target_pairs={{0,2},{1,3},{2,4},{3,5},{4,6},{5,7},{6,0},{7,1},{8,10},{9,11},{10,... | collective-permute-start | bytes 884744 | tf_op jit(solution)/shard_map/ppermute | solution.py:638
  792.2 19.0 %collective-permute-start.127 = (bf16[384,384]{1,0:T(8,128)(2,1)S(1)}, bf16[384,384]{1,0:T(8,128)(2,1)S(1)}, u32[]{:S(2)}, u32[]{:S(2)}) collective-permute-start(bf16[384,384]{1,0:T(8,128)(2,1)S(1)} %fusion.16), channel_id=1, source_target_pairs={{0,2},{1,3},{2,4},{3,5},{4,6},{5,7},{6,0},{7,1},{8,10},{9,11},{10,... | collective-permute-start | bytes 884744 | tf_op jit(solution)/shard_map/ppermute | solution.py:638
  811.2 19.3 %collective-permute-start.134 = (bf16[384,384]{1,0:T(8,128)(2,1)S(1)}, bf16[384,384]{1,0:T(8,128)(2,1)S(1)}, u32[]{:S(2)}, u32[]{:S(2)}) collective-permute-start(bf16[384,384]{1,0:T(8,128)(2,1)S(1)} %fusion.34), channel_id=1, source_target_pairs={{0,16},{8,24},{1,17},{9,25},{2,18},{10,26},{3,19},{11,27},{4,20},{... | collective-permute-start | bytes 884744 | tf_op jit(solution)/shard_map/ppermute | solution.py:629
  (216 other events, 3674.6 us)
Sparse Core Ops, SparseCore 0:
  11.5 88.8 all-gather.1
  593.1 129.9 reduce-scatter.1

commit v3 on v2

v3 whole, which is shorter than its diff:
```python
from functools import partial

import jax
import jax.numpy as jnp
import numpy as np
from jax import lax
from jax.experimental import pallas as pl
from jax.experimental.pallas import tpu as pltpu
from jax.sharding import PartitionSpec as P

HEADS = 12
NORM_EPS = 1e-12
MASKED = -1e30
BF = jnp.bfloat16
F32 = jnp.float32
NT = (((1,), (1,)), ((), ()))
NN = (((1,), (0,)), ((), ()))
TN = (((0,), (0,)), ((), ()))
VMEM_BYTES = 58 * 2**20
TILE = 768
SLACK = 1


def dot(a, b, dims=NN):
    return lax.dot_general(a, b, dims, preferred_element_type=F32)


def span(start, size, unit=128):
    return pl.ds(pl.multiple_of(start, unit), size)


def tiles(count, body):
    def step(i, carry):
        body(i)
        return carry

    lax.fori_loop(0, count, step, 0)


def fetch(copies, sems):
    started = [pltpu.make_async_copy(s, t, sems.at[i]) for i, (s, t) in enumerate(copies)]
    for copy in started:
        copy.start()
    return started


def settle(started):
    for copy in started:
        copy.wait()


def placed(refs, where_ref, layout, target, lanes):
    if len(refs) == 1:
        return [(refs[0], target)]
    core, z, y = where_ref[0], where_ref[1], where_ref[2]
    copies = []
    for i, ref in enumerate(refs):
        c_rel, y_rel, z_rel = i // 8, (i // 4) % 2, i % 4
        block = lax.rem(z - z_rel + 4, 4) * 2 + lax.rem(y + y_rel, 2)
        side = lax.rem(core + c_rel, 2)
        for first, rows, shift in layout:
            place = target.at[
                span(block * rows, rows, 16),
                span(side * lanes + shift * ref.shape[1], ref.shape[1]),
            ]
            copies.append((ref.at[pl.ds(first, rows)], place))
    return copies


def relative(where_ref, block):
    z = lax.rem(block // 2 - where_ref[1] + 4, 4)
    return z * 2 + lax.rem(block % 2 + where_ref[2], 2)


def norm_rows(u_ref, gain, offset, y_ref, low_ref, n_ref, r_ref):
    for i in range(0, u_ref.shape[0], 128):
        rows = pl.ds(i, 128)
        u = u_ref[rows, :]
        center = u - jnp.mean(u, axis=-1, keepdims=True)
        scale = lax.rsqrt(jnp.mean(center * center, axis=-1, keepdims=True) + NORM_EPS)
        normed = center * scale
        y = normed * gain + offset
        y_ref[rows, :] = y
        low_ref[rows, :] = y.astype(BF)
        n_ref[rows, :] = normed
        r_ref[rows, :] = scale


def norm_rows_back(dy_ref, n_ref, r_ref, gain, du_ref, db_ref):
    sums = [jnp.zeros((1, dy_ref.shape[1]), F32)] * 3
    for i in range(0, dy_ref.shape[0], 128):
        rows = pl.ds(i, 128)
        dy = dy_ref[rows, :].astype(F32)
        n = n_ref[rows, :]
        s = dy * gain
        du = r_ref[rows, :] * (
            s - jnp.mean(s, axis=-1, keepdims=True) - n * jnp.mean(s * n, axis=-1, keepdims=True)
        )
        db = du.astype(BF)
        du_ref[rows, :] = du
        db_ref[rows, :] = db
        sums = [
            sums[0] + jnp.sum(dy * n, axis=0, keepdims=True),
            sums[1] + jnp.sum(dy, axis=0, keepdims=True),
            sums[2] + jnp.sum(db.astype(F32), axis=0, keepdims=True),
        ]
    return sums


def split_heads(a):
    first = lax.broadcasted_iota(jnp.int32, a.shape, 1) < a.shape[1] // 2
    zero = jnp.zeros_like(a)
    return jnp.concatenate([jnp.where(first, a, zero), jnp.where(first, zero, a)], axis=0)


def join_heads(a):
    rows = a.shape[0] // 2
    first = lax.broadcasted_iota(jnp.int32, (rows, a.shape[1]), 1) < a.shape[1] // 2
    return jnp.where(first, a[:rows], a[rows:])


def softmax(scores, valid):
    scores = jnp.where(valid, scores * 0.125, MASKED)
    e = jnp.exp(scores - jnp.max(scores, axis=-1, keepdims=True))
    return (e / jnp.sum(e, axis=-1, keepdims=True)).astype(BF)


def score_back(weights, d_weights):
    a = weights.astype(F32)
    t = a * d_weights
    return (t - a * jnp.sum(t, axis=-1, keepdims=True)).astype(BF)


def project_and_norm(x_ref, o_ref, w_ref, dims, bias, gain, offset, outs):
    y_ref, low_ref, n_ref, r_ref = outs
    width = y_ref.shape[1]

    def tile(j):
        cols = span(j * TILE, TILE)
        w = w_ref[cols, :] if dims is NT else w_ref[:, cols]
        y_ref[:, cols] = dot(o_ref[...], w, dims)

    tiles(width // TILE, tile)
    for i in range(0, y_ref.shape[0], 128):
        rows = pl.ds(i, 128)
        y_ref[rows, :] = x_ref[rows, :].astype(F32) + (y_ref[rows, :] + bias)
    norm_rows(y_ref, gain, offset, y_ref, low_ref, n_ref, r_ref)


def self_forward_kernel(count, lengths, where_ref, x_ref, vec_ref, *rest):
    refs, rest = rest[:count], rest[count:]
    p_ref, a_ref, o_ref, y_ref, low_ref, n_ref, r_ref, qkv, out, bias_ref, sems, sems2 = rest
    width = x_ref.shape[1]
    n, m = qkv.shape[0] // 8, out.shape[0] // 8
    whole = count == 2
    first = fetch(placed(refs[:1] if whole else refs, where_ref, [(0, n, 0)], qkv, width // 2), sems)
    second = fetch(placed(refs[1:] if whole else refs, where_ref, [(n, m, 0)], out, width // 2), sems2)
    bias_ref[:, :width] = vec_ref[0:1, :]
    bias_ref[:, width : 2 * width] = jnp.zeros((1, width), F32)
    bias_ref[:, 2 * width :] = vec_ref[1:2, :]
    settle(first)

    def tile(j):
        cols = span(j * TILE, TILE)
        p_ref[:, cols] = (dot(x_ref[...], qkv[cols, :], NT) + bias_ref[:, cols]).astype(BF)

    tiles(3 * width // TILE, tile)
    pairs = width // 128
    row = lax.broadcasted_iota(jnp.int32, (256, 128), 0)
    lane = lax.broadcasted_iota(jnp.int32, (256, 128), 1)
    same = ((row // 64) % 2) == (lane // 64)
    key_lane = lax.broadcasted_iota(jnp.int32, (1, 128), 1)

    def attend(s):
        rows = span(s * 128, 128)
        length = jnp.where(key_lane < 64, lengths[2 * s], lengths[2 * s + 1])
        valid = same & (lax.rem(key_lane, 64) < length)
        for h in range(pairs):
            q = p_ref[rows, pl.ds(h * 128, 128)]
            k = p_ref[rows, pl.ds(width + h * 128, 128)]
            v = p_ref[rows, pl.ds(2 * width + h * 128, 128)]
            a = softmax(dot(split_heads(q), k, NT), valid)
            a_ref[s * pairs + h] = a
            o_ref[rows, pl.ds(h * 128, 128)] = join_heads(dot(a, v)).astype(BF)

    tiles(x_ref.shape[0] // 128, attend)
    settle(second)
    project_and_norm(
        x_ref, o_ref, out, NT, vec_ref[2:3, :], vec_ref[3:4, :], vec_ref[4:5, :], (y_ref, low_ref, n_ref, r_ref)
    )


def self_backward_kernel(count, where_ref, dy_ref, x_ref, vec_ref, p_ref, a_ref, o_ref, n_ref, r_ref, *rest):
    refs, rest = rest[:count], rest[count:]
    dx_ref, own_ref, other_ref, gv_ref = rest[:4]
    qkv, out, db_ref, dmix_ref, dp_ref, rel_ref, g_ref, sems, sems2 = rest[4:]
    width = x_ref.shape[1]
    half = width // 2
    n, m = qkv.shape[0] // 8, out.shape[0] // 8
    whole = count == 2
    second = fetch(placed(refs[1:] if whole else refs, where_ref, [(n, m, 0)], out, half), sems2)
    first = fetch(placed(refs[:1] if whole else refs, where_ref, [(0, n, 0)], qkv, half), sems)
    core = where_ref[0]
    g_gain, g_offset, g_bias = norm_rows_back(dy_ref, n_ref, r_ref, vec_ref[3:4, :], dx_ref, db_ref)
    settle(second)

    def mix(j):
        cols = span(j * TILE, TILE)
        dmix_ref[:, cols] = dot(db_ref[...], out[:, cols]).astype(BF)

    tiles(width // TILE, mix)
    rel_ref[:, :half] = o_ref[:, span(core * half, half)]
    rel_ref[:, half:] = o_ref[:, span((1 - core) * half, half)]

    g_ref[:width, :] = dot(db_ref[...], rel_ref[...], TN).astype(BF)
    for b in range(8):
        to, at = span(relative(where_ref, b) * (n + m) + n, m, 16), pl.ds(b * m, m)
        own_ref[to, :] = g_ref[at, :half]
        other_ref[to, :] = g_ref[at, half:]
    pairs = width // 128

    def attend(s):
        rows = span(s * 128, 128)
        for h in range(pairs):
            q2 = split_heads(p_ref[rows, pl.ds(h * 128, 128)])
            k = p_ref[rows, pl.ds(width + h * 128, 128)]
            v = p_ref[rows, pl.ds(2 * width + h * 128, 128)]
            do2 = split_heads(dmix_ref[rows, pl.ds(h * 128, 128)])
            a = a_ref[s * pairs + h]
            ds = score_back(a, dot(do2, v, NT))
            dp_ref[rows, pl.ds(h * 128, 128)] = (join_heads(dot(ds, k)) * 0.125).astype(BF)
            dp_ref[rows, pl.ds(width + h * 128, 128)] = (dot(ds, q2, TN) * 0.125).astype(BF)
            dp_ref[rows, pl.ds(2 * width + h * 128, 128)] = dot(a, do2, TN).astype(BF)

    tiles(x_ref.shape[0] // 128, attend)
    settle(first)

    def back(j):
        cols = span(j * TILE, TILE)
        dx_ref[:, cols] += dot(dp_ref[...], qkv[:, cols])

    tiles(width // TILE, back)
    rel_ref[:, :half] = x_ref[:, span(core * half, half)]
    rel_ref[:, half:] = x_ref[:, span((1 - core) * half, half)]

    def qkv_grad(j):
        rows = span(j * TILE, TILE)
        g_ref[rows, :] = dot(dp_ref[:, rows], rel_ref[...], TN).astype(BF)

    tiles(3 * width // TILE, qkv_grad)
    for b in range(8):
        to, at = span(relative(where_ref, b) * (n + m), n, 16), pl.ds(b * n, n)
        own_ref[to, :] = g_ref[at, :half]
        other_ref[to, :] = g_ref[at, half:]
    gv_ref[0:1, :] = jnp.sum(dp_ref[:, :width].astype(F32), axis=0, keepdims=True)
    gv_ref[1:2, :] = jnp.sum(dp_ref[:, 2 * width :].astype(F32), axis=0, keepdims=True)
    gv_ref[2:3, :] = g_bias
    gv_ref[3:4, :] = g_gain
    gv_ref[4:5, :] = g_offset


def cross_forward_kernel(x_ref, low_x_ref, keep_ref, k_ref, v_ref, vec_ref, wq_ref, wo_ref, *rest):
    q_ref, a_ref, o_ref, y_ref, low_ref, n_ref, r_ref = rest
    width = x_ref.shape[1]
    patches = k_ref.shape[0] // keep_ref.shape[0]

    def tile(j):
        cols = span(j * TILE, TILE)
        q_ref[:, cols] = (dot(low_x_ref[...], wq_ref[:, cols]) + vec_ref[0:1, cols]).astype(BF)

    tiles(width // TILE, tile)
    pairs = width // 128

    def attend(s):
        rows, keys = span(s * 64, 64, 64), span(s * patches, patches, 16)
        valid = keep_ref[pl.ds(s, 1), :] > 0
        for h in range(pairs):
            q = q_ref[rows, pl.ds(h * 128, 128)]
            k = k_ref[keys, pl.ds(h * 128, 128)]
            v = v_ref[keys, pl.ds(h * 128, 128)]
            a = softmax(dot(split_heads(q), k, NT), valid)
            a_ref[s * pairs + h] = a
            o_ref[rows, pl.ds(h * 128, 128)] = join_heads(dot(a, v)).astype(BF)

    tiles(keep_ref.shape[0], attend)
    project_and_norm(
        x_ref, o_ref, wo_ref, NN, vec_ref[2:3, :], vec_ref[3:4, :], vec_ref[4:5, :], (y_ref, low_ref, n_ref, r_ref)
    )


def cross_backward_kernel(dy_ref, low_x_ref, k_ref, v_ref, vec_ref, wq_ref, wo_ref, q_ref, a_ref, o_ref, n_ref, r_ref, *rest):
    dx_ref, dk_ref, dv_ref, gq_ref, go_ref, gv_ref, db_ref, dmix_ref, dq_ref = rest
    width = low_x_ref.shape[1]
    patches = a_ref.shape[2]
    g_gain, g_offset, g_bias = norm_rows_back(dy_ref, n_ref, r_ref, vec_ref[3:4, :], dx_ref, db_ref)

    def mix(j):
        cols = span(j * TILE, TILE)
        dmix_ref[:, cols] = dot(db_ref[...], wo_ref[cols, :], NT).astype(BF)
        go_ref[cols, :] = dot(o_ref[:, cols], db_ref[...], TN).astype(BF)

    tiles(width // TILE, mix)
    pairs = width // 128

    def attend(s):
        rows, keys = span(s * 64, 64, 64), span(s * patches, patches, 16)
        for h in range(pairs):
            q2 = split_heads(q_ref[rows, pl.ds(h * 128, 128)])
            k = k_ref[keys, pl.ds(h * 128, 128)]
            v = v_ref[keys, pl.ds(h * 128, 128)]
            do2 = split_heads(dmix_ref[rows, pl.ds(h * 128, 128)])
            a = a_ref[s * pairs + h]
            ds = score_back(a, dot(do2, v, NT))
            dq_ref[rows, pl.ds(h * 128, 128)] = (join_heads(dot(ds, k)) * 0.125).astype(BF)
            dk_ref[keys, pl.ds(h * 128, 128)] = (dot(ds, q2, TN) * 0.125).astype(BF)
            dv_ref[keys, pl.ds(h * 128, 128)] = dot(a, do2, TN).astype(BF)

    tiles(a_ref.shape[0] // pairs, attend)

    def back(j):
        cols = span(j * TILE, TILE)
        dx_ref[:, cols] += dot(dq_ref[...], wq_ref[cols, :], NT)
        gq_ref[cols, :] = dot(low_x_ref[:, cols], dq_ref[...], TN).astype(BF)

    tiles(width // TILE, back)
    gv_ref[0:1, :] = jnp.sum(dq_ref[...].astype(F32), axis=0, keepdims=True)
    gv_ref[1:2, :] = jnp.sum(dv_ref[...].astype(F32), axis=0, keepdims=True)
    gv_ref[2:3, :] = g_bias
    gv_ref[3:4, :] = g_gain
    gv_ref[4:5, :] = g_offset


def gelu_parts(h):
    size = jnp.abs(h) * 0.7071067811865476
    t = 1.0 / (1.0 + 0.3275911 * size)
    e = jnp.exp(-size * size)
    poly = t * (0.254829592 + t * (-0.284496736 + t * (1.421413741 + t * (-1.453152027 + t * 1.061405429))))
    tail = 0.5 * poly * e
    cdf = jnp.where(h < 0, tail, 1.0 - tail)
    return h * cdf, cdf + h * (e * 0.3989422804014327)


def feed_forward_kernel(count, base, where_ref, x_ref, low_x_ref, vec_ref, bias_ref, *rest):
    refs, rest = rest[:count], rest[count:]
    whole = count == 2
    act_ref, slope_ref, y_ref, low_ref, n_ref, r_ref, up, down, sems, sems2 = rest
    width, hidden = x_ref.shape[1], up.shape[0]
    n, m = hidden // 8, width // 8
    quarter = [(base + n + m * i, m, i) for i in range(hidden // width)]
    first = fetch(placed(refs[:1] if whole else refs, where_ref, [(base, n, 0)], up, width // 2), sems)
    second = fetch(placed(refs[1:] if whole else refs, where_ref, quarter, down, hidden // 2), sems2)
    settle(first)

    def tile(j):
        cols = span(j * TILE, TILE)
        h = dot(low_x_ref[...], up[cols, :], NT) + bias_ref[:, cols]
        act, slope = gelu_parts(h)
        act_ref[:, cols] = act.astype(BF)
        slope_ref[:, cols] = slope.astype(BF)

    tiles(hidden // TILE, tile)
    settle(second)
    project_and_norm(
        x_ref, act_ref, down, NT, vec_ref[5:6, :], vec_ref[6:7, :], vec_ref[7:8, :], (y_ref, low_ref, n_ref, r_ref)
    )


def feed_backward_kernel(count, base, where_ref, dy_ref, low_x_ref, vec_ref, act_ref, slope_ref, n_ref, r_ref, *rest):
    refs, rest = rest[:count], rest[count:]
    whole = count == 2
    dx_ref, own_ref, other_ref, gv_ref, gb_ref = rest[:5]
    up, down, db_ref, dbt_ref, dh_ref, rel_ref, sems, sems2 = rest[5:]
    width, hidden = low_x_ref.shape[1], up.shape[0]
    n, m, half = hidden // 8, width // 8, width // 2
    quarter = [(base + n + m * i, m, i) for i in range(hidden // width)]
    second = fetch(placed(refs[1:] if whole else refs, where_ref, quarter, down, hidden // 2), sems2)
    first = fetch(placed(refs[:1] if whole else refs, where_ref, [(base, n, 0)], up, half), sems)
    core = where_ref[0]
    g_gain, g_offset, g_bias = norm_rows_back(dy_ref, n_ref, r_ref, vec_ref[6:7, :], dx_ref, db_ref)
    settle(second)
    def down_tile(j):
        cols = span(j * TILE, TILE)
        dh = (dot(db_ref[...], down[:, cols]) * slope_ref[:, cols].astype(F32)).astype(BF)
        dh_ref[:, cols] = dh
        gb_ref[:, cols] = jnp.sum(dh.astype(F32), axis=0, keepdims=True)

    tiles(hidden // TILE, down_tile)
    dbt_ref[...] = db_ref[...].T

    def down_grad(j):
        for ref, side in ((own_ref, core), (other_ref, 1 - core)):
            g = dot(dbt_ref[...], act_ref[:, span(side * (hidden // 2) + j * width, width)]).astype(BF)
            for b in range(8):
                for k in range(2):
                    to = span(relative(where_ref, b) * (n + 4 * m) + n + (2 * j + k) * m, m, 16)
                    ref[to, :] = g[b * m : (b + 1) * m, k * half : (k + 1) * half]

    tiles(hidden // 2 // width, down_grad)
    rel_ref[:, :half] = low_x_ref[:, span(core * half, half)]
    rel_ref[:, half:] = low_x_ref[:, span((1 - core) * half, half)]

    def up_grad(j):
        g = dot(dh_ref[:, span(j * 2 * n, 2 * n)], rel_ref[...], TN).astype(BF)
        for k in range(2):
            to = span(relative(where_ref, 2 * j + k) * (n + 4 * m), n, 16)
            own_ref[to, :] = g[k * n : (k + 1) * n, :half]
            other_ref[to, :] = g[k * n : (k + 1) * n, half:]

    tiles(4, up_grad)
    settle(first)

    def back(j):
        cols = span(j * TILE, TILE)
        dx_ref[:, cols] += dot(dh_ref[...], up[:, cols])

    tiles(width // TILE, back)
    gv_ref[0:1, :] = g_bias
    gv_ref[1:2, :] = g_gain
    gv_ref[2:3, :] = g_offset


def struct(*shape, dtype=F32):
    return jax.ShapeDtypeStruct(shape, dtype)


VMEM = pl.BlockSpec(memory_space=pltpu.VMEM)
SMEM = pl.BlockSpec(memory_space=pltpu.SMEM)
ANYWHERE = pl.BlockSpec(memory_space=pl.ANY)


def call(kernel, outs, specs, scratch, us, args):
    return pl.pallas_call(
        kernel,
        out_shape=outs,
        in_specs=specs,
        out_specs=[VMEM] * len(outs),
        scratch_shapes=scratch,
        cost_estimate=pl.CostEstimate(flops=int(us * 1.1e9), bytes_accessed=int(us * 3.5e6), transcendentals=0),
        compiler_params=pltpu.CompilerParams(vmem_limit_bytes=VMEM_BYTES),
    )(*args)


def copy_sems(count, parts=1):
    return pltpu.SemaphoreType.DMA((max(1, (count if count > 2 else 1) * parts),))


def self_forward(x, lengths, where, vec, weights):
    rows, width = x.shape
    blocks = rows // 128 * (width // 128)
    count = len(weights)
    outs = [
        struct(rows, 3 * width, dtype=BF),
        struct(blocks, 256, 128, dtype=BF),
        struct(rows, width, dtype=BF),
        struct(rows, width),
        struct(rows, width, dtype=BF),
        struct(rows, width),
        struct(rows, 1),
    ]
    scratch = [
        pltpu.VMEM((3 * width, width), BF),
        pltpu.VMEM((width, width), BF),
        pltpu.VMEM((1, 3 * width), F32),
        copy_sems(count),
        copy_sems(count),
    ]
    p, a, o, y, low, n, r = call(
        partial(self_forward_kernel, count),
        outs,
        [SMEM, SMEM, VMEM, VMEM] + [ANYWHERE] * count,
        scratch,
        14,
        (lengths, where, x, vec, *weights),
    )
    return y, low, (x, p, a, o, n, r)


def self_backward(dy, saved, where, vec, weights):
    x, p, a, o, n, r = saved
    rows, width = x.shape
    half = width // 2
    count = len(weights)
    outs = [
        struct(rows, width),
        struct(4 * width, half, dtype=BF),
        struct(4 * width, half, dtype=BF),
        struct(8, width),
    ]
    scratch = [
        pltpu.VMEM((3 * width, width), BF),
        pltpu.VMEM((width, width), BF),
        pltpu.VMEM((rows, width), BF),
        pltpu.VMEM((rows, width), BF),
        pltpu.VMEM((rows, 3 * width), BF),
        pltpu.VMEM((rows, width), BF),
        pltpu.VMEM((3 * width, width), BF),
        copy_sems(count),
        copy_sems(count),
    ]
    return call(
        partial(self_backward_kernel, count),
        outs,
        [SMEM] + [VMEM] * 8 + [ANYWHERE] * count,
        scratch,
        22,
        (where, dy, x, vec, p, a, o, n, r, *weights),
    )


def cross_forward(x, low_x, keep, k, v, vec, wq, wo):
    rows, width = x.shape
    samples, patches = keep.shape
    outs = [
        struct(rows, width, dtype=BF),
        struct(samples * (width // 128), 128, patches, dtype=BF),
        struct(rows, width, dtype=BF),
        struct(rows, width),
        struct(rows, width, dtype=BF),
        struct(rows, width),
        struct(rows, 1),
    ]
    q, a, o, y, low, n, r = call(
        cross_forward_kernel, outs, [VMEM] * 8, [], 21, (x, low_x, keep, k, v, vec, wq, wo)
    )
    return y, low, (low_x, k, v, q, a, o, n, r)


def cross_backward(dy, saved, vec, wq, wo):
    low_x, k, v, q, a, o, n, r = saved
    rows, width = low_x.shape
    outs = [
        struct(rows, width),
        struct(*k.shape, dtype=BF),
        struct(*k.shape, dtype=BF),
        struct(width, width, dtype=BF),
        struct(width, width, dtype=BF),
        struct(8, width),
    ]
    scratch = [pltpu.VMEM((rows, width), BF)] * 3
    return call(
        cross_backward_kernel,
        outs,
        [VMEM] * 12,
        scratch,
        26,
        (dy, low_x, k, v, vec, wq, wo, q, a, o, n, r),
    )


def feed_forward(x, low_x, where, vec, bias, weights, base=0):
    rows, width = x.shape
    hidden = bias.shape[1]
    count = len(weights)
    outs = [
        struct(rows, hidden, dtype=BF),
        struct(rows, hidden, dtype=BF),
        struct(rows, width),
        struct(rows, width, dtype=BF),
        struct(rows, width),
        struct(rows, 1),
    ]
    scratch = [
        pltpu.VMEM((hidden, width), BF),
        pltpu.VMEM((width, hidden), BF),
        copy_sems(count),
        copy_sems(count, hidden // width),
    ]
    act, slope, y, low, n, r = call(
        partial(feed_forward_kernel, count, base),
        outs,
        [SMEM] + [VMEM] * 4 + [ANYWHERE] * count,
        scratch,
        20,
        (where, x, low_x, vec, bias, *weights),
    )
    return y, low, (low_x, act, slope, n, r)


def feed_backward(dy, saved, where, vec, weights, base=0):
    low_x, act, slope, n, r = saved
    rows, width = low_x.shape
    hidden = act.shape[1]
    count = len(weights)
    outs = [
        struct(rows, width),
        struct(2 * hidden, width // 2, dtype=BF),
        struct(2 * hidden, width // 2, dtype=BF),
        struct(8, width),
        struct(1, hidden),
    ]
    scratch = [
        pltpu.VMEM((hidden, width), BF),
        pltpu.VMEM((width, hidden), BF),
        pltpu.VMEM((rows, width), BF),
        pltpu.VMEM((width, rows), BF),
        pltpu.VMEM((rows, hidden), BF),
        pltpu.VMEM((rows, width), BF),
        copy_sems(count),
        copy_sems(count, hidden // width),
    ]
    return call(
        partial(feed_backward_kernel, count, base),
        outs,
        [SMEM] + [VMEM] * 7 + [ANYWHERE] * count,
        scratch,
        22,
        (where, dy, low_x, vec, act, slope, n, r, *weights),
    )


def lane_slices(a, lanes):
    return jnp.concatenate([a[:, i : i + lanes] for i in range(0, a.shape[1], lanes)], axis=0)


def lane_join(a, count):
    rows = a.shape[-2] // count
    return jnp.concatenate([a[..., i * rows : (i + 1) * rows, :] for i in range(count)], axis=-1)


def pad_to(a, rows, lanes):
    return jnp.pad(a, ((0, rows - a.shape[0]), (0, lanes - a.shape[1])))


def dynamic(a, index, axis):
    return lax.dynamic_index_in_dim(a, index, axis, keepdims=False)


def after(value, tokens):
    return lax.optimization_barrier((value, tokens))[0] if tokens else value


class Grid:
    def __init__(self):
        pipe, dp = lax.axis_index("pipe"), lax.axis_index("dp")
        self.x, self.core = pipe // 2, pipe % 2
        self.z, self.y = dp // 2, dp % 2
        self.arrived, self.computed = [()] * 2, ()

    def swap_x(self, a):
        return lax.ppermute(a, "pipe", [(i, i ^ 2) for i in range(4)])

    def to_text(self, a):
        return lax.ppermute(a, "pipe", [(2, 0), (3, 1)])

    def to_joining(self, a):
        return lax.ppermute(a, "pipe", [(0, 2), (1, 3)])

    def swap_core(self, a):
        return lax.ppermute(a, "pipe", [(i, i ^ 1) for i in range(4)])

    def swap_y(self, a):
        return lax.ppermute(a, "dp", [(i, i ^ 1) for i in range(8)])

    def ring_z(self, a, step=1):
        return lax.ppermute(a, "dp", [(i, (i + 2 * step) % 8) for i in range(8)])

    def in_order(self, place, own, other):
        return jnp.where(place == 0, jnp.stack([own, other]), jnp.stack([other, own]))

    def z_order(self, ring):
        order = jnp.stack([ring[0], ring[3], ring[2], ring[1]] * 2)
        return lax.dynamic_slice_in_dim(order, (4 - self.z) % 4, 4, 0)

    def turn(self, *moves, pre=(), compute=None, args=()):
        tokens = (*self.arrived[-SLACK], *self.computed)
        arrived = []

        def begin(asked):
            asked = [ask for group in asked for ask in group()]
            values = after([value for _, value, _ in asked], tokens)
            for (move, _, keep), value in zip(asked, values):
                result = move(value)
                arrived.append(result)
                keep(result)
            return tuple(values)

        begin(pre)
        values = begin(moves)
        self.arrived.append(tuple(arrived))
        self.computed = ()
        if compute is None:
            return None
        result = compute(*after(tuple(args), tokens + values))
        self.computed = tuple(jax.tree.leaves(result))
        return result


class Gather:
    def __init__(self, grid, piece, y_first=False):
        self.grid, self.y_first = grid, y_first
        self.ring, self.across, self.swapped = [piece], [], {}

    def z(self):
        rings = [self.ring, self.across] if self.y_first else [self.ring]
        return [(self.grid.ring_z, ring[-1], ring.append) for ring in rings]

    def y(self, count=1):
        at = len(self.across)
        return [(self.grid.swap_y, p, self.across.append) for p in self.ring[at : at + count]]

    def y2(self):
        return self.y(2)

    def c(self):
        here = dict([((0, k), p) for k, p in enumerate(self.ring)] + [((1, k), p) for k, p in enumerate(self.across)])
        return [
            (self.grid.swap_core, p, partial(self.swapped.__setitem__, key))
            for key, p in here.items()
            if key not in self.swapped
        ]

    def pieces(self):
        other = [self.swapped[side, k] for side in range(2) for k in range(4)]
        return [*self.ring, *self.across, *other]


class BlockGather:
    def __init__(self, grid, block):
        self.grid, self.ring, self.sets = grid, [block], {}

    def keep(self, *key):
        return partial(self.sets.__setitem__, key)

    def z(self):
        return [(self.grid.ring_z, self.ring[-1], self.ring.append)]

    def z_all(self):
        return [(partial(self.grid.ring_z, step=k), self.ring[0], self.ring.append) for k in (1, 2, 3)]

    def start(self):
        if (0, 0, 0) not in self.sets:
            self.sets[0, 0, 0] = self.grid.z_order(self.ring)

    def y(self):
        self.start()
        return [(self.grid.swap_y, self.sets[0, 0, 0], self.keep(0, 0, 1))]

    def x0(self):
        self.start()
        return [(self.grid.swap_x, self.sets[0, 0, 0], self.keep(0, 1, 0))]

    def x1(self):
        return [(self.grid.swap_x, self.sets[0, 0, 1], self.keep(0, 1, 1))]

    def c(self):
        return [
            (self.grid.swap_core, self.sets[0, x, y], self.keep(1, x, y)) for x in range(2) for y in range(2)
        ]

    def whole(self):
        g = self.grid
        rel = jnp.stack([self.sets[c, x, y] for c in range(2) for x in range(2) for y in range(2)])
        rows = []
        for x in range(2):
            for c in range(2):
                sides = [dynamic(rel, (g.core ^ c) * 4 + (g.x ^ x) * 2 + (g.y ^ y), 0) for y in range(2)]
                rows.append(jnp.stack(sides, axis=1))
        return jnp.stack(rows).reshape((2, 2) + rows[0].shape)


class Sum:
    def __init__(self, grid, own, other, z_first=False):
        self.grid, self.z_first = grid, z_first
        rows = own.shape[0] // 8
        self.own = own.reshape(4, 2, rows, own.shape[1])
        self.other = other
        self.across, self.ring = {}, [[], []]
        self.came = self.far = None

    def c(self):
        def keep(a):
            self.came = a.reshape(self.own.shape)

        return [(self.grid.swap_core, self.other, keep)]

    def both(self, step, side):
        return self.own[step, side].astype(F32) + self.came[step, side].astype(F32)

    def y(self, *steps):
        if self.z_first:
            value = self.both(0, 1) + self.ring[1][-1].astype(F32)
            return [(self.grid.swap_y, value.astype(BF), partial(self.across.__setitem__, 0))]
        return [
            (self.grid.swap_y, self.both(step, 1).astype(BF), partial(self.across.__setitem__, step)) for step in steps
        ]

    def y32(self):
        return self.y(3, 2)

    def y10(self):
        return self.y(1, 0)

    def y3210(self):
        return self.y(3, 2, 1, 0)

    def block(self, step, side):
        total = self.both(step, side)
        if not self.z_first:
            total = total + self.across[step].astype(F32)
        if self.ring[side]:
            total = total + self.ring[side][-1].astype(F32)
        return total

    def z(self):
        sides = (0, 1) if self.z_first else (0,)
        return [
            (self.grid.ring_z, self.block(3 - len(self.ring[side]), side).astype(BF), self.ring[side].append)
            for side in sides
        ]

    def near(self):
        total = self.block(0, 0)
        return total + self.across[0].astype(F32) if self.z_first else total

    def x(self, to):
        move = self.grid.to_joining if to else self.grid.to_text
        return [(move, self.near().astype(BF), partial(setattr, self, "far"))]

    def x_text(self):
        return self.x(0)

    def x_joining(self):
        return self.x(1)

    def total(self):
        return self.near() + self.far.astype(F32)


class BlockSum:
    def __init__(self, grid, a, dtype):
        self.grid, self.a, self.dtype = grid, a, dtype
        self.ring = None

    def step(self, swap, place, axis):
        own = dynamic(self.a, place, axis)

        def keep(came):
            self.a = own.astype(F32) + came.astype(F32)

        return [(swap, dynamic(self.a, 1 - place, axis).astype(self.dtype), keep)]

    def c(self):
        return self.step(self.grid.swap_core, self.grid.core, 1)

    def x(self):
        return self.step(self.grid.swap_x, self.grid.x, 0)

    def y(self):
        return self.step(self.grid.swap_y, self.grid.y, 1)

    def z(self):
        if self.ring is None:
            self.ring = []
        value = self.block(3 - len(self.ring))
        return [(self.grid.ring_z, value.astype(self.dtype), self.ring.append)]

    def block(self, step):
        value = dynamic(self.a, (self.grid.z + step) % 4, 0).astype(F32)
        return value + self.ring[-1].astype(F32) if self.ring else value

    def total(self):
        return self.block(0)


def masks(caption_len, phrase_len, box_count, patch_mask, text_rows, patches):
    slots = jnp.arange(phrase_len.shape[1], dtype=jnp.int32)
    phrase_total = jnp.sum(jnp.where(slots[None, :] < box_count[:, None], phrase_len, 0), axis=1)
    lengths = jnp.minimum(caption_len + phrase_total, text_rows)
    first_patch = (jnp.arange(patch_mask.shape[1], dtype=jnp.int32) == 0).astype(jnp.int32)
    keep = jnp.maximum(patch_mask, first_patch[None, :]).astype(F32)
    return lengths, jnp.pad(keep, ((0, 0), (0, patches - keep.shape[1])))


def on_device(
    text_embed,
    image_feats,
    caption_len,
    phrase_len,
    box_count,
    patch_mask,
    attn_qkv,
    attn_out,
    ffn_up,
    ffn_down,
    layer_vectors,
    cross_query,
    cross_kv,
    cross_out,
    cross_vectors,
    cotangent,
):
    n_pipe, n_dp = lax.axis_size("pipe"), lax.axis_size("dp")
    everyone = ("pipe", "dp")
    shards, half = n_pipe * n_dp, n_pipe // 2
    samples, text_rows, width = text_embed.shape
    hidden = ffn_up.shape[1] * n_dp
    lanes = attn_qkv.shape[0]
    patches = -(-image_feats.shape[1] // 32) * 32
    direct = (n_pipe, n_dp) == (4, 8) and lanes % 128 == 0
    lengths, patch_keep = masks(caption_len, phrase_len, box_count, patch_mask, text_rows, patches)
    x = text_embed.reshape(-1, width)
    image = jnp.pad(image_feats, ((0, 0), (0, patches - image_feats.shape[1]), (0, 0)))
    image = image.reshape(samples * patches, -1)

    c_rows = cross_query.shape[0]
    kv_slices = cross_kv.shape[1] // width
    cross_pack = jnp.concatenate([cross_query, cross_out, lane_slices(cross_kv, width)], axis=0)
    v_rows, v_lanes = layer_vectors.shape
    x_rows = cross_vectors.shape[1]
    small = jnp.concatenate([pad_to(layer_vectors, v_rows, 128), pad_to(cross_vectors.T, x_rows, 128)], axis=0)
    small = pad_to(small, 16, 128).astype(F32)
    pack_attn = jnp.concatenate([attn_qkv.T, attn_out.T], axis=0)
    pack_feed = jnp.concatenate([ffn_up.T, lane_slices(ffn_down.T, lanes)], axis=0)

    def cross_weights(blocks):
        blocks = blocks.reshape(shards, -1, width)
        i_rows = cross_kv.shape[0]
        ends = np.cumsum([0, c_rows, c_rows, i_rows, i_rows])
        return [blocks[:, a:b].reshape(-1, width) for a, b in zip(ends[:-1], ends[1:])]

    def vectors_of(blocks):
        blocks = blocks.reshape(n_pipe, n_dp, 16, 128)
        vecs = []
        for layer in range(2):
            v = blocks[layer * half : (layer + 1) * half, :, :v_rows, :v_lanes]
            vecs.append(jnp.moveaxis(v, 1, 2).reshape(12, width))
        cvec = blocks.reshape(shards, 16, 128)[:, v_rows : v_rows + x_rows, :c_rows]
        return vecs, [v[8:12].reshape(1, hidden) for v in vecs], jnp.moveaxis(cvec, 1, 0).reshape(x_rows, width)

    def keys_values(wk, wv, cvec):
        keys = jnp.dot(image, wk, preferred_element_type=F32).astype(BF)
        return keys, (jnp.dot(image, wv, preferred_element_type=F32) + cvec[1]).astype(BF)

    def pack_cross(dk, dv, g_cq, g_co):
        grads = [g_cq, g_co, dot(image, dk, TN).astype(BF), dot(image, dv, TN).astype(BF)]
        return jnp.concatenate([g.reshape(shards, -1, width) for g in grads], axis=1)

    def vector_block(v_self, v_feed, v_up):
        v = jnp.concatenate([v_self[:5], v_feed[:3], v_up.reshape(4, width)], axis=0)
        return jnp.moveaxis(v.reshape(half, v_rows, n_dp, v_lanes), 2, 1)

    def pack_vectors(text, joining, v_cross):
        section = jnp.concatenate([vector_block(*text), vector_block(*joining)], axis=0)
        cross = jnp.moveaxis(v_cross[:x_rows].reshape(x_rows, n_pipe, n_dp, c_rows), 0, 2)
        wide = [jnp.pad(v, ((0, 0), (0, 0), (0, 0), (0, 128 - v.shape[3]))) for v in (section, cross)]
        wide = jnp.concatenate(wide, axis=2)
        return jnp.pad(wide, ((0, 0), (0, 0), (0, 16 - wide.shape[2]), (0, 0)))

    seed = cotangent.reshape(-1, width)
    if direct:
        grid = Grid()
        turn = grid.turn
        n_attn = pack_attn.shape[0]
        where = jnp.stack([grid.core, grid.z, grid.y]).astype(jnp.int32)
        vec_gather = BlockGather(grid, small)
        cross_whole = lax.all_gather(cross_pack, everyone, axis=0, tiled=True)
        met = {}

        def meet(name, pack):
            return [(grid.swap_x, pack, partial(met.__setitem__, name))]

        def of_layer(layer, pack, other, **how):
            return Gather(grid, jnp.where(grid.x == layer, pack, other), **how)

        turn(partial(meet, "attn", pack_attn), partial(meet, "feed", pack_feed), vec_gather.z_all)
        both = [jnp.concatenate([pack_attn, pack_feed]), jnp.concatenate([met["attn"], met["feed"]])]
        text = of_layer(0, *both)
        attn2 = of_layer(1, pack_attn, met["attn"])
        feed2 = of_layer(1, pack_feed, met["feed"])
        turn(text.z, text.y, vec_gather.y)
        turn(text.z, text.y, vec_gather.x0, vec_gather.x1)
        turn(text.z, text.y, text.c, vec_gather.c)
        turn(text.y, text.c, attn2.z, attn2.y)
        vecs, biases, cvec = vectors_of(vec_gather.whole())
        state, low, s_self = turn(
            attn2.y, attn2.z, feed2.y, feed2.z, pre=(text.c,),
            compute=lambda x: self_forward(x, lengths, where, vecs[0], text.pieces()), args=(x,),
        )
        state, passed, s_feed = turn(
            attn2.y, attn2.z, feed2.y, feed2.z,
            compute=lambda state, low: feed_forward(state, low, where, vecs[0], biases[0], text.pieces(), n_attn),
            args=(state, low),
        )

        def third(cross_whole):
            wq, wo, wk, wv = cross_weights(cross_whole)
            return *keys_values(wk, wv, cvec), wq, wo

        keys, values, wq, wo = turn(
            attn2.y, feed2.y, feed2.z, attn2.c, compute=third, args=(cross_whole,)
        )
        state, low, s_self2 = turn(
            feed2.y, feed2.c, pre=(attn2.c,),
            compute=lambda passed: self_forward(passed, lengths, where, vecs[1], attn2.pieces()), args=(passed,),
        )
        state, low, s_cross = turn(
            feed2.c, compute=lambda *a: cross_forward(*a, patch_keep, keys, values, cvec, wq, wo), args=(state, low)
        )

        def last(state, low):
            joined, _, s_feed2 = feed_forward(state, low, where, vecs[1], biases[1], feed2.pieces())
            return joined, feed_backward(seed, s_feed2, where, vecs[1], feed2.pieces())

        joined, (grad, *g_feed2, v_feed2, v_up2) = turn(compute=last, args=(state, low))

        sum3 = Sum(grid, *g_feed2)
        grad, dk, dv, g_cq, g_co, v_cross = turn(
            sum3.y32, pre=(sum3.c,), compute=lambda grad: cross_backward(grad, s_cross, cvec, wq, wo), args=(grad,)
        )
        grad, *g_self2, v_self2 = turn(
            sum3.y10, sum3.z,
            compute=lambda grad: self_backward(grad, s_self2, where, vecs[1], attn2.pieces()), args=(grad,),
        )
        sum2 = Sum(grid, *g_self2)
        cross_grads, grad = turn(
            sum2.c, sum3.z, compute=lambda *a: (pack_cross(*a[:4]), a[4].astype(BF)), args=(dk, dv, g_cq, g_co, grad)
        )
        sum_cross = BlockSum(grid, cross_grads.reshape(2, 2, 4, 2, -1, width), BF)
        grad, *g_feed1, v_feed, v_up = turn(
            sum2.y3210, sum3.z, sum_cross.c,
            compute=lambda grad: feed_backward(grad, s_feed, where, vecs[0], text.pieces(), n_attn), args=(grad,),
        )
        sum1 = Sum(grid, *g_feed1)
        embed_grad, *g_self1, v_self = turn(
            sum1.y32, sum2.z, sum_cross.x, pre=(sum1.c,),
            compute=lambda grad: self_backward(grad, s_self, where, vecs[0], text.pieces()), args=(grad,),
        )
        sum0 = Sum(grid, *g_self1)
        sum_vec = BlockSum(
            grid,
            pack_vectors((v_self, v_feed, v_up), (v_self2, v_feed2, v_up2), v_cross).reshape(2, 2, 4, 2, 16, 128),
            F32,
        )
        turn(sum1.y10, sum1.z, sum2.z, sum3.x_joining, sum_vec.c, pre=(sum0.c,))
        turn(sum0.y3210, sum1.z, sum2.z, sum_vec.x)
        turn(sum0.z, sum1.z, sum2.x_joining, sum_cross.y, sum_vec.y)
        turn(sum0.z, sum1.x_text, sum_cross.z, sum_vec.z)
        turn(sum0.z, sum_cross.z, sum_vec.z)
        turn(sum0.x_text, sum_cross.z, sum_vec.z)
        text = grid.x == 0
        attn_grads = jnp.where(text, sum0.total(), sum2.total())
        feed_grads = jnp.where(text, sum1.total(), sum3.total())
        n_qkv, n_up = attn_qkv.shape[1], ffn_up.shape[1]
        mine = [attn_grads[:n_qkv], attn_grads[n_qkv:], feed_grads[:n_up], feed_grads[n_up:]]
        cross_grads, small = sum_cross.total(), sum_vec.total()
    else:
        where = jnp.zeros((3,), jnp.int32)
        vectors = lax.all_gather(small, everyone, axis=0, tiled=False)
        whole = lax.all_gather(jnp.concatenate([pack_attn, pack_feed], axis=0), everyone, axis=0, tiled=False)
        whole = whole.reshape(n_pipe, n_dp, -1, lanes)

        def section(piece, layer):
            piece = jnp.moveaxis(piece[layer * half : (layer + 1) * half], 0, 2)
            return piece.reshape(n_dp * piece.shape[1], half * piece.shape[-1])

        counts = [attn_qkv.shape[1], attn_out.shape[1], ffn_up.shape[1], attn_out.shape[1] * (hidden // width)]
        ends = np.cumsum([0] + counts)
        cut = [whole[:, :, a:b] for a, b in zip(ends[:-1], ends[1:])]
        cut[3] = lane_join(cut[3], hidden // width)
        (qkv1, out1, up1, down1), (qkv2, out2, up2, down2) = ([section(c, k) for c in cut] for k in range(2))
        vecs, biases, cvec = vectors_of(vectors)
        wq, wo, wk, wv = cross_weights(lax.all_gather(cross_pack, everyone, axis=0, tiled=False))
        state, low, s_self = self_forward(x, lengths, where, vecs[0], [qkv1, out1])
        state, passed, s_feed = feed_forward(state, low, where, vecs[0], biases[0], [up1, down1])
        state, low, s_self2 = self_forward(passed, lengths, where, vecs[1], [qkv2, out2])
        keys, values = keys_values(wk, wv, cvec)
        state, low, s_cross = cross_forward(state, low, patch_keep, keys, values, cvec, wq, wo)
        joined, _, s_feed2 = feed_forward(state, low, where, vecs[1], biases[1], [up2, down2])
        grad, *g_feed2, v_feed2, v_up2 = feed_backward(seed, s_feed2, where, vecs[1], [up2, down2])
        grad, dk, dv, g_cq, g_co, v_cross = cross_backward(grad, s_cross, cvec, wq, wo)
        grad, *g_self2, v_self2 = self_backward(grad, s_self2, where, vecs[1], [qkv2, out2])
        grad, *g_feed1, v_feed, v_up = feed_backward(grad.astype(BF), s_feed, where, vecs[0], [up1, down1])
        embed_grad, *g_self1, v_self = self_backward(grad, s_self, where, vecs[0], [qkv1, out1])

        def unpack(pair, rows, slices):
            parts = []
            at = 0
            for r, k in zip(rows, slices):
                sides = [p.reshape(8, -1, p.shape[1])[:, at : at + r * k] for p in pair]
                sides = [lane_join(p, k).reshape(8 * r, -1) for p in sides]
                parts.append(jnp.concatenate(sides, axis=1))
                at += r * k
            return parts

        def split(first, second):
            both = jnp.stack([first, second])
            rows, k = both.shape[1] // n_dp, both.shape[2] // (half * lanes)
            both = both.reshape(2, n_dp, rows, half, k, lanes)
            return both.transpose(0, 3, 1, 4, 2, 5).reshape(n_pipe, n_dp, k * rows, lanes)

        attn = ((3 * width // 8, width // 8), (1, 1))
        feed = ((hidden // 8, width // 8), (1, hidden // width))
        parts = []
        for first, second, shape in ((g_self1, g_self2, attn), (g_feed1, g_feed2, feed)):
            parts += [split(a, b) for a, b in zip(unpack(first, *shape), unpack(second, *shape))]
        packed = jnp.concatenate(parts, axis=2).reshape(-1, lanes)
        packed = lax.psum_scatter(packed, everyone, scatter_dimension=0, tiled=True).astype(F32)
        mine = [packed[a:b] for a, b in zip(ends[:-1], ends[1:])]
        cross_grads = pack_cross(dk, dv, g_cq, g_co).reshape(-1, width)
        cross_grads = lax.psum_scatter(cross_grads, everyone, scatter_dimension=0, tiled=True).astype(F32)
        small = pack_vectors((v_self, v_feed, v_up), (v_self2, v_feed2, v_up2), v_cross)
        small = lax.psum_scatter(small.reshape(-1, 128), everyone, scatter_dimension=0, tiled=True)
    mine[3] = lane_join(mine[3], hidden // width)
    return (
        joined.reshape(text_embed.shape),
        embed_grad.reshape(text_embed.shape),
        mine[0].T,
        mine[1].T,
        mine[2].T,
        mine[3].T,
        small[:v_rows, :v_lanes],
        cross_grads[:c_rows],
        lane_join(cross_grads[2 * c_rows :], kv_slices),
        cross_grads[c_rows : 2 * c_rows],
        small[v_rows : v_rows + x_rows, :c_rows].T,
    )


def solution(mesh):
    in_specs = (
        P(("pipe", "dp"), None, None),
        P(("pipe", "dp"), None, None),
        P(("pipe", "dp")),
        P(("pipe", "dp"), None),
        P(("pipe", "dp")),
        P(("pipe", "dp"), None),
        P("pipe", "dp"),
        P("pipe", "dp"),
        P("pipe", "dp"),
        P("pipe", "dp"),
        P("pipe", "dp"),
        P(("pipe", "dp"), None),
        P(("pipe", "dp"), None),
        P(("pipe", "dp"), None),
        P(("pipe", "dp"), None),
        P(("pipe", "dp"), None, None),
    )
    out_specs = (
        P(("pipe", "dp"), None, None),
        P(("pipe", "dp"), None, None),
        P("pipe", "dp"),
        P("pipe", "dp"),
        P("pipe", "dp"),
        P("pipe", "dp"),
        P("pipe", "dp"),
        P(("pipe", "dp"), None),
        P(("pipe", "dp"), None),
        P(("pipe", "dp"), None),
        P(("pipe", "dp"), None),
    )
    return jax.shard_map(
        on_device, mesh=mesh, in_specs=in_specs, out_specs=out_specs, check_vma=False
    )
```

time: 858 us -> 663 us (0.77)
  waiting for transfers between devices: 384 us -> 240 us
  Pallas kernels: 272 us -> 206 us
  other arithmetic: 48.5 us -> 58.9 us
    ppermute x56 -> x34, waiting for transfers between devices: 251 us -> 133 us  [the longest x30 126 us: ring_z(): return lax.ppermute(a, 'dp', [(i, (i + 2 * step) % 8) for i in range(8)])]
    pallas_call x10, Pallas kernels: 272 us -> 206 us  [call(): pl.pallas_call(kernel, out_shape=outs, in_specs=specs, out_specs=[VMEM] *...]
    ppermute x34 -> x31, waiting for transfers between devices: 122 us -> 66.7 us  [swap_y(): return lax.ppermute(a, 'dp', [(i, i ^ 1) for i in range(8)])]
    convert_element_type x41 -> x24, other arithmetic: 17.6 us -> 40.9 us  [the longest x12 20.9 us: z(): self.block(3 - len(self.ring[side]), side).astype(BF)]
    ppermute x5 -> x6, waiting for transfers between devices: 7.52 us -> 28.2 us  [swap_x(): return lax.ppermute(a, 'pipe', [(i, i ^ 2) for i in range(4)])]
    ppermute x56 -> x34, starting transfers between devices: 25 us -> 36.8 us  [the longest x30 27.8 us: ring_z(): return lax.ppermute(a, 'dp', [(i, (i + 2 * step) % 8) for i in range(8)])]
    unnamed x230 -> x212, local copies, waits for them, and re-layouts: 10.2 us -> 20.2 us
    ppermute x34 -> x31, starting transfers between devices: 40.4 us -> 31.7 us  [swap_y(): return lax.ppermute(a, 'dp', [(i, i ^ 1) for i in range(8)])]
  transfers between devices with their start and end apart: 155 -> 106, of which waited for: 68 -> 36; matrix products, arithmetic and copies ran while one was open for 9% -> 13% of each run, Pallas kernels for 12% -> 25%
where the time goes in v3:
time: 663 us; the launch traced here: 655 us
  waiting for transfers between devices  240 us (36%)
  Pallas kernels  206 us (31%)
  starting transfers between devices  84.6 us (13%)
  other arithmetic  58.9 us (9%)
  local copies, waits for them, and re-layouts  35.8 us (5%)
  between operations  16.5 us (2%)
  matrix products  13.2 us (2%)
    pallas_call x10, Pallas kernels, call(): pl.pallas_call(kernel, out_shape=outs, in_specs=specs, out_specs=[VMEM] *...  206 us
    ppermute x30, waiting for transfers between devices, ring_z(): return lax.ppermute(a, 'dp', [(i, (i + 2 * step) % 8) for i in range(8)])  126 us
    ppermute x31, waiting for transfers between devices, swap_y(): return lax.ppermute(a, 'dp', [(i, i ^ 1) for i in range(8)])  66.7 us
    ppermute x31, starting transfers between devices, swap_y(): return lax.ppermute(a, 'dp', [(i, i ^ 1) for i in range(8)])  31.7 us
    ppermute x6, waiting for transfers between devices, swap_x(): return lax.ppermute(a, 'pipe', [(i, i ^ 2) for i in range(4)])  28.2 us
    ppermute x30, starting transfers between devices, ring_z(): return lax.ppermute(a, 'dp', [(i, (i + 2 * step) % 8) for i in range(8)])  27.8 us
    convert_element_type x12, other arithmetic, z(): self.block(3 - len(self.ring[side]), side).astype(BF)  20.9 us
    unnamed x212, local copies, waits for them, and re-layouts  20.2 us
  transfers between devices with their start and end apart: 106, of which 36 were waited for; matrix products, arithmetic and copies ran while one was open for 13% of the time, Pallas kernels for 25%

profile of v3, /device:TPU:0, one launch (start us, length us, event | category | flops | bytes accessed | tf_op | source)
XLA Modules:
  0.0 655.0 jit_solution(5455502807187887760)
XLA Ops:
  8.0 5.1 collective-permute-start.2
  21.3 18.1 %collective-permute-done = bf16[384,384]{1,0:T(8,128)(2,1)S(1)} collective-permute-done((bf16[384,384]{1,0:T(8,128)(2,1)S(1)}, bf16[384,384]{1,0:T(8,128)(2,1)S(1)}, u32[]{:S(2)}, u32[]{:S(2)}) %collective-permute-start) | collective-permute-done | bytes 294944 | tf_op jit(solution)/shard_map/ppermute | solution.py:640
  44.2 20.6 %collective-permute-done.6 = f32[4,16,128]{2,1,0:T(8,128)S(1)} collective-permute-done((f32[4,16,128]{2,1,0:T(8,128)S(1)}, f32[4,16,128]{2,1,0:T(8,128)S(1)}, u32[]{:S(2)}, u32[]{:S(2)}) %collective-permute-start.6) | collective-permute-done | bytes 32800 | tf_op jit(solution)/shard_map/ppermute | solution.py:652
  64.7 4.2 collective-permute-done.5.rest_1_
  76.9 29.3 %collective-permute-done.8.rest_2_ = bf16[1152,384]{1,0:T(8,128)(2,1)} collective-permute-done((bf16[1152,384]{1,0:T(8,128)(2,1)S(1)}, bf16[1152,384]{1,0:T(8,128)(2,1)}, u32[]{:S(2)}, u32[]{:S(2)}) %collective-permute-start.8) | collective-permute-done | bytes 884768 | tf_op jit(solution)/shard_map/ppermute | solution.py:655
  108.3 3.0 copy.54
  117.0 6.7 %collective-permute-done.12.rest_3_ = bf16[1152,384]{1,0:T(8,128)(2,1)} collective-permute-done((bf16[1152,384]{1,0:T(8,128)(2,1)}, bf16[1152,384]{1,0:T(8,128)(2,1)}, u32[]{:S(2)}, u32[]{:S(2)}) %collective-permute-start.12) | collective-permute-done | bytes 884768 | tf_op jit(solution)/shard_map/ppermute | solution.py:655
  130.4 10.3 %collective-permute-done.26.rest_1_ = bf16[384,384]{1,0:T(8,128)(2,1)} collective-permute-done((bf16[384,384]{1,0:T(8,128)(2,1)}, bf16[384,384]{1,0:T(8,128)(2,1)}, u32[]{:S(2)}, u32[]{:S(2)}) %collective-permute-start.26) | collective-permute-done | bytes 294944 | tf_op jit(solution)/shard_map/ppermute | solution.py:655
  140.7 15.2 %collective-permute-done.27.rest_4_ = bf16[384,384]{1,0:T(8,128)(2,1)S(1)} collective-permute-done((bf16[384,384]{1,0:T(8,128)(2,1)}, bf16[384,384]{1,0:T(8,128)(2,1)S(1)}, u32[]{:S(2)}, u32[]{:S(2)}) %collective-permute-start.27) | collective-permute-done | bytes 294944 | tf_op jit(solution)/shard_map/ppermute | solution.py:652
  160.2 13.9 %shard_map.239 = (bf16[512,2304]{1,0:T(8,128)(2,1)}, bf16[24,256,128]{2,1,0:T(8,128)(2,1)}, bf16[512,768]{1,0:T(8,128)(2,1)}, f32[512,768]{1,0:T(8,128)}, bf16[5...) custom-call(s32[8]{0:T(128)} %add_minimum_fusion.lengths, s32[3]{0:T(128)} %pad_add_fusion.where_ref, ...), custom_call_target="tpu_custom_call" | custom-call | flops 15399999488 | bytes 49000000 | tf_op jit(solution)/shard_map/pallas_call | solution.py:432
  174.2 5.1 collective-permute-done.31.rest_4_
  179.3 3.0 collective-permute-done.32.rest_1_
  184.7 19.3 %shard_map.240 = (bf16[512,3072]{1,0:T(8,128)(2,1)}, bf16[512,3072]{1,0:T(8,128)(2,1)}, f32[512,768]{1,0:T(8,128)}, bf16[512,768]{1,0:T(8,128)(2,1)}, f32[512,768]{1,0:T(8,128)}, /*index=5*/f32[512,1]{1,0:T(8,128)}) custom-call(s32[3]{0:T(128)} %pad_add_fusion.where_ref, f32[512,768]{1,0:T(8,128)} %get-tuple-element.225.x_ref, ...), custom_call_target="tpu_custom_call" | custom-call | flops 22000001024 | bytes 70000000 | tf_op jit(solution)/shard_map/pallas_call | solution.py:432
  209.9 3.5 add_convert_fusion.v_ref
  215.1 3.5 convolution_convert_fusion.k_ref
  219.9 3.2 fusion.58
  228.0 10.8 %collective-permute-done.48.rest_7_ = bf16[768,384]{1,0:T(8,128)(2,1)} collective-permute-done((bf16[768,384]{1,0:T(8,128)(2,1)}, bf16[768,384]{1,0:T(8,128)(2,1)}, u32[]{:S(2)}, u32[]{:S(2)}) %collective-permute-start.48) | collective-permute-done | bytes 589856 | tf_op jit(solution)/shard_map/ppermute | solution.py:652
  239.4 14.1 %shard_map.241 = (bf16[512,2304]{1,0:T(8,128)(2,1)}, bf16[24,256,128]{2,1,0:T(8,128)(2,1)}, bf16[512,768]{1,0:T(8,128)(2,1)}, f32[512,768]{1,0:T(8,128)}, bf16[5...) custom-call(s32[8]{0:T(128)} %add_minimum_fusion.lengths, s32[3]{0:T(128)} %pad_add_fusion.where_ref, ...), custom_call_target="tpu_custom_call" | custom-call | flops 15399999488 | bytes 49000000 | tf_op jit(solution)/shard_map/pallas_call | solution.py:432
  254.1 21.1 %shard_map.242 = (bf16[512,768]{1,0:T(8,128)(2,1)}, bf16[48,128,160]{2,1,0:T(8,128)(2,1)}, bf16[512,768]{1,0:T(8,128)(2,1)}, f32[512,768]{1,0:T(8,128)}, bf16[51...) custom-call(f32[512,768]{1,0:T(8,128)} %get-tuple-element.262.x_ref, ...), custom_call_target="tpu_custom_call" | custom-call | flops 23100000256 | bytes 73500000 | tf_op jit(solution)/shard_map/pallas_call | solution.py:432
  275.3 19.4 %shard_map.243 = (bf16[512,3072]{1,0:T(8,128)(2,1)}, bf16[512,3072]{1,0:T(8,128)(2,1)}, f32[512,768]{1,0:T(8,128)}, bf16[512,768]{1,0:T(8,128)(2,1)}, f32[512,768]{1,0:T(8,128)}, /*index=5*/f32[512,1]{1,0:T(8,128)}) custom-call(s32[3]{0:T(128)} %pad_add_fusion.where_ref, f32[512,768]{1,0:T(8,128)} %get-tuple-element.271.x_ref, ...), custom_call_target="tpu_custom_call" | custom-call | flops 22000001024 | bytes 70000000 | tf_op jit(solution)/shard_map/pallas_call | solution.py:432
  294.7 22.8 %shard_map.244 = (f32[512,768]{1,0:T(8,128)}, bf16[6144,384]{1,0:T(8,128)(2,1)}, bf16[6144,384]{1,0:T(8,128)(2,1)}, f32[8,768]{1,0:T(8,128)}, f32[1,3072]{1,0:T(1,128)}) custom-call(s32[3]{0:T(128)} %pad_add_fusion.where_ref, bf16[512,768]{1,0:T(8,128)(2,1)} %bitcast.394, bf16[512,768]{1,0:T(8,128)(2,1)} %get-tuple-element.272.low_x_ref, ...), custom_call_target="tpu_custom_call" | custom-call | flops 24199999488 | bytes 77000000 | tf_op jit(solution)/shard_map/pallas_call | solution.py:432
  318.0 7.9 %collective-permute-done.57 = bf16[6144,384]{1,0:T(8,128)(2,1)} collective-permute-done((bf16[6144,384]{1,0:T(8,128)(2,1)}, bf16[6144,384]{1,0:T(8,128)(2,1)}, u32[]{:S(2)}, u32[]{:S(2)}) %collective-permute-start.57) | collective-permute-done | bytes 4718624 | tf_op jit(solution)/shard_map/ppermute | solution.py:649
  325.9 2.9 fusion.17
  330.9 26.7 %shard_map.245 = (f32[512,768]{1,0:T(8,128)}, bf16[1280,768]{1,0:T(8,128)(2,1)}, bf16[1280,768]{1,0:T(8,128)(2,1)}, bf16[768,768]{1,0:T(8,128)(2,1)}, bf16[768,768]{1,0:T(8,128)(2,1)}, /*index=5*/f32[8,768]{1,0:T(8,128)}) custom-call(f32[512,768]{1,0:T(8,128)} %get-tuple-element.286.dy_ref, bf16[512,768]{1,0:T(8,128)(2,1)} %get-tuple-element.263.low_x_ref, ...), custom_call_target="tpu_custom_call" | custom-call | flops 28600000512 | bytes 91000000 | tf_op jit(solution)/shard_map/pallas_call | solution.py:432
  362.9 3.3 collective-permute-start.62
  366.2 23.4 %shard_map.246 = (f32[512,768]{1,0:T(8,128)}, bf16[3072,384]{1,0:T(8,128)(2,1)}, bf16[3072,384]{1,0:T(8,128)(2,1)}, f32[8,768]{1,0:T(8,128)}) custom-call(s32[3]{0:T(128)} %pad_add_fusion.where_ref, f32[512,768]{1,0:T(8,128)} %get-tuple-element.296.dy_ref, bf16[512,768]{1,0:T(8,128)(2,1)} %get-tuple-element.252.x_ref, f32[12,768]{1,0:T(8,128)} %copy-done.46, ...), custom_call_target="tpu_custom_call" | custom-call | flops 24199999488 | bytes 77000000 | tf_op jit(solution)/shard_map/pallas_call | solution.py:432
  393.4 3.8 convolution_convert_fusion.1
  404.3 5.1 collective-permute-done.64
  416.6 5.8 collective-permute-done.65
  422.6 22.4 %shard_map.247 = (f32[512,768]{1,0:T(8,128)}, bf16[6144,384]{1,0:T(8,128)(2,1)}, bf16[6144,384]{1,0:T(8,128)(2,1)}, f32[8,768]{1,0:T(8,128)}, f32[1,3072]{1,0:T(1,128)}) custom-call(s32[3]{0:T(128)} %pad_add_fusion.where_ref, bf16[512,768]{1,0:T(8,128)(2,1)} %convert_element_type.634.dy_ref, bf16[512,768]{1,0:T(8,128)(2,1)} %get-tuple-element.226.low_x_ref, ...), custom_call_target="tpu_custom_call" | custom-call | flops 24199999488 | bytes 77000000 | tf_op jit(solution)/shard_map/pallas_call | solution.py:432
  451.4 2.7 convert_add_fusion
  454.6 4.8 fusion.21
  462.9 23.3 %shard_map.248 = (f32[512,768]{1,0:T(8,128)}, bf16[3072,384]{1,0:T(8,128)(2,1)}, bf16[3072,384]{1,0:T(8,128)(2,1)}, f32[8,768]{1,0:T(8,128)}) custom-call(s32[3]{0:T(128)} %pad_add_fusion.where_ref, f32[512,768]{1,0:T(8,128)} %get-tuple-element.325.dy_ref, bf16[512,768]{1,0:T(8,128)(2,1)} %bitcast.396, f32[12,768]{1,0:T(8,128)} %copy-done.45, ...), custom_call_target="tpu_custom_call" | custom-call | flops 24199999488 | bytes 77000000 | tf_op jit(solution)/shard_map/pallas_call | solution.py:432
  487.7 6.1 collective-permute-done.75
  499.6 4.3 collective-permute-start.78
  508.7 14.7 %collective-permute-done.78 = bf16[384,384]{1,0:T(8,128)(2,1)S(1)} collective-permute-done((bf16[384,384]{1,0:T(8,128)(2,1)S(1)}, bf16[384,384]{1,0:T(8,128)(2,1)S(1)}, u32[]{:S(2)}, u32[]{:S(2)}) %collective-permute-start.78) | collective-permute-done | bytes 294944 | tf_op jit(solution)/shard_map/ppermute | solution.py:655
  523.4 3.1 collective-permute-start.82
  532.5 6.6 %collective-permute-done.82 = bf16[768,384]{1,0:T(8,128)(2,1)S(1)} collective-permute-done((bf16[768,384]{1,0:T(8,128)(2,1)S(1)}, bf16[768,384]{1,0:T(8,128)(2,1)S(1)}, u32[]{:S(2)}, u32[]{:S(2)}) %collective-permute-start.82) | collective-permute-done | bytes 589856 | tf_op jit(solution)/shard_map/ppermute | solution.py:646
  547.5 4.9 collective-permute-done.86
  554.8 10.0 %collective-permute-done.88 = bf16[384,384]{1,0:T(8,128)(2,1)S(1)} collective-permute-done((bf16[384,384]{1,0:T(8,128)(2,1)S(1)}, bf16[384,384]{1,0:T(8,128)(2,1)S(1)}, u32[]{:S(2)}, u32[]{:S(2)}) %collective-permute-start.88) | collective-permute-done | bytes 294944 | tf_op jit(solution)/shard_map/ppermute | solution.py:655
  572.3 3.1 collective-permute-start.94
  576.5 10.9 %collective-permute-done.90 = bf16[384,384]{1,0:T(8,128)(2,1)S(1)} collective-permute-done((bf16[384,384]{1,0:T(8,128)(2,1)}, bf16[384,384]{1,0:T(8,128)(2,1)S(1)}, u32[]{:S(2)}, u32[]{:S(2)}) %collective-permute-start.90) | collective-permute-done | bytes 294944 | tf_op jit(solution)/shard_map/ppermute | solution.py:655
  589.4 6.8 %collective-permute-done.91 = bf16[768,384]{1,0:T(8,128)(2,1)S(1)} collective-permute-done((bf16[768,384]{1,0:T(8,128)(2,1)}, bf16[768,384]{1,0:T(8,128)(2,1)S(1)}, u32[]{:S(2)}, u32[]{:S(2)}) %collective-permute-start.91) | collective-permute-done | bytes 589856 | tf_op jit(solution)/shard_map/ppermute | solution.py:655
  602.5 3.2 collective-permute-done.97
  605.7 5.5 collective-permute-done.96
  614.1 3.8 collective-permute-start.101
  621.3 9.7 %collective-permute-done.100 = bf16[112,768]{1,0:T(8,128)(2,1)S(1)} collective-permute-done((bf16[112,768]{1,0:T(8,128)(2,1)S(1)}, bf16[112,768]{1,0:T(8,128)(2,1)S(1)}, u32[]{:S(2)}, u32[]{:S(2)}) %collective-permute-start.100) | collective-permute-done | bytes 172064 | tf_op jit(solution)/shard_map/ppermute | solution.py:655
  639.0 3.8 collective-permute-done.104
  (500 shorter events, 157.6 us)
Async XLA Ops:
  7.2 199.9 %all-gather.2.cloned.1.call-start = ((), (), s32[]{:S(2)}) async-start(), calls=%async_computation | async-start | bytes 5677056 | tf_op jit(solution)/shard_map/all_gather | solution.py:956
  17.5 21.8 %collective-permute-start.1 = (bf16[768,384]{1,0:T(8,128)(2,1)S(1)}, bf16[768,384]{1,0:T(8,128)(2,1)S(1)}, u32[]{:S(2)}, u32[]{:S(2)}) collective-permute-start(bf16[768,384]{1,0:T(8,128)(2,1)S(1)} %get-tuple-element.424), channel_id=1, source_target_pairs={{0,16},{8,24},{16,0},{24,8},{1,17},{9,25},{17,1},{25,9},{2,18},{10... | collective-permute-start | bytes 1769480 | tf_op jit(solution)/shard_map/ppermute | solution.py:640
  19.1 20.2 %collective-permute-start = (bf16[384,384]{1,0:T(8,128)(2,1)S(1)}, bf16[384,384]{1,0:T(8,128)(2,1)S(1)}, u32[]{:S(2)}, u32[]{:S(2)}) collective-permute-start(bf16[384,384]{1,0:T(8,128)(2,1)S(1)} %pad_maximum_fusion.2), channel_id=1, source_target_pairs={{0,16},{8,24},{16,0},{24,8},{1,17},{9,25},{17,1},{25,9},{2,18},{10... | collective-permute-start | bytes 884744 | tf_op jit(solution)/shard_map/ppermute | solution.py:640
  39.6 29.3 %collective-permute-start.5 = (bf16[1152,384]{1,0:T(8,128)(2,1)S(1)}, bf16[1152,384]{1,0:T(8,128)(2,1)S(1)}, u32[]{:S(2)}, u32[]{:S(2)}) collective-permute-start(bf16[1152,384]{1,0:T(8,128)(2,1)S(1)} %maximum_select_fusion.rest_0_), channel_id=1, source_target_pairs={{0,2},{1,3},{2,4},{3,5},{4,6},{5,7},{6,0},{7,1},{8,10},{9,11},{10,... | collective-permute-start | bytes 2654216 | tf_op jit(solution)/shard_map/ppermute | solution.py:655
  42.1 26.8 %collective-permute-start.7 = (bf16[1152,384]{1,0:T(8,128)(2,1)S(1)}, bf16[1152,384]{1,0:T(8,128)(2,1)S(1)}, u32[]{:S(2)}, u32[]{:S(2)}) collective-permute-start(bf16[1152,384]{1,0:T(8,128)(2,1)S(1)} %maximum_select_fusion.rest_0_), channel_id=1, source_target_pairs={{0,1},{1,0},{2,3},{3,2},{4,5},{5,4},{6,7},{7,6},{8,9},{9,8},{10,11... | collective-permute-start | bytes 2654216 | tf_op jit(solution)/shard_map/ppermute | solution.py:652
  43.7 21.1 %collective-permute-start.6 = (f32[4,16,128]{2,1,0:T(8,128)S(1)}, f32[4,16,128]{2,1,0:T(8,128)S(1)}, u32[]{:S(2)}, u32[]{:S(2)}) collective-permute-start(f32[4,16,128]{2,1,0:T(8,128)S(1)} %get-tuple-element.199), channel_id=1, source_target_pairs={{0,1},{1,0},{2,3},{3,2},{4,5},{5,4},{6,7},{7,6},{8,9},{9,8},{10,11... | collective-permute-start | bytes 98312 | tf_op jit(solution)/shard_map/ppermute | solution.py:652
  68.9 37.3 %collective-permute-start.8 = (bf16[1152,384]{1,0:T(8,128)(2,1)S(1)}, bf16[1152,384]{1,0:T(8,128)(2,1)}, u32[]{:S(2)}, u32[]{:S(2)}) collective-permute-start(bf16[1152,384]{1,0:T(8,128)(2,1)S(1)} %collective-permute-done.5.rest_1_), channel_id=1, source_target_pairs={{0,2},{1,3},{2,4},{3,5},{4,6},{5,7},{6,0},{7,1},{8,10},{9,11},{10,... | collective-permute-start | bytes 2654216 | tf_op jit(solution)/shard_map/ppermute | solution.py:655
  69.3 36.9 %collective-permute-start.9 = (bf16[1152,384]{1,0:T(8,128)(2,1)S(1)}, bf16[1152,384]{1,0:T(8,128)(2,1)}, u32[]{:S(2)}, u32[]{:S(2)}) collective-permute-start(bf16[1152,384]{1,0:T(8,128)(2,1)S(1)} %collective-permute-done.5.rest_1_), channel_id=1, source_target_pairs={{0,1},{1,0},{2,3},{3,2},{4,5},{5,4},{6,7},{7,6},{8,9},{9,8},{10,11... | collective-permute-start | bytes 2654216 | tf_op jit(solution)/shard_map/ppermute | solution.py:652
  127.7 28.2 %collective-permute-start.23 = (bf16[1152,384]{1,0:T(8,128)(2,1)}, bf16[1152,384]{1,0:T(8,128)(2,1)}, u32[]{:S(2)}, u32[]{:S(2)}) collective-permute-start(bf16[1152,384]{1,0:T(8,128)(2,1)} %collective-permute-done.12.rest_3_), channel_id=1, source_target_pairs={{0,1},{1,0},{2,3},{3,2},{4,5},{5,4},{6,7},{7,6},{8,9},{9,8},{10,11... | collective-permute-start | bytes 2654216 | tf_op jit(solution)/shard_map/ppermute | solution.py:652
  129.1 26.8 %collective-permute-start.24 = (bf16[1152,384]{1,0:T(8,128)(2,1)}, bf16[1152,384]{1,0:T(8,128)(2,1)S(1)}, u32[]{:S(2)}, u32[]{:S(2)}) collective-permute-start(bf16[1152,384]{1,0:T(8,128)(2,1)} %collective-permute-done.12.rest_3_), channel_id=1, source_target_pairs={{0,8},{8,0},{16,24},{24,16},{1,9},{9,1},{17,25},{25,17},{2,10},{10... | collective-permute-start | bytes 2654216 | tf_op jit(solution)/shard_map/ppermute | solution.py:649
  129.1 26.8 %collective-permute-start.25 = (bf16[1152,384]{1,0:T(8,128)(2,1)}, bf16[1152,384]{1,0:T(8,128)(2,1)S(1)}, u32[]{:S(2)}, u32[]{:S(2)}) collective-permute-start(bf16[1152,384]{1,0:T(8,128)(2,1)} %collective-permute-done.13.rest_6_), channel_id=1, source_target_pairs={{0,8},{8,0},{16,24},{24,16},{1,9},{9,1},{17,25},{25,17},{2,10},{10... | collective-permute-start | bytes 2654216 | tf_op jit(solution)/shard_map/ppermute | solution.py:649
  129.7 26.2 %collective-permute-start.27 = (bf16[384,384]{1,0:T(8,128)(2,1)}, bf16[384,384]{1,0:T(8,128)(2,1)S(1)}, u32[]{:S(2)}, u32[]{:S(2)}) collective-permute-start(bf16[384,384]{1,0:T(8,128)(2,1)} %broadcast_select_fusion.1.rest_0_), channel_id=1, source_target_pairs={{0,1},{1,0},{2,3},{3,2},{4,5},{5,4},{6,7},{7,6},{8,9},{9,8},{10,11... | collective-permute-start | bytes 884744 | tf_op jit(solution)/shard_map/ppermute | solution.py:652
  159.6 19.7 %collective-permute-start.31 = (bf16[768,384]{1,0:T(8,128)(2,1)S(1)}, bf16[768,384]{1,0:T(8,128)(2,1)S(1)}, u32[]{:S(2)}, u32[]{:S(2)}) collective-permute-start(bf16[768,384]{1,0:T(8,128)(2,1)S(1)} %broadcast_select_fusion.rest_0_), channel_id=1, source_target_pairs={{0,1},{1,0},{2,3},{3,2},{4,5},{5,4},{6,7},{7,6},{8,9},{9,8},{10,11... | collective-permute-start | bytes 1769480 | tf_op jit(solution)/shard_map/ppermute | solution.py:652
  160.2 22.2 %collective-permute-start.32 = (bf16[768,384]{1,0:T(8,128)(2,1)S(1)}, bf16[768,384]{1,0:T(8,128)(2,1)}, u32[]{:S(2)}, u32[]{:S(2)}) collective-permute-start(bf16[768,384]{1,0:T(8,128)(2,1)S(1)} %broadcast_select_fusion.rest_0_), channel_id=1, source_target_pairs={{0,2},{1,3},{2,4},{3,5},{4,6},{5,7},{6,0},{7,1},{8,10},{9,11},{10,... | collective-permute-start | bytes 1769480 | tf_op jit(solution)/shard_map/ppermute | solution.py:655
  182.4 21.6 %collective-permute-start.33 = (bf16[384,384]{1,0:T(8,128)(2,1)S(1)}, bf16[384,384]{1,0:T(8,128)(2,1)}, u32[]{:S(2)}, u32[]{:S(2)}) collective-permute-start(bf16[384,384]{1,0:T(8,128)(2,1)S(1)} %collective-permute-done.30.rest_2_), channel_id=1, source_target_pairs={{0,2},{1,3},{2,4},{3,5},{4,6},{5,7},{6,0},{7,1},{8,10},{9,11},{10,... | collective-permute-start | bytes 884744 | tf_op jit(solution)/shard_map/ppermute | solution.py:655
  182.4 21.7 %collective-permute-start.34 = (bf16[768,384]{1,0:T(8,128)(2,1)}, bf16[768,384]{1,0:T(8,128)(2,1)}, u32[]{:S(2)}, u32[]{:S(2)}) collective-permute-start(bf16[768,384]{1,0:T(8,128)(2,1)} %collective-permute-done.32.rest_1_), channel_id=1, source_target_pairs={{0,2},{1,3},{2,4},{3,5},{4,6},{5,7},{6,0},{7,1},{8,10},{9,11},{10,... | collective-permute-start | bytes 1769480 | tf_op jit(solution)/shard_map/ppermute | solution.py:655
  182.6 21.5 %collective-permute-start.35 = (bf16[384,384]{1,0:T(8,128)(2,1)S(1)}, bf16[384,384]{1,0:T(8,128)(2,1)S(1)}, u32[]{:S(2)}, u32[]{:S(2)}) collective-permute-start(bf16[384,384]{1,0:T(8,128)(2,1)S(1)} %collective-permute-done.30.rest_2_), channel_id=1, source_target_pairs={{0,1},{1,0},{2,3},{3,2},{4,5},{5,4},{6,7},{7,6},{8,9},{9,8},{10,11... | collective-permute-start | bytes 884744 | tf_op jit(solution)/shard_map/ppermute | solution.py:652
  183.2 20.8 %collective-permute-start.36 = (bf16[768,384]{1,0:T(8,128)(2,1)}, bf16[768,384]{1,0:T(8,128)(2,1)}, u32[]{:S(2)}, u32[]{:S(2)}) collective-permute-start(bf16[768,384]{1,0:T(8,128)(2,1)} %collective-permute-done.32.rest_1_), channel_id=1, source_target_pairs={{0,1},{1,0},{2,3},{3,2},{4,5},{5,4},{6,7},{7,6},{8,9},{9,8},{10,11... | collective-permute-start | bytes 1769480 | tf_op jit(solution)/shard_map/ppermute | solution.py:652
  227.0 26.5 %collective-permute-start.51 = (bf16[768,384]{1,0:T(8,128)(2,1)}, bf16[768,384]{1,0:T(8,128)(2,1)S(1)}, u32[]{:S(2)}, u32[]{:S(2)}) collective-permute-start(bf16[768,384]{1,0:T(8,128)(2,1)} %collective-permute-done.34.rest_2_), channel_id=1, source_target_pairs={{0,8},{8,0},{16,24},{24,16},{1,9},{9,1},{17,25},{25,17},{2,10},{10... | collective-permute-start | bytes 1769480 | tf_op jit(solution)/shard_map/ppermute | solution.py:649
  227.9 25.7 %collective-permute-start.52 = (bf16[768,384]{1,0:T(8,128)(2,1)}, bf16[768,384]{1,0:T(8,128)(2,1)S(1)}, u32[]{:S(2)}, u32[]{:S(2)}) collective-permute-start(bf16[768,384]{1,0:T(8,128)(2,1)} %collective-permute-done.39.rest_3_), channel_id=1, source_target_pairs={{0,8},{8,0},{16,24},{24,16},{1,9},{9,1},{17,25},{25,17},{2,10},{10... | collective-permute-start | bytes 1769480 | tf_op jit(solution)/shard_map/ppermute | solution.py:649
  253.6 21.7 %collective-permute-start.56 = (bf16[768,384]{1,0:T(8,128)(2,1)}, bf16[768,384]{1,0:T(8,128)(2,1)}, u32[]{:S(2)}, u32[]{:S(2)}) collective-permute-start(bf16[768,384]{1,0:T(8,128)(2,1)} %collective-permute-done.48.rest_7_), channel_id=1, source_target_pairs={{0,8},{8,0},{16,24},{24,16},{1,9},{9,1},{17,25},{25,17},{2,10},{10... | collective-permute-start | bytes 1769480 | tf_op jit(solution)/shard_map/ppermute | solution.py:649
  328.8 28.8 %collective-permute-start.58 = (bf16[768,384]{1,0:T(8,128)(2,1)S(1)}, bf16[768,384]{1,0:T(8,128)(2,1)}, u32[]{:S(2)}, u32[]{:S(2)}) collective-permute-start(bf16[768,384]{1,0:T(8,128)(2,1)S(1)} %get-tuple-element.284), channel_id=1, source_target_pairs={{0,1},{1,0},{2,3},{3,2},{4,5},{5,4},{6,7},{7,6},{8,9},{9,8},{10,11... | collective-permute-start | bytes 1769480 | tf_op jit(solution)/shard_map/ppermute | solution.py:652
  329.5 30.6 %collective-permute-start.59 = (bf16[768,384]{1,0:T(8,128)(2,1)S(1)}, bf16[768,384]{1,0:T(8,128)(2,1)S(1)}, u32[]{:S(2)}, u32[]{:S(2)}) collective-permute-start(bf16[768,384]{1,0:T(8,128)(2,1)S(1)} %get-tuple-element.285), channel_id=1, source_target_pairs={{0,1},{1,0},{2,3},{3,2},{4,5},{5,4},{6,7},{7,6},{8,9},{9,8},{10,11... | collective-permute-start | bytes 1769480 | tf_op jit(solution)/shard_map/ppermute | solution.py:652
  360.9 30.7 %collective-permute-start.60 = (bf16[768,384]{1,0:T(8,128)(2,1)S(1)}, bf16[768,384]{1,0:T(8,128)(2,1)S(1)}, u32[]{:S(2)}, u32[]{:S(2)}) collective-permute-start(bf16[768,384]{1,0:T(8,128)(2,1)S(1)} %get-tuple-element.293), channel_id=1, source_target_pairs={{0,1},{1,0},{2,3},{3,2},{4,5},{5,4},{6,7},{7,6},{8,9},{9,8},{10,11... | collective-permute-start | bytes 1769480 | tf_op jit(solution)/shard_map/ppermute | solution.py:652
  361.5 30.1 %collective-permute-start.61 = (bf16[768,384]{1,0:T(8,128)(2,1)S(1)}, bf16[768,384]{1,0:T(8,128)(2,1)S(1)}, u32[]{:S(2)}, u32[]{:S(2)}) collective-permute-start(bf16[768,384]{1,0:T(8,128)(2,1)S(1)} %get-tuple-element.294), channel_id=1, source_target_pairs={{0,1},{1,0},{2,3},{3,2},{4,5},{5,4},{6,7},{7,6},{8,9},{9,8},{10,11... | collective-permute-start | bytes 1769480 | tf_op jit(solution)/shard_map/ppermute | solution.py:652
  362.9 26.8 %collective-permute-start.62 = (bf16[768,384]{1,0:T(8,128)(2,1)}, bf16[768,384]{1,0:T(8,128)(2,1)}, u32[]{:S(2)}, u32[]{:S(2)}) collective-permute-start(bf16[768,384]{1,0:T(8,128)(2,1)} %fusion.12), channel_id=1, source_target_pairs={{0,2},{1,3},{2,4},{3,5},{4,6},{5,7},{6,0},{7,1},{8,10},{9,11},{10,... | collective-permute-start | bytes 1769480 | tf_op jit(solution)/shard_map/ppermute | solution.py:655
  391.9 19.1 %collective-permute-start.63 = (bf16[3072,384]{1,0:T(8,128)(2,1)S(1)}, bf16[3072,384]{1,0:T(8,128)(2,1)S(1)}, u32[]{:S(2)}, u32[]{:S(2)}) collective-permute-start(bf16[3072,384]{1,0:T(8,128)(2,1)S(1)} %copy-done.57), channel_id=1, source_target_pairs={{0,8},{8,0},{16,24},{24,16},{1,9},{9,1},{17,25},{25,17},{2,10},{10... | collective-permute-start | bytes 7077896 | tf_op jit(solution)/shard_map/ppermute | solution.py:649
  412.4 33.4 %collective-permute-start.70 = (bf16[2,4,2,112,768]{4,3,1,2,0:T(8,128)(2,1)}, bf16[2,4,2,112,768]{4,3,1,2,0:T(8,128)(2,1)}, u32[]{:S(2)}, u32[]{:S(2)}) collective-permute-start(bf16[2,4,2,112,768]{4,3,1,2,0:T(8,128)(2,1)} %bitcast.315), channel_id=1, source_target_pairs={{0,8},{8,0},{16,24},{24,16},{1,9},{9,1},{17,25},{25,17},{2,10},{10... | collective-permute-start | bytes 8257544 | tf_op jit(solution)/shard_map/ppermute | solution.py:649
  413.2 31.8 %collective-permute-start.66 = (bf16[384,384]{1,0:T(8,128)(2,1)S(1)}, bf16[384,384]{1,0:T(8,128)(2,1)S(1)}, u32[]{:S(2)}, u32[]{:S(2)}) collective-permute-start(bf16[384,384]{1,0:T(8,128)(2,1)S(1)} %get-tuple-element.309), channel_id=1, source_target_pairs={{0,1},{1,0},{2,3},{3,2},{4,5},{5,4},{6,7},{7,6},{8,9},{9,8},{10,11... | collective-permute-start | bytes 884744 | tf_op jit(solution)/shard_map/ppermute | solution.py:652
  414.6 30.4 %collective-permute-start.67 = (bf16[384,384]{1,0:T(8,128)(2,1)S(1)}, bf16[384,384]{1,0:T(8,128)(2,1)S(1)}, u32[]{:S(2)}, u32[]{:S(2)}) collective-permute-start(bf16[384,384]{1,0:T(8,128)(2,1)S(1)} %get-tuple-element.310), channel_id=1, source_target_pairs={{0,1},{1,0},{2,3},{3,2},{4,5},{5,4},{6,7},{7,6},{8,9},{9,8},{10,11... | collective-permute-start | bytes 884744 | tf_op jit(solution)/shard_map/ppermute | solution.py:652
  415.2 29.8 %collective-permute-start.68 = (bf16[384,384]{1,0:T(8,128)(2,1)S(1)}, bf16[384,384]{1,0:T(8,128)(2,1)}, u32[]{:S(2)}, u32[]{:S(2)}) collective-permute-start(bf16[384,384]{1,0:T(8,128)(2,1)S(1)} %get-tuple-element.311), channel_id=1, source_target_pairs={{0,1},{1,0},{2,3},{3,2},{4,5},{5,4},{6,7},{7,6},{8,9},{9,8},{10,11... | collective-permute-start | bytes 884744 | tf_op jit(solution)/shard_map/ppermute | solution.py:652
  422.4 22.7 %collective-permute-start.69 = (bf16[768,384]{1,0:T(8,128)(2,1)S(1)}, bf16[768,384]{1,0:T(8,128)(2,1)}, u32[]{:S(2)}, u32[]{:S(2)}) collective-permute-start(bf16[768,384]{1,0:T(8,128)(2,1)S(1)} %fusion.9), channel_id=1, source_target_pairs={{0,2},{1,3},{2,4},{3,5},{4,6},{5,7},{6,0},{7,1},{8,10},{9,11},{10,... | collective-permute-start | bytes 1769480 | tf_op jit(solution)/shard_map/ppermute | solution.py:655
  459.3 26.8 %collective-permute-start.72 = (bf16[768,384]{1,0:T(8,128)(2,1)S(1)}, bf16[768,384]{1,0:T(8,128)(2,1)S(1)}, u32[]{:S(2)}, u32[]{:S(2)}) collective-permute-start(bf16[768,384]{1,0:T(8,128)(2,1)S(1)} %get-tuple-element.321), channel_id=1, source_target_pairs={{0,1},{1,0},{2,3},{3,2},{4,5},{5,4},{6,7},{7,6},{8,9},{9,8},{10,11... | collective-permute-start | bytes 1769480 | tf_op jit(solution)/shard_map/ppermute | solution.py:652
  460.0 27.8 %collective-permute-start.73 = (bf16[768,384]{1,0:T(8,128)(2,1)S(1)}, bf16[768,384]{1,0:T(8,128)(2,1)S(1)}, u32[]{:S(2)}, u32[]{:S(2)}) collective-permute-start(bf16[768,384]{1,0:T(8,128)(2,1)S(1)} %get-tuple-element.322), channel_id=1, source_target_pairs={{0,1},{1,0},{2,3},{3,2},{4,5},{5,4},{6,7},{7,6},{8,9},{9,8},{10,11... | collective-permute-start | bytes 1769480 | tf_op jit(solution)/shard_map/ppermute | solution.py:652
  461.4 24.8 %collective-permute-start.74 = (bf16[384,384]{1,0:T(8,128)(2,1)}, bf16[384,384]{1,0:T(8,128)(2,1)S(1)}, u32[]{:S(2)}, u32[]{:S(2)}) collective-permute-start(bf16[384,384]{1,0:T(8,128)(2,1)} %fusion.33), channel_id=1, source_target_pairs={{0,2},{1,3},{2,4},{3,5},{4,6},{5,7},{6,0},{7,1},{8,10},{9,11},{10,... | collective-permute-start | bytes 884744 | tf_op jit(solution)/shard_map/ppermute | solution.py:655
  461.6 32.2 %collective-permute-start.75 = (bf16[4,2,112,768]{3,2,0,1:T(8,128)(2,1)S(1)}, bf16[4,2,112,768]{3,2,0,1:T(8,128)(2,1)}, u32[]{:S(2)}, u32[]{:S(2)}) collective-permute-start(bf16[4,2,112,768]{3,2,0,1:T(8,128)(2,1)S(1)} %fusion), channel_id=1, source_target_pairs={{0,16},{8,24},{16,0},{24,8},{1,17},{9,25},{17,1},{25,9},{2,18},{10... | collective-permute-start | bytes 4128776 | tf_op jit(solution)/shard_map/ppermute | solution.py:640
  493.8 35.7 %collective-permute-start.76 = (bf16[3072,384]{1,0:T(8,128)(2,1)}, bf16[3072,384]{1,0:T(8,128)(2,1)}, u32[]{:S(2)}, u32[]{:S(2)}) collective-permute-start(bf16[3072,384]{1,0:T(8,128)(2,1)} %get-tuple-element.330), channel_id=1, source_target_pairs={{0,8},{8,0},{16,24},{24,16},{1,9},{9,1},{17,25},{25,17},{2,10},{10... | collective-permute-start | bytes 7077896 | tf_op jit(solution)/shard_map/ppermute | solution.py:649
  499.3 28.5 %collective-permute-start.77 = (bf16[768,384]{1,0:T(8,128)(2,1)S(1)}, bf16[768,384]{1,0:T(8,128)(2,1)S(1)}, u32[]{:S(2)}, u32[]{:S(2)}) collective-permute-start(bf16[768,384]{1,0:T(8,128)(2,1)S(1)} %fusion.5), channel_id=1, source_target_pairs={{0,2},{1,3},{2,4},{3,5},{4,6},{5,7},{6,0},{7,1},{8,10},{9,11},{10,... | collective-permute-start | bytes 1769480 | tf_op jit(solution)/shard_map/ppermute | solution.py:655
  499.6 23.8 %collective-permute-start.78 = (bf16[384,384]{1,0:T(8,128)(2,1)S(1)}, bf16[384,384]{1,0:T(8,128)(2,1)S(1)}, u32[]{:S(2)}, u32[]{:S(2)}) collective-permute-start(bf16[384,384]{1,0:T(8,128)(2,1)S(1)} %fusion.31), channel_id=1, source_target_pairs={{0,2},{1,3},{2,4},{3,5},{4,6},{5,7},{6,0},{7,1},{8,10},{9,11},{10,... | collective-permute-start | bytes 884744 | tf_op jit(solution)/shard_map/ppermute | solution.py:655
  503.9 27.4 %collective-permute-start.80 = (bf16[768,384]{1,0:T(8,128)(2,1)}, bf16[768,384]{1,0:T(8,128)(2,1)S(1)}, u32[]{:S(2)}, u32[]{:S(2)}) collective-permute-start(bf16[768,384]{1,0:T(8,128)(2,1)} %get-tuple-element.334), channel_id=1, source_target_pairs={{0,1},{1,0},{2,3},{3,2},{4,5},{5,4},{6,7},{7,6},{8,9},{9,8},{10,11... | collective-permute-start | bytes 1769480 | tf_op jit(solution)/shard_map/ppermute | solution.py:652
  507.1 25.4 %collective-permute-start.81 = (bf16[768,384]{1,0:T(8,128)(2,1)S(1)}, bf16[768,384]{1,0:T(8,128)(2,1)S(1)}, u32[]{:S(2)}, u32[]{:S(2)}) collective-permute-start(bf16[768,384]{1,0:T(8,128)(2,1)S(1)} %copy-done.27), channel_id=1, source_target_pairs={{0,1},{1,0},{2,3},{3,2},{4,5},{5,4},{6,7},{7,6},{8,9},{9,8},{10,11... | collective-permute-start | bytes 1769480 | tf_op jit(solution)/shard_map/ppermute | solution.py:652
  543.1 24.5 %collective-permute-start.87 = (bf16[768,384]{1,0:T(8,128)(2,1)S(1)}, bf16[768,384]{1,0:T(8,128)(2,1)S(1)}, u32[]{:S(2)}, u32[]{:S(2)}) collective-permute-start(bf16[768,384]{1,0:T(8,128)(2,1)S(1)} %fusion.7), channel_id=1, source_target_pairs={{0,2},{1,3},{2,4},{3,5},{4,6},{5,7},{6,0},{7,1},{8,10},{9,11},{10,... | collective-permute-start | bytes 1769480 | tf_op jit(solution)/shard_map/ppermute | solution.py:655
  543.1 21.8 %collective-permute-start.88 = (bf16[384,384]{1,0:T(8,128)(2,1)S(1)}, bf16[384,384]{1,0:T(8,128)(2,1)S(1)}, u32[]{:S(2)}, u32[]{:S(2)}) collective-permute-start(bf16[384,384]{1,0:T(8,128)(2,1)S(1)} %fusion.29), channel_id=1, source_target_pairs={{0,2},{1,3},{2,4},{3,5},{4,6},{5,7},{6,0},{7,1},{8,10},{9,11},{10,... | collective-permute-start | bytes 884744 | tf_op jit(solution)/shard_map/ppermute | solution.py:655
  545.4 24.6 %collective-permute-start.85 = (bf16[384,384]{1,0:T(8,128)(2,1)S(1)}, bf16[384,384]{1,0:T(8,128)(2,1)S(1)}, u32[]{:S(2)}, u32[]{:S(2)}) collective-permute-start(bf16[384,384]{1,0:T(8,128)(2,1)S(1)} %get-tuple-element.339), channel_id=1, source_target_pairs={{0,1},{1,0},{2,3},{3,2},{4,5},{5,4},{6,7},{7,6},{8,9},{9,8},{10,11... | collective-permute-start | bytes 884744 | tf_op jit(solution)/shard_map/ppermute | solution.py:652
  546.9 23.1 %collective-permute-start.84 = (bf16[384,384]{1,0:T(8,128)(2,1)S(1)}, bf16[384,384]{1,0:T(8,128)(2,1)S(1)}, u32[]{:S(2)}, u32[]{:S(2)}) collective-permute-start(bf16[384,384]{1,0:T(8,128)(2,1)S(1)} %get-tuple-element.338), channel_id=1, source_target_pairs={{0,1},{1,0},{2,3},{3,2},{4,5},{5,4},{6,7},{7,6},{8,9},{9,8},{10,11... | collective-permute-start | bytes 884744 | tf_op jit(solution)/shard_map/ppermute | solution.py:652
  572.3 27.8 %collective-permute-start.94 = (bf16[384,384]{1,0:T(8,128)(2,1)}, bf16[384,384]{1,0:T(8,128)(2,1)}, u32[]{:S(2)}, u32[]{:S(2)}) collective-permute-start(bf16[384,384]{1,0:T(8,128)(2,1)} %fusion.48), channel_id=1, source_target_pairs={{0,16},{8,24},{1,17},{9,25},{2,18},{10,26},{3,19},{11,27},{4,20},{... | collective-permute-start | bytes 884744 | tf_op jit(solution)/shard_map/ppermute | solution.py:646
  575.4 20.8 %collective-permute-start.91 = (bf16[768,384]{1,0:T(8,128)(2,1)}, bf16[768,384]{1,0:T(8,128)(2,1)S(1)}, u32[]{:S(2)}, u32[]{:S(2)}) collective-permute-start(bf16[768,384]{1,0:T(8,128)(2,1)} %fusion.3), channel_id=1, source_target_pairs={{0,2},{1,3},{2,4},{3,5},{4,6},{5,7},{6,0},{7,1},{8,10},{9,11},{10,... | collective-permute-start | bytes 1769480 | tf_op jit(solution)/shard_map/ppermute | solution.py:655
  575.8 23.0 %collective-permute-start.92 = (bf16[4,112,768]{2,1,0:T(8,128)(2,1)}, bf16[4,112,768]{2,1,0:T(8,128)(2,1)S(1)}, u32[]{:S(2)}, u32[]{:S(2)}) collective-permute-start(bf16[4,112,768]{2,1,0:T(8,128)(2,1)} %fusion.13), channel_id=1, source_target_pairs={{0,1},{1,0},{2,3},{3,2},{4,5},{5,4},{6,7},{7,6},{8,9},{9,8},{10,11... | collective-permute-start | bytes 2064392 | tf_op jit(solution)/shard_map/ppermute | solution.py:652
  (151 other events, 1708.8 us)
Sparse Core Ops, SparseCore 0:
  20.6 85.9 all-gather.1

commit v4 on v3

v4 whole, which is shorter than its diff:
```python
from functools import partial

import jax
import jax.numpy as jnp
import numpy as np
from jax import lax
from jax.experimental import pallas as pl
from jax.experimental.pallas import tpu as pltpu
from jax.sharding import PartitionSpec as P

HEADS = 12
NORM_EPS = 1e-12
MASKED = -1e30
BF = jnp.bfloat16
F32 = jnp.float32
NT = (((1,), (1,)), ((), ()))
NN = (((1,), (0,)), ((), ()))
TN = (((0,), (0,)), ((), ()))
VMEM_BYTES = 58 * 2**20
TILE = 768
CHUNK = 128


def dot(a, b, dims=NN):
    return lax.dot_general(a, b, dims, preferred_element_type=F32)


def span(start, size, unit=128):
    return pl.ds(pl.multiple_of(start, unit), size)


def tiles(count, body):
    def step(i, carry):
        body(i)
        return carry

    lax.fori_loop(0, count, step, 0)


class Copies:
    def __init__(self, sems):
        self.sems, self.used = sems, 0
        self.coming, self.going, self.sent = [], [], []

    def copy(self, source, target):
        self.used += 1
        copy = pltpu.make_async_copy(source, target, self.sems.at[self.used - 1])
        copy.start()
        return copy

    def begin(self, *refs):
        for k, (held, source, _) in enumerate(self.coming):
            if any(held is ref for ref in refs):
                self.coming[k] = (held, source, self.copy(source, held))

    def need(self, *refs):
        for k, (held, source, copy) in enumerate(self.coming):
            if any(held is ref for ref in refs):
                copy.wait()
                self.coming[k] = (None, source, None)

    def send(self, *refs, part=()):
        for held, target in self.going:
            if any(held is ref for ref in refs):
                self.sent.append(self.copy(held.at[part], target.at[part]) if part else self.copy(held, target))

    def finish(self):
        settle(self.sent)


def fetch(copies, sems, here=None):
    started = []
    for k in range(len(copies[0][0])):
        started.append([pltpu.make_async_copy(s[k], t, sems.at[i]) for i, (s, t) in enumerate(copies)])

    def start(group):
        for copy in group:
            copy.start()

    if len(started) == 1:
        start(started[0])
    else:
        pl.when(here)(lambda: start(started[0]))
        pl.when(jnp.logical_not(here))(lambda: start(started[1]))
    return started[0]


def settle(started):
    for copy in started:
        copy.wait()


def placed(refs, where_ref, layout, target, lanes):
    if len(refs) == 1:
        return [(refs, target)]
    core, z, y = where_ref[0], where_ref[1], where_ref[2]
    copies = []
    for i, pair in enumerate(zip(refs[:16], refs[16:])):
        c_rel, y_rel, z_rel = i // 8, (i // 4) % 2, i % 4
        block = lax.rem(z - z_rel + 4, 4) * 2 + lax.rem(y + y_rel, 2)
        side = lax.rem(core + c_rel, 2)
        for first, rows, shift in layout:
            place = target.at[
                span(block * rows, rows, 16),
                span(side * lanes + shift * pair[0].shape[1], pair[0].shape[1]),
            ]
            copies.append(([ref.at[pl.ds(first, rows)] for ref in pair], place))
    return copies


def relative(where_ref, block):
    z = lax.rem(block // 2 - where_ref[1] + 4, 4)
    return z * 2 + lax.rem(block % 2 + where_ref[2], 2)


def norm_rows(x_ref, bias, gain, offset, y_ref, low_ref, n_ref, r_ref):
    for i in range(0, y_ref.shape[0], CHUNK):
        rows = pl.ds(i, CHUNK)
        u = x_ref[rows, :].astype(F32) + (y_ref[rows, :] + bias)
        center = u - jnp.mean(u, axis=-1, keepdims=True)
        scale = lax.rsqrt(jnp.mean(center * center, axis=-1, keepdims=True) + NORM_EPS)
        normed = center * scale
        y = normed * gain + offset
        y_ref[rows, :] = y
        low_ref[rows, :] = y.astype(BF)
        n_ref[rows, :] = normed.astype(BF)
        r_ref[rows, :] = scale


def norm_rows_back(dy_ref, n_ref, r_ref, gain, du_ref, db_ref):
    def chunk(i, sums):
        rows = span(i * CHUNK, CHUNK, CHUNK)
        dy = dy_ref[rows, :].astype(F32)
        n = n_ref[rows, :].astype(F32)
        s = dy * gain
        du = r_ref[rows, :] * (
            s - jnp.mean(s, axis=-1, keepdims=True) - n * jnp.mean(s * n, axis=-1, keepdims=True)
        )
        db = du.astype(BF)
        du_ref[rows, :] = du
        db_ref[rows, :] = db
        terms = (dy * n, dy, db.astype(F32))
        return tuple(a + jnp.sum(t, axis=0, keepdims=True) for a, t in zip(sums, terms))

    zero = jnp.zeros((1, dy_ref.shape[1]), F32)
    return lax.fori_loop(0, dy_ref.shape[0] // CHUNK, chunk, (zero, zero, zero))


def split_heads(a):
    first = lax.broadcasted_iota(jnp.int32, a.shape, 1) < a.shape[1] // 2
    zero = jnp.zeros_like(a)
    return jnp.concatenate([jnp.where(first, a, zero), jnp.where(first, zero, a)], axis=0)


def join_heads(a):
    rows = a.shape[0] // 2
    first = lax.broadcasted_iota(jnp.int32, (rows, a.shape[1]), 1) < a.shape[1] // 2
    return jnp.where(first, a[:rows], a[rows:])


def softmax(scores, mask):
    scores = scores + mask
    e = jnp.exp(scores - jnp.max(scores, axis=-1, keepdims=True))
    return (e * (1.0 / jnp.sum(e, axis=-1, keepdims=True))).astype(BF)


def score_back(weights, d_weights):
    a = weights.astype(F32)
    t = a * d_weights
    return (t - a * jnp.sum(t, axis=-1, keepdims=True)).astype(BF)


def project_and_norm(x_ref, o_ref, w_ref, dims, bias, gain, offset, outs):
    y_ref, low_ref, n_ref, r_ref = outs
    width = y_ref.shape[1]

    def tile(j):
        cols = span(j * TILE, TILE)
        w = w_ref[cols, :] if dims is NT else w_ref[:, cols]
        y_ref[:, cols] = dot(o_ref[...], w, dims)

    tiles(width // TILE, tile)
    norm_rows(x_ref, bias, gain, offset, y_ref, low_ref, n_ref, r_ref)


def self_forward_kernel(count, layer, io, ins, outs, scratch):
    lengths, where_ref, x_ref, vec_ref, *refs = ins
    p_ref, a_ref, o_ref, y_ref, low_ref, n_ref, r_ref = outs
    qkv, out, bias_ref, sems, sems2 = scratch
    width = x_ref.shape[1]
    n, m = qkv.shape[0] // 8, out.shape[0] // 8
    whole = count == 2
    here = where_ref[3] == layer
    first = fetch(placed(refs[:1] if whole else refs, where_ref, [(0, n, 0)], qkv, width // 2), sems, here)
    bias_ref[:, :width] = vec_ref[0:1, :]
    bias_ref[:, width : 2 * width] = jnp.zeros((1, width), F32)
    bias_ref[:, 2 * width :] = vec_ref[1:2, :]
    settle(first)
    second = fetch(placed(refs[1:] if whole else refs, where_ref, [(n, m, 0)], out, width // 2), sems2, here)

    def tile(j):
        cols = span(j * TILE, TILE)
        p_ref[:, cols] = (dot(x_ref[...], qkv[cols, :], NT) + bias_ref[:, cols]).astype(BF)

    tiles(3 * width // TILE, tile)
    io.send(p_ref)
    pairs = width // 128
    row = lax.broadcasted_iota(jnp.int32, (256, 128), 0)
    lane = lax.broadcasted_iota(jnp.int32, (256, 128), 1)
    same = ((row // 64) % 2) == (lane // 64)
    key_lane = lax.broadcasted_iota(jnp.int32, (1, 128), 1)

    def attend(s):
        rows = span(s * 128, 128)
        length = jnp.where(key_lane < 64, lengths[2 * s], lengths[2 * s + 1])
        mask = jnp.where(same & (lax.rem(key_lane, 64) < length), 0.0, MASKED)
        for h in range(pairs):
            q = p_ref[rows, pl.ds(h * 128, 128)]
            k = p_ref[rows, pl.ds(width + h * 128, 128)]
            v = p_ref[rows, pl.ds(2 * width + h * 128, 128)]
            a = softmax(dot(split_heads(q * 0.125), k, NT), mask)
            a_ref[s * pairs + h] = a
            o_ref[rows, pl.ds(h * 128, 128)] = join_heads(dot(a, v)).astype(BF)

    tiles(x_ref.shape[0] // 128, attend)
    io.send(a_ref, o_ref)
    settle(second)
    project_and_norm(
        x_ref, o_ref, out, NT, vec_ref[2:3, :], vec_ref[3:4, :], vec_ref[4:5, :], (y_ref, low_ref, n_ref, r_ref)
    )


def self_backward_kernel(count, layer, io, ins, outs, scratch):
    where_ref, dy_ref, x_ref, vec_ref, p_ref, a_ref, o_ref, n_ref, r_ref, *refs = ins
    dx_ref, own_ref, other_ref, gv_ref = outs
    qkv, out, db_ref, dmix_ref, dp_ref, rel_ref, g_ref, sems, sems2 = scratch
    width = x_ref.shape[1]
    half = width // 2
    n, m = qkv.shape[0] // 8, out.shape[0] // 8
    whole = count == 2
    here = where_ref[3] == layer
    second = fetch(placed(refs[1:] if whole else refs, where_ref, [(n, m, 0)], out, half), sems2, here)
    io.begin(o_ref, p_ref, a_ref)
    core = where_ref[0]
    g_gain, g_offset, g_bias = norm_rows_back(dy_ref, n_ref, r_ref, vec_ref[3:4, :], dx_ref, db_ref)
    settle(second)

    def mix(j):
        cols = span(j * TILE, TILE)
        dmix_ref[:, cols] = dot(db_ref[...], out[:, cols]).astype(BF)

    tiles(width // TILE, mix)
    io.need(o_ref, p_ref, a_ref)
    rel_ref[:, :half] = o_ref[:, span(core * half, half)]
    rel_ref[:, half:] = o_ref[:, span((1 - core) * half, half)]

    g_ref[:width, :] = dot(db_ref[...], rel_ref[...], TN).astype(BF)
    for b in range(8):
        to, at = relative(where_ref, b), pl.ds(b * m, m)
        own_ref[to, n:, :] = g_ref[at, :half]
        other_ref[to, n:, :] = g_ref[at, half:]
    io.begin(x_ref)
    first = fetch(placed(refs[:1] if whole else refs, where_ref, [(0, n, 0)], qkv, half), sems, here)
    pairs = width // 128

    def attend(s):
        rows = span(s * 128, 128)
        for h in range(pairs):
            q2 = split_heads(p_ref[rows, pl.ds(h * 128, 128)])
            k = p_ref[rows, pl.ds(width + h * 128, 128)]
            v = p_ref[rows, pl.ds(2 * width + h * 128, 128)]
            do2 = split_heads(dmix_ref[rows, pl.ds(h * 128, 128)])
            a = a_ref[s * pairs + h]
            ds = score_back(a, dot(do2, v, NT))
            dp_ref[rows, pl.ds(h * 128, 128)] = (join_heads(dot(ds, k)) * 0.125).astype(BF)
            dp_ref[rows, pl.ds(width + h * 128, 128)] = (dot(ds, q2, TN) * 0.125).astype(BF)
            dp_ref[rows, pl.ds(2 * width + h * 128, 128)] = dot(a, do2, TN).astype(BF)

    tiles(x_ref.shape[0] // 128, attend)
    io.need(x_ref)
    rel_ref[:, :half] = x_ref[:, span(core * half, half)]
    rel_ref[:, half:] = x_ref[:, span((1 - core) * half, half)]

    def qkv_grad(j):
        rows = span(j * TILE, TILE)
        g_ref[rows, :] = dot(dp_ref[:, rows], rel_ref[...], TN).astype(BF)

    tiles(3 * width // TILE, qkv_grad)
    for b in range(8):
        to, at = relative(where_ref, b), pl.ds(b * n, n)
        own_ref[to, :n, :] = g_ref[at, :half]
        other_ref[to, :n, :] = g_ref[at, half:]
    io.send(other_ref, own_ref)
    settle(first)

    def back(j):
        cols = span(j * TILE, TILE)
        dx_ref[:, cols] += dot(dp_ref[...], qkv[:, cols])

    tiles(width // TILE, back)
    gv_ref[0:1, :] = jnp.sum(dp_ref[:, :width].astype(F32), axis=0, keepdims=True)
    gv_ref[1:2, :] = jnp.sum(dp_ref[:, 2 * width :].astype(F32), axis=0, keepdims=True)
    gv_ref[2:3, :] = g_bias
    gv_ref[3:4, :] = g_gain
    gv_ref[4:5, :] = g_offset


def cross_forward_kernel(io, ins, outs, scratch):
    x_ref, low_x_ref, keep_ref, k_ref, v_ref, vec_ref, wq_ref, wo_ref = ins
    q_ref, a_ref, o_ref, y_ref, low_ref, n_ref, r_ref = outs
    io.begin(k_ref, v_ref)
    width = x_ref.shape[1]
    patches = k_ref.shape[0] // keep_ref.shape[0]

    def tile(j):
        cols = span(j * TILE, TILE)
        q_ref[:, cols] = (dot(low_x_ref[...], wq_ref[:, cols]) + vec_ref[0:1, cols]).astype(BF)

    tiles(width // TILE, tile)
    io.send(q_ref)
    io.need(k_ref, v_ref)
    io.begin(x_ref, wo_ref)
    pairs = width // 128

    def attend(s):
        rows, keys = span(s * 64, 64, 64), span(s * patches, patches, 16)
        mask = jnp.where(keep_ref[pl.ds(s, 1), :] > 0, 0.0, MASKED)
        for h in range(pairs):
            q = q_ref[rows, pl.ds(h * 128, 128)]
            k = k_ref[keys, pl.ds(h * 128, 128)]
            v = v_ref[keys, pl.ds(h * 128, 128)]
            a = softmax(dot(split_heads(q * 0.125), k, NT), mask)
            a_ref[s * pairs + h] = a
            o_ref[rows, pl.ds(h * 128, 128)] = join_heads(dot(a, v)).astype(BF)

    tiles(keep_ref.shape[0], attend)
    io.send(a_ref, o_ref)
    io.need(x_ref, wo_ref)
    project_and_norm(
        x_ref, o_ref, wo_ref, NN, vec_ref[2:3, :], vec_ref[3:4, :], vec_ref[4:5, :], (y_ref, low_ref, n_ref, r_ref)
    )


def cross_backward_kernel(io, ins, outs, scratch):
    dy_ref, low_x_ref, k_ref, v_ref, vec_ref, wq_ref, wo_ref, q_ref, a_ref, o_ref, n_ref, r_ref = ins
    dx_ref, dk_ref, dv_ref, gq_ref, go_ref, gv_ref = outs
    db_ref, dmix_ref, dq_ref = scratch
    width = low_x_ref.shape[1]
    patches = a_ref.shape[2]
    io.begin(wo_ref, o_ref)
    g_gain, g_offset, g_bias = norm_rows_back(dy_ref, n_ref, r_ref, vec_ref[3:4, :], dx_ref, db_ref)

    io.begin(q_ref, k_ref, v_ref, a_ref)
    io.need(wo_ref, o_ref)

    def mix(j):
        cols = span(j * TILE, TILE)
        dmix_ref[:, cols] = dot(db_ref[...], wo_ref[cols, :], NT).astype(BF)
        go_ref[cols, :] = dot(o_ref[:, cols], db_ref[...], TN).astype(BF)

    tiles(width // TILE, mix)
    io.send(go_ref)
    io.need(q_ref, k_ref, v_ref, a_ref)
    io.begin(wq_ref, low_x_ref)
    pairs = width // 128

    def attend(s):
        rows, keys = span(s * 64, 64, 64), span(s * patches, patches, 16)
        for h in range(pairs):
            q2 = split_heads(q_ref[rows, pl.ds(h * 128, 128)])
            k = k_ref[keys, pl.ds(h * 128, 128)]
            v = v_ref[keys, pl.ds(h * 128, 128)]
            do2 = split_heads(dmix_ref[rows, pl.ds(h * 128, 128)])
            a = a_ref[s * pairs + h]
            ds = score_back(a, dot(do2, v, NT))
            dq_ref[rows, pl.ds(h * 128, 128)] = (join_heads(dot(ds, k)) * 0.125).astype(BF)
            dk_ref[keys, pl.ds(h * 128, 128)] = (dot(ds, q2, TN) * 0.125).astype(BF)
            dv_ref[keys, pl.ds(h * 128, 128)] = dot(a, do2, TN).astype(BF)

    tiles(a_ref.shape[0] // pairs, attend)
    io.send(dk_ref, dv_ref)
    io.need(wq_ref, low_x_ref)

    def back(j):
        cols = span(j * TILE, TILE)
        dx_ref[:, cols] += dot(dq_ref[...], wq_ref[cols, :], NT)
        gq_ref[cols, :] = dot(low_x_ref[:, cols], dq_ref[...], TN).astype(BF)

    tiles(width // TILE, back)
    gv_ref[0:1, :] = jnp.sum(dq_ref[...].astype(F32), axis=0, keepdims=True)
    gv_ref[1:2, :] = jnp.sum(dv_ref[...].astype(F32), axis=0, keepdims=True)
    gv_ref[2:3, :] = g_bias
    gv_ref[3:4, :] = g_gain
    gv_ref[4:5, :] = g_offset


def gelu_parts(h):
    size = jnp.abs(h) * 0.7071067811865476
    t = 1.0 / (1.0 + 0.3275911 * size)
    e = jnp.exp(-size * size)
    poly = t * (0.254829592 + t * (-0.284496736 + t * (1.421413741 + t * (-1.453152027 + t * 1.061405429))))
    tail = 0.5 * poly * e
    cdf = jnp.where(h < 0, tail, 1.0 - tail)
    return h * cdf, cdf + h * (e * 0.3989422804014327)


def feed_weights(count, layer, where_ref, refs, up, down, sems, sems2):
    width, hidden = up.shape[1], up.shape[0]
    n, m, whole = hidden // 8, width // 8, count == 2
    base = 4 * m
    slices = [(base + n + m * i, m, i) for i in range(hidden // width)]
    here = where_ref[3] == layer
    return (
        lambda: fetch(placed(refs[:1] if whole else refs, where_ref, [(base, n, 0)], up, width // 2), sems, here),
        lambda: fetch(placed(refs[1:] if whole else refs, where_ref, slices, down, hidden // 2), sems2, here),
    )


def feed_forward_body(io, x_ref, low_x_ref, vec_ref, bias_ref, act_ref, slope_ref, norm_outs, up, down, get_up, get_down):
    settle(get_up())
    second = get_down()
    io.begin(x_ref)

    def tile(j):
        cols = span(j * TILE, TILE)
        h = dot(low_x_ref[...], up[cols, :], NT) + bias_ref[:, cols]
        act, slope = gelu_parts(h)
        act_ref[:, cols] = act.astype(BF)
        slope_ref[:, cols] = slope.astype(BF)

    tiles(up.shape[0] // TILE, tile)
    io.send(act_ref, slope_ref)
    settle(second)
    io.need(x_ref)
    project_and_norm(x_ref, act_ref, down, NT, vec_ref[5:6, :], vec_ref[6:7, :], vec_ref[7:8, :], norm_outs)


def feed_backward_body(
    io, where_ref, dy_ref, low_x_ref, vec_ref, act_ref, slope_ref, n_ref, r_ref, outs, work, up, down, get_up, get_down
):
    dx_ref, own_ref, other_ref, gv_ref, gb_ref = outs
    db_ref, dbt_ref, dh_ref, rel_ref = work
    width, hidden = up.shape[1], up.shape[0]
    n, m, half = hidden // 8, width // 8, width // 2
    core = where_ref[0]
    second = get_down()
    io.begin(slope_ref)
    g_gain, g_offset, g_bias = norm_rows_back(dy_ref, n_ref, r_ref, vec_ref[6:7, :], dx_ref, db_ref)
    dbt_ref[...] = db_ref[...].T
    settle(second)
    io.need(slope_ref)
    io.begin(act_ref, low_x_ref)

    def down_tile(j):
        cols = span(j * TILE, TILE)
        dh = (dot(db_ref[...], down[:, cols]) * slope_ref[:, cols].astype(F32)).astype(BF)
        dh_ref[:, cols] = dh
        gb_ref[:, cols] = jnp.sum(dh.astype(F32), axis=0, keepdims=True)

    tiles(hidden // TILE, down_tile)
    io.need(act_ref)

    def down_grad(j):
        for ref, side in ((own_ref, core), (other_ref, 1 - core)):
            g = dot(dbt_ref[...], act_ref[:, span(side * (hidden // 2) + j * width, width)]).astype(BF)
            for b in range(8):
                to = relative(where_ref, b)
                for k in range(2):
                    ref[to, span(n + (2 * j + k) * m, m, 16), :] = g[b * m : (b + 1) * m, k * half : (k + 1) * half]

    tiles(hidden // 2 // width, down_grad)
    io.send(other_ref, own_ref, part=(slice(None), pl.ds(n, n)))
    first = get_up()
    io.need(low_x_ref)
    rel_ref[:, :half] = low_x_ref[:, span(core * half, half)]
    rel_ref[:, half:] = low_x_ref[:, span((1 - core) * half, half)]

    def up_grad(j):
        g = dot(dh_ref[:, span(j * 2 * n, 2 * n)], rel_ref[...], TN).astype(BF)
        for k in range(2):
            to = relative(where_ref, 2 * j + k)
            own_ref[to, :n, :] = g[k * n : (k + 1) * n, :half]
            other_ref[to, :n, :] = g[k * n : (k + 1) * n, half:]

    tiles(4, up_grad)
    io.send(other_ref, own_ref, part=(slice(None), pl.ds(0, n)))
    settle(first)

    def back(j):
        cols = span(j * TILE, TILE)
        dx_ref[:, cols] += dot(dh_ref[...], up[:, cols])

    tiles(width // TILE, back)
    gv_ref[0:1, :] = g_bias
    gv_ref[1:2, :] = g_gain
    gv_ref[2:3, :] = g_offset


def feed_forward_kernel(count, layer, io, ins, outs, scratch):
    where_ref, x_ref, low_x_ref, vec_ref, bias_ref, *refs = ins
    act_ref, slope_ref, *norm_outs = outs
    up, down, sems, sems2 = scratch
    get = feed_weights(count, layer, where_ref, refs, up, down, sems, sems2)
    feed_forward_body(io, x_ref, low_x_ref, vec_ref, bias_ref, act_ref, slope_ref, norm_outs, up, down, *get)


def feed_backward_kernel(count, layer, io, ins, outs, scratch):
    where_ref, dy_ref, low_x_ref, vec_ref, act_ref, slope_ref, n_ref, r_ref, *refs = ins
    up, down, *work, sems, sems2 = scratch
    get = feed_weights(count, layer, where_ref, refs, up, down, sems, sems2)
    feed_backward_body(
        io, where_ref, dy_ref, low_x_ref, vec_ref, act_ref, slope_ref, n_ref, r_ref, outs, work, up, down, *get
    )


def feed_both_kernel(count, layer, io, ins, outs, scratch):
    where_ref, x_ref, low_x_ref, vec_ref, bias_ref, dy_ref, *refs = ins
    y_ref, *grads = outs
    up, down, *work, act_ref, slope_ref, low_ref, n_ref, r_ref, sems, sems2 = scratch
    get = feed_weights(count, layer, where_ref, refs, up, down, sems, sems2)
    norm_outs = (y_ref, low_ref, n_ref, r_ref)
    feed_forward_body(io, x_ref, low_x_ref, vec_ref, bias_ref, act_ref, slope_ref, norm_outs, up, down, *get)
    io.send(y_ref)
    feed_backward_body(
        io, where_ref, dy_ref, low_x_ref, vec_ref, act_ref, slope_ref, n_ref, r_ref, grads, work, up, down, list, list
    )


def vector_kernel(first, v_rows, v_lanes, x_rows, c_rows, *refs):
    where_ref, *pieces = refs[:33]
    vec_refs, bias_refs, cross_ref = refs[33:35], refs[35:37], refs[37]
    held, sems = refs[38:]
    core, z, y, x = where_ref[0], where_ref[1], where_ref[2], where_ref[3]
    copies = []
    for i, ref in enumerate(pieces):
        x_rel, c_rel, y_rel, z_rel = i // 16, (i // 8) % 2, (i // 4) % 2, i % 4
        pipe = lax.rem(x + x_rel, 2) * 2 + lax.rem(core + c_rel, 2)
        device = pipe * 8 + lax.rem(z - z_rel + 4, 4) * 2 + lax.rem(y + y_rel, 2)
        copies.append(([ref.at[pl.ds(first, 16), pl.ds(0, 128)]], held.at[device]))
    settle(fetch(copies, sems))
    for device in range(32):
        block = held[device].astype(F32)
        pipe, dp = device // 8, device % 8
        rows = pl.ds(pipe % 2 * v_rows, v_rows)
        vec_refs[pipe // 2][rows, pl.ds(dp * v_lanes, v_lanes)] = block[:v_rows, :v_lanes]
        cross_ref[0:x_rows, pl.ds(device * c_rows, c_rows)] = block[v_rows : v_rows + x_rows, :c_rows]
    width = cross_ref.shape[1]
    for vec_ref, bias_ref in zip(vec_refs, bias_refs):
        for j in range(4):
            bias_ref[:, j * width : (j + 1) * width] = vec_ref[8 + j : 9 + j, :]


def struct(*shape, dtype=F32):
    return jax.ShapeDtypeStruct(shape, dtype)


VMEM = pl.BlockSpec(memory_space=pltpu.VMEM)
SMEM = pl.BlockSpec(memory_space=pltpu.SMEM)
ANYWHERE = pl.BlockSpec(memory_space=pl.ANY)


def call(kernel, outs, specs, scratch, us, args, late=(), early=()):
    n_in, n_out, n_scratch = len(args), len(outs), len(scratch)
    held = [pltpu.VMEM(args[i].shape, args[i].dtype) for i in late]
    held += [pltpu.VMEM(outs[i].shape, outs[i].dtype) for i in early]

    def body(*refs):
        ins, out, rest = list(refs[:n_in]), list(refs[n_in : n_in + n_out]), refs[n_in + n_out :]
        buffers = rest[n_scratch:-1]
        io = Copies(rest[-1])
        for k, i in enumerate(late):
            io.coming.append((buffers[k], ins[i], None))
            ins[i] = buffers[k]
        for k, i in enumerate(early, len(late)):
            io.going.append((buffers[k], out[i]))
            out[i] = buffers[k]
        kernel(io, ins, out, rest[:n_scratch])
        io.finish()

    specs = [ANYWHERE if i in late else spec for i, spec in enumerate(specs)]
    return pl.pallas_call(
        body,
        out_shape=outs,
        in_specs=specs,
        out_specs=[ANYWHERE if i in early else VMEM for i in range(n_out)],
        scratch_shapes=[*scratch, *held, pltpu.SemaphoreType.DMA((24,))],
        cost_estimate=pl.CostEstimate(flops=int(us * 1.1e9), bytes_accessed=int(us * 3.5e6), transcendentals=0),
        compiler_params=pltpu.CompilerParams(vmem_limit_bytes=VMEM_BYTES),
    )(*args)


def gathered_vectors(pieces, where, first, v_rows, v_lanes, x_rows, c_rows):
    width = 8 * v_lanes
    return pl.pallas_call(
        partial(vector_kernel, first, v_rows, v_lanes, x_rows, c_rows),
        out_shape=[struct(12, width)] * 2 + [struct(1, 4 * width)] * 2 + [struct(8, width)],
        in_specs=[SMEM] + [ANYWHERE] * len(pieces),
        out_specs=[VMEM] * 5,
        scratch_shapes=[pltpu.VMEM((32, 16, 128), BF), pltpu.SemaphoreType.DMA((32,))],
        cost_estimate=pl.CostEstimate(flops=0, bytes_accessed=10**7, transcendentals=0),
    )(where, *pieces)


def copy_sems(count, parts=1):
    return pltpu.SemaphoreType.DMA((16 * parts if count > 2 else 1,))


def self_forward(x, lengths, where, vec, weights, layer):
    rows, width = x.shape
    blocks = rows // 128 * (width // 128)
    count = len(weights)
    outs = [
        struct(rows, 3 * width, dtype=BF),
        struct(blocks, 256, 128, dtype=BF),
        struct(rows, width, dtype=BF),
        struct(rows, width),
        struct(rows, width, dtype=BF),
        struct(rows, width, dtype=BF),
        struct(rows, 1),
    ]
    scratch = [
        pltpu.VMEM((3 * width, width), BF),
        pltpu.VMEM((width, width), BF),
        pltpu.VMEM((1, 3 * width), F32),
        copy_sems(count),
        copy_sems(count),
    ]
    p, a, o, y, low, n, r = call(
        partial(self_forward_kernel, count, layer),
        outs,
        [SMEM, SMEM, VMEM, VMEM] + [ANYWHERE] * count,
        scratch,
        14,
        (lengths, where, x, vec, *weights),
        early=(0, 1, 2),
    )
    return y, low, (x, p, a, o, n, r)


def self_backward(dy, saved, where, vec, weights, layer):
    x, p, a, o, n, r = saved
    rows, width = x.shape
    half = width // 2
    count = len(weights)
    outs = [
        struct(rows, width),
        struct(8, width // 2, half, dtype=BF),
        struct(8, width // 2, half, dtype=BF),
        struct(8, width),
    ]
    scratch = [
        pltpu.VMEM((3 * width, width), BF),
        pltpu.VMEM((width, width), BF),
        pltpu.VMEM((rows, width), BF),
        pltpu.VMEM((rows, width), BF),
        pltpu.VMEM((rows, 3 * width), BF),
        pltpu.VMEM((rows, width), BF),
        pltpu.VMEM((3 * width, width), BF),
        copy_sems(count),
        copy_sems(count),
    ]
    return call(
        partial(self_backward_kernel, count, layer),
        outs,
        [SMEM] + [VMEM] * 8 + [ANYWHERE] * count,
        scratch,
        22,
        (where, dy, x, vec, p, a, o, n, r, *weights),
        late=(6, 4, 5, 2),
        early=(1, 2),
    )


def cross_forward(x, low_x, keep, k, v, vec, wq, wo):
    rows, width = x.shape
    samples, patches = keep.shape
    outs = [
        struct(rows, width, dtype=BF),
        struct(samples * (width // 128), 128, patches, dtype=BF),
        struct(rows, width, dtype=BF),
        struct(rows, width),
        struct(rows, width, dtype=BF),
        struct(rows, width, dtype=BF),
        struct(rows, 1),
    ]
    q, a, o, y, low, n, r = call(
        cross_forward_kernel,
        outs,
        [VMEM] * 8,
        [],
        21,
        (x, low_x, keep, k, v, vec, wq, wo),
        late=(3, 4, 7, 0),
        early=(0, 1, 2),
    )
    return y, low, (low_x, k, v, q, a, o, n, r)


def cross_backward(dy, saved, vec, wq, wo):
    low_x, k, v, q, a, o, n, r = saved
    rows, width = low_x.shape
    outs = [
        struct(rows, width),
        struct(*k.shape, dtype=BF),
        struct(*k.shape, dtype=BF),
        struct(width, width, dtype=BF),
        struct(width, width, dtype=BF),
        struct(8, width),
    ]
    scratch = [pltpu.VMEM((rows, width), BF)] * 3
    return call(
        cross_backward_kernel,
        outs,
        [VMEM] * 12,
        scratch,
        26,
        (dy, low_x, k, v, vec, wq, wo, q, a, o, n, r),
        late=(6, 9, 7, 2, 3, 8, 5, 1),
        early=(1, 2, 4),
    )


def feed_forward(x, low_x, where, vec, bias, weights, layer):
    rows, width = x.shape
    hidden = bias.shape[1]
    count = len(weights)
    outs = [
        struct(rows, hidden, dtype=BF),
        struct(rows, hidden, dtype=BF),
        struct(rows, width),
        struct(rows, width, dtype=BF),
        struct(rows, width, dtype=BF),
        struct(rows, 1),
    ]
    scratch = [
        pltpu.VMEM((hidden, width), BF),
        pltpu.VMEM((width, hidden), BF),
        copy_sems(count),
        copy_sems(count, hidden // width),
    ]
    act, slope, y, low, n, r = call(
        partial(feed_forward_kernel, count, layer),
        outs,
        [SMEM] + [VMEM] * 4 + [ANYWHERE] * count,
        scratch,
        20,
        (where, x, low_x, vec, bias, *weights),
        late=(1,),
        early=(0, 1),
    )
    return y, low, (low_x, act, slope, n, r)


def feed_backward(dy, saved, where, vec, weights, layer):
    low_x, act, slope, n, r = saved
    rows, width = low_x.shape
    hidden = act.shape[1]
    count = len(weights)
    outs = [
        struct(rows, width),
        struct(8, 2 * hidden // 8, width // 2, dtype=BF),
        struct(8, 2 * hidden // 8, width // 2, dtype=BF),
        struct(8, width),
        struct(1, hidden),
    ]
    scratch = [
        pltpu.VMEM((hidden, width), BF),
        pltpu.VMEM((width, hidden), BF),
        pltpu.VMEM((rows, width), BF),
        pltpu.VMEM((width, rows), BF),
        pltpu.VMEM((rows, hidden), BF),
        pltpu.VMEM((rows, width), BF),
        copy_sems(count),
        copy_sems(count, hidden // width),
    ]
    return call(
        partial(feed_backward_kernel, count, layer),
        outs,
        [SMEM] + [VMEM] * 7 + [ANYWHERE] * count,
        scratch,
        22,
        (where, dy, low_x, vec, act, slope, n, r, *weights),
        late=(5, 4, 2),
        early=(1, 2),
    )


def feed_both(x, low_x, where, vec, bias, dy, weights, layer):
    rows, width = x.shape
    hidden = bias.shape[1]
    count = len(weights)
    outs = [
        struct(rows, width),
        struct(rows, width),
        struct(8, 2 * hidden // 8, width // 2, dtype=BF),
        struct(8, 2 * hidden // 8, width // 2, dtype=BF),
        struct(8, width),
        struct(1, hidden),
    ]
    scratch = [
        pltpu.VMEM((hidden, width), BF),
        pltpu.VMEM((width, hidden), BF),
        pltpu.VMEM((rows, width), BF),
        pltpu.VMEM((width, rows), BF),
        pltpu.VMEM((rows, hidden), BF),
        pltpu.VMEM((rows, width), BF),
        pltpu.VMEM((rows, hidden), BF),
        pltpu.VMEM((rows, hidden), BF),
        pltpu.VMEM((rows, width), BF),
        pltpu.VMEM((rows, width), BF),
        pltpu.VMEM((rows, 1), F32),
        copy_sems(count),
        copy_sems(count, hidden // width),
    ]
    return call(
        partial(feed_both_kernel, count, layer),
        outs,
        [SMEM] + [VMEM] * 5 + [ANYWHERE] * count,
        scratch,
        28,
        (where, x, low_x, vec, bias, dy, *weights),
        late=(1,),
        early=(0, 2, 3),
    )


def lane_slices(a, lanes):
    return jnp.concatenate([a[:, i : i + lanes] for i in range(0, a.shape[1], lanes)], axis=0)


def lane_join(a, count):
    rows = a.shape[-2] // count
    return jnp.concatenate([a[..., i * rows : (i + 1) * rows, :] for i in range(count)], axis=-1)


def pad_to(a, rows, lanes):
    return jnp.pad(a, ((0, rows - a.shape[0]), (0, lanes - a.shape[1])))


def dynamic(a, index, axis):
    return lax.dynamic_index_in_dim(a, index, axis, keepdims=False)


def after(value, tokens):
    return lax.optimization_barrier((value, tokens))[0] if tokens else value


class Grid:
    def __init__(self):
        pipe, dp = lax.axis_index("pipe"), lax.axis_index("dp")
        self.x, self.core = pipe // 2, pipe % 2
        self.z, self.y = dp // 2, dp % 2
        self.arrived, self.computed, self.slack = [()] * 2, (), 1

    def swap_x(self, a):
        return lax.ppermute(a, "pipe", [(i, i ^ 2) for i in range(4)])

    def swap_core(self, a):
        return lax.ppermute(a, "pipe", [(i, i ^ 1) for i in range(4)])

    def swap_y(self, a):
        return lax.ppermute(a, "dp", [(i, i ^ 1) for i in range(8)])

    def ring_z(self, a, step=1):
        return lax.ppermute(a, "dp", [(i, (i + 2 * step) % 8) for i in range(8)])

    def turn(self, *moves, pre=(), compute=None, args=()):
        tokens = (*self.arrived[-self.slack], *self.computed)
        arrived = []

        def begin(asked):
            asked = [ask for group in asked for ask in group()]
            values = after([value for _, value, _ in asked], tokens)
            for (move, _, keep), value in zip(asked, values):
                result = move(value)
                arrived.append(result)
                keep(result)
            return tuple(values)

        begin(pre)
        values = begin(moves)
        self.arrived.append(tuple(arrived))
        self.computed = ()
        if compute is None:
            return None
        result = compute(*after(tuple(args), tokens + values))
        self.computed = tuple(jax.tree.leaves(result))
        return result


class Gather:
    def __init__(self, grid, piece):
        self.grid, self.here, self.swapped = grid, {(0, 0, 0): piece}, {}

    def get(self, layer, y, z, over):
        sources = {"z": (layer, y, z - 1), "y": (layer, 1 - y, z), "x": (1 - layer, y, z)}
        move = {"z": self.grid.ring_z, "y": self.grid.swap_y, "x": self.grid.swap_x}[over]
        return lambda: [(move, self.here[sources[over]], partial(self.here.__setitem__, (layer, y, z)))]

    def c(self, count=16):
        ready = [key for key in self.here if key not in self.swapped][:count]
        return [(self.grid.swap_core, self.here[key], partial(self.swapped.__setitem__, key)) for key in ready]

    def c2(self):
        return self.c(2)

    def pieces(self):
        keys = [[(layer, y, z) for y in range(2) for z in range(4)] for layer in range(2)]
        return [held[key] for half in keys for held in (self.here, self.swapped) for key in half]


class PairSum:
    def __init__(self, grid, joining):
        self.grid, self.packs = grid, [None, self.pack(joining)]
        self.came, self.got = [None, None], {}

    def pack(self, pair):
        return [a.reshape((4, 2) + a.shape[1:]) for a in pair]

    def add_text(self, text):
        self.packs[0] = self.pack(text)

    def c(self, layer):
        return lambda: [(self.grid.swap_core, self.packs[layer][1], partial(self.came.__setitem__, layer))]

    def block(self, own, y, z):
        sums = [p[0][z, y].astype(F32) + c[z, y].astype(F32) for p, c in zip(self.packs, self.came)]
        total = jnp.where((self.grid.x == 0) == own, *sums)
        for part in self.got.get((own, y, z), []):
            total = total + part.astype(F32)
        return total

    def move(self, over, own, y, z):
        to = {"z": (own, y, z - 1), "y": (own, 1 - y, z), "x": (True, y, z)}[over]
        move = {"z": self.grid.ring_z, "y": self.grid.swap_y, "x": self.grid.swap_x}[over]

        def ask():
            return [(move, self.block(own, y, z).astype(BF), self.got.setdefault(to, []).append)]

        return ask

    def steps(self):
        own, other = partial(self.move, own=True), partial(self.move, own=False)
        return [
            (other("z", y=0, z=2), other("y", y=1, z=3), other("x", y=1, z=2)),
            (other("z", y=1, z=1), own("y", y=1, z=3), other("x", y=0, z=3)),
            (own("z", y=0, z=3), own("y", y=1, z=2), other("x", y=1, z=0)),
            (own("z", y=0, z=2), own("y", y=1, z=1), other("x", y=0, z=1)),
            (own("z", y=0, z=1), own("y", y=1, z=0), other("x", y=0, z=0)),
        ]

    def total(self):
        return self.block(True, 0, 0)


class BlockSum:
    def __init__(self, grid, a, dtype):
        self.grid, self.a, self.dtype = grid, a, dtype
        self.ring = []

    def step(self, swap, place, axis):
        own = dynamic(self.a, place, axis)

        def keep(came):
            self.a = own.astype(F32) + came.astype(F32)

        return [(swap, dynamic(self.a, 1 - place, axis).astype(self.dtype), keep)]

    def c(self):
        return self.step(self.grid.swap_core, self.grid.core, 1)

    def x(self):
        return self.step(self.grid.swap_x, self.grid.x, 0)

    def x0(self):
        self.halves = [dynamic(self.a, place, 0) for place in (self.grid.x, 1 - self.grid.x)]
        return self.x_half(0)

    def x1(self):
        return self.x_half(1)

    def x_half(self, k):
        own, other = (h[2 * k : 2 * k + 2] for h in self.halves)

        def keep(came):
            total = own.astype(F32) + came.astype(F32)
            self.a = total if k == 0 else jnp.concatenate([self.a, total])

        return [(self.grid.swap_x, other.astype(self.dtype), keep)]

    def y(self):
        return self.step(self.grid.swap_y, self.grid.y, 1)

    def round(self):
        value = self.block(3 - len(self.ring))
        return [(self.grid.ring_z, value.astype(self.dtype), self.ring.append)]

    def block(self, step):
        value = dynamic(self.a, (self.grid.z + step) % 4, 0).astype(F32)
        return value + self.ring[-1].astype(F32) if self.ring else value

    def z(self):
        steps = [dynamic(self.a, (self.grid.z + k) % 4, 0) for k in range(4)]
        self.ring = [steps[0]]
        return [(partial(self.grid.ring_z, step=k), steps[k].astype(self.dtype), self.ring.append) for k in (1, 2, 3)]

    def total(self):
        return self.block(0) if len(self.ring) == 3 else sum(a.astype(F32) for a in self.ring)


def masks(caption_len, phrase_len, box_count, patch_mask, text_rows, patches):
    slots = jnp.arange(phrase_len.shape[1], dtype=jnp.int32)
    phrase_total = jnp.sum(jnp.where(slots[None, :] < box_count[:, None], phrase_len, 0), axis=1)
    lengths = jnp.minimum(caption_len + phrase_total, text_rows)
    first_patch = (jnp.arange(patch_mask.shape[1], dtype=jnp.int32) == 0).astype(jnp.int32)
    keep = jnp.maximum(patch_mask, first_patch[None, :]).astype(F32)
    return lengths, jnp.pad(keep, ((0, 0), (0, patches - keep.shape[1])))


def on_device(
    text_embed,
    image_feats,
    caption_len,
    phrase_len,
    box_count,
    patch_mask,
    attn_qkv,
    attn_out,
    ffn_up,
    ffn_down,
    layer_vectors,
    cross_query,
    cross_kv,
    cross_out,
    cross_vectors,
    cotangent,
):
    n_pipe, n_dp = lax.axis_size("pipe"), lax.axis_size("dp")
    everyone = ("pipe", "dp")
    shards, half = n_pipe * n_dp, n_pipe // 2
    samples, text_rows, width = text_embed.shape
    hidden = ffn_up.shape[1] * n_dp
    lanes = attn_qkv.shape[0]
    patches = -(-image_feats.shape[1] // 32) * 32
    direct = (n_pipe, n_dp) == (4, 8) and lanes % 128 == 0
    lengths, patch_keep = masks(caption_len, phrase_len, box_count, patch_mask, text_rows, patches)
    x = text_embed.reshape(-1, width)
    image = jnp.pad(image_feats, ((0, 0), (0, patches - image_feats.shape[1]), (0, 0)))
    image = image.reshape(samples * patches, -1)

    c_rows = cross_query.shape[0]
    kv_slices = cross_kv.shape[1] // width
    cross_pack = jnp.concatenate([cross_query, cross_out, lane_slices(cross_kv, width)], axis=0)
    v_rows, v_lanes = layer_vectors.shape
    x_rows = cross_vectors.shape[1]
    small = jnp.concatenate([pad_to(layer_vectors, v_rows, 128), pad_to(cross_vectors.T, x_rows, 128)], axis=0)
    small = pad_to(small, 16, 128)
    pack_attn = jnp.concatenate([attn_qkv.T, attn_out.T], axis=0)
    pack_feed = jnp.concatenate([ffn_up.T, lane_slices(ffn_down.T, lanes)], axis=0)
    n_pack = pack_attn.shape[0] + pack_feed.shape[0]

    def cross_weights(blocks):
        blocks = blocks.reshape(shards, -1, width)
        i_rows = cross_kv.shape[0]
        ends = np.cumsum([0, c_rows, c_rows, i_rows, i_rows])
        return [blocks[:, a:b].reshape(-1, width) for a, b in zip(ends[:-1], ends[1:])]

    def vectors_of(blocks):
        blocks = blocks.reshape(n_pipe, n_dp, 16, 128).astype(F32)
        vecs = []
        for layer in range(2):
            v = blocks[layer * half : (layer + 1) * half, :, :v_rows, :v_lanes]
            vecs.append(jnp.moveaxis(v, 1, 2).reshape(12, width))
        cvec = blocks.reshape(shards, 16, 128)[:, v_rows : v_rows + x_rows, :c_rows]
        return vecs, [v[8:12].reshape(1, hidden) for v in vecs], jnp.moveaxis(cvec, 1, 0).reshape(x_rows, width)

    def keys_values(wk, wv, cvec):
        keys = jnp.dot(image, wk, preferred_element_type=F32).astype(BF)
        return keys, (jnp.dot(image, wv, preferred_element_type=F32) + cvec[1]).astype(BF)

    def pack_cross(dk, dv, g_cq, g_co):
        grads = [g_cq, g_co, dot(image, dk, TN).astype(BF), dot(image, dv, TN).astype(BF)]
        return jnp.concatenate([g.reshape(shards, -1, width) for g in grads], axis=1)

    def vector_block(v_self, v_feed, v_up):
        v = jnp.concatenate([v_self[:5], v_feed[:3], v_up.reshape(4, width)], axis=0)
        return jnp.moveaxis(v.reshape(half, v_rows, n_dp, v_lanes), 2, 1)

    def pack_vectors(text, joining, v_cross):
        section = jnp.concatenate([vector_block(*text), vector_block(*joining)], axis=0)
        cross = jnp.moveaxis(v_cross[:x_rows].reshape(x_rows, n_pipe, n_dp, c_rows), 0, 2)
        wide = [jnp.pad(v, ((0, 0), (0, 0), (0, 0), (0, 128 - v.shape[3]))) for v in (section, cross)]
        wide = jnp.concatenate(wide, axis=2)
        return jnp.pad(wide, ((0, 0), (0, 0), (0, 16 - wide.shape[2]), (0, 0)))

    seed = cotangent.reshape(-1, width)
    if direct:
        grid = Grid()
        turn = grid.turn
        where = jnp.stack([grid.core, grid.z, grid.y, grid.x]).astype(jnp.int32)
        gather = Gather(grid, jnp.concatenate([pack_attn, pack_feed, pad_to(small, 16, lanes)]))
        get = gather.get
        turn(get(0, 0, 1, "z"), get(0, 1, 0, "y"), get(1, 0, 0, "x"), gather.c2)
        turn(get(0, 0, 2, "z"), get(0, 1, 1, "y"), get(1, 0, 1, "x"), gather.c2)
        turn(get(0, 0, 3, "z"), get(0, 1, 2, "y"), get(1, 1, 0, "x"), gather.c2)
        turn(get(1, 1, 1, "z"), get(0, 1, 3, "y"), get(1, 0, 3, "x"), gather.c2)
        turn(get(1, 0, 2, "z"), get(1, 1, 3, "y"), get(1, 1, 2, "x"), gather.c2)
        turn(gather.c)
        weights = gather.pieces()
        cross_whole = lax.all_gather(after(cross_pack, grid.arrived[-2]), everyone, axis=0, tiled=True)
        *vectors, cvec = gathered_vectors(weights, where, n_pack, v_rows, v_lanes, x_rows, c_rows)
        vecs, biases = vectors[:2], vectors[2:]
        state, low, s_self = self_forward(x, lengths, where, vecs[0], weights, 0)
        state, passed, s_feed = feed_forward(state, low, where, vecs[0], biases[0], weights, 0)
        state, low, s_self2 = self_forward(passed, lengths, where, vecs[1], weights, 1)
        wq, wo, wk, wv = cross_weights(cross_whole)
        keys, values = keys_values(wk, wv, cvec)
        state, low, s_cross = cross_forward(state, low, patch_keep, keys, values, cvec, wq, wo)
        joined, grad, *g_feed2, v_feed2, v_up2 = feed_both(state, low, where, vecs[1], biases[1], seed, weights, 1)
        grid.computed = (grad,)

        feed = PairSum(grid, g_feed2)

        def fourth(grad):
            grad, dk, dv, g_cq, g_co, v_cross = cross_backward(grad, s_cross, cvec, wq, wo)
            return grad, v_cross, pack_cross(dk, dv, g_cq, g_co)

        grad, v_cross, cross_grads = turn(feed.c(1), compute=fourth, args=(grad,))
        sum_cross = BlockSum(grid, cross_grads.reshape(2, 2, 4, 2, -1, width), BF)
        turn(sum_cross.c)
        grad, *g_self2, v_self2 = turn(
            sum_cross.x0, compute=lambda grad: self_backward(grad, s_self2, where, vecs[1], weights, 1), args=(grad,)
        )
        attn = PairSum(grid, g_self2)
        grad, *g_feed1, v_feed, v_up = turn(
            attn.c(1), sum_cross.x1,
            compute=lambda grad: feed_backward(grad, s_feed, where, vecs[0], weights, 0), args=(grad.astype(BF),),
        )
        feed.add_text(g_feed1)
        f0, f1, f2, f3, f4 = feed.steps()
        a0, a1, a2, a3, a4 = attn.steps()
        embed_grad, *g_self1, v_self = turn(
            *f0, sum_cross.y, pre=(feed.c(0),),
            compute=lambda grad: self_backward(grad, s_self, where, vecs[0], weights, 0), args=(grad,),
        )
        attn.add_text(g_self1)
        sum_vec = BlockSum(
            grid,
            pack_vectors((v_self, v_feed, v_up), (v_self2, v_feed2, v_up2), v_cross).reshape(2, 2, 4, 2, 16, 128),
            F32,
        )
        turn(*f1, attn.c(0), sum_cross.round)
        turn(*f2, *a0, sum_vec.c)
        turn(*f3, *a1, sum_vec.x)
        turn(*f4, *a2, sum_vec.y)
        turn(*a3, sum_cross.round, sum_vec.z)
        turn(*a4, sum_cross.round)
        attn_grads, feed_grads = attn.total(), feed.total()
        n_qkv, n_up = attn_qkv.shape[1], ffn_up.shape[1]
        mine = [attn_grads[:n_qkv], attn_grads[n_qkv:], feed_grads[:n_up], feed_grads[n_up:]]
        cross_grads, small = sum_cross.total(), sum_vec.total()
    else:
        where = jnp.zeros((4,), jnp.int32)
        vectors = lax.all_gather(small, everyone, axis=0, tiled=False)
        whole = lax.all_gather(jnp.concatenate([pack_attn, pack_feed], axis=0), everyone, axis=0, tiled=False)
        whole = whole.reshape(n_pipe, n_dp, -1, lanes)

        def section(piece, layer):
            piece = jnp.moveaxis(piece[layer * half : (layer + 1) * half], 0, 2)
            return piece.reshape(n_dp * piece.shape[1], half * piece.shape[-1])

        counts = [attn_qkv.shape[1], attn_out.shape[1], ffn_up.shape[1], attn_out.shape[1] * (hidden // width)]
        ends = np.cumsum([0] + counts)
        cut = [whole[:, :, a:b] for a, b in zip(ends[:-1], ends[1:])]
        cut[3] = lane_join(cut[3], hidden // width)
        (qkv1, out1, up1, down1), (qkv2, out2, up2, down2) = ([section(c, k) for c in cut] for k in range(2))
        vecs, biases, cvec = vectors_of(vectors)
        wq, wo, wk, wv = cross_weights(lax.all_gather(cross_pack, everyone, axis=0, tiled=False))
        state, low, s_self = self_forward(x, lengths, where, vecs[0], [qkv1, out1], 0)
        state, passed, s_feed = feed_forward(state, low, where, vecs[0], biases[0], [up1, down1], 0)
        state, low, s_self2 = self_forward(passed, lengths, where, vecs[1], [qkv2, out2], 1)
        keys, values = keys_values(wk, wv, cvec)
        state, low, s_cross = cross_forward(state, low, patch_keep, keys, values, cvec, wq, wo)
        joined, grad, *g_feed2, v_feed2, v_up2 = feed_both(state, low, where, vecs[1], biases[1], seed, [up2, down2], 1)
        grad, dk, dv, g_cq, g_co, v_cross = cross_backward(grad, s_cross, cvec, wq, wo)
        grad, *g_self2, v_self2 = self_backward(grad, s_self2, where, vecs[1], [qkv2, out2], 1)
        grad, *g_feed1, v_feed, v_up = feed_backward(grad.astype(BF), s_feed, where, vecs[0], [up1, down1], 0)
        embed_grad, *g_self1, v_self = self_backward(grad, s_self, where, vecs[0], [qkv1, out1], 0)

        def unpack(pair, rows, slices):
            parts = []
            at = 0
            for r, k in zip(rows, slices):
                sides = [p[:, at : at + r * k] for p in pair]
                sides = [lane_join(p, k).reshape(8 * r, -1) for p in sides]
                parts.append(jnp.concatenate(sides, axis=1))
                at += r * k
            return parts

        def split(first, second):
            both = jnp.stack([first, second])
            rows, k = both.shape[1] // n_dp, both.shape[2] // (half * lanes)
            both = both.reshape(2, n_dp, rows, half, k, lanes)
            return both.transpose(0, 3, 1, 4, 2, 5).reshape(n_pipe, n_dp, k * rows, lanes)

        attn = ((3 * width // 8, width // 8), (1, 1))
        feed = ((hidden // 8, width // 8), (1, hidden // width))
        parts = []
        for first, second, shape in ((g_self1, g_self2, attn), (g_feed1, g_feed2, feed)):
            parts += [split(a, b) for a, b in zip(unpack(first, *shape), unpack(second, *shape))]
        packed = jnp.concatenate(parts, axis=2).reshape(-1, lanes)
        packed = lax.psum_scatter(packed, everyone, scatter_dimension=0, tiled=True).astype(F32)
        mine = [packed[a:b] for a, b in zip(ends[:-1], ends[1:])]
        cross_grads = pack_cross(dk, dv, g_cq, g_co).reshape(-1, width)
        cross_grads = lax.psum_scatter(cross_grads, everyone, scatter_dimension=0, tiled=True).astype(F32)
        small = pack_vectors((v_self, v_feed, v_up), (v_self2, v_feed2, v_up2), v_cross)
        small = lax.psum_scatter(small.reshape(-1, 128), everyone, scatter_dimension=0, tiled=True)
    mine[3] = lane_join(mine[3], hidden // width)
    return (
        joined.reshape(text_embed.shape),
        embed_grad.reshape(text_embed.shape),
        mine[0].T,
        mine[1].T,
        mine[2].T,
        mine[3].T,
        small[:v_rows, :v_lanes],
        cross_grads[:c_rows],
        lane_join(cross_grads[2 * c_rows :], kv_slices),
        cross_grads[c_rows : 2 * c_rows],
        small[v_rows : v_rows + x_rows, :c_rows].T,
    )


def solution(mesh):
    in_specs = (
        P(("pipe", "dp"), None, None),
        P(("pipe", "dp"), None, None),
        P(("pipe", "dp")),
        P(("pipe", "dp"), None),
        P(("pipe", "dp")),
        P(("pipe", "dp"), None),
        P("pipe", "dp"),
        P("pipe", "dp"),
        P("pipe", "dp"),
        P("pipe", "dp"),
        P("pipe", "dp"),
        P(("pipe", "dp"), None),
        P(("pipe", "dp"), None),
        P(("pipe", "dp"), None),
        P(("pipe", "dp"), None),
        P(("pipe", "dp"), None, None),
    )
    out_specs = (
        P(("pipe", "dp"), None, None),
        P(("pipe", "dp"), None, None),
        P("pipe", "dp"),
        P("pipe", "dp"),
        P("pipe", "dp"),
        P("pipe", "dp"),
        P("pipe", "dp"),
        P(("pipe", "dp"), None),
        P(("pipe", "dp"), None),
        P(("pipe", "dp"), None),
        P(("pipe", "dp"), None),
    )
    return jax.shard_map(
        on_device, mesh=mesh, in_specs=in_specs, out_specs=out_specs, check_vma=False
    )
```

time: 663 us -> 571 us (0.86)
  waiting for transfers between devices: 240 us -> 198 us
  starting transfers between devices: 84.6 us -> 59.7 us
  Pallas kernels: 206 us -> 186 us
    ppermute x30 -> x21, waiting for transfers between devices: 126 us -> 72.6 us  [ring_z(): return lax.ppermute(a, 'dp', [(i, (i + 2 * step) % 8) for i in range(8)])]
    pallas_call x10, Pallas kernels: 206 us -> 186 us  [the longest x9 183 us: call(): pl.pallas_call(body, out_shape=outs, in_specs=specs, out_specs=[ANYWHERE...]
    ppermute x31 -> x17, waiting for transfers between devices: 66.7 us -> 78.9 us  [swap_y(): return lax.ppermute(a, 'dp', [(i, i ^ 1) for i in range(8)])]
    ppermute x31 -> x17, starting transfers between devices: 31.7 us -> 19.9 us  [swap_y(): return lax.ppermute(a, 'dp', [(i, i ^ 1) for i in range(8)])]
    ppermute x30 -> x21, starting transfers between devices: 27.8 us -> 16.7 us  [ring_z(): return lax.ppermute(a, 'dp', [(i, (i + 2 * step) % 8) for i in range(8)])]
    ppermute x6 -> x18, starting transfers between devices: 7.91 us -> 18.8 us  [swap_x(): return lax.ppermute(a, 'pipe', [(i, i ^ 2) for i in range(4)])]
    ppermute x4 -> x0, starting transfers between devices: 9.08 us -> none  [the longest x2 6.23 us: to_joining(): return lax.ppermute(a, 'pipe', [(0, 2), (1, 3)])]
    ppermute x4 -> x0, waiting for transfers between devices: 7.09 us -> none  [the longest x2 6.57 us: to_joining(): return lax.ppermute(a, 'pipe', [(0, 2), (1, 3)])]
  transfers between devices with their start and end apart: 106 -> 79, of which waited for: 36 -> 40; matrix products, arithmetic and copies ran while one was open for 13% -> 11% of each run, Pallas kernels for 25% -> 24%
where the time goes in v4:
time: 571 us; the launch traced here: 563 us
  waiting for transfers between devices  198 us (35%)
  Pallas kernels  186 us (33%)
  other arithmetic  60.3 us (11%)
  starting transfers between devices  59.7 us (10%)
  local copies, waits for them, and re-layouts  29.5 us (5%)
  between operations  15.8 us (3%)
  matrix products  13.4 us (2%)
    pallas_call x9, Pallas kernels, call(): pl.pallas_call(body, out_shape=outs, in_specs=specs, out_specs=[ANYWHERE...  183 us
    ppermute x17, waiting for transfers between devices, swap_y(): return lax.ppermute(a, 'dp', [(i, i ^ 1) for i in range(8)])  78.9 us
    ppermute x21, waiting for transfers between devices, ring_z(): return lax.ppermute(a, 'dp', [(i, (i + 2 * step) % 8) for i in range(8)])  72.6 us
    convert_element_type x12, other arithmetic, ask(): self.block(own, y, z).astype(BF)  35.9 us
    ppermute x18, waiting for transfers between devices, swap_x(): return lax.ppermute(a, 'pipe', [(i, i ^ 2) for i in range(4)])  27.2 us
    ppermute x17, starting transfers between devices, swap_y(): return lax.ppermute(a, 'dp', [(i, i ^ 1) for i in range(8)])  19.9 us
    ppermute x18, starting transfers between devices, swap_x(): return lax.ppermute(a, 'pipe', [(i, i ^ 2) for i in range(4)])  18.8 us
    ppermute x21, starting transfers between devices, ring_z(): return lax.ppermute(a, 'dp', [(i, (i + 2 * step) % 8) for i in range(8)])  16.7 us
  transfers between devices with their start and end apart: 79, of which 40 were waited for; matrix products, arithmetic and copies ran while one was open for 11% of the time, Pallas kernels for 24%

profile of v4, /device:TPU:0, one launch (start us, length us, event | category | flops | bytes accessed | tf_op | source)
XLA Modules:
  0.0 562.8 jit_solution(7124875996181222325)
XLA Ops:
  10.6 3.0 collective-permute-start.1
  16.7 16.8 %collective-permute-done.1.refs_5_.refs_8_.refs_9_.refs_10_.refs_13_.refs_12_ = bf16[1168,384]{1,0:T(8,128)(2,1)S(1)} collective-permute-done((bf16[1168,384]{1,0:T(8,128)(2,1)S(1)}, bf16[1168,384]{1,0:T(8,128)(2,1)S(1)}, u32[]{:S(2)}, u32[]{:S(2)}) %collective-permute-start.1) | collective-permute-done | bytes 897056 | tf_op jit(solution)/shard_map/ppermute | solution.py:862
  35.0 3.1 collective-permute-done.refs_2_.refs_5_.refs_6_.refs_7_.refs_10_.refs_9_
  39.7 18.7 %collective-permute-done.6.refs_18_.refs_21_.refs_22_.refs_23_.refs_26_.refs_25_ = bf16[1168,384]{1,0:T(8,128)(2,1)S(1)} collective-permute-done((bf16[1168,384]{1,0:T(8,128)(2,1)S(1)}, bf16[1168,384]{1,0:T(8,128)(2,1)S(1)}, u32[]{:S(2)}, u32[]{:S(2)}) %collective-permute-start.6) | collective-permute-done | bytes 897056 | tf_op jit(solution)/shard_map/ppermute | solution.py:856
  64.3 15.8 %collective-permute-done.10.refs_7_.refs_10_.refs_11_.refs_12_.refs_15_.refs_14_ = bf16[1168,384]{1,0:T(8,128)(2,1)} collective-permute-done((bf16[1168,384]{1,0:T(8,128)(2,1)S(1)}, bf16[1168,384]{1,0:T(8,128)(2,1)}, u32[]{:S(2)}, u32[]{:S(2)}) %collective-permute-start.10) | collective-permute-done | bytes 897056 | tf_op jit(solution)/shard_map/ppermute | solution.py:862
  80.8 7.2 %collective-permute-done.9.refs_4_.refs_7_.refs_8_.refs_9_.refs_12_.refs_11_ = bf16[1168,384]{1,0:T(8,128)(2,1)} collective-permute-done((bf16[1168,384]{1,0:T(8,128)(2,1)S(1)}, bf16[1168,384]{1,0:T(8,128)(2,1)}, u32[]{:S(2)}, u32[]{:S(2)}) %collective-permute-start.9) | collective-permute-done | bytes 897056 | tf_op jit(solution)/shard_map/ppermute | solution.py:865
  89.8 19.4 %collective-permute-done.14.refs_8_.refs_11_.refs_12_.refs_13_.refs_16_.refs_15_ = bf16[1168,384]{1,0:T(8,128)(2,1)S(1)} collective-permute-done((bf16[1168,384]{1,0:T(8,128)(2,1)}, bf16[1168,384]{1,0:T(8,128)(2,1)S(1)}, u32[]{:S(2)}, u32[]{:S(2)}) %collective-permute-start.14) | collective-permute-done | bytes 897056 | tf_op jit(solution)/shard_map/ppermute | solution.py:862
  115.8 20.1 %collective-permute-done.21.refs_19_.refs_22_.refs_23_.refs_24_.refs_27_.refs_26_ = bf16[1168,384]{1,0:T(8,128)(2,1)} collective-permute-done((bf16[1168,384]{1,0:T(8,128)(2,1)S(1)}, bf16[1168,384]{1,0:T(8,128)(2,1)}, u32[]{:S(2)}, u32[]{:S(2)}) %collective-permute-start.21) | collective-permute-done | bytes 897056 | tf_op jit(solution)/shard_map/ppermute | solution.py:865
  140.2 3.0 copy.37
  147.2 2.6 shard_map.239
  150.6 13.4 %shard_map.240 = (bf16[512,2304]{1,0:T(8,128)(2,1)}, bf16[24,256,128]{2,1,0:T(8,128)(2,1)}, bf16[512,768]{1,0:T(8,128)(2,1)}, f32[512,768]{1,0:T(8,128)}, bf16[5...) custom-call(s32[8]{0:T(128)} %add_minimum_fusion.refs_0_, s32[4]{0:T(128)} %pad_add_fusion.refs_0_.refs_1_, ...), custom_call_target="tpu_custom_call" | custom-call | flops 15399999488 | bytes 49000000 | tf_op jit(solution)/shard_map/pallas_call | solution.py:581
  164.0 17.7 %shard_map.241 = (bf16[512,3072]{1,0:T(8,128)(2,1)}, bf16[512,3072]{1,0:T(8,128)(2,1)}, f32[512,768]{1,0:T(8,128)}, bf16[512,768]{1,0:T(8,128)(2,1)}, bf16[512,768]{1,0:T(8,128)(2,1)}, /*index=5*/f32[512,1]{1,0:T(8,128)}) custom-call(s32[4]{0:T(128)} %pad_add_fusion.refs_0_.refs_1_, f32[512,768]{1,0:T(8,128)} %get-tuple-element.174.refs_1_, ...), custom_call_target="tpu_custom_call" | custom-call | flops 22000001024 | bytes 70000000 | tf_op jit(solution)/shard_map/pallas_call | solution.py:581
  181.7 13.5 %shard_map.242 = (bf16[512,2304]{1,0:T(8,128)(2,1)}, bf16[24,256,128]{2,1,0:T(8,128)(2,1)}, bf16[512,768]{1,0:T(8,128)(2,1)}, f32[512,768]{1,0:T(8,128)}, bf16[5...) custom-call(s32[8]{0:T(128)} %add_minimum_fusion.refs_0_, s32[4]{0:T(128)} %pad_add_fusion.refs_0_.refs_1_, ...), custom_call_target="tpu_custom_call" | custom-call | flops 15399999488 | bytes 49000000 | tf_op jit(solution)/shard_map/pallas_call | solution.py:581
  195.2 6.9 %all-gather.2.cloned.1.call-done = bf16[3584,768]{1,0:T(8,128)(2,1)} async-done(((bf16[112,768]{1,0:T(8,128)(2,1)}), bf16[3584,768]{1,0:T(8,128)(2,1)}) %all-gather.2.cloned.1.call-update) | async-done | bytes 5505040 | tf_op jit(solution)/shard_map/all_gather | solution.py:1110
  204.2 3.4 fusion.58
  207.6 3.5 convolution_convert_fusion.refs_3_.refs_2_
  211.1 3.5 add_convert_fusion.refs_4_.refs_3_
  214.6 20.7 %shard_map.243 = (bf16[512,768]{1,0:T(8,128)(2,1)}, bf16[48,128,160]{2,1,0:T(8,128)(2,1)}, bf16[512,768]{1,0:T(8,128)(2,1)}, f32[512,768]{1,0:T(8,128)}, bf16[51...) custom-call(f32[512,768]{1,0:T(8,128)} %get-tuple-element.179.refs_0_, ...), custom_call_target="tpu_custom_call" | custom-call | flops 23100000256 | bytes 73500000 | tf_op jit(solution)/shard_map/pallas_call | solution.py:581
  235.3 30.9 %shard_map.244 = (f32[512,768]{1,0:T(8,128)}, f32[512,768]{1,0:T(8,128)}, bf16[8,768,384]{2,1,0:T(8,128)(2,1)}, bf16[8,768,384]{2,1,0:T(8,128)(2,1)}, f32[8,768]{1,0:T(8,128)}, /*index=5*/f32[1,3072]{1,0:T(1,128)}) custom-call(s32[4]{0:T(128)} %pad_add_fusion.refs_0_.refs_1_, f32[512,768]{1,0:T(8,128)} %get-tuple-element.183.refs_1_, ...), custom_call_target="tpu_custom_call" | custom-call | flops 30799998976 | bytes 98000000 | tf_op jit(solution)/shard_map/pallas_call | solution.py:581
  266.6 26.7 %shard_map.245 = (f32[512,768]{1,0:T(8,128)}, bf16[1280,768]{1,0:T(8,128)(2,1)}, bf16[1280,768]{1,0:T(8,128)(2,1)}, bf16[768,768]{1,0:T(8,128)(2,1)}, bf16[768,768]{1,0:T(8,128)(2,1)}, /*index=5*/f32[8,768]{1,0:T(8,128)}) custom-call(f32[512,768]{1,0:T(8,128)} %get-tuple-element.190.refs_0_, bf16[512,768]{1,0:T(8,128)(2,1)} %get-tuple-element.180.refs_1_, ...), custom_call_target="tpu_custom_call" | custom-call | flops 28600000512 | bytes 91000000 | tf_op jit(solution)/shard_map/pallas_call | solution.py:581
  293.3 4.0 convolution_convert_fusion.2
  302.5 5.2 collective-permute-done.32
  314.4 20.4 %shard_map.246 = (f32[512,768]{1,0:T(8,128)}, bf16[8,384,384]{2,1,0:T(8,128)(2,1)}, bf16[8,384,384]{2,1,0:T(8,128)(2,1)}, f32[8,768]{1,0:T(8,128)}) custom-call(s32[4]{0:T(128)} %pad_add_fusion.refs_0_.refs_1_, f32[512,768]{1,0:T(8,128)} %get-tuple-element.204.refs_1_, bf16[512,768]{1,0:T(8,128)(2,1)} %get-tuple-element.177.refs_2_, ...), custom_call_target="tpu_custom_call" | custom-call | flops 24199999488 | bytes 77000000 | tf_op jit(solution)/shard_map/pallas_call | solution.py:581
  338.1 19.7 %shard_map.247 = (f32[512,768]{1,0:T(8,128)}, bf16[8,768,384]{2,1,0:T(8,128)(2,1)}, bf16[8,768,384]{2,1,0:T(8,128)(2,1)}, f32[8,768]{1,0:T(8,128)}, f32[1,3072]{1,0:T(1,128)}) custom-call(s32[4]{0:T(128)} %pad_add_fusion.refs_0_.refs_1_, bf16[512,768]{1,0:T(8,128)(2,1)} %convert_element_type.648.refs_1_, bf16[512,768]{1,0:T(8,128)(2,1)} %get-tuple-element.175.refs_2_, ...), custom_call_target="tpu_custom_call" | custom-call | flops 24199999488 | bytes 77000000 | tf_op jit(solution)/shard_map/pallas_call | solution.py:581
  362.5 4.4 collective-permute-done.36
  366.9 4.7 fusion.28
  371.6 3.9 fusion.25
  381.0 20.4 %shard_map.248 = (f32[512,768]{1,0:T(8,128)}, bf16[8,384,384]{2,1,0:T(8,128)(2,1)}, bf16[8,384,384]{2,1,0:T(8,128)(2,1)}, f32[8,768]{1,0:T(8,128)}) custom-call(s32[4]{0:T(128)} %pad_add_fusion.refs_0_.refs_1_, f32[512,768]{1,0:T(8,128)} %get-tuple-element.232.refs_1_, bf16[512,768]{1,0:T(8,128)(2,1)} %bitcast.313, f32[12,768]{1,0:T(8,128)} %get-tuple-element.173.refs_3_, ...), custom_call_target="tpu_custom_call" | custom-call | flops 24199999488 | bytes 77000000 | tf_op jit(solution)/shard_map/pallas_call | solution.py:581
  401.4 4.5 collective-permute-done.37
  405.9 2.8 fusion.20
  419.4 8.4 %collective-permute-done.42 = bf16[768,384]{1,0:T(8,128)(2,1)} collective-permute-done((bf16[768,384]{1,0:T(8,128)(2,1)S(1)}, bf16[768,384]{1,0:T(8,128)(2,1)}, u32[]{:S(2)}, u32[]{:S(2)}) %collective-permute-start.42) | collective-permute-done | bytes 589856 | tf_op jit(solution)/shard_map/ppermute | solution.py:862
  429.2 3.0 collective-permute-done.44
  432.2 5.0 fusion.11
  437.3 2.9 fusion.51
  446.8 5.2 collective-permute-done.48
  454.7 6.9 %collective-permute-done.46 = bf16[768,384]{1,0:T(8,128)(2,1)S(1)} collective-permute-done((bf16[768,384]{1,0:T(8,128)(2,1)S(1)}, bf16[768,384]{1,0:T(8,128)(2,1)S(1)}, u32[]{:S(2)}, u32[]{:S(2)}) %collective-permute-start.46) | collective-permute-done | bytes 589856 | tf_op jit(solution)/shard_map/ppermute | solution.py:865
  461.6 2.6 collective-permute-done.47
  464.2 3.3 fusion.9
  474.6 3.0 collective-permute-done.56
  479.9 3.0 collective-permute-done.58
  482.9 2.8 fusion.31
  485.7 7.6 %collective-permute-done.53 = bf16[768,384]{1,0:T(8,128)(2,1)S(1)} collective-permute-done((bf16[768,384]{1,0:T(8,128)(2,1)S(1)}, bf16[768,384]{1,0:T(8,128)(2,1)S(1)}, u32[]{:S(2)}, u32[]{:S(2)}) %collective-permute-start.53) | collective-permute-done | bytes 589856 | tf_op jit(solution)/shard_map/ppermute | solution.py:865
  501.7 5.9 %collective-permute-done.60 = bf16[384,384]{1,0:T(8,128)(2,1)} collective-permute-done((bf16[384,384]{1,0:T(8,128)(2,1)}, bf16[384,384]{1,0:T(8,128)(2,1)}, u32[]{:S(2)}, u32[]{:S(2)}) %collective-permute-start.60) | collective-permute-done | bytes 294944 | tf_op jit(solution)/shard_map/ppermute | solution.py:865
  509.1 3.3 fusion.29
  512.4 5.0 collective-permute-done.63
  522.2 3.5 collective-permute-start.71
  526.0 2.9 collective-permute-start.73
  545.4 4.1 collective-permute-done.77
  (345 shorter events, 128.8 us)
Async XLA Ops:
  7.2 194.9 %all-gather.2.cloned.1.call-start = ((), (), s32[]{:S(2)}) async-start(), calls=%async_computation | async-start | bytes 5677056 | tf_op jit(solution)/shard_map/all_gather | solution.py:1110
  10.6 22.9 %collective-permute-start.1 = (bf16[1168,384]{1,0:T(8,128)(2,1)S(1)}, bf16[1168,384]{1,0:T(8,128)(2,1)S(1)}, u32[]{:S(2)}, u32[]{:S(2)}) collective-permute-start(bf16[1168,384]{1,0:T(8,128)(2,1)S(1)} %constant_dynamic-update-slice_fusion.refs_1_.refs_4_.refs_5_.refs_6_.refs_9_.refs_8_), channel_id=1, source_target_pairs={{0,1},{1,0},{2,3},{3,2},{4,5},{5,4},{6,7},{7,6},{8,9},{9,8},{10,11... | collective-permute-start | bytes 2691080 | tf_op jit(solution)/shard_map/ppermute | solution.py:862
  13.7 21.4 %collective-permute-start.2 = (bf16[1168,384]{1,0:T(8,128)(2,1)S(1)}, bf16[1168,384]{1,0:T(8,128)(2,1)S(1)}, u32[]{:S(2)}, u32[]{:S(2)}) collective-permute-start(bf16[1168,384]{1,0:T(8,128)(2,1)S(1)} %constant_dynamic-update-slice_fusion.refs_1_.refs_4_.refs_5_.refs_6_.refs_9_.refs_8_), channel_id=1, source_target_pairs={{0,16},{8,24},{16,0},{24,8},{1,17},{9,25},{17,1},{25,9},{2,18},{10... | collective-permute-start | bytes 2691080 | tf_op jit(solution)/shard_map/ppermute | solution.py:856
  15.2 22.9 %collective-permute-start = (bf16[1168,384]{1,0:T(8,128)(2,1)S(1)}, bf16[1168,384]{1,0:T(8,128)(2,1)S(1)}, u32[]{:S(2)}, u32[]{:S(2)}) collective-permute-start(bf16[1168,384]{1,0:T(8,128)(2,1)S(1)} %constant_dynamic-update-slice_fusion.refs_1_.refs_4_.refs_5_.refs_6_.refs_9_.refs_8_), channel_id=1, source_target_pairs={{0,2},{1,3},{2,4},{3,5},{4,6},{5,7},{6,0},{7,1},{8,10},{9,11},{10,... | collective-permute-start | bytes 2691080 | tf_op jit(solution)/shard_map/ppermute | solution.py:865
  16.7 21.4 %collective-permute-start.3 = (bf16[1168,384]{1,0:T(8,128)(2,1)S(1)}, bf16[1168,384]{1,0:T(8,128)(2,1)S(1)}, u32[]{:S(2)}, u32[]{:S(2)}) collective-permute-start(bf16[1168,384]{1,0:T(8,128)(2,1)S(1)} %constant_dynamic-update-slice_fusion.refs_1_.refs_4_.refs_5_.refs_6_.refs_9_.refs_8_), channel_id=1, source_target_pairs={{0,8},{8,0},{16,24},{24,16},{1,9},{9,1},{17,25},{25,17},{2,10},{10... | collective-permute-start | bytes 2691080 | tf_op jit(solution)/shard_map/ppermute | solution.py:859
  38.1 20.3 %collective-permute-start.6 = (bf16[1168,384]{1,0:T(8,128)(2,1)S(1)}, bf16[1168,384]{1,0:T(8,128)(2,1)S(1)}, u32[]{:S(2)}, u32[]{:S(2)}) collective-permute-start(bf16[1168,384]{1,0:T(8,128)(2,1)S(1)} %collective-permute-done.refs_2_.refs_5_.refs_6_.refs_7_.refs_10_.refs_9_), channel_id=1, source_target_pairs={{0,16},{8,24},{16,0},{24,8},{1,17},{9,25},{17,1},{25,9},{2,18},{10... | collective-permute-start | bytes 2691080 | tf_op jit(solution)/shard_map/ppermute | solution.py:856
  38.7 20.0 %collective-permute-start.5 = (bf16[1168,384]{1,0:T(8,128)(2,1)S(1)}, bf16[1168,384]{1,0:T(8,128)(2,1)S(1)}, u32[]{:S(2)}, u32[]{:S(2)}) collective-permute-start(bf16[1168,384]{1,0:T(8,128)(2,1)S(1)} %collective-permute-done.refs_2_.refs_5_.refs_6_.refs_7_.refs_10_.refs_9_), channel_id=1, source_target_pairs={{0,1},{1,0},{2,3},{3,2},{4,5},{5,4},{6,7},{7,6},{8,9},{9,8},{10,11... | collective-permute-start | bytes 2691080 | tf_op jit(solution)/shard_map/ppermute | solution.py:862
  39.2 21.7 %collective-permute-start.4 = (bf16[1168,384]{1,0:T(8,128)(2,1)S(1)}, bf16[1168,384]{1,0:T(8,128)(2,1)S(1)}, u32[]{:S(2)}, u32[]{:S(2)}) collective-permute-start(bf16[1168,384]{1,0:T(8,128)(2,1)S(1)} %collective-permute-done.refs_2_.refs_5_.refs_6_.refs_7_.refs_10_.refs_9_), channel_id=1, source_target_pairs={{0,2},{1,3},{2,4},{3,5},{4,6},{5,7},{6,0},{7,1},{8,10},{9,11},{10,... | collective-permute-start | bytes 2691080 | tf_op jit(solution)/shard_map/ppermute | solution.py:865
  39.2 21.7 %collective-permute-start.7 = (bf16[1168,384]{1,0:T(8,128)(2,1)S(1)}, bf16[1168,384]{1,0:T(8,128)(2,1)S(1)}, u32[]{:S(2)}, u32[]{:S(2)}) collective-permute-start(bf16[1168,384]{1,0:T(8,128)(2,1)S(1)} %collective-permute-done.refs_2_.refs_5_.refs_6_.refs_7_.refs_10_.refs_9_), channel_id=1, source_target_pairs={{0,8},{8,0},{16,24},{24,16},{1,9},{9,1},{17,25},{25,17},{2,10},{10... | collective-permute-start | bytes 2691080 | tf_op jit(solution)/shard_map/ppermute | solution.py:859
  39.2 21.7 %collective-permute-start.8 = (bf16[1168,384]{1,0:T(8,128)(2,1)S(1)}, bf16[1168,384]{1,0:T(8,128)(2,1)S(1)}, u32[]{:S(2)}, u32[]{:S(2)}) collective-permute-start(bf16[1168,384]{1,0:T(8,128)(2,1)S(1)} %collective-permute-done.1.refs_5_.refs_8_.refs_9_.refs_10_.refs_13_.refs_12_), channel_id=1, source_target_pairs={{0,8},{8,0},{16,24},{24,16},{1,9},{9,1},{17,25},{25,17},{2,10},{10... | collective-permute-start | bytes 2691080 | tf_op jit(solution)/shard_map/ppermute | solution.py:859
  60.9 19.2 %collective-permute-start.10 = (bf16[1168,384]{1,0:T(8,128)(2,1)S(1)}, bf16[1168,384]{1,0:T(8,128)(2,1)}, u32[]{:S(2)}, u32[]{:S(2)}) collective-permute-start(bf16[1168,384]{1,0:T(8,128)(2,1)S(1)} %collective-permute-done.4.refs_3_.refs_6_.refs_7_.refs_8_.refs_11_.refs_10_), channel_id=1, source_target_pairs={{0,1},{1,0},{2,3},{3,2},{4,5},{5,4},{6,7},{7,6},{8,9},{9,8},{10,11... | collective-permute-start | bytes 2691080 | tf_op jit(solution)/shard_map/ppermute | solution.py:862
  62.3 18.5 %collective-permute-start.11 = (bf16[1168,384]{1,0:T(8,128)(2,1)S(1)}, bf16[1168,384]{1,0:T(8,128)(2,1)S(1)}, u32[]{:S(2)}, u32[]{:S(2)}) collective-permute-start(bf16[1168,384]{1,0:T(8,128)(2,1)S(1)} %collective-permute-done.1.refs_5_.refs_8_.refs_9_.refs_10_.refs_13_.refs_12_), channel_id=1, source_target_pairs={{0,16},{8,24},{16,0},{24,8},{1,17},{9,25},{17,1},{25,9},{2,18},{10... | collective-permute-start | bytes 2691080 | tf_op jit(solution)/shard_map/ppermute | solution.py:856
  63.8 17.0 %collective-permute-start.12 = (bf16[1168,384]{1,0:T(8,128)(2,1)S(1)}, bf16[1168,384]{1,0:T(8,128)(2,1)S(1)}, u32[]{:S(2)}, u32[]{:S(2)}) collective-permute-start(bf16[1168,384]{1,0:T(8,128)(2,1)S(1)} %collective-permute-done.2.refs_17_.refs_20_.refs_21_.refs_22_.refs_25_.refs_24_), channel_id=1, source_target_pairs={{0,8},{8,0},{16,24},{24,16},{1,9},{9,1},{17,25},{25,17},{2,10},{10... | collective-permute-start | bytes 2691080 | tf_op jit(solution)/shard_map/ppermute | solution.py:859
  63.8 17.0 %collective-permute-start.13 = (bf16[1168,384]{1,0:T(8,128)(2,1)S(1)}, bf16[1168,384]{1,0:T(8,128)(2,1)S(1)}, u32[]{:S(2)}, u32[]{:S(2)}) collective-permute-start(bf16[1168,384]{1,0:T(8,128)(2,1)S(1)} %collective-permute-done.4.refs_3_.refs_6_.refs_7_.refs_8_.refs_11_.refs_10_), channel_id=1, source_target_pairs={{0,8},{8,0},{16,24},{24,16},{1,9},{9,1},{17,25},{25,17},{2,10},{10... | collective-permute-start | bytes 2691080 | tf_op jit(solution)/shard_map/ppermute | solution.py:859
  64.3 23.7 %collective-permute-start.9 = (bf16[1168,384]{1,0:T(8,128)(2,1)S(1)}, bf16[1168,384]{1,0:T(8,128)(2,1)}, u32[]{:S(2)}, u32[]{:S(2)}) collective-permute-start(bf16[1168,384]{1,0:T(8,128)(2,1)S(1)} %collective-permute-done.4.refs_3_.refs_6_.refs_7_.refs_8_.refs_11_.refs_10_), channel_id=1, source_target_pairs={{0,2},{1,3},{2,4},{3,5},{4,6},{5,7},{6,0},{7,1},{8,10},{9,11},{10,... | collective-permute-start | bytes 2691080 | tf_op jit(solution)/shard_map/ppermute | solution.py:865
  88.0 21.2 %collective-permute-start.14 = (bf16[1168,384]{1,0:T(8,128)(2,1)}, bf16[1168,384]{1,0:T(8,128)(2,1)S(1)}, u32[]{:S(2)}, u32[]{:S(2)}) collective-permute-start(bf16[1168,384]{1,0:T(8,128)(2,1)} %collective-permute-done.9.refs_4_.refs_7_.refs_8_.refs_9_.refs_12_.refs_11_), channel_id=1, source_target_pairs={{0,1},{1,0},{2,3},{3,2},{4,5},{5,4},{6,7},{7,6},{8,9},{9,8},{10,11... | collective-permute-start | bytes 2691080 | tf_op jit(solution)/shard_map/ppermute | solution.py:862
  88.5 21.0 %collective-permute-start.15 = (bf16[1168,384]{1,0:T(8,128)(2,1)}, bf16[1168,384]{1,0:T(8,128)(2,1)}, u32[]{:S(2)}, u32[]{:S(2)}) collective-permute-start(bf16[1168,384]{1,0:T(8,128)(2,1)} %collective-permute-done.9.refs_4_.refs_7_.refs_8_.refs_9_.refs_12_.refs_11_), channel_id=1, source_target_pairs={{0,16},{8,24},{16,0},{24,8},{1,17},{9,25},{17,1},{25,9},{2,18},{10... | collective-permute-start | bytes 2691080 | tf_op jit(solution)/shard_map/ppermute | solution.py:856
  89.3 22.2 %collective-permute-start.16 = (bf16[1168,384]{1,0:T(8,128)(2,1)S(1)}, bf16[1168,384]{1,0:T(8,128)(2,1)S(1)}, u32[]{:S(2)}, u32[]{:S(2)}) collective-permute-start(bf16[1168,384]{1,0:T(8,128)(2,1)S(1)} %collective-permute-done.11.refs_21_.refs_24_.refs_25_.refs_26_.refs_29_.refs_28_), channel_id=1, source_target_pairs={{0,2},{1,3},{2,4},{3,5},{4,6},{5,7},{6,0},{7,1},{8,10},{9,11},{10,... | collective-permute-start | bytes 2691080 | tf_op jit(solution)/shard_map/ppermute | solution.py:865
  89.3 22.2 %collective-permute-start.17 = (bf16[1168,384]{1,0:T(8,128)(2,1)S(1)}, bf16[1168,384]{1,0:T(8,128)(2,1)S(1)}, u32[]{:S(2)}, u32[]{:S(2)}) collective-permute-start(bf16[1168,384]{1,0:T(8,128)(2,1)S(1)} %collective-permute-done.5.refs_6_.refs_9_.refs_10_.refs_11_.refs_14_.refs_13_), channel_id=1, source_target_pairs={{0,8},{8,0},{16,24},{24,16},{1,9},{9,1},{17,25},{25,17},{2,10},{10... | collective-permute-start | bytes 2691080 | tf_op jit(solution)/shard_map/ppermute | solution.py:859
  89.3 22.2 %collective-permute-start.18 = (bf16[1168,384]{1,0:T(8,128)(2,1)S(1)}, bf16[1168,384]{1,0:T(8,128)(2,1)S(1)}, u32[]{:S(2)}, u32[]{:S(2)}) collective-permute-start(bf16[1168,384]{1,0:T(8,128)(2,1)S(1)} %collective-permute-done.6.refs_18_.refs_21_.refs_22_.refs_23_.refs_26_.refs_25_), channel_id=1, source_target_pairs={{0,8},{8,0},{16,24},{24,16},{1,9},{9,1},{17,25},{25,17},{2,10},{10... | collective-permute-start | bytes 2691080 | tf_op jit(solution)/shard_map/ppermute | solution.py:859
  112.1 23.8 %collective-permute-start.21 = (bf16[1168,384]{1,0:T(8,128)(2,1)S(1)}, bf16[1168,384]{1,0:T(8,128)(2,1)}, u32[]{:S(2)}, u32[]{:S(2)}) collective-permute-start(bf16[1168,384]{1,0:T(8,128)(2,1)S(1)} %collective-permute-done.6.refs_18_.refs_21_.refs_22_.refs_23_.refs_26_.refs_25_), channel_id=1, source_target_pairs={{0,2},{1,3},{2,4},{3,5},{4,6},{5,7},{6,0},{7,1},{8,10},{9,11},{10,... | collective-permute-start | bytes 2691080 | tf_op jit(solution)/shard_map/ppermute | solution.py:865
  112.1 23.8 %collective-permute-start.22 = (bf16[1168,384]{1,0:T(8,128)(2,1)}, bf16[1168,384]{1,0:T(8,128)(2,1)}, u32[]{:S(2)}, u32[]{:S(2)}) collective-permute-start(bf16[1168,384]{1,0:T(8,128)(2,1)} %collective-permute-done.15.refs_20_.refs_23_.refs_24_.refs_25_.refs_28_.refs_27_), channel_id=1, source_target_pairs={{0,1},{1,0},{2,3},{3,2},{4,5},{5,4},{6,7},{7,6},{8,9},{9,8},{10,11... | collective-permute-start | bytes 2691080 | tf_op jit(solution)/shard_map/ppermute | solution.py:862
  113.5 22.4 %collective-permute-start.23 = (bf16[1168,384]{1,0:T(8,128)(2,1)}, bf16[1168,384]{1,0:T(8,128)(2,1)}, u32[]{:S(2)}, u32[]{:S(2)}) collective-permute-start(bf16[1168,384]{1,0:T(8,128)(2,1)} %collective-permute-done.10.refs_7_.refs_10_.refs_11_.refs_12_.refs_15_.refs_14_), channel_id=1, source_target_pairs={{0,16},{8,24},{16,0},{24,8},{1,17},{9,25},{17,1},{25,9},{2,18},{10... | collective-permute-start | bytes 2691080 | tf_op jit(solution)/shard_map/ppermute | solution.py:856
  266.3 36.0 %collective-permute-start.31 = (bf16[4,2,768,384]{3,2,1,0:T(8,128)(2,1)}, bf16[4,2,768,384]{3,2,1,0:T(8,128)(2,1)}, u32[]{:S(2)}, u32[]{:S(2)}) collective-permute-start(bf16[4,2,768,384]{3,2,1,0:T(8,128)(2,1)} %bitcast.309), channel_id=1, source_target_pairs={{0,8},{8,0},{16,24},{24,16},{1,9},{9,1},{17,25},{25,17},{2,10},{10... | collective-permute-start | bytes 14155784 | tf_op jit(solution)/shard_map/ppermute | solution.py:859
  312.9 22.0 %collective-permute-start.33 = (bf16[2,2,112,768]{3,2,0,1:T(8,128)(2,1)S(1)}, bf16[2,2,112,768]{3,2,0,1:T(8,128)(2,1)S(1)}, u32[]{:S(2)}, u32[]{:S(2)}) collective-permute-start(bf16[2,2,112,768]{3,2,0,1:T(8,128)(2,1)S(1)} %get-tuple-element.203), channel_id=1, source_target_pairs={{0,16},{8,24},{16,0},{24,8},{1,17},{9,25},{17,1},{25,9},{2,18},{10... | collective-permute-start | bytes 2064392 | tf_op jit(solution)/shard_map/ppermute | solution.py:856
  334.9 23.8 %collective-permute-start.34 = (bf16[4,2,384,384]{3,2,1,0:T(8,128)(2,1)}, bf16[4,2,384,384]{3,2,1,0:T(8,128)(2,1)}, u32[]{:S(2)}, u32[]{:S(2)}) collective-permute-start(bf16[4,2,384,384]{3,2,1,0:T(8,128)(2,1)} %bitcast.310), channel_id=1, source_target_pairs={{0,8},{8,0},{16,24},{24,16},{1,9},{9,1},{17,25},{25,17},{2,10},{10... | collective-permute-start | bytes 7077896 | tf_op jit(solution)/shard_map/ppermute | solution.py:859
  337.5 20.3 %collective-permute-start.35 = (bf16[2,2,112,768]{3,2,0,1:T(8,128)(2,1)S(1)}, bf16[2,2,112,768]{3,2,0,1:T(8,128)(2,1)S(1)}, u32[]{:S(2)}, u32[]{:S(2)}) collective-permute-start(bf16[2,2,112,768]{3,2,0,1:T(8,128)(2,1)S(1)} %get-tuple-element.215), channel_id=1, source_target_pairs={{0,16},{8,24},{16,0},{24,8},{1,17},{9,25},{17,1},{25,9},{2,18},{10... | collective-permute-start | bytes 2064392 | tf_op jit(solution)/shard_map/ppermute | solution.py:856
  375.5 33.3 %collective-permute-start.38 = (bf16[4,112,768]{2,1,0:T(8,128)(2,1)}, bf16[4,112,768]{2,1,0:T(8,128)(2,1)}, u32[]{:S(2)}, u32[]{:S(2)}) collective-permute-start(bf16[4,112,768]{2,1,0:T(8,128)(2,1)} %fusion.21), channel_id=1, source_target_pairs={{0,1},{1,0},{2,3},{3,2},{4,5},{5,4},{6,7},{7,6},{8,9},{9,8},{10,11... | collective-permute-start | bytes 2064392 | tf_op jit(solution)/shard_map/ppermute | solution.py:862
  376.9 29.0 %collective-permute-start.37 = (bf16[768,384]{1,0:T(8,128)(2,1)}, bf16[768,384]{1,0:T(8,128)(2,1)}, u32[]{:S(2)}, u32[]{:S(2)}) collective-permute-start(bf16[768,384]{1,0:T(8,128)(2,1)} %get-tuple-element.229), channel_id=1, source_target_pairs={{0,1},{1,0},{2,3},{3,2},{4,5},{5,4},{6,7},{7,6},{8,9},{9,8},{10,11... | collective-permute-start | bytes 1769480 | tf_op jit(solution)/shard_map/ppermute | solution.py:862
  377.5 34.5 %collective-permute-start.39 = (bf16[768,384]{1,0:T(8,128)(2,1)}, bf16[768,384]{1,0:T(8,128)(2,1)}, u32[]{:S(2)}, u32[]{:S(2)}) collective-permute-start(bf16[768,384]{1,0:T(8,128)(2,1)} %get-tuple-element.228), channel_id=1, source_target_pairs={{0,2},{1,3},{2,4},{3,5},{4,6},{5,7},{6,0},{7,1},{8,10},{9,11},{10,... | collective-permute-start | bytes 1769480 | tf_op jit(solution)/shard_map/ppermute | solution.py:865
  379.5 32.5 %collective-permute-start.40 = (bf16[768,384]{1,0:T(8,128)(2,1)}, bf16[768,384]{1,0:T(8,128)(2,1)}, u32[]{:S(2)}, u32[]{:S(2)}) collective-permute-start(bf16[768,384]{1,0:T(8,128)(2,1)} %get-tuple-element.230), channel_id=1, source_target_pairs={{0,16},{8,24},{16,0},{24,8},{1,17},{9,25},{17,1},{25,9},{2,18},{10... | collective-permute-start | bytes 1769480 | tf_op jit(solution)/shard_map/ppermute | solution.py:856
  411.9 25.3 %collective-permute-start.41 = (bf16[4,2,384,384]{3,2,1,0:T(8,128)(2,1)}, bf16[4,2,384,384]{3,2,1,0:T(8,128)(2,1)}, u32[]{:S(2)}, u32[]{:S(2)}) collective-permute-start(bf16[4,2,384,384]{3,2,1,0:T(8,128)(2,1)} %bitcast.42), channel_id=1, source_target_pairs={{0,8},{8,0},{16,24},{24,16},{1,9},{9,1},{17,25},{25,17},{2,10},{10... | collective-permute-start | bytes 7077896 | tf_op jit(solution)/shard_map/ppermute | solution.py:859
  412.0 15.8 %collective-permute-start.42 = (bf16[768,384]{1,0:T(8,128)(2,1)S(1)}, bf16[768,384]{1,0:T(8,128)(2,1)}, u32[]{:S(2)}, u32[]{:S(2)}) collective-permute-start(bf16[768,384]{1,0:T(8,128)(2,1)S(1)} %copy-done.32), channel_id=1, source_target_pairs={{0,1},{1,0},{2,3},{3,2},{4,5},{5,4},{6,7},{7,6},{8,9},{9,8},{10,11... | collective-permute-start | bytes 1769480 | tf_op jit(solution)/shard_map/ppermute | solution.py:862
  413.5 15.7 %collective-permute-start.43 = (bf16[768,384]{1,0:T(8,128)(2,1)}, bf16[768,384]{1,0:T(8,128)(2,1)}, u32[]{:S(2)}, u32[]{:S(2)}) collective-permute-start(bf16[768,384]{1,0:T(8,128)(2,1)} %fusion.20), channel_id=1, source_target_pairs={{0,16},{8,24},{16,0},{24,8},{1,17},{9,25},{17,1},{25,9},{2,18},{10... | collective-permute-start | bytes 1769480 | tf_op jit(solution)/shard_map/ppermute | solution.py:856
  414.1 18.1 %collective-permute-start.44 = (bf16[768,384]{1,0:T(8,128)(2,1)S(1)}, bf16[768,384]{1,0:T(8,128)(2,1)}, u32[]{:S(2)}, u32[]{:S(2)}) collective-permute-start(bf16[768,384]{1,0:T(8,128)(2,1)S(1)} %copy-done.31), channel_id=1, source_target_pairs={{0,2},{1,3},{2,4},{3,5},{4,6},{5,7},{6,0},{7,1},{8,10},{9,11},{10,... | collective-permute-start | bytes 1769480 | tf_op jit(solution)/shard_map/ppermute | solution.py:865
  418.5 23.5 %collective-permute-start.45 = (bf16[112,768]{1,0:T(8,128)(2,1)}, bf16[112,768]{1,0:T(8,128)(2,1)S(1)}, u32[]{:S(2)}, u32[]{:S(2)}) collective-permute-start(bf16[112,768]{1,0:T(8,128)(2,1)} %fusion.52), channel_id=1, source_target_pairs={{0,2},{1,3},{2,4},{3,5},{4,6},{5,7},{6,0},{7,1},{8,10},{9,11},{10,... | collective-permute-start | bytes 516104 | tf_op jit(solution)/shard_map/ppermute | solution.py:865
  443.6 18.0 %collective-permute-start.46 = (bf16[768,384]{1,0:T(8,128)(2,1)S(1)}, bf16[768,384]{1,0:T(8,128)(2,1)S(1)}, u32[]{:S(2)}, u32[]{:S(2)}) collective-permute-start(bf16[768,384]{1,0:T(8,128)(2,1)S(1)} %get-tuple-element.249), channel_id=1, source_target_pairs={{0,2},{1,3},{2,4},{3,5},{4,6},{5,7},{6,0},{7,1},{8,10},{9,11},{10,... | collective-permute-start | bytes 1769480 | tf_op jit(solution)/shard_map/ppermute | solution.py:865
  443.8 20.4 %collective-permute-start.47 = (bf16[768,384]{1,0:T(8,128)(2,1)S(1)}, bf16[768,384]{1,0:T(8,128)(2,1)S(1)}, u32[]{:S(2)}, u32[]{:S(2)}) collective-permute-start(bf16[768,384]{1,0:T(8,128)(2,1)S(1)} %get-tuple-element.250), channel_id=1, source_target_pairs={{0,1},{1,0},{2,3},{3,2},{4,5},{5,4},{6,7},{7,6},{8,9},{9,8},{10,11... | collective-permute-start | bytes 1769480 | tf_op jit(solution)/shard_map/ppermute | solution.py:862
  444.4 19.8 %collective-permute-start.50 = (bf16[768,384]{1,0:T(8,128)(2,1)S(1)}, bf16[768,384]{1,0:T(8,128)(2,1)S(1)}, u32[]{:S(2)}, u32[]{:S(2)}) collective-permute-start(bf16[768,384]{1,0:T(8,128)(2,1)S(1)} %get-tuple-element.253), channel_id=1, source_target_pairs={{0,16},{8,24},{16,0},{24,8},{1,17},{9,25},{17,1},{25,9},{2,18},{10... | collective-permute-start | bytes 1769480 | tf_op jit(solution)/shard_map/ppermute | solution.py:856
  445.9 21.7 %collective-permute-start.51 = (bf16[384,384]{1,0:T(8,128)(2,1)S(1)}, bf16[384,384]{1,0:T(8,128)(2,1)S(1)}, u32[]{:S(2)}, u32[]{:S(2)}) collective-permute-start(bf16[384,384]{1,0:T(8,128)(2,1)S(1)} %get-tuple-element.254), channel_id=1, source_target_pairs={{0,2},{1,3},{2,4},{3,5},{4,6},{5,7},{6,0},{7,1},{8,10},{9,11},{10,... | collective-permute-start | bytes 884744 | tf_op jit(solution)/shard_map/ppermute | solution.py:865
  452.0 15.6 %collective-permute-start.52 = (bf16[384,384]{1,0:T(8,128)(2,1)S(1)}, bf16[384,384]{1,0:T(8,128)(2,1)S(1)}, u32[]{:S(2)}, u32[]{:S(2)}) collective-permute-start(bf16[384,384]{1,0:T(8,128)(2,1)S(1)} %get-tuple-element.255), channel_id=1, source_target_pairs={{0,16},{8,24},{16,0},{24,8},{1,17},{9,25},{17,1},{25,9},{2,18},{10... | collective-permute-start | bytes 884744 | tf_op jit(solution)/shard_map/ppermute | solution.py:856
  471.3 22.0 %collective-permute-start.53 = (bf16[768,384]{1,0:T(8,128)(2,1)S(1)}, bf16[768,384]{1,0:T(8,128)(2,1)S(1)}, u32[]{:S(2)}, u32[]{:S(2)}) collective-permute-start(bf16[768,384]{1,0:T(8,128)(2,1)S(1)} %get-tuple-element.256), channel_id=1, source_target_pairs={{0,2},{1,3},{2,4},{3,5},{4,6},{5,7},{6,0},{7,1},{8,10},{9,11},{10,... | collective-permute-start | bytes 1769480 | tf_op jit(solution)/shard_map/ppermute | solution.py:865
  474.1 19.2 %collective-permute-start.54 = (bf16[768,384]{1,0:T(8,128)(2,1)S(1)}, bf16[768,384]{1,0:T(8,128)(2,1)S(1)}, u32[]{:S(2)}, u32[]{:S(2)}) collective-permute-start(bf16[768,384]{1,0:T(8,128)(2,1)S(1)} %copy-done.30), channel_id=1, source_target_pairs={{0,1},{1,0},{2,3},{3,2},{4,5},{5,4},{6,7},{7,6},{8,9},{9,8},{10,11... | collective-permute-start | bytes 1769480 | tf_op jit(solution)/shard_map/ppermute | solution.py:862
  477.6 15.7 %collective-permute-start.55 = (bf16[768,384]{1,0:T(8,128)(2,1)S(1)}, bf16[768,384]{1,0:T(8,128)(2,1)S(1)}, u32[]{:S(2)}, u32[]{:S(2)}) collective-permute-start(bf16[768,384]{1,0:T(8,128)(2,1)S(1)} %get-tuple-element.258), channel_id=1, source_target_pairs={{0,16},{8,24},{16,0},{24,8},{1,17},{9,25},{17,1},{25,9},{2,18},{10... | collective-permute-start | bytes 1769480 | tf_op jit(solution)/shard_map/ppermute | solution.py:856
  500.3 17.1 %collective-permute-start.63 = (bf16[768,384]{1,0:T(8,128)(2,1)}, bf16[768,384]{1,0:T(8,128)(2,1)S(1)}, u32[]{:S(2)}, u32[]{:S(2)}) collective-permute-start(bf16[768,384]{1,0:T(8,128)(2,1)} %fusion.19), channel_id=1, source_target_pairs={{0,2},{1,3},{2,4},{3,5},{4,6},{5,7},{6,0},{7,1},{8,10},{9,11},{10,... | collective-permute-start | bytes 1769480 | tf_op jit(solution)/shard_map/ppermute | solution.py:865
  500.4 17.6 %collective-permute-start.64 = (bf16[768,384]{1,0:T(8,128)(2,1)S(1)}, bf16[768,384]{1,0:T(8,128)(2,1)S(1)}, u32[]{:S(2)}, u32[]{:S(2)}) collective-permute-start(bf16[768,384]{1,0:T(8,128)(2,1)S(1)} %get-tuple-element.267), channel_id=1, source_target_pairs={{0,1},{1,0},{2,3},{3,2},{4,5},{5,4},{6,7},{7,6},{8,9},{9,8},{10,11... | collective-permute-start | bytes 1769480 | tf_op jit(solution)/shard_map/ppermute | solution.py:862
  521.5 14.4 %collective-permute-start.70 = (bf16[112,768]{1,0:T(8,128)(2,1)}, bf16[112,768]{1,0:T(8,128)(2,1)}, u32[]{:S(2)}, u32[]{:S(2)}) collective-permute-start(bf16[112,768]{1,0:T(8,128)(2,1)} %fusion.44), channel_id=1, source_target_pairs={{0,2},{1,3},{2,4},{3,5},{4,6},{5,7},{6,0},{7,1},{8,10},{9,11},{10,... | collective-permute-start | bytes 516104 | tf_op jit(solution)/shard_map/ppermute | solution.py:865
  521.5 15.5 %collective-permute-start.67 = (bf16[384,384]{1,0:T(8,128)(2,1)}, bf16[384,384]{1,0:T(8,128)(2,1)}, u32[]{:S(2)}, u32[]{:S(2)}) collective-permute-start(bf16[384,384]{1,0:T(8,128)(2,1)} %get-tuple-element.270), channel_id=1, source_target_pairs={{0,2},{1,3},{2,4},{3,5},{4,6},{5,7},{6,0},{7,1},{8,10},{9,11},{10,... | collective-permute-start | bytes 884744 | tf_op jit(solution)/shard_map/ppermute | solution.py:865
  (96 other events, 1728.0 us)
Sparse Core Ops, SparseCore 0:
  136.1 65.9 all-gather.1

commit v5 on v4

--- a/solution.py
+++ b/solution.py
@@ -158,16 +158,16 @@
     return jnp.where(first, a[:rows], a[rows:])
 
 
-def softmax(scores, mask):
+def softmax(scores, mask, axis):
     scores = scores + mask
-    e = jnp.exp(scores - jnp.max(scores, axis=-1, keepdims=True))
-    return (e * (1.0 / jnp.sum(e, axis=-1, keepdims=True))).astype(BF)
+    e = jnp.exp(scores - jnp.max(scores, axis=axis, keepdims=True))
+    return (e * (1.0 / jnp.sum(e, axis=axis, keepdims=True))).astype(BF)
 
 
 def score_back(weights, d_weights):
     a = weights.astype(F32)
     t = a * d_weights
-    return (t - a * jnp.sum(t, axis=-1, keepdims=True)).astype(BF)
+    return (t - a * jnp.sum(t, axis=0, keepdims=True)).astype(BF)
 
 
 def project_and_norm(x_ref, o_ref, w_ref, dims, bias, gain, offset, outs):
@@ -205,22 +205,21 @@
     tiles(3 * width // TILE, tile)
     io.send(p_ref)
     pairs = width // 128
-    row = lax.broadcasted_iota(jnp.int32, (256, 128), 0)
-    lane = lax.broadcasted_iota(jnp.int32, (256, 128), 1)
-    same = ((row // 64) % 2) == (lane // 64)
-    key_lane = lax.broadcasted_iota(jnp.int32, (1, 128), 1)
+    key = lax.broadcasted_iota(jnp.int32, (128, 256), 0)
+    query = lax.broadcasted_iota(jnp.int32, (128, 256), 1)
+    same = ((query // 64) % 2) == (key // 64)
 
     def attend(s):
         rows = span(s * 128, 128)
-        length = jnp.where(key_lane < 64, lengths[2 * s], lengths[2 * s + 1])
-        mask = jnp.where(same & (lax.rem(key_lane, 64) < length), 0.0, MASKED)
+        length = jnp.where(key < 64, lengths[2 * s], lengths[2 * s + 1])
+        mask = jnp.where(same & (lax.rem(key, 64) < length), 0.0, MASKED)
         for h in range(pairs):
             q = p_ref[rows, pl.ds(h * 128, 128)]
             k = p_ref[rows, pl.ds(width + h * 128, 128)]
             v = p_ref[rows, pl.ds(2 * width + h * 128, 128)]
-            a = softmax(dot(split_heads(q * 0.125), k, NT), mask)
+            a = softmax(dot(k, split_heads(q * 0.125), NT), mask, 0)
             a_ref[s * pairs + h] = a
-            o_ref[rows, pl.ds(h * 128, 128)] = join_heads(dot(a, v)).astype(BF)
+            o_ref[rows, pl.ds(h * 128, 128)] = join_heads(dot(a, v, TN)).astype(BF)
 
     tiles(x_ref.shape[0] // 128, attend)
     io.send(a_ref, o_ref)
@@ -233,7 +232,7 @@
 def self_backward_kernel(count, layer, io, ins, outs, scratch):
     where_ref, dy_ref, x_ref, vec_ref, p_ref, a_ref, o_ref, n_ref, r_ref, *refs = ins
     dx_ref, own_ref, other_ref, gv_ref = outs
-    qkv, out, db_ref, dmix_ref, dp_ref, rel_ref, g_ref, sems, sems2 = scratch
+    qkv, out, du_ref, db_ref, dmix_ref, dp_ref, rel_ref, g_ref, sems, sems2 = scratch
     width = x_ref.shape[1]
     half = width // 2
     n, m = qkv.shape[0] // 8, out.shape[0] // 8
@@ -242,7 +241,7 @@
     second = fetch(placed(refs[1:] if whole else refs, where_ref, [(n, m, 0)], out, half), sems2, here)
     io.begin(o_ref, p_ref, a_ref)
     core = where_ref[0]
-    g_gain, g_offset, g_bias = norm_rows_back(dy_ref, n_ref, r_ref, vec_ref[3:4, :], dx_ref, db_ref)
+    g_gain, g_offset, g_bias = norm_rows_back(dy_ref, n_ref, r_ref, vec_ref[3:4, :], du_ref, db_ref)
     settle(second)
 
     def mix(j):
@@ -271,10 +270,10 @@
             v = p_ref[rows, pl.ds(2 * width + h * 128, 128)]
             do2 = split_heads(dmix_ref[rows, pl.ds(h * 128, 128)])
             a = a_ref[s * pairs + h]
-            ds = score_back(a, dot(do2, v, NT))
-            dp_ref[rows, pl.ds(h * 128, 128)] = (join_heads(dot(ds, k)) * 0.125).astype(BF)
-            dp_ref[rows, pl.ds(width + h * 128, 128)] = (dot(ds, q2, TN) * 0.125).astype(BF)
-            dp_ref[rows, pl.ds(2 * width + h * 128, 128)] = dot(a, do2, TN).astype(BF)
+            ds = score_back(a, dot(v, do2, NT))
+            dp_ref[rows, pl.ds(h * 128, 128)] = (join_heads(dot(ds, k, TN)) * 0.125).astype(BF)
+            dp_ref[rows, pl.ds(width + h * 128, 128)] = (dot(ds, q2) * 0.125).astype(BF)
+            dp_ref[rows, pl.ds(2 * width + h * 128, 128)] = dot(a, do2).astype(BF)
 
     tiles(x_ref.shape[0] // 128, attend)
     io.need(x_ref)
@@ -295,7 +294,7 @@
 
     def back(j):
         cols = span(j * TILE, TILE)
-        dx_ref[:, cols] += dot(dp_ref[...], qkv[:, cols])
+        dx_ref[:, cols] = (du_ref[:, cols] + dot(dp_ref[...], qkv[:, cols])).astype(dx_ref.dtype)
 
     tiles(width // TILE, back)
     gv_ref[0:1, :] = jnp.sum(dp_ref[:, :width].astype(F32), axis=0, keepdims=True)
@@ -329,8 +328,8 @@
             q = q_ref[rows, pl.ds(h * 128, 128)]
             k = k_ref[keys, pl.ds(h * 128, 128)]
             v = v_ref[keys, pl.ds(h * 128, 128)]
-            a = softmax(dot(split_heads(q * 0.125), k, NT), mask)
-            a_ref[s * pairs + h] = a
+            a = softmax(dot(split_heads(q * 0.125), k, NT), mask, 1)
+            a_ref[s * pairs + h] = a.T
             o_ref[rows, pl.ds(h * 128, 128)] = join_heads(dot(a, v)).astype(BF)
 
     tiles(keep_ref.shape[0], attend)
@@ -346,7 +345,7 @@
     dx_ref, dk_ref, dv_ref, gq_ref, go_ref, gv_ref = outs
     db_ref, dmix_ref, dq_ref = scratch
     width = low_x_ref.shape[1]
-    patches = a_ref.shape[2]
+    patches = a_ref.shape[1]
     io.begin(wo_ref, o_ref)
     g_gain, g_offset, g_bias = norm_rows_back(dy_ref, n_ref, r_ref, vec_ref[3:4, :], dx_ref, db_ref)
 
@@ -372,10 +371,10 @@
             v = v_ref[keys, pl.ds(h * 128, 128)]
             do2 = split_heads(dmix_ref[rows, pl.ds(h * 128, 128)])
             a = a_ref[s * pairs + h]
-            ds = score_back(a, dot(do2, v, NT))
-            dq_ref[rows, pl.ds(h * 128, 128)] = (join_heads(dot(ds, k)) * 0.125).astype(BF)
-            dk_ref[keys, pl.ds(h * 128, 128)] = (dot(ds, q2, TN) * 0.125).astype(BF)
-            dv_ref[keys, pl.ds(h * 128, 128)] = dot(a, do2, TN).astype(BF)
+            ds = score_back(a, dot(v, do2, NT))
+            dq_ref[rows, pl.ds(h * 128, 128)] = (join_heads(dot(ds, k, TN)) * 0.125).astype(BF)
+            dk_ref[keys, pl.ds(h * 128, 128)] = (dot(ds, q2) * 0.125).astype(BF)
+            dv_ref[keys, pl.ds(h * 128, 128)] = dot(a, do2).astype(BF)
 
     tiles(a_ref.shape[0] // pairs, attend)
     io.send(dk_ref, dv_ref)
@@ -559,34 +558,40 @@
 ANYWHERE = pl.BlockSpec(memory_space=pl.ANY)
 
 
-def call(kernel, outs, specs, scratch, us, args, late=(), early=()):
+def call(kernel, outs, specs, scratch, us, args, late=(), early=(), packs=(), layer=0, onto=None):
     n_in, n_out, n_scratch = len(args), len(outs), len(scratch)
+    early = (*early, *packs)
     held = [pltpu.VMEM(args[i].shape, args[i].dtype) for i in late]
     held += [pltpu.VMEM(outs[i].shape, outs[i].dtype) for i in early]
+    outs = [struct(2, *o.shape, dtype=o.dtype) if i in packs else o for i, o in enumerate(outs)]
+    taken = tuple(onto) if onto else ()
+    n_all = n_in + len(taken)
 
     def body(*refs):
-        ins, out, rest = list(refs[:n_in]), list(refs[n_in : n_in + n_out]), refs[n_in + n_out :]
+        ins, out, rest = list(refs[:n_in]), list(refs[n_all : n_all + n_out]), refs[n_all + n_out :]
         buffers = rest[n_scratch:-1]
         io = Copies(rest[-1])
         for k, i in enumerate(late):
             io.coming.append((buffers[k], ins[i], None))
             ins[i] = buffers[k]
         for k, i in enumerate(early, len(late)):
-            io.going.append((buffers[k], out[i]))
+            target = out[i].at[lax.rem(ins[0][3] + layer, 2)] if i in packs else out[i]
+            io.going.append((buffers[k], target))
             out[i] = buffers[k]
         kernel(io, ins, out, rest[:n_scratch])
         io.finish()
 
-    specs = [ANYWHERE if i in late else spec for i, spec in enumerate(specs)]
+    specs = [ANYWHERE if i in late else spec for i, spec in enumerate(specs)] + [ANYWHERE] * len(taken)
     return pl.pallas_call(
         body,
         out_shape=outs,
         in_specs=specs,
         out_specs=[ANYWHERE if i in early else VMEM for i in range(n_out)],
         scratch_shapes=[*scratch, *held, pltpu.SemaphoreType.DMA((24,))],
+        input_output_aliases={n_in + k: i for k, i in enumerate(packs)} if taken else {},
         cost_estimate=pl.CostEstimate(flops=int(us * 1.1e9), bytes_accessed=int(us * 3.5e6), transcendentals=0),
         compiler_params=pltpu.CompilerParams(vmem_limit_bytes=VMEM_BYTES),
-    )(*args)
+    )(*args, *taken)
 
 
 def gathered_vectors(pieces, where, first, v_rows, v_lanes, x_rows, c_rows):
@@ -611,7 +616,7 @@
     count = len(weights)
     outs = [
         struct(rows, 3 * width, dtype=BF),
-        struct(blocks, 256, 128, dtype=BF),
+        struct(blocks, 128, 256, dtype=BF),
         struct(rows, width, dtype=BF),
         struct(rows, width),
         struct(rows, width, dtype=BF),
@@ -637,13 +642,13 @@
     return y, low, (x, p, a, o, n, r)
 
 
-def self_backward(dy, saved, where, vec, weights, layer):
+def self_backward(dy, saved, where, vec, weights, layer, dtype=F32, onto=None):
     x, p, a, o, n, r = saved
     rows, width = x.shape
     half = width // 2
     count = len(weights)
     outs = [
-        struct(rows, width),
+        struct(rows, width, dtype=dtype),
         struct(8, width // 2, half, dtype=BF),
         struct(8, width // 2, half, dtype=BF),
         struct(8, width),
@@ -651,6 +656,7 @@
     scratch = [
         pltpu.VMEM((3 * width, width), BF),
         pltpu.VMEM((width, width), BF),
+        pltpu.VMEM((rows, width), F32),
         pltpu.VMEM((rows, width), BF),
         pltpu.VMEM((rows, width), BF),
         pltpu.VMEM((rows, 3 * width), BF),
@@ -667,7 +673,9 @@
         22,
         (where, dy, x, vec, p, a, o, n, r, *weights),
         late=(6, 4, 5, 2),
-        early=(1, 2),
+        packs=(1, 2),
+        layer=layer,
+        onto=onto,
     )
 
 
@@ -676,7 +684,7 @@
     samples, patches = keep.shape
     outs = [
         struct(rows, width, dtype=BF),
-        struct(samples * (width // 128), 128, patches, dtype=BF),
+        struct(samples * (width // 128), patches, 128, dtype=BF),
         struct(rows, width, dtype=BF),
         struct(rows, width),
         struct(rows, width, dtype=BF),
@@ -751,7 +759,7 @@
     return y, low, (low_x, act, slope, n, r)
 
 
-def feed_backward(dy, saved, where, vec, weights, layer):
+def feed_backward(dy, saved, where, vec, weights, layer, onto=None):
     low_x, act, slope, n, r = saved
     rows, width = low_x.shape
     hidden = act.shape[1]
@@ -781,7 +789,9 @@
         22,
         (where, dy, low_x, vec, act, slope, n, r, *weights),
         late=(5, 4, 2),
-        early=(1, 2),
+        packs=(1, 2),
+        layer=layer,
+        onto=onto,
     )
 
 
@@ -820,7 +830,9 @@
         28,
         (where, x, low_x, vec, bias, dy, *weights),
         late=(1,),
-        early=(0, 2, 3),
+        early=(0,),
+        packs=(2, 3),
+        layer=layer,
     )
 
 
@@ -910,25 +922,21 @@
 
 
 class PairSum:
-    def __init__(self, grid, joining):
-        self.grid, self.packs = grid, [None, self.pack(joining)]
-        self.came, self.got = [None, None], {}
-
-    def pack(self, pair):
-        return [a.reshape((4, 2) + a.shape[1:]) for a in pair]
-
-    def add_text(self, text):
-        self.packs[0] = self.pack(text)
-
-    def c(self, layer):
-        return lambda: [(self.grid.swap_core, self.packs[layer][1], partial(self.came.__setitem__, layer))]
+    def __init__(self, grid, own, other):
+        self.grid, self.other = grid, other
+        self.own = own.reshape((2, 4, 2) + own.shape[2:])
+        self.came, self.got = None, {}
+
+    def c(self):
+        def keep(a):
+            self.came = a.reshape(self.own.shape)
+
+        return [(self.grid.swap_core, self.other, keep)]
 
     def block(self, own, y, z):
-        sums = [p[0][z, y].astype(F32) + c[z, y].astype(F32) for p, c in zip(self.packs, self.came)]
-        total = jnp.where((self.grid.x == 0) == own, *sums)
-        for part in self.got.get((own, y, z), []):
-            total = total + part.astype(F32)
-        return total
+        layer = 0 if own else 1
+        parts = [self.own[layer, z, y], self.came[layer, z, y], *self.got.get((own, y, z), [])]
+        return sum(part.astype(F32) for part in parts)
 
     def move(self, over, own, y, z):
         to = {"z": (own, y, z - 1), "y": (own, 1 - y, z), "x": (True, y, z)}[over]
@@ -1045,8 +1053,11 @@
     direct = (n_pipe, n_dp) == (4, 8) and lanes % 128 == 0
     lengths, patch_keep = masks(caption_len, phrase_len, box_count, patch_mask, text_rows, patches)
     x = text_embed.reshape(-1, width)
-    image = jnp.pad(image_feats, ((0, 0), (0, patches - image_feats.shape[1]), (0, 0)))
-    image = image.reshape(samples * patches, -1)
+
+    def padded(image_feats):
+        wide = jnp.pad(image_feats, ((0, 0), (0, patches - image_feats.shape[1]), (0, 0)))
+        return wide.reshape(samples * patches, -1)
+
 
     c_rows = cross_query.shape[0]
     kv_slices = cross_kv.shape[1] // width
@@ -1074,11 +1085,11 @@
         cvec = blocks.reshape(shards, 16, 128)[:, v_rows : v_rows + x_rows, :c_rows]
         return vecs, [v[8:12].reshape(1, hidden) for v in vecs], jnp.moveaxis(cvec, 1, 0).reshape(x_rows, width)
 
-    def keys_values(wk, wv, cvec):
+    def keys_values(image, wk, wv, cvec):
         keys = jnp.dot(image, wk, preferred_element_type=F32).astype(BF)
         return keys, (jnp.dot(image, wv, preferred_element_type=F32) + cvec[1]).astype(BF)
 
-    def pack_cross(dk, dv, g_cq, g_co):
+    def pack_cross(image, dk, dv, g_cq, g_co):
         grads = [g_cq, g_co, dot(image, dk, TN).astype(BF), dot(image, dv, TN).astype(BF)]
         return jnp.concatenate([g.reshape(shards, -1, width) for g in grads], axis=1)
 
@@ -1101,66 +1112,67 @@
         gather = Gather(grid, jnp.concatenate([pack_attn, pack_feed, pad_to(small, 16, lanes)]))
         get = gather.get
         turn(get(0, 0, 1, "z"), get(0, 1, 0, "y"), get(1, 0, 0, "x"), gather.c2)
-        turn(get(0, 0, 2, "z"), get(0, 1, 1, "y"), get(1, 0, 1, "x"), gather.c2)
+        image = turn(
+            get(0, 0, 2, "z"), get(0, 1, 1, "y"), get(1, 0, 1, "x"), gather.c2, compute=padded, args=(image_feats,)
+        )
         turn(get(0, 0, 3, "z"), get(0, 1, 2, "y"), get(1, 1, 0, "x"), gather.c2)
         turn(get(1, 1, 1, "z"), get(0, 1, 3, "y"), get(1, 0, 3, "x"), gather.c2)
         turn(get(1, 0, 2, "z"), get(1, 1, 3, "y"), get(1, 1, 2, "x"), gather.c2)
         turn(gather.c)
         weights = gather.pieces()
-        cross_whole = lax.all_gather(after(cross_pack, grid.arrived[-2]), everyone, axis=0, tiled=True)
+        cross_whole = lax.all_gather(after(cross_pack, grid.arrived[-3]), everyone, axis=0, tiled=True)
         *vectors, cvec = gathered_vectors(weights, where, n_pack, v_rows, v_lanes, x_rows, c_rows)
         vecs, biases = vectors[:2], vectors[2:]
         state, low, s_self = self_forward(x, lengths, where, vecs[0], weights, 0)
         state, passed, s_feed = feed_forward(state, low, where, vecs[0], biases[0], weights, 0)
         state, low, s_self2 = self_forward(passed, lengths, where, vecs[1], weights, 1)
         wq, wo, wk, wv = cross_weights(cross_whole)
-        keys, values = keys_values(wk, wv, cvec)
+        keys, values = keys_values(image, wk, wv, cvec)
         state, low, s_cross = cross_forward(state, low, patch_keep, keys, values, cvec, wq, wo)
         joined, grad, *g_feed2, v_feed2, v_up2 = feed_both(state, low, where, vecs[1], biases[1], seed, weights, 1)
         grid.computed = (grad,)
 
-        feed = PairSum(grid, g_feed2)
-
         def fourth(grad):
             grad, dk, dv, g_cq, g_co, v_cross = cross_backward(grad, s_cross, cvec, wq, wo)
-            return grad, v_cross, pack_cross(dk, dv, g_cq, g_co)
-
-        grad, v_cross, cross_grads = turn(feed.c(1), compute=fourth, args=(grad,))
+            return grad, v_cross, pack_cross(image, dk, dv, g_cq, g_co)
+
+        grad, v_cross, cross_grads = fourth(grad)
         sum_cross = BlockSum(grid, cross_grads.reshape(2, 2, 4, 2, -1, width), BF)
         turn(sum_cross.c)
-        grad, *g_self2, v_self2 = turn(
-            sum_cross.x0, compute=lambda grad: self_backward(grad, s_self2, where, vecs[1], weights, 1), args=(grad,)
+        grad, *g_self, v_self2 = turn(
+            sum_cross.x0,
+            compute=lambda grad: self_backward(grad, s_self2, where, vecs[1], weights, 1, BF), args=(grad,),
         )
-        attn = PairSum(grid, g_self2)
-        grad, *g_feed1, v_feed, v_up = turn(
-            attn.c(1), sum_cross.x1,
-            compute=lambda grad: feed_backward(grad, s_feed, where, vecs[0], weights, 0), args=(grad.astype(BF),),
+        grad, *g_feed, v_feed, v_up = turn(
+            sum_cross.x1,
+            compute=lambda grad: feed_backward(grad, s_feed, where, vecs[0], weights, 0, g_feed2), args=(grad,),
         )
-        feed.add_text(g_feed1)
-        f0, f1, f2, f3, f4 = feed.steps()
-        a0, a1, a2, a3, a4 = attn.steps()
-        embed_grad, *g_self1, v_self = turn(
-            *f0, sum_cross.y, pre=(feed.c(0),),
-            compute=lambda grad: self_backward(grad, s_self, where, vecs[0], weights, 0), args=(grad,),
+        feed = PairSum(grid, *g_feed)
+        embed_grad, *g_self, v_self = turn(
+            feed.c, sum_cross.y,
+            compute=lambda grad: self_backward(grad, s_self, where, vecs[0], weights, 0, F32, g_self), args=(grad,),
         )
-        attn.add_text(g_self1)
+        attn = PairSum(grid, *g_self)
         sum_vec = BlockSum(
             grid,
             pack_vectors((v_self, v_feed, v_up), (v_self2, v_feed2, v_up2), v_cross).reshape(2, 2, 4, 2, 16, 128),
             F32,
         )
-        turn(*f1, attn.c(0), sum_cross.round)
-        turn(*f2, *a0, sum_vec.c)
-        turn(*f3, *a1, sum_vec.x)
-        turn(*f4, *a2, sum_vec.y)
-        turn(*a3, sum_cross.round, sum_vec.z)
-        turn(*a4, sum_cross.round)
+        f0, f1, f2, f3, f4 = feed.steps()
+        a0, a1, a2, a3, a4 = attn.steps()
+        turn(*f0, attn.c, sum_cross.round)
+        turn(*f1, *a0, sum_vec.c, sum_cross.round)
+        turn(*f2, *a1, sum_vec.x, sum_cross.round)
+        turn(*f3, *a2, sum_vec.y)
+        turn(*f4, *a3)
+        turn(*a4, sum_vec.z)
         attn_grads, feed_grads = attn.total(), feed.total()
         n_qkv, n_up = attn_qkv.shape[1], ffn_up.shape[1]
         mine = [attn_grads[:n_qkv], attn_grads[n_qkv:], feed_grads[:n_up], feed_grads[n_up:]]
         cross_grads, small = sum_cross.total(), sum_vec.total()
     else:
         where = jnp.zeros((4,), jnp.int32)
+        image = padded(image_feats)
         vectors = lax.all_gather(small, everyone, axis=0, tiled=False)
         whole = lax.all_gather(jnp.concatenate([pack_attn, pack_feed], axis=0), everyone, axis=0, tiled=False)
         whole = whole.reshape(n_pipe, n_dp, -1, lanes)
@@ -1179,13 +1191,15 @@
         state, low, s_self = self_forward(x, lengths, where, vecs[0], [qkv1, out1], 0)
         state, passed, s_feed = feed_forward(state, low, where, vecs[0], biases[0], [up1, down1], 0)
         state, low, s_self2 = self_forward(passed, lengths, where, vecs[1], [qkv2, out2], 1)
-        keys, values = keys_values(wk, wv, cvec)
+        keys, values = keys_values(image, wk, wv, cvec)
         state, low, s_cross = cross_forward(state, low, patch_keep, keys, values, cvec, wq, wo)
         joined, grad, *g_feed2, v_feed2, v_up2 = feed_both(state, low, where, vecs[1], biases[1], seed, [up2, down2], 1)
         grad, dk, dv, g_cq, g_co, v_cross = cross_backward(grad, s_cross, cvec, wq, wo)
-        grad, *g_self2, v_self2 = self_backward(grad, s_self2, where, vecs[1], [qkv2, out2], 1)
-        grad, *g_feed1, v_feed, v_up = feed_backward(grad.astype(BF), s_feed, where, vecs[0], [up1, down1], 0)
-        embed_grad, *g_self1, v_self = self_backward(grad, s_self, where, vecs[0], [qkv1, out1], 0)
+        grad, *g_self, v_self2 = self_backward(grad, s_self2, where, vecs[1], [qkv2, out2], 1, BF)
+        grad, *g_feed, v_feed, v_up = feed_backward(grad, s_feed, where, vecs[0], [up1, down1], 0, g_feed2)
+        embed_grad, *g_self, v_self = self_backward(grad, s_self, where, vecs[0], [qkv1, out1], 0, F32, g_self)
+        g_self1, g_self2 = ([g[k] for g in g_self] for k in range(2))
+        g_feed1, g_feed2 = ([g[k] for g in g_feed] for k in range(2))
 
         def unpack(pair, rows, slices):
             parts = []
@@ -1211,7 +1225,7 @@
         packed = jnp.concatenate(parts, axis=2).reshape(-1, lanes)
         packed = lax.psum_scatter(packed, everyone, scatter_dimension=0, tiled=True).astype(F32)
         mine = [packed[a:b] for a, b in zip(ends[:-1], ends[1:])]
-        cross_grads = pack_cross(dk, dv, g_cq, g_co).reshape(-1, width)
+        cross_grads = pack_cross(image, dk, dv, g_cq, g_co).reshape(-1, width)
         cross_grads = lax.psum_scatter(cross_grads, everyone, scatter_dimension=0, tiled=True).astype(F32)
         small = pack_vectors((v_self, v_feed, v_up), (v_self2, v_feed2, v_up2), v_cross)
         small = lax.psum_scatter(small.reshape(-1, 128), everyone, scatter_dimension=0, tiled=True)

time: 571 us -> 539 us (0.944)
  other arithmetic: 60.3 us -> 43.2 us
  Pallas kernels: 186 us -> 174 us
  starting transfers between devices: 59.7 us -> 51.4 us
    ppermute x21, waiting for transfers between devices: 72.6 us -> 86.6 us  [ring_z(): return lax.ppermute(a, 'dp', [(i, (i + 2 * step) % 8) for i in range(8)])]
    pallas_call x9, Pallas kernels: 183 us -> 171 us  [call(): pl.pallas_call(body, out_shape=outs, in_specs=specs, out_specs=[ANYWHERE...]
    ppermute x21, starting transfers between devices: 16.7 us -> 6.56 us  [ring_z(): return lax.ppermute(a, 'dp', [(i, (i + 2 * step) % 8) for i in range(8)])]
    ppermute x17, waiting for transfers between devices: 78.9 us -> 70.6 us  [swap_y(): return lax.ppermute(a, 'dp', [(i, i ^ 1) for i in range(8)])]
    convert_element_type x12 -> x10, other arithmetic: 35.9 us -> 27.8 us  [ask(): self.block(own, y, z).astype(BF)]
    all_gather x1, waiting for transfers between devices: 6.91 us -> 0.02 us  [on_device(): lax.all_gather(after(cross_pack, grid.arrived[-3]), everyone, axis=0, til...]
    ppermute x18, waiting for transfers between devices: 27.2 us -> 32.9 us  [swap_x(): return lax.ppermute(a, 'pipe', [(i, i ^ 2) for i in range(4)])]
    unnamed x141 -> x104, local copies, waits for them, and re-layouts: 13.9 us -> 15.4 us
  transfers between devices with their start and end apart: 79 -> 77, of which waited for: 40 -> 41; matrix products, arithmetic and copies ran while one was open for 11% -> 7% of each run, Pallas kernels for 24% -> 19%
where the time goes in v5:
time: 539 us; the launch traced here: 531 us
  waiting for transfers between devices  202 us (37%)
  Pallas kernels  174 us (32%)
  starting transfers between devices  51.4 us (10%)
  other arithmetic  43.2 us (8%)
  local copies, waits for them, and re-layouts  31.7 us (6%)
  between operations  15.6 us (3%)
  matrix products  13.3 us (2%)
    pallas_call x9, Pallas kernels, call(): pl.pallas_call(body, out_shape=outs, in_specs=specs, out_specs=[ANYWHERE...  171 us
    ppermute x21, waiting for transfers between devices, ring_z(): return lax.ppermute(a, 'dp', [(i, (i + 2 * step) % 8) for i in range(8)])  86.6 us
    ppermute x17, waiting for transfers between devices, swap_y(): return lax.ppermute(a, 'dp', [(i, i ^ 1) for i in range(8)])  70.6 us
    ppermute x18, waiting for transfers between devices, swap_x(): return lax.ppermute(a, 'pipe', [(i, i ^ 2) for i in range(4)])  32.9 us
    convert_element_type x10, other arithmetic, ask(): self.block(own, y, z).astype(BF)  27.8 us
    ppermute x18, starting transfers between devices, swap_x(): return lax.ppermute(a, 'pipe', [(i, i ^ 2) for i in range(4)])  21.7 us
    ppermute x17, starting transfers between devices, swap_y(): return lax.ppermute(a, 'dp', [(i, i ^ 1) for i in range(8)])  18.9 us
    unnamed x104, local copies, waits for them, and re-layouts  15.4 us
  transfers between devices with their start and end apart: 77, of which 41 were waited for; matrix products, arithmetic and copies ran while one was open for 7% of the time, Pallas kernels for 19%

profile of v5, /device:TPU:0, one launch (start us, length us, event | category | flops | bytes accessed | tf_op | source)
XLA Modules:
  0.0 530.8 jit_solution(17621237411550799544)
XLA Ops:
  15.8 3.0 collective-permute-start.1
  21.9 16.8 %collective-permute-done.1.refs_5_.refs_8_.refs_9_.refs_10_.refs_13_.refs_12_ = bf16[1168,384]{1,0:T(8,128)(2,1)S(1)} collective-permute-done((bf16[1168,384]{1,0:T(8,128)(2,1)S(1)}, bf16[1168,384]{1,0:T(8,128)(2,1)S(1)}, u32[]{:S(2)}, u32[]{:S(2)}) %collective-permute-start.1) | collective-permute-done | bytes 897056 | tf_op jit(solution)/shard_map/ppermute | solution.py:874
  40.2 3.1 collective-permute-done.refs_2_.refs_5_.refs_6_.refs_7_.refs_10_.refs_9_
  46.7 17.0 %collective-permute-done.6.refs_18_.refs_21_.refs_22_.refs_23_.refs_26_.refs_25_ = bf16[1168,384]{1,0:T(8,128)(2,1)} collective-permute-done((bf16[1168,384]{1,0:T(8,128)(2,1)S(1)}, bf16[1168,384]{1,0:T(8,128)(2,1)}, u32[]{:S(2)}, u32[]{:S(2)}) %collective-permute-start.6) | collective-permute-done | bytes 897056 | tf_op jit(solution)/shard_map/ppermute | solution.py:868
  69.5 15.7 %collective-permute-done.10.refs_7_.refs_10_.refs_11_.refs_12_.refs_15_.refs_14_ = bf16[1168,384]{1,0:T(8,128)(2,1)S(1)} collective-permute-done((bf16[1168,384]{1,0:T(8,128)(2,1)S(1)}, bf16[1168,384]{1,0:T(8,128)(2,1)S(1)}, u32[]{:S(2)}, u32[]{:S(2)}) %collective-permute-start.10) | collective-permute-done | bytes 897056 | tf_op jit(solution)/shard_map/ppermute | solution.py:874
  86.1 7.1 %collective-permute-done.9.refs_4_.refs_7_.refs_8_.refs_9_.refs_12_.refs_11_ = bf16[1168,384]{1,0:T(8,128)(2,1)} collective-permute-done((bf16[1168,384]{1,0:T(8,128)(2,1)S(1)}, bf16[1168,384]{1,0:T(8,128)(2,1)}, u32[]{:S(2)}, u32[]{:S(2)}) %collective-permute-start.9) | collective-permute-done | bytes 897056 | tf_op jit(solution)/shard_map/ppermute | solution.py:877
  95.8 18.7 %collective-permute-done.14.refs_8_.refs_11_.refs_12_.refs_13_.refs_16_.refs_15_ = bf16[1168,384]{1,0:T(8,128)(2,1)} collective-permute-done((bf16[1168,384]{1,0:T(8,128)(2,1)}, bf16[1168,384]{1,0:T(8,128)(2,1)}, u32[]{:S(2)}, u32[]{:S(2)}) %collective-permute-start.14) | collective-permute-done | bytes 897056 | tf_op jit(solution)/shard_map/ppermute | solution.py:874
  120.8 24.4 %collective-permute-done.21.refs_19_.refs_22_.refs_23_.refs_24_.refs_27_.refs_26_ = bf16[1168,384]{1,0:T(8,128)(2,1)S(1)} collective-permute-done((bf16[1168,384]{1,0:T(8,128)(2,1)}, bf16[1168,384]{1,0:T(8,128)(2,1)S(1)}, u32[]{:S(2)}, u32[]{:S(2)}) %collective-permute-start.21) | collective-permute-done | bytes 897056 | tf_op jit(solution)/shard_map/ppermute | solution.py:877
  155.8 2.5 shard_map.239
  159.1 12.9 %shard_map.240 = (bf16[512,2304]{1,0:T(8,128)(2,1)}, bf16[24,128,256]{2,1,0:T(8,128)(2,1)}, bf16[512,768]{1,0:T(8,128)(2,1)}, f32[512,768]{1,0:T(8,128)}, bf16[5...) custom-call(s32[8]{0:T(128)} %add_minimum_fusion.refs_0_, s32[4]{0:T(128)} %pad_add_fusion.refs_0_.refs_1_, ...), custom_call_target="tpu_custom_call" | custom-call | flops 15399999488 | bytes 49000000 | tf_op jit(solution)/shard_map/pallas_call | solution.py:585
  172.0 17.8 %shard_map.241 = (bf16[512,3072]{1,0:T(8,128)(2,1)}, bf16[512,3072]{1,0:T(8,128)(2,1)}, f32[512,768]{1,0:T(8,128)}, bf16[512,768]{1,0:T(8,128)(2,1)}, bf16[512,768]{1,0:T(8,128)(2,1)}, /*index=5*/f32[512,1]{1,0:T(8,128)}) custom-call(s32[4]{0:T(128)} %pad_add_fusion.refs_0_.refs_1_, f32[512,768]{1,0:T(8,128)} %get-tuple-element.173.refs_1_, ...), custom_call_target="tpu_custom_call" | custom-call | flops 22000001024 | bytes 70000000 | tf_op jit(solution)/shard_map/pallas_call | solution.py:585
  189.7 12.9 %shard_map.242 = (bf16[512,2304]{1,0:T(8,128)(2,1)}, bf16[24,128,256]{2,1,0:T(8,128)(2,1)}, bf16[512,768]{1,0:T(8,128)(2,1)}, f32[512,768]{1,0:T(8,128)}, bf16[5...) custom-call(s32[8]{0:T(128)} %add_minimum_fusion.refs_0_, s32[4]{0:T(128)} %pad_add_fusion.refs_0_.refs_1_, ...), custom_call_target="tpu_custom_call" | custom-call | flops 15399999488 | bytes 49000000 | tf_op jit(solution)/shard_map/pallas_call | solution.py:585
  204.8 3.2 fusion.58
  208.0 3.5 convolution_convert_fusion.refs_3_.refs_2_
  211.5 3.5 add_convert_fusion.refs_4_.refs_3_
  215.0 20.4 %shard_map.243 = (bf16[512,768]{1,0:T(8,128)(2,1)}, bf16[48,160,128]{2,1,0:T(8,128)(2,1)}, bf16[512,768]{1,0:T(8,128)(2,1)}, f32[512,768]{1,0:T(8,128)}, bf16[51...) custom-call(f32[512,768]{1,0:T(8,128)} %get-tuple-element.178.refs_0_, ...), custom_call_target="tpu_custom_call" | custom-call | flops 23100000256 | bytes 73500000 | tf_op jit(solution)/shard_map/pallas_call | solution.py:585
  235.4 31.1 %shard_map.244 = (f32[512,768]{1,0:T(8,128)}, f32[512,768]{1,0:T(8,128)}, bf16[2,8,768,384]{3,2,1,0:T(8,128)(2,1)}, bf16[2,8,768,384]{3,2,1,0:T(8,128)(2,1)}, f32[8,768]{1,0:T(8,128)}, /*index=5*/f32[1,3072]{1,0:T(1,128)}) custom-call(s32[4]{0:T(128)} %pad_add_fusion.refs_0_.refs_1_, f32[512,768]{1,0:T(8,128)} %get-tuple-element.182.refs_1_, ...), custom_call_target="tpu_custom_call" | custom-call | flops 30799998976 | bytes 98000000 | tf_op jit(solution)/shard_map/pallas_call | solution.py:585
  266.6 20.0 %shard_map.245 = (f32[512,768]{1,0:T(8,128)}, bf16[1280,768]{1,0:T(8,128)(2,1)}, bf16[1280,768]{1,0:T(8,128)(2,1)}, bf16[768,768]{1,0:T(8,128)(2,1)}, bf16[768,768]{1,0:T(8,128)(2,1)}, /*index=5*/f32[8,768]{1,0:T(8,128)}) custom-call(f32[512,768]{1,0:T(8,128)} %get-tuple-element.186.refs_0_, bf16[512,768]{1,0:T(8,128)(2,1)} %get-tuple-element.179.refs_1_, ...), custom_call_target="tpu_custom_call" | custom-call | flops 28600000512 | bytes 91000000 | tf_op jit(solution)/shard_map/pallas_call | solution.py:585
  286.6 4.0 convolution_convert_fusion.2
  290.6 2.3 convolution_convert_fusion.1
  297.3 5.2 collective-permute-done.31
  304.0 3.4 convert_add_fusion
  309.7 18.1 %shard_map.246 = (bf16[512,768]{1,0:T(8,128)(2,1)}, bf16[2,8,384,384]{3,2,1,0:T(8,128)(2,1)}, bf16[2,8,384,384]{3,2,1,0:T(8,128)(2,1)}, f32[8,768]{1,0:T(8,128)}) custom-call(s32[4]{0:T(128)} %pad_add_fusion.refs_0_.refs_1_, f32[512,768]{1,0:T(8,128)} %get-tuple-element.199.refs_1_, bf16[512,768]{1,0:T(8,128)(2,1)} %get-tuple-element.176.refs_2_, ...), custom_call_target="tpu_custom_call" | custom-call | flops 24199999488 | bytes 77000000 | tf_op jit(solution)/shard_map/pallas_call | solution.py:585
  328.7 19.5 %shard_map.247 = (f32[512,768]{1,0:T(8,128)}, bf16[2,8,768,384]{3,2,1,0:T(8,128)(2,1)}, bf16[2,8,768,384]{3,2,1,0:T(8,128)(2,1)}, f32[8,768]{1,0:T(8,128)}, f32[1,3072]{1,0:T(1,128)}) custom-call(s32[4]{0:T(128)} %pad_add_fusion.refs_0_.refs_1_, bf16[512,768]{1,0:T(8,128)(2,1)} %get-tuple-element.210.refs_1_, ...), custom_call_target="tpu_custom_call", output_to_operand_aliasing={{1}: (40, {}), {2}: (41, {})} | custom-call | flops 24199999488 | bytes 77000000 | tf_op jit(solution)/shard_map/pallas_call | solution.py:585
  352.7 18.5 %shard_map.248 = (f32[512,768]{1,0:T(8,128)}, bf16[2,8,384,384]{3,2,1,0:T(8,128)(2,1)}, bf16[2,8,384,384]{3,2,1,0:T(8,128)(2,1)}, f32[8,768]{1,0:T(8,128)}) custom-call(s32[4]{0:T(128)} %pad_add_fusion.refs_0_.refs_1_, f32[512,768]{1,0:T(8,128)} %get-tuple-element.224.refs_1_, ...), custom_call_target="tpu_custom_call", output_to_operand_aliasing={{1}: (41, {}), {2}: (42, {})} | custom-call | flops 24199999488 | bytes 77000000 | tf_op jit(solution)/shard_map/pallas_call | solution.py:585
  372.1 5.6 %fusion.28 = (bf16[768,384]{1,0:T(8,128)(2,1)S(1)}, bf16[768,384]{1,0:T(8,128)(2,1)S(1)}, bf16[768,384]{1,0:T(8,128)(2,1)}, bf16[768,384]{1,0:T(8,128)(2,1)S(1)}...) fusion(bf16[2,4,2,768,384]{4,3,2,1,0:T(8,128)(2,1)} %bitcast.32, ...), kind=kLoop, calls=%fused_computation.61 | loop fusion | flops 8257536 | bytes 12386304 | tf_op jit(solution)/shard_map/convert_element_type | solution.py:946
  382.5 7.8 %collective-permute-done.38 = bf16[112,768]{1,0:T(8,128)(2,1)S(1)} collective-permute-done((bf16[112,768]{1,0:T(8,128)(2,1)}, bf16[112,768]{1,0:T(8,128)(2,1)S(1)}, u32[]{:S(2)}, u32[]{:S(2)}) %collective-permute-start.38) | collective-permute-done | bytes 172064 | tf_op jit(solution)/shard_map/ppermute | solution.py:877
  391.1 5.0 collective-permute-done.37
  396.1 2.5 fusion.13
  398.5 3.6 fusion.51
  406.9 4.7 collective-permute-done.46
  415.0 9.5 %collective-permute-done.41 = bf16[768,384]{1,0:T(8,128)(2,1)S(1)} collective-permute-done((bf16[768,384]{1,0:T(8,128)(2,1)}, bf16[768,384]{1,0:T(8,128)(2,1)S(1)}, u32[]{:S(2)}, u32[]{:S(2)}) %collective-permute-start.41) | collective-permute-done | bytes 589856 | tf_op jit(solution)/shard_map/ppermute | solution.py:874
  424.5 2.9 fusion.11
  427.4 2.6 collective-permute-done.47
  433.4 2.8 collective-permute-done.54
  437.0 3.0 collective-permute-done.51
  445.1 2.6 fusion.33
  447.7 9.7 %collective-permute-done.49 = bf16[768,384]{1,0:T(8,128)(2,1)S(1)} collective-permute-done((bf16[768,384]{1,0:T(8,128)(2,1)S(1)}, bf16[768,384]{1,0:T(8,128)(2,1)S(1)}, u32[]{:S(2)}, u32[]{:S(2)}) %collective-permute-start.49) | collective-permute-done | bytes 589856 | tf_op jit(solution)/shard_map/ppermute | solution.py:877
  457.4 3.9 fusion.9
  464.8 8.6 %collective-permute-done.60 = bf16[384,384]{1,0:T(8,128)(2,1)} collective-permute-done((bf16[384,384]{1,0:T(8,128)(2,1)}, bf16[384,384]{1,0:T(8,128)(2,1)}, u32[]{:S(2)}, u32[]{:S(2)}) %collective-permute-start.60) | collective-permute-done | bytes 294944 | tf_op jit(solution)/shard_map/ppermute | solution.py:877
  475.6 2.7 fusion.29
  478.3 2.7 collective-permute-done.57
  481.0 3.6 collective-permute-done.59
  491.1 3.8 collective-permute-done.64
  498.6 2.7 collective-permute-done.67
  501.3 3.6 collective-permute-done.69
  507.5 3.0 collective-permute-start.75
  516.1 2.8 collective-permute-done.70
  (299 shorter events, 110.8 us)
Async XLA Ops:
  7.2 195.5 %all-gather.2.cloned.1.call-start = ((), (), s32[]{:S(2)}) async-start(), calls=%async_computation | async-start | bytes 5677056 | tf_op jit(solution)/shard_map/all_gather | solution.py:1123
  15.8 22.9 %collective-permute-start.1 = (bf16[1168,384]{1,0:T(8,128)(2,1)S(1)}, bf16[1168,384]{1,0:T(8,128)(2,1)S(1)}, u32[]{:S(2)}, u32[]{:S(2)}) collective-permute-start(bf16[1168,384]{1,0:T(8,128)(2,1)S(1)} %constant_dynamic-update-slice_fusion.refs_1_.refs_4_.refs_5_.refs_6_.refs_9_.refs_8_), channel_id=1, source_target_pairs={{0,1},{1,0},{2,3},{3,2},{4,5},{5,4},{6,7},{7,6},{8,9},{9,8},{10,11... | collective-permute-start | bytes 2691080 | tf_op jit(solution)/shard_map/ppermute | solution.py:874
  18.8 21.4 %collective-permute-start.2 = (bf16[1168,384]{1,0:T(8,128)(2,1)S(1)}, bf16[1168,384]{1,0:T(8,128)(2,1)S(1)}, u32[]{:S(2)}, u32[]{:S(2)}) collective-permute-start(bf16[1168,384]{1,0:T(8,128)(2,1)S(1)} %constant_dynamic-update-slice_fusion.refs_1_.refs_4_.refs_5_.refs_6_.refs_9_.refs_8_), channel_id=1, source_target_pairs={{0,16},{8,24},{16,0},{24,8},{1,17},{9,25},{17,1},{25,9},{2,18},{10... | collective-permute-start | bytes 2691080 | tf_op jit(solution)/shard_map/ppermute | solution.py:868
  20.3 22.9 %collective-permute-start = (bf16[1168,384]{1,0:T(8,128)(2,1)S(1)}, bf16[1168,384]{1,0:T(8,128)(2,1)S(1)}, u32[]{:S(2)}, u32[]{:S(2)}) collective-permute-start(bf16[1168,384]{1,0:T(8,128)(2,1)S(1)} %constant_dynamic-update-slice_fusion.refs_1_.refs_4_.refs_5_.refs_6_.refs_9_.refs_8_), channel_id=1, source_target_pairs={{0,2},{1,3},{2,4},{3,5},{4,6},{5,7},{6,0},{7,1},{8,10},{9,11},{10,... | collective-permute-start | bytes 2691080 | tf_op jit(solution)/shard_map/ppermute | solution.py:877
  21.9 21.4 %collective-permute-start.3 = (bf16[1168,384]{1,0:T(8,128)(2,1)S(1)}, bf16[1168,384]{1,0:T(8,128)(2,1)S(1)}, u32[]{:S(2)}, u32[]{:S(2)}) collective-permute-start(bf16[1168,384]{1,0:T(8,128)(2,1)S(1)} %constant_dynamic-update-slice_fusion.refs_1_.refs_4_.refs_5_.refs_6_.refs_9_.refs_8_), channel_id=1, source_target_pairs={{0,8},{8,0},{16,24},{24,16},{1,9},{9,1},{17,25},{25,17},{2,10},{10... | collective-permute-start | bytes 2691080 | tf_op jit(solution)/shard_map/ppermute | solution.py:871
  43.3 20.4 %collective-permute-start.6 = (bf16[1168,384]{1,0:T(8,128)(2,1)S(1)}, bf16[1168,384]{1,0:T(8,128)(2,1)}, u32[]{:S(2)}, u32[]{:S(2)}) collective-permute-start(bf16[1168,384]{1,0:T(8,128)(2,1)S(1)} %collective-permute-done.refs_2_.refs_5_.refs_6_.refs_7_.refs_10_.refs_9_), channel_id=1, source_target_pairs={{0,16},{8,24},{16,0},{24,8},{1,17},{9,25},{17,1},{25,9},{2,18},{10... | collective-permute-start | bytes 2691080 | tf_op jit(solution)/shard_map/ppermute | solution.py:868
  43.9 20.1 %collective-permute-start.5 = (bf16[1168,384]{1,0:T(8,128)(2,1)S(1)}, bf16[1168,384]{1,0:T(8,128)(2,1)}, u32[]{:S(2)}, u32[]{:S(2)}) collective-permute-start(bf16[1168,384]{1,0:T(8,128)(2,1)S(1)} %collective-permute-done.refs_2_.refs_5_.refs_6_.refs_7_.refs_10_.refs_9_), channel_id=1, source_target_pairs={{0,1},{1,0},{2,3},{3,2},{4,5},{5,4},{6,7},{7,6},{8,9},{9,8},{10,11... | collective-permute-start | bytes 2691080 | tf_op jit(solution)/shard_map/ppermute | solution.py:874
  44.4 21.7 %collective-permute-start.4 = (bf16[1168,384]{1,0:T(8,128)(2,1)S(1)}, bf16[1168,384]{1,0:T(8,128)(2,1)S(1)}, u32[]{:S(2)}, u32[]{:S(2)}) collective-permute-start(bf16[1168,384]{1,0:T(8,128)(2,1)S(1)} %collective-permute-done.refs_2_.refs_5_.refs_6_.refs_7_.refs_10_.refs_9_), channel_id=1, source_target_pairs={{0,2},{1,3},{2,4},{3,5},{4,6},{5,7},{6,0},{7,1},{8,10},{9,11},{10,... | collective-permute-start | bytes 2691080 | tf_op jit(solution)/shard_map/ppermute | solution.py:877
  44.4 21.7 %collective-permute-start.7 = (bf16[1168,384]{1,0:T(8,128)(2,1)S(1)}, bf16[1168,384]{1,0:T(8,128)(2,1)S(1)}, u32[]{:S(2)}, u32[]{:S(2)}) collective-permute-start(bf16[1168,384]{1,0:T(8,128)(2,1)S(1)} %collective-permute-done.refs_2_.refs_5_.refs_6_.refs_7_.refs_10_.refs_9_), channel_id=1, source_target_pairs={{0,8},{8,0},{16,24},{24,16},{1,9},{9,1},{17,25},{25,17},{2,10},{10... | collective-permute-start | bytes 2691080 | tf_op jit(solution)/shard_map/ppermute | solution.py:871
  44.4 21.7 %collective-permute-start.8 = (bf16[1168,384]{1,0:T(8,128)(2,1)S(1)}, bf16[1168,384]{1,0:T(8,128)(2,1)S(1)}, u32[]{:S(2)}, u32[]{:S(2)}) collective-permute-start(bf16[1168,384]{1,0:T(8,128)(2,1)S(1)} %collective-permute-done.1.refs_5_.refs_8_.refs_9_.refs_10_.refs_13_.refs_12_), channel_id=1, source_target_pairs={{0,8},{8,0},{16,24},{24,16},{1,9},{9,1},{17,25},{25,17},{2,10},{10... | collective-permute-start | bytes 2691080 | tf_op jit(solution)/shard_map/ppermute | solution.py:871
  66.1 19.0 %collective-permute-start.10 = (bf16[1168,384]{1,0:T(8,128)(2,1)S(1)}, bf16[1168,384]{1,0:T(8,128)(2,1)S(1)}, u32[]{:S(2)}, u32[]{:S(2)}) collective-permute-start(bf16[1168,384]{1,0:T(8,128)(2,1)S(1)} %collective-permute-done.4.refs_3_.refs_6_.refs_7_.refs_8_.refs_11_.refs_10_), channel_id=1, source_target_pairs={{0,1},{1,0},{2,3},{3,2},{4,5},{5,4},{6,7},{7,6},{8,9},{9,8},{10,11... | collective-permute-start | bytes 2691080 | tf_op jit(solution)/shard_map/ppermute | solution.py:874
  67.5 18.6 %collective-permute-start.11 = (bf16[1168,384]{1,0:T(8,128)(2,1)S(1)}, bf16[1168,384]{1,0:T(8,128)(2,1)}, u32[]{:S(2)}, u32[]{:S(2)}) collective-permute-start(bf16[1168,384]{1,0:T(8,128)(2,1)S(1)} %collective-permute-done.1.refs_5_.refs_8_.refs_9_.refs_10_.refs_13_.refs_12_), channel_id=1, source_target_pairs={{0,16},{8,24},{16,0},{24,8},{1,17},{9,25},{17,1},{25,9},{2,18},{10... | collective-permute-start | bytes 2691080 | tf_op jit(solution)/shard_map/ppermute | solution.py:868
  69.0 17.1 %collective-permute-start.12 = (bf16[1168,384]{1,0:T(8,128)(2,1)S(1)}, bf16[1168,384]{1,0:T(8,128)(2,1)S(1)}, u32[]{:S(2)}, u32[]{:S(2)}) collective-permute-start(bf16[1168,384]{1,0:T(8,128)(2,1)S(1)} %collective-permute-done.2.refs_17_.refs_20_.refs_21_.refs_22_.refs_25_.refs_24_), channel_id=1, source_target_pairs={{0,8},{8,0},{16,24},{24,16},{1,9},{9,1},{17,25},{25,17},{2,10},{10... | collective-permute-start | bytes 2691080 | tf_op jit(solution)/shard_map/ppermute | solution.py:871
  69.0 17.1 %collective-permute-start.13 = (bf16[1168,384]{1,0:T(8,128)(2,1)S(1)}, bf16[1168,384]{1,0:T(8,128)(2,1)S(1)}, u32[]{:S(2)}, u32[]{:S(2)}) collective-permute-start(bf16[1168,384]{1,0:T(8,128)(2,1)S(1)} %collective-permute-done.4.refs_3_.refs_6_.refs_7_.refs_8_.refs_11_.refs_10_), channel_id=1, source_target_pairs={{0,8},{8,0},{16,24},{24,16},{1,9},{9,1},{17,25},{25,17},{2,10},{10... | collective-permute-start | bytes 2691080 | tf_op jit(solution)/shard_map/ppermute | solution.py:871
  69.5 23.7 %collective-permute-start.9 = (bf16[1168,384]{1,0:T(8,128)(2,1)S(1)}, bf16[1168,384]{1,0:T(8,128)(2,1)}, u32[]{:S(2)}, u32[]{:S(2)}) collective-permute-start(bf16[1168,384]{1,0:T(8,128)(2,1)S(1)} %collective-permute-done.4.refs_3_.refs_6_.refs_7_.refs_8_.refs_11_.refs_10_), channel_id=1, source_target_pairs={{0,2},{1,3},{2,4},{3,5},{4,6},{5,7},{6,0},{7,1},{8,10},{9,11},{10,... | collective-permute-start | bytes 2691080 | tf_op jit(solution)/shard_map/ppermute | solution.py:877
  93.2 21.3 %collective-permute-start.14 = (bf16[1168,384]{1,0:T(8,128)(2,1)}, bf16[1168,384]{1,0:T(8,128)(2,1)}, u32[]{:S(2)}, u32[]{:S(2)}) collective-permute-start(bf16[1168,384]{1,0:T(8,128)(2,1)} %collective-permute-done.9.refs_4_.refs_7_.refs_8_.refs_9_.refs_12_.refs_11_), channel_id=1, source_target_pairs={{0,1},{1,0},{2,3},{3,2},{4,5},{5,4},{6,7},{7,6},{8,9},{9,8},{10,11... | collective-permute-start | bytes 2691080 | tf_op jit(solution)/shard_map/ppermute | solution.py:874
  93.7 21.0 %collective-permute-start.15 = (bf16[1168,384]{1,0:T(8,128)(2,1)}, bf16[1168,384]{1,0:T(8,128)(2,1)}, u32[]{:S(2)}, u32[]{:S(2)}) collective-permute-start(bf16[1168,384]{1,0:T(8,128)(2,1)} %collective-permute-done.9.refs_4_.refs_7_.refs_8_.refs_9_.refs_12_.refs_11_), channel_id=1, source_target_pairs={{0,16},{8,24},{16,0},{24,8},{1,17},{9,25},{17,1},{25,9},{2,18},{10... | collective-permute-start | bytes 2691080 | tf_op jit(solution)/shard_map/ppermute | solution.py:868
  94.5 22.5 %collective-permute-start.16 = (bf16[1168,384]{1,0:T(8,128)(2,1)}, bf16[1168,384]{1,0:T(8,128)(2,1)}, u32[]{:S(2)}, u32[]{:S(2)}) collective-permute-start(bf16[1168,384]{1,0:T(8,128)(2,1)} %collective-permute-done.11.refs_21_.refs_24_.refs_25_.refs_26_.refs_29_.refs_28_), channel_id=1, source_target_pairs={{0,2},{1,3},{2,4},{3,5},{4,6},{5,7},{6,0},{7,1},{8,10},{9,11},{10,... | collective-permute-start | bytes 2691080 | tf_op jit(solution)/shard_map/ppermute | solution.py:877
  94.5 22.5 %collective-permute-start.17 = (bf16[1168,384]{1,0:T(8,128)(2,1)}, bf16[1168,384]{1,0:T(8,128)(2,1)}, u32[]{:S(2)}, u32[]{:S(2)}) collective-permute-start(bf16[1168,384]{1,0:T(8,128)(2,1)} %collective-permute-done.5.refs_6_.refs_9_.refs_10_.refs_11_.refs_14_.refs_13_), channel_id=1, source_target_pairs={{0,8},{8,0},{16,24},{24,16},{1,9},{9,1},{17,25},{25,17},{2,10},{10... | collective-permute-start | bytes 2691080 | tf_op jit(solution)/shard_map/ppermute | solution.py:871
  94.6 22.4 %collective-permute-start.18 = (bf16[1168,384]{1,0:T(8,128)(2,1)}, bf16[1168,384]{1,0:T(8,128)(2,1)}, u32[]{:S(2)}, u32[]{:S(2)}) collective-permute-start(bf16[1168,384]{1,0:T(8,128)(2,1)} %collective-permute-done.6.refs_18_.refs_21_.refs_22_.refs_23_.refs_26_.refs_25_), channel_id=1, source_target_pairs={{0,8},{8,0},{16,24},{24,16},{1,9},{9,1},{17,25},{25,17},{2,10},{10... | collective-permute-start | bytes 2691080 | tf_op jit(solution)/shard_map/ppermute | solution.py:871
  117.6 27.6 %collective-permute-start.21 = (bf16[1168,384]{1,0:T(8,128)(2,1)}, bf16[1168,384]{1,0:T(8,128)(2,1)S(1)}, u32[]{:S(2)}, u32[]{:S(2)}) collective-permute-start(bf16[1168,384]{1,0:T(8,128)(2,1)} %collective-permute-done.6.refs_18_.refs_21_.refs_22_.refs_23_.refs_26_.refs_25_), channel_id=1, source_target_pairs={{0,2},{1,3},{2,4},{3,5},{4,6},{5,7},{6,0},{7,1},{8,10},{9,11},{10,... | collective-permute-start | bytes 2691080 | tf_op jit(solution)/shard_map/ppermute | solution.py:877
  117.6 27.6 %collective-permute-start.22 = (bf16[1168,384]{1,0:T(8,128)(2,1)}, bf16[1168,384]{1,0:T(8,128)(2,1)}, u32[]{:S(2)}, u32[]{:S(2)}) collective-permute-start(bf16[1168,384]{1,0:T(8,128)(2,1)} %collective-permute-done.15.refs_20_.refs_23_.refs_24_.refs_25_.refs_28_.refs_27_), channel_id=1, source_target_pairs={{0,1},{1,0},{2,3},{3,2},{4,5},{5,4},{6,7},{7,6},{8,9},{9,8},{10,11... | collective-permute-start | bytes 2691080 | tf_op jit(solution)/shard_map/ppermute | solution.py:874
  118.9 26.3 %collective-permute-start.23 = (bf16[1168,384]{1,0:T(8,128)(2,1)S(1)}, bf16[1168,384]{1,0:T(8,128)(2,1)}, u32[]{:S(2)}, u32[]{:S(2)}) collective-permute-start(bf16[1168,384]{1,0:T(8,128)(2,1)S(1)} %collective-permute-done.10.refs_7_.refs_10_.refs_11_.refs_12_.refs_15_.refs_14_), channel_id=1, source_target_pairs={{0,16},{8,24},{16,0},{24,8},{1,17},{9,25},{17,1},{25,9},{2,18},{10... | collective-permute-start | bytes 2691080 | tf_op jit(solution)/shard_map/ppermute | solution.py:868
  308.5 19.4 %collective-permute-start.32 = (bf16[2,2,112,768]{3,2,0,1:T(8,128)(2,1)}, bf16[2,2,112,768]{3,2,0,1:T(8,128)(2,1)}, u32[]{:S(2)}, u32[]{:S(2)}) collective-permute-start(bf16[2,2,112,768]{3,2,0,1:T(8,128)(2,1)} %get-tuple-element.198), channel_id=1, source_target_pairs={{0,16},{8,24},{16,0},{24,8},{1,17},{9,25},{17,1},{25,9},{2,18},{10... | collective-permute-start | bytes 2064392 | tf_op jit(solution)/shard_map/ppermute | solution.py:868
  327.9 20.3 %collective-permute-start.33 = (bf16[2,2,112,768]{3,2,0,1:T(8,128)(2,1)S(1)}, bf16[2,2,112,768]{3,2,0,1:T(8,128)(2,1)}, u32[]{:S(2)}, u32[]{:S(2)}) collective-permute-start(bf16[2,2,112,768]{3,2,0,1:T(8,128)(2,1)S(1)} %get-tuple-element.209), channel_id=1, source_target_pairs={{0,16},{8,24},{16,0},{24,8},{1,17},{9,25},{17,1},{25,9},{2,18},{10... | collective-permute-start | bytes 2064392 | tf_op jit(solution)/shard_map/ppermute | solution.py:868
  351.4 20.7 %collective-permute-start.34 = (bf16[2,8,768,384]{3,2,1,0:T(8,128)(2,1)}, bf16[2,8,768,384]{3,2,1,0:T(8,128)(2,1)}, u32[]{:S(2)}, u32[]{:S(2)}) collective-permute-start(bf16[2,8,768,384]{3,2,1,0:T(8,128)(2,1)} %get-tuple-element.222), channel_id=1, source_target_pairs={{0,8},{8,0},{16,24},{24,16},{1,9},{9,1},{17,25},{25,17},{2,10},{10... | collective-permute-start | bytes 28311560 | tf_op jit(solution)/shard_map/ppermute | solution.py:871
  351.4 19.9 %collective-permute-start.35 = (bf16[4,112,768]{2,1,0:T(8,128)(2,1)S(1)}, bf16[4,112,768]{2,1,0:T(8,128)(2,1)S(1)}, u32[]{:S(2)}, u32[]{:S(2)}) collective-permute-start(bf16[4,112,768]{2,1,0:T(8,128)(2,1)S(1)} %fusion.21), channel_id=1, source_target_pairs={{0,1},{1,0},{2,3},{3,2},{4,5},{5,4},{6,7},{7,6},{8,9},{9,8},{10,11... | collective-permute-start | bytes 2064392 | tf_op jit(solution)/shard_map/ppermute | solution.py:874
  377.7 20.8 %collective-permute-start.36 = (bf16[2,8,384,384]{3,2,1,0:T(8,128)(2,1)}, bf16[2,8,384,384]{3,2,1,0:T(8,128)(2,1)}, u32[]{:S(2)}, u32[]{:S(2)}) collective-permute-start(bf16[2,8,384,384]{3,2,1,0:T(8,128)(2,1)} %get-tuple-element.234), channel_id=1, source_target_pairs={{0,8},{8,0},{16,24},{24,16},{1,9},{9,1},{17,25},{25,17},{2,10},{10... | collective-permute-start | bytes 14155784 | tf_op jit(solution)/shard_map/ppermute | solution.py:871
  380.2 15.9 %collective-permute-start.37 = (bf16[768,384]{1,0:T(8,128)(2,1)}, bf16[768,384]{1,0:T(8,128)(2,1)}, u32[]{:S(2)}, u32[]{:S(2)}) collective-permute-start(bf16[768,384]{1,0:T(8,128)(2,1)} %get-tuple-element.235), channel_id=1, source_target_pairs={{0,1},{1,0},{2,3},{3,2},{4,5},{5,4},{6,7},{7,6},{8,9},{9,8},{10,11... | collective-permute-start | bytes 1769480 | tf_op jit(solution)/shard_map/ppermute | solution.py:874
  381.2 21.0 %collective-permute-start.39 = (bf16[768,384]{1,0:T(8,128)(2,1)}, bf16[768,384]{1,0:T(8,128)(2,1)}, u32[]{:S(2)}, u32[]{:S(2)}) collective-permute-start(bf16[768,384]{1,0:T(8,128)(2,1)} %get-tuple-element.240), channel_id=1, source_target_pairs={{0,2},{1,3},{2,4},{3,5},{4,6},{5,7},{6,0},{7,1},{8,10},{9,11},{10,... | collective-permute-start | bytes 1769480 | tf_op jit(solution)/shard_map/ppermute | solution.py:877
  381.3 20.9 %collective-permute-start.40 = (bf16[768,384]{1,0:T(8,128)(2,1)}, bf16[768,384]{1,0:T(8,128)(2,1)}, u32[]{:S(2)}, u32[]{:S(2)}) collective-permute-start(bf16[768,384]{1,0:T(8,128)(2,1)} %get-tuple-element.241), channel_id=1, source_target_pairs={{0,16},{8,24},{16,0},{24,8},{1,17},{9,25},{17,1},{25,9},{2,18},{10... | collective-permute-start | bytes 1769480 | tf_op jit(solution)/shard_map/ppermute | solution.py:868
  403.6 21.0 %collective-permute-start.41 = (bf16[768,384]{1,0:T(8,128)(2,1)}, bf16[768,384]{1,0:T(8,128)(2,1)S(1)}, u32[]{:S(2)}, u32[]{:S(2)}) collective-permute-start(bf16[768,384]{1,0:T(8,128)(2,1)} %get-tuple-element.242), channel_id=1, source_target_pairs={{0,1},{1,0},{2,3},{3,2},{4,5},{5,4},{6,7},{7,6},{8,9},{9,8},{10,11... | collective-permute-start | bytes 1769480 | tf_op jit(solution)/shard_map/ppermute | solution.py:874
  404.5 20.1 %collective-permute-start.42 = (bf16[768,384]{1,0:T(8,128)(2,1)}, bf16[768,384]{1,0:T(8,128)(2,1)S(1)}, u32[]{:S(2)}, u32[]{:S(2)}) collective-permute-start(bf16[768,384]{1,0:T(8,128)(2,1)} %fusion.13), channel_id=1, source_target_pairs={{0,16},{8,24},{16,0},{24,8},{1,17},{9,25},{17,1},{25,9},{2,18},{10... | collective-permute-start | bytes 1769480 | tf_op jit(solution)/shard_map/ppermute | solution.py:868
  405.8 18.7 %collective-permute-start.43 = (bf16[768,384]{1,0:T(8,128)(2,1)S(1)}, bf16[768,384]{1,0:T(8,128)(2,1)S(1)}, u32[]{:S(2)}, u32[]{:S(2)}) collective-permute-start(bf16[768,384]{1,0:T(8,128)(2,1)S(1)} %get-tuple-element.244), channel_id=1, source_target_pairs={{0,2},{1,3},{2,4},{3,5},{4,6},{5,7},{6,0},{7,1},{8,10},{9,11},{10,... | collective-permute-start | bytes 1769480 | tf_op jit(solution)/shard_map/ppermute | solution.py:877
  411.5 18.5 %collective-permute-start.47 = (bf16[384,384]{1,0:T(8,128)(2,1)}, bf16[384,384]{1,0:T(8,128)(2,1)S(1)}, u32[]{:S(2)}, u32[]{:S(2)}) collective-permute-start(bf16[384,384]{1,0:T(8,128)(2,1)} %get-tuple-element.248), channel_id=1, source_target_pairs={{0,2},{1,3},{2,4},{3,5},{4,6},{5,7},{6,0},{7,1},{8,10},{9,11},{10,... | collective-permute-start | bytes 884744 | tf_op jit(solution)/shard_map/ppermute | solution.py:877
  412.5 17.6 %collective-permute-start.48 = (bf16[384,384]{1,0:T(8,128)(2,1)}, bf16[384,384]{1,0:T(8,128)(2,1)S(1)}, u32[]{:S(2)}, u32[]{:S(2)}) collective-permute-start(bf16[384,384]{1,0:T(8,128)(2,1)} %get-tuple-element.249), channel_id=1, source_target_pairs={{0,16},{8,24},{16,0},{24,8},{1,17},{9,25},{17,1},{25,9},{2,18},{10... | collective-permute-start | bytes 884744 | tf_op jit(solution)/shard_map/ppermute | solution.py:868
  433.3 11.7 %collective-permute-start.53 = (bf16[384,384]{1,0:T(8,128)(2,1)S(1)}, bf16[384,384]{1,0:T(8,128)(2,1)S(1)}, u32[]{:S(2)}, u32[]{:S(2)}) collective-permute-start(bf16[384,384]{1,0:T(8,128)(2,1)S(1)} %copy-done.26), channel_id=1, source_target_pairs={{0,2},{1,3},{2,4},{3,5},{4,6},{5,7},{6,0},{7,1},{8,10},{9,11},{10,... | collective-permute-start | bytes 884744 | tf_op jit(solution)/shard_map/ppermute | solution.py:877
  433.4 24.1 %collective-permute-start.49 = (bf16[768,384]{1,0:T(8,128)(2,1)S(1)}, bf16[768,384]{1,0:T(8,128)(2,1)S(1)}, u32[]{:S(2)}, u32[]{:S(2)}) collective-permute-start(bf16[768,384]{1,0:T(8,128)(2,1)S(1)} %get-tuple-element.250), channel_id=1, source_target_pairs={{0,2},{1,3},{2,4},{3,5},{4,6},{5,7},{6,0},{7,1},{8,10},{9,11},{10,... | collective-permute-start | bytes 1769480 | tf_op jit(solution)/shard_map/ppermute | solution.py:877
  436.2 21.2 %collective-permute-start.50 = (bf16[768,384]{1,0:T(8,128)(2,1)S(1)}, bf16[768,384]{1,0:T(8,128)(2,1)S(1)}, u32[]{:S(2)}, u32[]{:S(2)}) collective-permute-start(bf16[768,384]{1,0:T(8,128)(2,1)S(1)} %get-tuple-element.251), channel_id=1, source_target_pairs={{0,1},{1,0},{2,3},{3,2},{4,5},{5,4},{6,7},{7,6},{8,9},{9,8},{10,11... | collective-permute-start | bytes 1769480 | tf_op jit(solution)/shard_map/ppermute | solution.py:874
  440.0 17.4 %collective-permute-start.55 = (bf16[768,384]{1,0:T(8,128)(2,1)S(1)}, bf16[768,384]{1,0:T(8,128)(2,1)S(1)}, u32[]{:S(2)}, u32[]{:S(2)}) collective-permute-start(bf16[768,384]{1,0:T(8,128)(2,1)S(1)} %get-tuple-element.256), channel_id=1, source_target_pairs={{0,16},{8,24},{16,0},{24,8},{1,17},{9,25},{17,1},{25,9},{2,18},{10... | collective-permute-start | bytes 1769480 | tf_op jit(solution)/shard_map/ppermute | solution.py:868
  442.6 18.7 %collective-permute-start.56 = (bf16[112,768]{1,0:T(8,128)(2,1)S(1)}, bf16[112,768]{1,0:T(8,128)(2,1)S(1)}, u32[]{:S(2)}, u32[]{:S(2)}) collective-permute-start(bf16[112,768]{1,0:T(8,128)(2,1)S(1)} %fusion.43), channel_id=1, source_target_pairs={{0,2},{1,3},{2,4},{3,5},{4,6},{5,7},{6,0},{7,1},{8,10},{9,11},{10,... | collective-permute-start | bytes 516104 | tf_op jit(solution)/shard_map/ppermute | solution.py:877
  461.3 12.1 %collective-permute-start.60 = (bf16[384,384]{1,0:T(8,128)(2,1)}, bf16[384,384]{1,0:T(8,128)(2,1)}, u32[]{:S(2)}, u32[]{:S(2)}) collective-permute-start(bf16[384,384]{1,0:T(8,128)(2,1)} %get-tuple-element.261), channel_id=1, source_target_pairs={{0,2},{1,3},{2,4},{3,5},{4,6},{5,7},{6,0},{7,1},{8,10},{9,11},{10,... | collective-permute-start | bytes 884744 | tf_op jit(solution)/shard_map/ppermute | solution.py:877
  461.3 13.5 %collective-permute-start.61 = (bf16[384,384]{1,0:T(8,128)(2,1)}, bf16[384,384]{1,0:T(8,128)(2,1)S(1)}, u32[]{:S(2)}, u32[]{:S(2)}) collective-permute-start(bf16[384,384]{1,0:T(8,128)(2,1)} %get-tuple-element.262), channel_id=1, source_target_pairs={{0,1},{1,0},{2,3},{3,2},{4,5},{5,4},{6,7},{7,6},{8,9},{9,8},{10,11... | collective-permute-start | bytes 884744 | tf_op jit(solution)/shard_map/ppermute | solution.py:874
  462.1 13.5 %collective-permute-start.62 = (bf16[384,384]{1,0:T(8,128)(2,1)}, bf16[384,384]{1,0:T(8,128)(2,1)S(1)}, u32[]{:S(2)}, u32[]{:S(2)}) collective-permute-start(bf16[384,384]{1,0:T(8,128)(2,1)} %get-tuple-element.263), channel_id=1, source_target_pairs={{0,16},{8,24},{16,0},{24,8},{1,17},{9,25},{17,1},{25,9},{2,18},{10... | collective-permute-start | bytes 884744 | tf_op jit(solution)/shard_map/ppermute | solution.py:868
  463.5 17.5 %collective-permute-start.57 = (bf16[768,384]{1,0:T(8,128)(2,1)}, bf16[768,384]{1,0:T(8,128)(2,1)S(1)}, u32[]{:S(2)}, u32[]{:S(2)}) collective-permute-start(bf16[768,384]{1,0:T(8,128)(2,1)} %get-tuple-element.258), channel_id=1, source_target_pairs={{0,2},{1,3},{2,4},{3,5},{4,6},{5,7},{6,0},{7,1},{8,10},{9,11},{10,... | collective-permute-start | bytes 1769480 | tf_op jit(solution)/shard_map/ppermute | solution.py:877
  463.5 17.5 %collective-permute-start.58 = (bf16[768,384]{1,0:T(8,128)(2,1)S(1)}, bf16[768,384]{1,0:T(8,128)(2,1)S(1)}, u32[]{:S(2)}, u32[]{:S(2)}) collective-permute-start(bf16[768,384]{1,0:T(8,128)(2,1)S(1)} %get-tuple-element.259), channel_id=1, source_target_pairs={{0,1},{1,0},{2,3},{3,2},{4,5},{5,4},{6,7},{7,6},{8,9},{9,8},{10,11... | collective-permute-start | bytes 1769480 | tf_op jit(solution)/shard_map/ppermute | solution.py:874
  489.2 12.1 %collective-permute-start.67 = (bf16[768,384]{1,0:T(8,128)(2,1)S(1)}, bf16[768,384]{1,0:T(8,128)(2,1)S(1)}, u32[]{:S(2)}, u32[]{:S(2)}) collective-permute-start(bf16[768,384]{1,0:T(8,128)(2,1)S(1)} %fusion.20), channel_id=1, source_target_pairs={{0,2},{1,3},{2,4},{3,5},{4,6},{5,7},{6,0},{7,1},{8,10},{9,11},{10,... | collective-permute-start | bytes 1769480 | tf_op jit(solution)/shard_map/ppermute | solution.py:877
  489.2 12.1 %collective-permute-start.68 = (bf16[768,384]{1,0:T(8,128)(2,1)S(1)}, bf16[768,384]{1,0:T(8,128)(2,1)S(1)}, u32[]{:S(2)}, u32[]{:S(2)}) collective-permute-start(bf16[768,384]{1,0:T(8,128)(2,1)S(1)} %get-tuple-element.269), channel_id=1, source_target_pairs={{0,1},{1,0},{2,3},{3,2},{4,5},{5,4},{6,7},{7,6},{8,9},{9,8},{10,11... | collective-permute-start | bytes 1769480 | tf_op jit(solution)/shard_map/ppermute | solution.py:874
  (76 other events, 1321.1 us)
Sparse Core Ops, SparseCore 0:
  117.2 72.8 all-gather.1

commit v6 on v5

--- a/solution.py
+++ b/solution.py
@@ -183,27 +183,31 @@
     norm_rows(x_ref, bias, gain, offset, y_ref, low_ref, n_ref, r_ref)
 
 
-def self_forward_kernel(count, layer, io, ins, outs, scratch):
-    lengths, where_ref, x_ref, vec_ref, *refs = ins
-    p_ref, a_ref, o_ref, y_ref, low_ref, n_ref, r_ref = outs
-    qkv, out, bias_ref, sems, sems2 = scratch
+def self_weights(count, layer, where_ref, refs, qkv, out, sems, sems2):
+    width, whole = out.shape[1], count == 2
+    n, m = qkv.shape[0] // 8, out.shape[0] // 8
+    here = where_ref[3] == layer
+    return (
+        lambda: fetch(placed(refs[:1] if whole else refs, where_ref, [(0, n, 0)], qkv, width // 2), sems, here),
+        lambda: fetch(placed(refs[1:] if whole else refs, where_ref, [(n, m, 0)], out, width // 2), sems2, here),
+    )
+
+
+def self_project(x_ref, vec_ref, p_ref, qkv, bias_ref):
     width = x_ref.shape[1]
-    n, m = qkv.shape[0] // 8, out.shape[0] // 8
-    whole = count == 2
-    here = where_ref[3] == layer
-    first = fetch(placed(refs[:1] if whole else refs, where_ref, [(0, n, 0)], qkv, width // 2), sems, here)
     bias_ref[:, :width] = vec_ref[0:1, :]
     bias_ref[:, width : 2 * width] = jnp.zeros((1, width), F32)
     bias_ref[:, 2 * width :] = vec_ref[1:2, :]
-    settle(first)
-    second = fetch(placed(refs[1:] if whole else refs, where_ref, [(n, m, 0)], out, width // 2), sems2, here)
 
     def tile(j):
         cols = span(j * TILE, TILE)
         p_ref[:, cols] = (dot(x_ref[...], qkv[cols, :], NT) + bias_ref[:, cols]).astype(BF)
 
     tiles(3 * width // TILE, tile)
-    io.send(p_ref)
+
+
+def self_attend(lengths, p_ref, a_ref, o_ref):
+    width = o_ref.shape[1]
     pairs = width // 128
     key = lax.broadcasted_iota(jnp.int32, (128, 256), 0)
     query = lax.broadcasted_iota(jnp.int32, (128, 256), 1)
@@ -221,12 +225,7 @@
             a_ref[s * pairs + h] = a
             o_ref[rows, pl.ds(h * 128, 128)] = join_heads(dot(a, v, TN)).astype(BF)
 
-    tiles(x_ref.shape[0] // 128, attend)
-    io.send(a_ref, o_ref)
-    settle(second)
-    project_and_norm(
-        x_ref, o_ref, out, NT, vec_ref[2:3, :], vec_ref[3:4, :], vec_ref[4:5, :], (y_ref, low_ref, n_ref, r_ref)
-    )
+    tiles(o_ref.shape[0] // 128, attend)
 
 
 def self_backward_kernel(count, layer, io, ins, outs, scratch):
@@ -415,11 +414,7 @@
     )
 
 
-def feed_forward_body(io, x_ref, low_x_ref, vec_ref, bias_ref, act_ref, slope_ref, norm_outs, up, down, get_up, get_down):
-    settle(get_up())
-    second = get_down()
-    io.begin(x_ref)
-
+def feed_activate(low_x_ref, up, bias_ref, act_ref, slope_ref):
     def tile(j):
         cols = span(j * TILE, TILE)
         h = dot(low_x_ref[...], up[cols, :], NT) + bias_ref[:, cols]
@@ -428,10 +423,46 @@
         slope_ref[:, cols] = slope.astype(BF)
 
     tiles(up.shape[0] // TILE, tile)
-    io.send(act_ref, slope_ref)
-    settle(second)
-    io.need(x_ref)
-    project_and_norm(x_ref, act_ref, down, NT, vec_ref[5:6, :], vec_ref[6:7, :], vec_ref[7:8, :], norm_outs)
+
+
+def text_forward_kernel(count, io, ins, outs, scratch):
+    lengths, where_ref, x_ref, vec_ref, vec2_ref, up_bias_ref, *refs = ins
+    p1, a1, o1, low1, n1, act, slope, low2, n2, p2, a2, o2, r1, r2, y3, low3, n3, r3 = outs
+    qkv, out, up, down, y1, y2, bias_ref, *sems = scratch
+    whole = count == 6
+    count = 2 if whole else count
+    get_qkv, get_out = self_weights(count, 0, where_ref, refs[:2] if whole else refs, qkv, out, *sems[:2])
+    get_up, get_down = feed_weights(count, 0, where_ref, refs[2:4] if whole else refs, up, down, *sems[2:])
+    get_qkv2, get_out2 = self_weights(count, 1, where_ref, refs[4:] if whole else refs, qkv, out, *sems[:2])
+    settle(get_qkv())
+    coming = get_out()
+    self_project(x_ref, vec_ref, p1, qkv, bias_ref)
+    io.send(p1)
+    coming_up = get_up()
+    self_attend(lengths, p1, a1, o1)
+    io.send(a1, o1)
+    settle(coming)
+    norm = vec_ref[2:3, :], vec_ref[3:4, :], vec_ref[4:5, :]
+    project_and_norm(x_ref, o1, out, NT, *norm, (y1, low1, n1, r1))
+    io.send(low1, n1)
+    coming_down = get_down()
+    settle(coming_up)
+    coming = get_qkv2()
+    feed_activate(low1, up, up_bias_ref, act, slope)
+    io.send(act, slope)
+    settle(coming_down)
+    coming_out = get_out2()
+    norm = vec_ref[5:6, :], vec_ref[6:7, :], vec_ref[7:8, :]
+    project_and_norm(y1, act, down, NT, *norm, (y2, low2, n2, r2))
+    io.send(low2, n2)
+    settle(coming)
+    self_project(low2, vec2_ref, p2, qkv, bias_ref)
+    io.send(p2)
+    self_attend(lengths, p2, a2, o2)
+    io.send(a2, o2)
+    settle(coming_out)
+    norm = vec2_ref[2:3, :], vec2_ref[3:4, :], vec2_ref[4:5, :]
+    project_and_norm(low2, o2, out, NT, *norm, (y3, low3, n3, r3))
 
 
 def feed_backward_body(
@@ -495,14 +526,6 @@
     gv_ref[2:3, :] = g_offset
 
 
-def feed_forward_kernel(count, layer, io, ins, outs, scratch):
-    where_ref, x_ref, low_x_ref, vec_ref, bias_ref, *refs = ins
-    act_ref, slope_ref, *norm_outs = outs
-    up, down, sems, sems2 = scratch
-    get = feed_weights(count, layer, where_ref, refs, up, down, sems, sems2)
-    feed_forward_body(io, x_ref, low_x_ref, vec_ref, bias_ref, act_ref, slope_ref, norm_outs, up, down, *get)
-
-
 def feed_backward_kernel(count, layer, io, ins, outs, scratch):
     where_ref, dy_ref, low_x_ref, vec_ref, act_ref, slope_ref, n_ref, r_ref, *refs = ins
     up, down, *work, sems, sems2 = scratch
@@ -517,8 +540,14 @@
     y_ref, *grads = outs
     up, down, *work, act_ref, slope_ref, low_ref, n_ref, r_ref, sems, sems2 = scratch
     get = feed_weights(count, layer, where_ref, refs, up, down, sems, sems2)
-    norm_outs = (y_ref, low_ref, n_ref, r_ref)
-    feed_forward_body(io, x_ref, low_x_ref, vec_ref, bias_ref, act_ref, slope_ref, norm_outs, up, down, *get)
+    settle(get[0]())
+    second = get[1]()
+    io.begin(x_ref)
+    feed_activate(low_x_ref, up, bias_ref, act_ref, slope_ref)
+    settle(second)
+    io.need(x_ref)
+    norm = vec_ref[5:6, :], vec_ref[6:7, :], vec_ref[7:8, :]
+    project_and_norm(x_ref, act_ref, down, NT, *norm, (y_ref, low_ref, n_ref, r_ref))
     io.send(y_ref)
     feed_backward_body(
         io, where_ref, dy_ref, low_x_ref, vec_ref, act_ref, slope_ref, n_ref, r_ref, grads, work, up, down, list, list
@@ -610,36 +639,52 @@
     return pltpu.SemaphoreType.DMA((16 * parts if count > 2 else 1,))
 
 
-def self_forward(x, lengths, where, vec, weights, layer):
+def text_forward(x, lengths, where, vecs, bias, weights):
     rows, width = x.shape
+    hidden = bias.shape[1]
     blocks = rows // 128 * (width // 128)
     count = len(weights)
+    low = struct(rows, width, dtype=BF)
+    attention = [struct(rows, 3 * width, dtype=BF), struct(blocks, 128, 256, dtype=BF), low]
     outs = [
-        struct(rows, 3 * width, dtype=BF),
-        struct(blocks, 128, 256, dtype=BF),
-        struct(rows, width, dtype=BF),
+        *attention,
+        low,
+        low,
+        struct(rows, hidden, dtype=BF),
+        struct(rows, hidden, dtype=BF),
+        low,
+        low,
+        *attention,
+        struct(rows, 1),
+        struct(rows, 1),
         struct(rows, width),
-        struct(rows, width, dtype=BF),
-        struct(rows, width, dtype=BF),
+        low,
+        low,
         struct(rows, 1),
     ]
     scratch = [
         pltpu.VMEM((3 * width, width), BF),
         pltpu.VMEM((width, width), BF),
+        pltpu.VMEM((hidden, width), BF),
+        pltpu.VMEM((width, hidden), BF),
+        pltpu.VMEM((rows, width), F32),
+        pltpu.VMEM((rows, width), F32),
         pltpu.VMEM((1, 3 * width), F32),
         copy_sems(count),
         copy_sems(count),
+        copy_sems(count),
+        copy_sems(count, hidden // width),
     ]
-    p, a, o, y, low, n, r = call(
-        partial(self_forward_kernel, count, layer),
+    p1, a1, o1, low1, n1, act, slope, low2, n2, p2, a2, o2, r1, r2, y3, low3, n3, r3 = call(
+        partial(text_forward_kernel, count),
         outs,
-        [SMEM, SMEM, VMEM, VMEM] + [ANYWHERE] * count,
+        [SMEM, SMEM] + [VMEM] * 4 + [ANYWHERE] * count,
         scratch,
-        14,
-        (lengths, where, x, vec, *weights),
-        early=(0, 1, 2),
-    )
-    return y, low, (x, p, a, o, n, r)
+        38,
+        (lengths, where, x, *vecs, bias, *weights),
+        early=tuple(range(12)),
+    )
+    return y3, low3, (x, p1, a1, o1, n1, r1), (low1, act, slope, n2, r2), (low2, p2, a2, o2, n3, r3)
 
 
 def self_backward(dy, saved, where, vec, weights, layer, dtype=F32, onto=None):
@@ -726,37 +771,6 @@
         late=(6, 9, 7, 2, 3, 8, 5, 1),
         early=(1, 2, 4),
     )
-
-
-def feed_forward(x, low_x, where, vec, bias, weights, layer):
-    rows, width = x.shape
-    hidden = bias.shape[1]
-    count = len(weights)
-    outs = [
-        struct(rows, hidden, dtype=BF),
-        struct(rows, hidden, dtype=BF),
-        struct(rows, width),
-        struct(rows, width, dtype=BF),
-        struct(rows, width, dtype=BF),
-        struct(rows, 1),
-    ]
-    scratch = [
-        pltpu.VMEM((hidden, width), BF),
-        pltpu.VMEM((width, hidden), BF),
-        copy_sems(count),
-        copy_sems(count, hidden // width),
-    ]
-    act, slope, y, low, n, r = call(
-        partial(feed_forward_kernel, count, layer),
-        outs,
-        [SMEM] + [VMEM] * 4 + [ANYWHERE] * count,
-        scratch,
-        20,
-        (where, x, low_x, vec, bias, *weights),
-        late=(1,),
-        early=(0, 1),
-    )
-    return y, low, (low_x, act, slope, n, r)
 
 
 def feed_backward(dy, saved, where, vec, weights, layer, onto=None):
@@ -876,17 +890,18 @@
     def ring_z(self, a, step=1):
         return lax.ppermute(a, "dp", [(i, (i + 2 * step) % 8) for i in range(8)])
 
-    def turn(self, *moves, pre=(), compute=None, args=()):
+    def turn(self, *moves, pre=(), compute=None, args=(), chain=False):
         tokens = (*self.arrived[-self.slack], *self.computed)
         arrived = []
 
         def begin(asked):
             asked = [ask for group in asked for ask in group()]
             values = after([value for _, value, _ in asked], tokens)
-            for (move, _, keep), value in zip(asked, values):
-                result = move(value)
-                arrived.append(result)
-                keep(result)
+            results = []
+            for i, ((move, _, keep), value) in enumerate(zip(asked, values)):
+                results.append(move(after(value, (results[i - 2],)) if chain and i >= 5 else value))
+                keep(results[-1])
+            arrived.extend(results)
             return tuple(values)
 
         begin(pre)
@@ -913,8 +928,8 @@
         ready = [key for key in self.here if key not in self.swapped][:count]
         return [(self.grid.swap_core, self.here[key], partial(self.swapped.__setitem__, key)) for key in ready]
 
-    def c2(self):
-        return self.c(2)
+    def c3(self):
+        return self.c(3)
 
     def pieces(self):
         keys = [[(layer, y, z) for y in range(2) for z in range(4)] for layer in range(2)]
@@ -1111,21 +1126,19 @@
         where = jnp.stack([grid.core, grid.z, grid.y, grid.x]).astype(jnp.int32)
         gather = Gather(grid, jnp.concatenate([pack_attn, pack_feed, pad_to(small, 16, lanes)]))
         get = gather.get
-        turn(get(0, 0, 1, "z"), get(0, 1, 0, "y"), get(1, 0, 0, "x"), gather.c2)
+        turn(get(0, 0, 1, "z"), get(0, 1, 0, "y"), get(1, 0, 0, "x"), gather.c3, chain=True)
         image = turn(
-            get(0, 0, 2, "z"), get(0, 1, 1, "y"), get(1, 0, 1, "x"), gather.c2, compute=padded, args=(image_feats,)
+            get(0, 0, 2, "z"), get(0, 1, 1, "y"), get(1, 0, 1, "x"), gather.c3, chain=True, compute=padded, args=(image_feats,)
         )
-        turn(get(0, 0, 3, "z"), get(0, 1, 2, "y"), get(1, 1, 0, "x"), gather.c2)
-        turn(get(1, 1, 1, "z"), get(0, 1, 3, "y"), get(1, 0, 3, "x"), gather.c2)
-        turn(get(1, 0, 2, "z"), get(1, 1, 3, "y"), get(1, 1, 2, "x"), gather.c2)
+        turn(get(0, 0, 3, "z"), get(0, 1, 2, "y"), get(1, 1, 0, "x"), gather.c3, chain=True)
+        turn(get(1, 1, 1, "z"), get(0, 1, 3, "y"), get(1, 0, 3, "x"), gather.c3, chain=True)
+        turn(get(1, 0, 2, "z"), get(1, 1, 3, "y"), get(1, 1, 2, "x"), gather.c3, chain=True)
         turn(gather.c)
         weights = gather.pieces()
         cross_whole = lax.all_gather(after(cross_pack, grid.arrived[-3]), everyone, axis=0, tiled=True)
         *vectors, cvec = gathered_vectors(weights, where, n_pack, v_rows, v_lanes, x_rows, c_rows)
         vecs, biases = vectors[:2], vectors[2:]
-        state, low, s_self = self_forward(x, lengths, where, vecs[0], weights, 0)
-        state, passed, s_feed = feed_forward(state, low, where, vecs[0], biases[0], weights, 0)
-        state, low, s_self2 = self_forward(passed, lengths, where, vecs[1], weights, 1)
+        state, low, s_self, s_feed, s_self2 = text_forward(x, lengths, where, vecs, biases[0], weights)
         wq, wo, wk, wv = cross_weights(cross_whole)
         keys, values = keys_values(image, wk, wv, cvec)
         state, low, s_cross = cross_forward(state, low, patch_keep, keys, values, cvec, wq, wo)
@@ -1188,9 +1201,9 @@
         (qkv1, out1, up1, down1), (qkv2, out2, up2, down2) = ([section(c, k) for c in cut] for k in range(2))
         vecs, biases, cvec = vectors_of(vectors)
         wq, wo, wk, wv = cross_weights(lax.all_gather(cross_pack, everyone, axis=0, tiled=False))
-        state, low, s_self = self_forward(x, lengths, where, vecs[0], [qkv1, out1], 0)
-        state, passed, s_feed = feed_forward(state, low, where, vecs[0], biases[0], [up1, down1], 0)
-        state, low, s_self2 = self_forward(passed, lengths, where, vecs[1], [qkv2, out2], 1)
+        state, low, s_self, s_feed, s_self2 = text_forward(
+            x, lengths, where, vecs, biases[0], [qkv1, out1, up1, down1, qkv2, out2]
+        )
         keys, values = keys_values(image, wk, wv, cvec)
         state, low, s_cross = cross_forward(state, low, patch_keep, keys, values, cvec, wq, wo)
         joined, grad, *g_feed2, v_feed2, v_up2 = feed_both(state, low, where, vecs[1], biases[1], seed, [up2, down2], 1)

time: 539 us -> 526 us (0.976)
  Pallas kernels: 174 us -> 163 us
    ppermute x17, waiting for transfers between devices: 70.6 us -> 56.7 us  [swap_y(): return lax.ppermute(a, 'dp', [(i, i ^ 1) for i in range(8)])]
    pallas_call x9 -> x7, Pallas kernels: 171 us -> 160 us  [call(): pl.pallas_call(body, out_shape=outs, in_specs=specs, out_specs=[ANYWHERE...]
    ppermute x21, waiting for transfers between devices: 86.6 us -> 96.9 us  [ring_z(): return lax.ppermute(a, 'dp', [(i, (i + 2 * step) % 8) for i in range(8)])]
    ppermute x21, starting transfers between devices: 6.56 us -> 14.3 us  [ring_z(): return lax.ppermute(a, 'dp', [(i, (i + 2 * step) % 8) for i in range(8)])]
    ppermute x18, starting transfers between devices: 21.7 us -> 15.7 us  [swap_x(): return lax.ppermute(a, 'pipe', [(i, i ^ 2) for i in range(4)])]
    unnamed x104 -> x102, local copies, waits for them, and re-layouts: 15.4 us -> 16.3 us
  transfers between devices with their start and end apart: 77 -> 77, of which waited for: 41 -> 38; matrix products, arithmetic and copies ran while one was open for 7% -> 7% of each run, Pallas kernels for 19% -> 18%
where the time goes in v6:
time: 526 us; the launch traced here: 517 us
  waiting for transfers between devices  198 us (38%)
  Pallas kernels  163 us (31%)
  starting transfers between devices  51.9 us (10%)
  other arithmetic  43.3 us (8%)
  local copies, waits for them, and re-layouts  32.6 us (6%)
  between operations  15.6 us (3%)
  matrix products  13.3 us (3%)
    pallas_call x7, Pallas kernels, call(): pl.pallas_call(body, out_shape=outs, in_specs=specs, out_specs=[ANYWHERE...  160 us
    ppermute x21, waiting for transfers between devices, ring_z(): return lax.ppermute(a, 'dp', [(i, (i + 2 * step) % 8) for i in range(8)])  96.9 us
    ppermute x17, waiting for transfers between devices, swap_y(): return lax.ppermute(a, 'dp', [(i, i ^ 1) for i in range(8)])  56.7 us
    ppermute x18, waiting for transfers between devices, swap_x(): return lax.ppermute(a, 'pipe', [(i, i ^ 2) for i in range(4)])  30.5 us
    convert_element_type x10, other arithmetic, ask(): self.block(own, y, z).astype(BF)  27.9 us
    ppermute x17, starting transfers between devices, swap_y(): return lax.ppermute(a, 'dp', [(i, i ^ 1) for i in range(8)])  18.9 us
    unnamed x102, local copies, waits for them, and re-layouts  16.3 us
    ppermute x18, starting transfers between devices, swap_x(): return lax.ppermute(a, 'pipe', [(i, i ^ 2) for i in range(4)])  15.7 us
  transfers between devices with their start and end apart: 77, of which 38 were waited for; matrix products, arithmetic and copies ran while one was open for 7% of the time, Pallas kernels for 18%

profile of v6, /device:TPU:0, one launch (start us, length us, event | category | flops | bytes accessed | tf_op | source)
XLA Modules:
  0.0 517.0 jit_solution(8325924176775667866)
XLA Ops:
  15.8 3.0 collective-permute-start.1
  21.9 16.8 %collective-permute-done.1.refs_5_.refs_10_.refs_13_.refs_12_ = bf16[1168,384]{1,0:T(8,128)(2,1)S(1)} collective-permute-done((bf16[1168,384]{1,0:T(8,128)(2,1)S(1)}, bf16[1168,384]{1,0:T(8,128)(2,1)S(1)}, u32[]{:S(2)}, u32[]{:S(2)}) %collective-permute-start.1) | collective-permute-done | bytes 897056 | tf_op jit(solution)/shard_map/ppermute | solution.py:888
  38.8 3.3 collective-permute-done.refs_2_.refs_7_.refs_10_.refs_9_
  48.5 16.0 %collective-permute-done.6.refs_18_.refs_23_.refs_26_.refs_25_ = bf16[1168,384]{1,0:T(8,128)(2,1)S(1)} collective-permute-done((bf16[1168,384]{1,0:T(8,128)(2,1)S(1)}, bf16[1168,384]{1,0:T(8,128)(2,1)S(1)}, u32[]{:S(2)}, u32[]{:S(2)}) %collective-permute-start.6) | collective-permute-done | bytes 897056 | tf_op jit(solution)/shard_map/ppermute | solution.py:882
  64.5 3.0 collective-permute-done.4.refs_3_.refs_8_.refs_11_.refs_10_
  70.2 21.6 %collective-permute-done.10.refs_4_.refs_9_.refs_12_.refs_11_ = bf16[1168,384]{1,0:T(8,128)(2,1)} collective-permute-done((bf16[1168,384]{1,0:T(8,128)(2,1)S(1)}, bf16[1168,384]{1,0:T(8,128)(2,1)}, u32[]{:S(2)}, u32[]{:S(2)}) %collective-permute-start.10) | collective-permute-done | bytes 897056 | tf_op jit(solution)/shard_map/ppermute | solution.py:891
  96.4 18.2 %collective-permute-done.16.refs_8_.refs_13_.refs_16_.refs_15_ = bf16[1168,384]{1,0:T(8,128)(2,1)} collective-permute-done((bf16[1168,384]{1,0:T(8,128)(2,1)}, bf16[1168,384]{1,0:T(8,128)(2,1)}, u32[]{:S(2)}, u32[]{:S(2)}) %collective-permute-start.16) | collective-permute-done | bytes 897056 | tf_op jit(solution)/shard_map/ppermute | solution.py:888
  121.4 24.1 %collective-permute-done.23.refs_19_.refs_24_.refs_27_.refs_26_ = bf16[1168,384]{1,0:T(8,128)(2,1)} collective-permute-done((bf16[1168,384]{1,0:T(8,128)(2,1)}, bf16[1168,384]{1,0:T(8,128)(2,1)}, u32[]{:S(2)}, u32[]{:S(2)}) %collective-permute-start.23) | collective-permute-done | bytes 897056 | tf_op jit(solution)/shard_map/ppermute | solution.py:891
  151.0 2.5 shard_map.239
  154.3 32.9 %shard_map.240 = (bf16[512,2304]{1,0:T(8,128)(2,1)}, bf16[24,128,256]{2,1,0:T(8,128)(2,1)}, bf16[512,768]{1,0:T(8,128)(2,1)}, bf16[512,768]{1,0:T(8,128)(2,1)}, ...) custom-call(s32[8]{0:T(128)} %add_minimum_fusion.refs_0_, ...), custom_call_target="tpu_custom_call" | custom-call | flops 41799999488 | bytes 133000000 | tf_op jit(solution)/shard_map/pallas_call | solution.py:614
  187.2 3.0 all-gather.2.cloned.1.call-done
  192.3 3.2 fusion.58
  195.6 3.5 convolution_convert_fusion.refs_3_.refs_2_
  199.1 3.5 add_convert_fusion.refs_4_.refs_3_
  202.6 20.4 %shard_map.241 = (bf16[512,768]{1,0:T(8,128)(2,1)}, bf16[48,160,128]{2,1,0:T(8,128)(2,1)}, bf16[512,768]{1,0:T(8,128)(2,1)}, f32[512,768]{1,0:T(8,128)}, bf16[51...) custom-call(f32[512,768]{1,0:T(8,128)} %get-tuple-element.182.refs_0_, ...), custom_call_target="tpu_custom_call" | custom-call | flops 23100000256 | bytes 73500000 | tf_op jit(solution)/shard_map/pallas_call | solution.py:614
  223.0 30.7 %shard_map.242 = (f32[512,768]{1,0:T(8,128)}, f32[512,768]{1,0:T(8,128)}, bf16[2,8,768,384]{3,2,1,0:T(8,128)(2,1)}, bf16[2,8,768,384]{3,2,1,0:T(8,128)(2,1)}, f32[8,768]{1,0:T(8,128)}, /*index=5*/f32[1,3072]{1,0:T(1,128)}) custom-call(s32[4]{0:T(128)} %pad_add_fusion.refs_0_.refs_1_, f32[512,768]{1,0:T(8,128)} %get-tuple-element.186.refs_1_, ...), custom_call_target="tpu_custom_call" | custom-call | flops 30799998976 | bytes 98000000 | tf_op jit(solution)/shard_map/pallas_call | solution.py:614
  253.7 20.0 %shard_map.243 = (f32[512,768]{1,0:T(8,128)}, bf16[1280,768]{1,0:T(8,128)(2,1)}, bf16[1280,768]{1,0:T(8,128)(2,1)}, bf16[768,768]{1,0:T(8,128)(2,1)}, bf16[768,768]{1,0:T(8,128)(2,1)}, /*index=5*/f32[8,768]{1,0:T(8,128)}) custom-call(f32[512,768]{1,0:T(8,128)} %get-tuple-element.190.refs_0_, bf16[512,768]{1,0:T(8,128)(2,1)} %get-tuple-element.183.refs_1_, ...), custom_call_target="tpu_custom_call" | custom-call | flops 28600000512 | bytes 91000000 | tf_op jit(solution)/shard_map/pallas_call | solution.py:614
  273.7 4.0 convolution_convert_fusion.2
  277.7 2.3 convolution_convert_fusion.1
  284.5 5.0 collective-permute-done.31
  291.1 3.4 convert_add_fusion
  297.0 18.1 %shard_map.244 = (bf16[512,768]{1,0:T(8,128)(2,1)}, bf16[2,8,384,384]{3,2,1,0:T(8,128)(2,1)}, bf16[2,8,384,384]{3,2,1,0:T(8,128)(2,1)}, f32[8,768]{1,0:T(8,128)}) custom-call(s32[4]{0:T(128)} %pad_add_fusion.refs_0_.refs_1_, f32[512,768]{1,0:T(8,128)} %get-tuple-element.203.refs_1_, bf16[512,768]{1,0:T(8,128)(2,1)} %get-tuple-element.204.refs_2_, ...), custom_call_target="tpu_custom_call" | custom-call | flops 24199999488 | bytes 77000000 | tf_op jit(solution)/shard_map/pallas_call | solution.py:614
  315.9 19.5 %shard_map.245 = (f32[512,768]{1,0:T(8,128)}, bf16[2,8,768,384]{3,2,1,0:T(8,128)(2,1)}, bf16[2,8,768,384]{3,2,1,0:T(8,128)(2,1)}, f32[8,768]{1,0:T(8,128)}, f32[1,3072]{1,0:T(1,128)}) custom-call(s32[4]{0:T(128)} %pad_add_fusion.refs_0_.refs_1_, bf16[512,768]{1,0:T(8,128)(2,1)} %get-tuple-element.215.refs_1_, ...), custom_call_target="tpu_custom_call", output_to_operand_aliasing={{1}: (40, {}), {2}: (41, {})} | custom-call | flops 24199999488 | bytes 77000000 | tf_op jit(solution)/shard_map/pallas_call | solution.py:614
  340.0 18.5 %shard_map.246 = (f32[512,768]{1,0:T(8,128)}, bf16[2,8,384,384]{3,2,1,0:T(8,128)(2,1)}, bf16[2,8,384,384]{3,2,1,0:T(8,128)(2,1)}, f32[8,768]{1,0:T(8,128)}) custom-call(s32[4]{0:T(128)} %pad_add_fusion.refs_0_.refs_1_, f32[512,768]{1,0:T(8,128)} %get-tuple-element.230.refs_1_, ...), custom_call_target="tpu_custom_call", output_to_operand_aliasing={{1}: (41, {}), {2}: (42, {})} | custom-call | flops 24199999488 | bytes 77000000 | tf_op jit(solution)/shard_map/pallas_call | solution.py:614
  359.4 5.6 %fusion.28 = (bf16[768,384]{1,0:T(8,128)(2,1)S(1)}, bf16[768,384]{1,0:T(8,128)(2,1)S(1)}, bf16[768,384]{1,0:T(8,128)(2,1)}, bf16[768,384]{1,0:T(8,128)(2,1)S(1)}...) fusion(bf16[2,4,2,768,384]{4,3,2,1,0:T(8,128)(2,1)} %bitcast.32, ...), kind=kLoop, calls=%fused_computation.61 | loop fusion | flops 8257536 | bytes 12386304 | tf_op jit(solution)/shard_map/convert_element_type | solution.py:961
  372.6 5.0 collective-permute-done.38
  378.3 5.1 collective-permute-done.37
  383.4 2.5 fusion.13
  385.9 3.6 fusion.51
  396.0 2.9 collective-permute-done.46
  399.1 2.6 collective-permute-done.44
  403.4 10.2 %collective-permute-done.41 = bf16[768,384]{1,0:T(8,128)(2,1)S(1)} collective-permute-done((bf16[768,384]{1,0:T(8,128)(2,1)}, bf16[768,384]{1,0:T(8,128)(2,1)S(1)}, u32[]{:S(2)}, u32[]{:S(2)}) %collective-permute-start.41) | collective-permute-done | bytes 589856 | tf_op jit(solution)/shard_map/ppermute | solution.py:888
  413.6 2.9 fusion.11
  421.0 2.6 collective-permute-done.54
  424.5 2.9 collective-permute-done.51
  429.1 3.3 collective-permute-done.53
  432.4 2.6 fusion.33
  435.1 8.7 %collective-permute-done.49 = bf16[768,384]{1,0:T(8,128)(2,1)S(1)} collective-permute-done((bf16[768,384]{1,0:T(8,128)(2,1)S(1)}, bf16[768,384]{1,0:T(8,128)(2,1)S(1)}, u32[]{:S(2)}, u32[]{:S(2)}) %collective-permute-start.49) | collective-permute-done | bytes 589856 | tf_op jit(solution)/shard_map/ppermute | solution.py:891
  443.7 3.9 fusion.9
  450.5 9.2 %collective-permute-done.60 = bf16[384,384]{1,0:T(8,128)(2,1)} collective-permute-done((bf16[384,384]{1,0:T(8,128)(2,1)}, bf16[384,384]{1,0:T(8,128)(2,1)}, u32[]{:S(2)}, u32[]{:S(2)}) %collective-permute-start.60) | collective-permute-done | bytes 294944 | tf_op jit(solution)/shard_map/ppermute | solution.py:891
  461.4 2.7 fusion.29
  464.1 2.2 collective-permute-done.57
  466.3 4.7 collective-permute-done.59
  476.7 4.5 collective-permute-done.64
  484.6 3.0 collective-permute-done.67
  487.6 3.5 collective-permute-done.69
  494.3 2.4 collective-permute-start.75
  502.0 3.2 collective-permute-done.70
  (295 shorter events, 104.9 us)
Async XLA Ops:
  7.2 183.0 %all-gather.2.cloned.1.call-start = ((), (), s32[]{:S(2)}) async-start(), calls=%async_computation | async-start | bytes 5677056 | tf_op jit(solution)/shard_map/all_gather | solution.py:1138
  15.8 22.9 %collective-permute-start.1 = (bf16[1168,384]{1,0:T(8,128)(2,1)S(1)}, bf16[1168,384]{1,0:T(8,128)(2,1)S(1)}, u32[]{:S(2)}, u32[]{:S(2)}) collective-permute-start(bf16[1168,384]{1,0:T(8,128)(2,1)S(1)} %constant_dynamic-update-slice_fusion.refs_1_.refs_6_.refs_9_.refs_8_), channel_id=1, source_target_pairs={{0,1},{1,0},{2,3},{3,2},{4,5},{5,4},{6,7},{7,6},{8,9},{9,8},{10,11... | collective-permute-start | bytes 2691080 | tf_op jit(solution)/shard_map/ppermute | solution.py:888
  18.8 23.2 %collective-permute-start = (bf16[1168,384]{1,0:T(8,128)(2,1)S(1)}, bf16[1168,384]{1,0:T(8,128)(2,1)S(1)}, u32[]{:S(2)}, u32[]{:S(2)}) collective-permute-start(bf16[1168,384]{1,0:T(8,128)(2,1)S(1)} %constant_dynamic-update-slice_fusion.refs_1_.refs_6_.refs_9_.refs_8_), channel_id=1, source_target_pairs={{0,2},{1,3},{2,4},{3,5},{4,6},{5,7},{6,0},{7,1},{8,10},{9,11},{10,... | collective-permute-start | bytes 2691080 | tf_op jit(solution)/shard_map/ppermute | solution.py:891
  20.4 21.7 %collective-permute-start.2 = (bf16[1168,384]{1,0:T(8,128)(2,1)S(1)}, bf16[1168,384]{1,0:T(8,128)(2,1)S(1)}, u32[]{:S(2)}, u32[]{:S(2)}) collective-permute-start(bf16[1168,384]{1,0:T(8,128)(2,1)S(1)} %constant_dynamic-update-slice_fusion.refs_1_.refs_6_.refs_9_.refs_8_), channel_id=1, source_target_pairs={{0,16},{8,24},{16,0},{24,8},{1,17},{9,25},{17,1},{25,9},{2,18},{10... | collective-permute-start | bytes 2691080 | tf_op jit(solution)/shard_map/ppermute | solution.py:882
  21.9 20.2 %collective-permute-start.3 = (bf16[1168,384]{1,0:T(8,128)(2,1)S(1)}, bf16[1168,384]{1,0:T(8,128)(2,1)S(1)}, u32[]{:S(2)}, u32[]{:S(2)}) collective-permute-start(bf16[1168,384]{1,0:T(8,128)(2,1)S(1)} %constant_dynamic-update-slice_fusion.refs_1_.refs_6_.refs_9_.refs_8_), channel_id=1, source_target_pairs={{0,8},{8,0},{16,24},{24,16},{1,9},{9,1},{17,25},{25,17},{2,10},{10... | collective-permute-start | bytes 2691080 | tf_op jit(solution)/shard_map/ppermute | solution.py:885
  42.2 22.3 %collective-permute-start.6 = (bf16[1168,384]{1,0:T(8,128)(2,1)S(1)}, bf16[1168,384]{1,0:T(8,128)(2,1)S(1)}, u32[]{:S(2)}, u32[]{:S(2)}) collective-permute-start(bf16[1168,384]{1,0:T(8,128)(2,1)S(1)} %collective-permute-done.refs_2_.refs_7_.refs_10_.refs_9_), channel_id=1, source_target_pairs={{0,16},{8,24},{16,0},{24,8},{1,17},{9,25},{17,1},{25,9},{2,18},{10... | collective-permute-start | bytes 2691080 | tf_op jit(solution)/shard_map/ppermute | solution.py:882
  43.7 23.8 %collective-permute-start.4 = (bf16[1168,384]{1,0:T(8,128)(2,1)S(1)}, bf16[1168,384]{1,0:T(8,128)(2,1)S(1)}, u32[]{:S(2)}, u32[]{:S(2)}) collective-permute-start(bf16[1168,384]{1,0:T(8,128)(2,1)S(1)} %collective-permute-done.refs_2_.refs_7_.refs_10_.refs_9_), channel_id=1, source_target_pairs={{0,2},{1,3},{2,4},{3,5},{4,6},{5,7},{6,0},{7,1},{8,10},{9,11},{10,... | collective-permute-start | bytes 2691080 | tf_op jit(solution)/shard_map/ppermute | solution.py:891
  44.7 22.8 %collective-permute-start.5 = (bf16[1168,384]{1,0:T(8,128)(2,1)S(1)}, bf16[1168,384]{1,0:T(8,128)(2,1)S(1)}, u32[]{:S(2)}, u32[]{:S(2)}) collective-permute-start(bf16[1168,384]{1,0:T(8,128)(2,1)S(1)} %collective-permute-done.refs_2_.refs_7_.refs_10_.refs_9_), channel_id=1, source_target_pairs={{0,1},{1,0},{2,3},{3,2},{4,5},{5,4},{6,7},{7,6},{8,9},{9,8},{10,11... | collective-permute-start | bytes 2691080 | tf_op jit(solution)/shard_map/ppermute | solution.py:888
  45.2 22.3 %collective-permute-start.8 = (bf16[1168,384]{1,0:T(8,128)(2,1)S(1)}, bf16[1168,384]{1,0:T(8,128)(2,1)S(1)}, u32[]{:S(2)}, u32[]{:S(2)}) collective-permute-start(bf16[1168,384]{1,0:T(8,128)(2,1)S(1)} %collective-permute-done.1.refs_5_.refs_10_.refs_13_.refs_12_), channel_id=1, source_target_pairs={{0,8},{8,0},{16,24},{24,16},{1,9},{9,1},{17,25},{25,17},{2,10},{10... | collective-permute-start | bytes 2691080 | tf_op jit(solution)/shard_map/ppermute | solution.py:885
  46.2 21.3 %collective-permute-start.9 = (bf16[1168,384]{1,0:T(8,128)(2,1)S(1)}, bf16[1168,384]{1,0:T(8,128)(2,1)S(1)}, u32[]{:S(2)}, u32[]{:S(2)}) collective-permute-start(bf16[1168,384]{1,0:T(8,128)(2,1)S(1)} %collective-permute-done.2.refs_17_.refs_22_.refs_25_.refs_24_), channel_id=1, source_target_pairs={{0,8},{8,0},{16,24},{24,16},{1,9},{9,1},{17,25},{25,17},{2,10},{10... | collective-permute-start | bytes 2691080 | tf_op jit(solution)/shard_map/ppermute | solution.py:885
  67.6 24.2 %collective-permute-start.10 = (bf16[1168,384]{1,0:T(8,128)(2,1)S(1)}, bf16[1168,384]{1,0:T(8,128)(2,1)}, u32[]{:S(2)}, u32[]{:S(2)}) collective-permute-start(bf16[1168,384]{1,0:T(8,128)(2,1)S(1)} %collective-permute-done.4.refs_3_.refs_8_.refs_11_.refs_10_), channel_id=1, source_target_pairs={{0,2},{1,3},{2,4},{3,5},{4,6},{5,7},{6,0},{7,1},{8,10},{9,11},{10,... | collective-permute-start | bytes 2691080 | tf_op jit(solution)/shard_map/ppermute | solution.py:891
  68.2 23.7 %collective-permute-start.11 = (bf16[1168,384]{1,0:T(8,128)(2,1)S(1)}, bf16[1168,384]{1,0:T(8,128)(2,1)}, u32[]{:S(2)}, u32[]{:S(2)}) collective-permute-start(bf16[1168,384]{1,0:T(8,128)(2,1)S(1)} %collective-permute-done.4.refs_3_.refs_8_.refs_11_.refs_10_), channel_id=1, source_target_pairs={{0,1},{1,0},{2,3},{3,2},{4,5},{5,4},{6,7},{7,6},{8,9},{9,8},{10,11... | collective-permute-start | bytes 2691080 | tf_op jit(solution)/shard_map/ppermute | solution.py:888
  68.7 23.2 %collective-permute-start.12 = (bf16[1168,384]{1,0:T(8,128)(2,1)S(1)}, bf16[1168,384]{1,0:T(8,128)(2,1)}, u32[]{:S(2)}, u32[]{:S(2)}) collective-permute-start(bf16[1168,384]{1,0:T(8,128)(2,1)S(1)} %collective-permute-done.1.refs_5_.refs_10_.refs_13_.refs_12_), channel_id=1, source_target_pairs={{0,16},{8,24},{16,0},{24,8},{1,17},{9,25},{17,1},{25,9},{2,18},{10... | collective-permute-start | bytes 2691080 | tf_op jit(solution)/shard_map/ppermute | solution.py:882
  69.2 22.7 %collective-permute-start.14 = (bf16[1168,384]{1,0:T(8,128)(2,1)S(1)}, bf16[1168,384]{1,0:T(8,128)(2,1)S(1)}, u32[]{:S(2)}, u32[]{:S(2)}) collective-permute-start(bf16[1168,384]{1,0:T(8,128)(2,1)S(1)} %collective-permute-done.5.refs_6_.refs_11_.refs_14_.refs_13_), channel_id=1, source_target_pairs={{0,8},{8,0},{16,24},{24,16},{1,9},{9,1},{17,25},{25,17},{2,10},{10... | collective-permute-start | bytes 2691080 | tf_op jit(solution)/shard_map/ppermute | solution.py:885
  70.1 21.8 %collective-permute-start.15 = (bf16[1168,384]{1,0:T(8,128)(2,1)S(1)}, bf16[1168,384]{1,0:T(8,128)(2,1)S(1)}, u32[]{:S(2)}, u32[]{:S(2)}) collective-permute-start(bf16[1168,384]{1,0:T(8,128)(2,1)S(1)} %collective-permute-done.6.refs_18_.refs_23_.refs_26_.refs_25_), channel_id=1, source_target_pairs={{0,8},{8,0},{16,24},{24,16},{1,9},{9,1},{17,25},{25,17},{2,10},{10... | collective-permute-start | bytes 2691080 | tf_op jit(solution)/shard_map/ppermute | solution.py:885
  92.0 22.6 %collective-permute-start.16 = (bf16[1168,384]{1,0:T(8,128)(2,1)}, bf16[1168,384]{1,0:T(8,128)(2,1)}, u32[]{:S(2)}, u32[]{:S(2)}) collective-permute-start(bf16[1168,384]{1,0:T(8,128)(2,1)} %collective-permute-done.10.refs_4_.refs_9_.refs_12_.refs_11_), channel_id=1, source_target_pairs={{0,1},{1,0},{2,3},{3,2},{4,5},{5,4},{6,7},{7,6},{8,9},{9,8},{10,11... | collective-permute-start | bytes 2691080 | tf_op jit(solution)/shard_map/ppermute | solution.py:888
  92.6 22.1 %collective-permute-start.18 = (bf16[1168,384]{1,0:T(8,128)(2,1)}, bf16[1168,384]{1,0:T(8,128)(2,1)}, u32[]{:S(2)}, u32[]{:S(2)}) collective-permute-start(bf16[1168,384]{1,0:T(8,128)(2,1)} %collective-permute-done.11.refs_7_.refs_12_.refs_15_.refs_14_), channel_id=1, source_target_pairs={{0,8},{8,0},{16,24},{24,16},{1,9},{9,1},{17,25},{25,17},{2,10},{10... | collective-permute-start | bytes 2691080 | tf_op jit(solution)/shard_map/ppermute | solution.py:885
  92.7 22.5 %collective-permute-start.19 = (bf16[1168,384]{1,0:T(8,128)(2,1)}, bf16[1168,384]{1,0:T(8,128)(2,1)}, u32[]{:S(2)}, u32[]{:S(2)}) collective-permute-start(bf16[1168,384]{1,0:T(8,128)(2,1)} %collective-permute-done.10.refs_4_.refs_9_.refs_12_.refs_11_), channel_id=1, source_target_pairs={{0,16},{8,24},{16,0},{24,8},{1,17},{9,25},{17,1},{25,9},{2,18},{10... | collective-permute-start | bytes 2691080 | tf_op jit(solution)/shard_map/ppermute | solution.py:882
  93.3 24.0 %collective-permute-start.20 = (bf16[1168,384]{1,0:T(8,128)(2,1)}, bf16[1168,384]{1,0:T(8,128)(2,1)}, u32[]{:S(2)}, u32[]{:S(2)}) collective-permute-start(bf16[1168,384]{1,0:T(8,128)(2,1)} %collective-permute-done.12.refs_21_.refs_26_.refs_29_.refs_28_), channel_id=1, source_target_pairs={{0,2},{1,3},{2,4},{3,5},{4,6},{5,7},{6,0},{7,1},{8,10},{9,11},{10,... | collective-permute-start | bytes 2691080 | tf_op jit(solution)/shard_map/ppermute | solution.py:891
  95.5 21.7 %collective-permute-start.21 = (bf16[1168,384]{1,0:T(8,128)(2,1)}, bf16[1168,384]{1,0:T(8,128)(2,1)}, u32[]{:S(2)}, u32[]{:S(2)}) collective-permute-start(bf16[1168,384]{1,0:T(8,128)(2,1)} %collective-permute-done.12.refs_21_.refs_26_.refs_29_.refs_28_), channel_id=1, source_target_pairs={{0,8},{8,0},{16,24},{24,16},{1,9},{9,1},{17,25},{25,17},{2,10},{10... | collective-permute-start | bytes 2691080 | tf_op jit(solution)/shard_map/ppermute | solution.py:885
  117.9 27.7 %collective-permute-start.23 = (bf16[1168,384]{1,0:T(8,128)(2,1)}, bf16[1168,384]{1,0:T(8,128)(2,1)}, u32[]{:S(2)}, u32[]{:S(2)}) collective-permute-start(bf16[1168,384]{1,0:T(8,128)(2,1)} %copy-done.14), channel_id=1, source_target_pairs={{0,2},{1,3},{2,4},{3,5},{4,6},{5,7},{6,0},{7,1},{8,10},{9,11},{10,... | collective-permute-start | bytes 2691080 | tf_op jit(solution)/shard_map/ppermute | solution.py:891
  117.9 27.7 %collective-permute-start.24 = (bf16[1168,384]{1,0:T(8,128)(2,1)}, bf16[1168,384]{1,0:T(8,128)(2,1)}, u32[]{:S(2)}, u32[]{:S(2)}) collective-permute-start(bf16[1168,384]{1,0:T(8,128)(2,1)} %collective-permute-done.11.refs_7_.refs_12_.refs_15_.refs_14_), channel_id=1, source_target_pairs={{0,16},{8,24},{16,0},{24,8},{1,17},{9,25},{17,1},{25,9},{2,18},{10... | collective-permute-start | bytes 2691080 | tf_op jit(solution)/shard_map/ppermute | solution.py:882
  119.4 26.2 %collective-permute-start.25 = (bf16[1168,384]{1,0:T(8,128)(2,1)}, bf16[1168,384]{1,0:T(8,128)(2,1)}, u32[]{:S(2)}, u32[]{:S(2)}) collective-permute-start(bf16[1168,384]{1,0:T(8,128)(2,1)} %collective-permute-done.19.refs_20_.refs_25_.refs_28_.refs_27_), channel_id=1, source_target_pairs={{0,1},{1,0},{2,3},{3,2},{4,5},{5,4},{6,7},{7,6},{8,9},{9,8},{10,11... | collective-permute-start | bytes 2691080 | tf_op jit(solution)/shard_map/ppermute | solution.py:888
  120.9 24.7 %collective-permute-start.27 = (bf16[1168,384]{1,0:T(8,128)(2,1)}, bf16[1168,384]{1,0:T(8,128)(2,1)}, u32[]{:S(2)}, u32[]{:S(2)}) collective-permute-start(bf16[1168,384]{1,0:T(8,128)(2,1)} %collective-permute-done.19.refs_20_.refs_25_.refs_28_.refs_27_), channel_id=1, source_target_pairs={{0,8},{8,0},{16,24},{24,16},{1,9},{9,1},{17,25},{25,17},{2,10},{10... | collective-permute-start | bytes 2691080 | tf_op jit(solution)/shard_map/ppermute | solution.py:885
  295.6 19.6 %collective-permute-start.32 = (bf16[2,2,112,768]{3,2,0,1:T(8,128)(2,1)}, bf16[2,2,112,768]{3,2,0,1:T(8,128)(2,1)}, u32[]{:S(2)}, u32[]{:S(2)}) collective-permute-start(bf16[2,2,112,768]{3,2,0,1:T(8,128)(2,1)} %get-tuple-element.202), channel_id=1, source_target_pairs={{0,16},{8,24},{16,0},{24,8},{1,17},{9,25},{17,1},{25,9},{2,18},{10... | collective-permute-start | bytes 2064392 | tf_op jit(solution)/shard_map/ppermute | solution.py:882
  315.2 20.2 %collective-permute-start.33 = (bf16[2,2,112,768]{3,2,0,1:T(8,128)(2,1)S(1)}, bf16[2,2,112,768]{3,2,0,1:T(8,128)(2,1)}, u32[]{:S(2)}, u32[]{:S(2)}) collective-permute-start(bf16[2,2,112,768]{3,2,0,1:T(8,128)(2,1)S(1)} %get-tuple-element.214), channel_id=1, source_target_pairs={{0,16},{8,24},{16,0},{24,8},{1,17},{9,25},{17,1},{25,9},{2,18},{10... | collective-permute-start | bytes 2064392 | tf_op jit(solution)/shard_map/ppermute | solution.py:882
  338.5 20.9 %collective-permute-start.34 = (bf16[2,8,768,384]{3,2,1,0:T(8,128)(2,1)}, bf16[2,8,768,384]{3,2,1,0:T(8,128)(2,1)}, u32[]{:S(2)}, u32[]{:S(2)}) collective-permute-start(bf16[2,8,768,384]{3,2,1,0:T(8,128)(2,1)} %get-tuple-element.228), channel_id=1, source_target_pairs={{0,8},{8,0},{16,24},{24,16},{1,9},{9,1},{17,25},{25,17},{2,10},{10... | collective-permute-start | bytes 28311560 | tf_op jit(solution)/shard_map/ppermute | solution.py:885
  338.5 20.0 %collective-permute-start.35 = (bf16[4,112,768]{2,1,0:T(8,128)(2,1)S(1)}, bf16[4,112,768]{2,1,0:T(8,128)(2,1)S(1)}, u32[]{:S(2)}, u32[]{:S(2)}) collective-permute-start(bf16[4,112,768]{2,1,0:T(8,128)(2,1)S(1)} %fusion.21), channel_id=1, source_target_pairs={{0,1},{1,0},{2,3},{3,2},{4,5},{5,4},{6,7},{7,6},{8,9},{9,8},{10,11... | collective-permute-start | bytes 2064392 | tf_op jit(solution)/shard_map/ppermute | solution.py:888
  365.0 20.8 %collective-permute-start.36 = (bf16[2,8,384,384]{3,2,1,0:T(8,128)(2,1)}, bf16[2,8,384,384]{3,2,1,0:T(8,128)(2,1)}, u32[]{:S(2)}, u32[]{:S(2)}) collective-permute-start(bf16[2,8,384,384]{3,2,1,0:T(8,128)(2,1)} %get-tuple-element.240), channel_id=1, source_target_pairs={{0,8},{8,0},{16,24},{24,16},{1,9},{9,1},{17,25},{25,17},{2,10},{10... | collective-permute-start | bytes 14155784 | tf_op jit(solution)/shard_map/ppermute | solution.py:885
  367.5 15.9 %collective-permute-start.37 = (bf16[768,384]{1,0:T(8,128)(2,1)}, bf16[768,384]{1,0:T(8,128)(2,1)}, u32[]{:S(2)}, u32[]{:S(2)}) collective-permute-start(bf16[768,384]{1,0:T(8,128)(2,1)} %get-tuple-element.241), channel_id=1, source_target_pairs={{0,1},{1,0},{2,3},{3,2},{4,5},{5,4},{6,7},{7,6},{8,9},{9,8},{10,11... | collective-permute-start | bytes 1769480 | tf_op jit(solution)/shard_map/ppermute | solution.py:888
  370.4 19.1 %collective-permute-start.39 = (bf16[768,384]{1,0:T(8,128)(2,1)}, bf16[768,384]{1,0:T(8,128)(2,1)}, u32[]{:S(2)}, u32[]{:S(2)}) collective-permute-start(bf16[768,384]{1,0:T(8,128)(2,1)} %get-tuple-element.246), channel_id=1, source_target_pairs={{0,2},{1,3},{2,4},{3,5},{4,6},{5,7},{6,0},{7,1},{8,10},{9,11},{10,... | collective-permute-start | bytes 1769480 | tf_op jit(solution)/shard_map/ppermute | solution.py:891
  371.2 18.3 %collective-permute-start.40 = (bf16[768,384]{1,0:T(8,128)(2,1)}, bf16[768,384]{1,0:T(8,128)(2,1)}, u32[]{:S(2)}, u32[]{:S(2)}) collective-permute-start(bf16[768,384]{1,0:T(8,128)(2,1)} %get-tuple-element.247), channel_id=1, source_target_pairs={{0,16},{8,24},{16,0},{24,8},{1,17},{9,25},{17,1},{25,9},{2,18},{10... | collective-permute-start | bytes 1769480 | tf_op jit(solution)/shard_map/ppermute | solution.py:882
  392.2 21.4 %collective-permute-start.41 = (bf16[768,384]{1,0:T(8,128)(2,1)}, bf16[768,384]{1,0:T(8,128)(2,1)S(1)}, u32[]{:S(2)}, u32[]{:S(2)}) collective-permute-start(bf16[768,384]{1,0:T(8,128)(2,1)} %get-tuple-element.248), channel_id=1, source_target_pairs={{0,1},{1,0},{2,3},{3,2},{4,5},{5,4},{6,7},{7,6},{8,9},{9,8},{10,11... | collective-permute-start | bytes 1769480 | tf_op jit(solution)/shard_map/ppermute | solution.py:888
  393.7 19.9 %collective-permute-start.42 = (bf16[768,384]{1,0:T(8,128)(2,1)}, bf16[768,384]{1,0:T(8,128)(2,1)S(1)}, u32[]{:S(2)}, u32[]{:S(2)}) collective-permute-start(bf16[768,384]{1,0:T(8,128)(2,1)} %fusion.13), channel_id=1, source_target_pairs={{0,16},{8,24},{16,0},{24,8},{1,17},{9,25},{17,1},{25,9},{2,18},{10... | collective-permute-start | bytes 1769480 | tf_op jit(solution)/shard_map/ppermute | solution.py:882
  394.1 19.5 %collective-permute-start.43 = (bf16[768,384]{1,0:T(8,128)(2,1)S(1)}, bf16[768,384]{1,0:T(8,128)(2,1)S(1)}, u32[]{:S(2)}, u32[]{:S(2)}) collective-permute-start(bf16[768,384]{1,0:T(8,128)(2,1)S(1)} %get-tuple-element.250), channel_id=1, source_target_pairs={{0,2},{1,3},{2,4},{3,5},{4,6},{5,7},{6,0},{7,1},{8,10},{9,11},{10,... | collective-permute-start | bytes 1769480 | tf_op jit(solution)/shard_map/ppermute | solution.py:891
  398.9 18.5 %collective-permute-start.47 = (bf16[384,384]{1,0:T(8,128)(2,1)}, bf16[384,384]{1,0:T(8,128)(2,1)S(1)}, u32[]{:S(2)}, u32[]{:S(2)}) collective-permute-start(bf16[384,384]{1,0:T(8,128)(2,1)} %get-tuple-element.254), channel_id=1, source_target_pairs={{0,2},{1,3},{2,4},{3,5},{4,6},{5,7},{6,0},{7,1},{8,10},{9,11},{10,... | collective-permute-start | bytes 884744 | tf_op jit(solution)/shard_map/ppermute | solution.py:891
  401.7 15.6 %collective-permute-start.48 = (bf16[384,384]{1,0:T(8,128)(2,1)}, bf16[384,384]{1,0:T(8,128)(2,1)S(1)}, u32[]{:S(2)}, u32[]{:S(2)}) collective-permute-start(bf16[384,384]{1,0:T(8,128)(2,1)} %get-tuple-element.255), channel_id=1, source_target_pairs={{0,16},{8,24},{16,0},{24,8},{1,17},{9,25},{17,1},{25,9},{2,18},{10... | collective-permute-start | bytes 884744 | tf_op jit(solution)/shard_map/ppermute | solution.py:882
  420.7 23.1 %collective-permute-start.49 = (bf16[768,384]{1,0:T(8,128)(2,1)S(1)}, bf16[768,384]{1,0:T(8,128)(2,1)S(1)}, u32[]{:S(2)}, u32[]{:S(2)}) collective-permute-start(bf16[768,384]{1,0:T(8,128)(2,1)S(1)} %get-tuple-element.256), channel_id=1, source_target_pairs={{0,2},{1,3},{2,4},{3,5},{4,6},{5,7},{6,0},{7,1},{8,10},{9,11},{10,... | collective-permute-start | bytes 1769480 | tf_op jit(solution)/shard_map/ppermute | solution.py:891
  423.7 20.1 %collective-permute-start.50 = (bf16[768,384]{1,0:T(8,128)(2,1)S(1)}, bf16[768,384]{1,0:T(8,128)(2,1)S(1)}, u32[]{:S(2)}, u32[]{:S(2)}) collective-permute-start(bf16[768,384]{1,0:T(8,128)(2,1)S(1)} %get-tuple-element.257), channel_id=1, source_target_pairs={{0,1},{1,0},{2,3},{3,2},{4,5},{5,4},{6,7},{7,6},{8,9},{9,8},{10,11... | collective-permute-start | bytes 1769480 | tf_op jit(solution)/shard_map/ppermute | solution.py:888
  427.4 16.4 %collective-permute-start.55 = (bf16[768,384]{1,0:T(8,128)(2,1)S(1)}, bf16[768,384]{1,0:T(8,128)(2,1)S(1)}, u32[]{:S(2)}, u32[]{:S(2)}) collective-permute-start(bf16[768,384]{1,0:T(8,128)(2,1)S(1)} %get-tuple-element.262), channel_id=1, source_target_pairs={{0,16},{8,24},{16,0},{24,8},{1,17},{9,25},{17,1},{25,9},{2,18},{10... | collective-permute-start | bytes 1769480 | tf_op jit(solution)/shard_map/ppermute | solution.py:882
  428.8 18.8 %collective-permute-start.56 = (bf16[112,768]{1,0:T(8,128)(2,1)S(1)}, bf16[112,768]{1,0:T(8,128)(2,1)S(1)}, u32[]{:S(2)}, u32[]{:S(2)}) collective-permute-start(bf16[112,768]{1,0:T(8,128)(2,1)S(1)} %fusion.43), channel_id=1, source_target_pairs={{0,2},{1,3},{2,4},{3,5},{4,6},{5,7},{6,0},{7,1},{8,10},{9,11},{10,... | collective-permute-start | bytes 516104 | tf_op jit(solution)/shard_map/ppermute | solution.py:891
  447.6 12.1 %collective-permute-start.60 = (bf16[384,384]{1,0:T(8,128)(2,1)}, bf16[384,384]{1,0:T(8,128)(2,1)}, u32[]{:S(2)}, u32[]{:S(2)}) collective-permute-start(bf16[384,384]{1,0:T(8,128)(2,1)} %get-tuple-element.267), channel_id=1, source_target_pairs={{0,2},{1,3},{2,4},{3,5},{4,6},{5,7},{6,0},{7,1},{8,10},{9,11},{10,... | collective-permute-start | bytes 884744 | tf_op jit(solution)/shard_map/ppermute | solution.py:891
  447.6 12.8 %collective-permute-start.61 = (bf16[384,384]{1,0:T(8,128)(2,1)}, bf16[384,384]{1,0:T(8,128)(2,1)S(1)}, u32[]{:S(2)}, u32[]{:S(2)}) collective-permute-start(bf16[384,384]{1,0:T(8,128)(2,1)} %get-tuple-element.268), channel_id=1, source_target_pairs={{0,1},{1,0},{2,3},{3,2},{4,5},{5,4},{6,7},{7,6},{8,9},{9,8},{10,11... | collective-permute-start | bytes 884744 | tf_op jit(solution)/shard_map/ppermute | solution.py:888
  448.8 12.6 %collective-permute-start.62 = (bf16[384,384]{1,0:T(8,128)(2,1)}, bf16[384,384]{1,0:T(8,128)(2,1)S(1)}, u32[]{:S(2)}, u32[]{:S(2)}) collective-permute-start(bf16[384,384]{1,0:T(8,128)(2,1)} %get-tuple-element.269), channel_id=1, source_target_pairs={{0,16},{8,24},{16,0},{24,8},{1,17},{9,25},{17,1},{25,9},{2,18},{10... | collective-permute-start | bytes 884744 | tf_op jit(solution)/shard_map/ppermute | solution.py:882
  449.3 17.0 %collective-permute-start.57 = (bf16[768,384]{1,0:T(8,128)(2,1)}, bf16[768,384]{1,0:T(8,128)(2,1)S(1)}, u32[]{:S(2)}, u32[]{:S(2)}) collective-permute-start(bf16[768,384]{1,0:T(8,128)(2,1)} %get-tuple-element.264), channel_id=1, source_target_pairs={{0,2},{1,3},{2,4},{3,5},{4,6},{5,7},{6,0},{7,1},{8,10},{9,11},{10,... | collective-permute-start | bytes 1769480 | tf_op jit(solution)/shard_map/ppermute | solution.py:891
  449.3 17.0 %collective-permute-start.58 = (bf16[768,384]{1,0:T(8,128)(2,1)S(1)}, bf16[768,384]{1,0:T(8,128)(2,1)S(1)}, u32[]{:S(2)}, u32[]{:S(2)}) collective-permute-start(bf16[768,384]{1,0:T(8,128)(2,1)S(1)} %get-tuple-element.265), channel_id=1, source_target_pairs={{0,1},{1,0},{2,3},{3,2},{4,5},{5,4},{6,7},{7,6},{8,9},{9,8},{10,11... | collective-permute-start | bytes 1769480 | tf_op jit(solution)/shard_map/ppermute | solution.py:888
  460.4 12.2 %collective-permute-start.63 = (f32[4,16,128]{2,1,0:T(8,128)S(1)}, f32[4,16,128]{2,1,0:T(8,128)S(1)}, u32[]{:S(2)}, u32[]{:S(2)}) collective-permute-start(f32[4,16,128]{2,1,0:T(8,128)S(1)} %dynamic-slice_bitcast_fusion.3), channel_id=1, source_target_pairs={{0,1},{1,0},{2,3},{3,2},{4,5},{5,4},{6,7},{7,6},{8,9},{9,8},{10,11... | collective-permute-start | bytes 98312 | tf_op jit(solution)/shard_map/ppermute | solution.py:888
  475.6 11.9 %collective-permute-start.67 = (bf16[768,384]{1,0:T(8,128)(2,1)S(1)}, bf16[768,384]{1,0:T(8,128)(2,1)S(1)}, u32[]{:S(2)}, u32[]{:S(2)}) collective-permute-start(bf16[768,384]{1,0:T(8,128)(2,1)S(1)} %fusion.20), channel_id=1, source_target_pairs={{0,2},{1,3},{2,4},{3,5},{4,6},{5,7},{6,0},{7,1},{8,10},{9,11},{10,... | collective-permute-start | bytes 1769480 | tf_op jit(solution)/shard_map/ppermute | solution.py:891
  (75 other events, 1264.4 us)
Sparse Core Ops, SparseCore 0:
  117.4 72.7 all-gather.1

commit v7 on v6

--- a/solution.py
+++ b/solution.py
@@ -19,6 +19,7 @@
 VMEM_BYTES = 58 * 2**20
 TILE = 768
 CHUNK = 128
+SMALL = 16
 
 
 def dot(a, b, dims=NN):
@@ -255,8 +256,8 @@
     g_ref[:width, :] = dot(db_ref[...], rel_ref[...], TN).astype(BF)
     for b in range(8):
         to, at = relative(where_ref, b), pl.ds(b * m, m)
-        own_ref[to, n:, :] = g_ref[at, :half]
-        other_ref[to, n:, :] = g_ref[at, half:]
+        own_ref[to, n : n + m, :] = g_ref[at, :half]
+        other_ref[to, n : n + m, :] = g_ref[at, half:]
     io.begin(x_ref)
     first = fetch(placed(refs[:1] if whole else refs, where_ref, [(0, n, 0)], qkv, half), sems, here)
     pairs = width // 128
@@ -288,7 +289,7 @@
         to, at = relative(where_ref, b), pl.ds(b * n, n)
         own_ref[to, :n, :] = g_ref[at, :half]
         other_ref[to, :n, :] = g_ref[at, half:]
-    io.send(other_ref, own_ref)
+    io.send(other_ref, own_ref, part=(slice(None), pl.ds(0, n + m)))
     settle(first)
 
     def back(j):
@@ -303,21 +304,9 @@
     gv_ref[4:5, :] = g_offset
 
 
-def cross_forward_kernel(io, ins, outs, scratch):
-    x_ref, low_x_ref, keep_ref, k_ref, v_ref, vec_ref, wq_ref, wo_ref = ins
-    q_ref, a_ref, o_ref, y_ref, low_ref, n_ref, r_ref = outs
-    io.begin(k_ref, v_ref)
-    width = x_ref.shape[1]
+def cross_attend(keep_ref, q_ref, k_ref, v_ref, a_ref, o_ref):
+    width = o_ref.shape[1]
     patches = k_ref.shape[0] // keep_ref.shape[0]
-
-    def tile(j):
-        cols = span(j * TILE, TILE)
-        q_ref[:, cols] = (dot(low_x_ref[...], wq_ref[:, cols]) + vec_ref[0:1, cols]).astype(BF)
-
-    tiles(width // TILE, tile)
-    io.send(q_ref)
-    io.need(k_ref, v_ref)
-    io.begin(x_ref, wo_ref)
     pairs = width // 128
 
     def attend(s):
@@ -332,11 +321,6 @@
             o_ref[rows, pl.ds(h * 128, 128)] = join_heads(dot(a, v)).astype(BF)
 
     tiles(keep_ref.shape[0], attend)
-    io.send(a_ref, o_ref)
-    io.need(x_ref, wo_ref)
-    project_and_norm(
-        x_ref, o_ref, wo_ref, NN, vec_ref[2:3, :], vec_ref[3:4, :], vec_ref[4:5, :], (y_ref, low_ref, n_ref, r_ref)
-    )
 
 
 def cross_backward_kernel(io, ins, outs, scratch):
@@ -468,8 +452,8 @@
 def feed_backward_body(
     io, where_ref, dy_ref, low_x_ref, vec_ref, act_ref, slope_ref, n_ref, r_ref, outs, work, up, down, get_up, get_down
 ):
-    dx_ref, own_ref, other_ref, gv_ref, gb_ref = outs
-    db_ref, dbt_ref, dh_ref, rel_ref = work
+    dx_ref, own_ref, other_ref, gv_ref = outs
+    db_ref, dbt_ref, dh_ref, rel_ref, gb_ref = work
     width, hidden = up.shape[1], up.shape[0]
     n, m, half = hidden // 8, width // 8, width // 2
     core = where_ref[0]
@@ -524,6 +508,8 @@
     gv_ref[0:1, :] = g_bias
     gv_ref[1:2, :] = g_gain
     gv_ref[2:3, :] = g_offset
+    for j in range(hidden // width):
+        gv_ref[3 + j : 4 + j, :] = gb_ref[:, j * width : (j + 1) * width]
 
 
 def feed_backward_kernel(count, layer, io, ins, outs, scratch):
@@ -535,22 +521,37 @@
     )
 
 
-def feed_both_kernel(count, layer, io, ins, outs, scratch):
-    where_ref, x_ref, low_x_ref, vec_ref, bias_ref, dy_ref, *refs = ins
-    y_ref, *grads = outs
-    up, down, *work, act_ref, slope_ref, low_ref, n_ref, r_ref, sems, sems2 = scratch
-    get = feed_weights(count, layer, where_ref, refs, up, down, sems, sems2)
-    settle(get[0]())
-    second = get[1]()
-    io.begin(x_ref)
-    feed_activate(low_x_ref, up, bias_ref, act_ref, slope_ref)
+def joining_kernel(count, io, ins, outs, scratch):
+    where_ref, x_ref, low_x_ref, keep_ref, k_ref, v_ref, cross_ref, wq_ref, wo_ref, vec_ref, bias_ref, dy_ref, *refs = ins
+    q_ref, a_ref, o_ref, cross_n, cross_r, y_ref, *grads = outs
+    up, down, *work, act_ref, slope_ref, state, low_state, low_ref, n_ref, r_ref, sems, sems2 = scratch
+    get_up, get_down = feed_weights(count, 1, where_ref, refs, up, down, sems, sems2)
+    width = x_ref.shape[1]
+    io.begin(k_ref, v_ref)
+
+    def tile(j):
+        cols = span(j * TILE, TILE)
+        q_ref[:, cols] = (dot(low_x_ref[...], wq_ref[:, cols]) + cross_ref[0:1, cols]).astype(BF)
+
+    tiles(width // TILE, tile)
+    io.need(k_ref, v_ref)
+    io.begin(x_ref, wo_ref)
+    first = get_up()
+    cross_attend(keep_ref, q_ref, k_ref, v_ref, a_ref, o_ref)
+    io.send(q_ref, a_ref, o_ref)
+    io.need(x_ref, wo_ref)
+    norm = cross_ref[2:3, :], cross_ref[3:4, :], cross_ref[4:5, :]
+    project_and_norm(x_ref, o_ref, wo_ref, NN, *norm, (state, low_state, cross_n, cross_r))
+    io.send(cross_n)
+    second = get_down()
+    settle(first)
+    feed_activate(low_state, up, bias_ref, act_ref, slope_ref)
     settle(second)
-    io.need(x_ref)
     norm = vec_ref[5:6, :], vec_ref[6:7, :], vec_ref[7:8, :]
-    project_and_norm(x_ref, act_ref, down, NT, *norm, (y_ref, low_ref, n_ref, r_ref))
+    project_and_norm(state, act_ref, down, NT, *norm, (y_ref, low_ref, n_ref, r_ref))
     io.send(y_ref)
     feed_backward_body(
-        io, where_ref, dy_ref, low_x_ref, vec_ref, act_ref, slope_ref, n_ref, r_ref, grads, work, up, down, list, list
+        io, where_ref, dy_ref, low_state, vec_ref, act_ref, slope_ref, n_ref, r_ref, grads, work, up, down, list, list
     )
 
 
@@ -694,8 +695,8 @@
     count = len(weights)
     outs = [
         struct(rows, width, dtype=dtype),
-        struct(8, width // 2, half, dtype=BF),
-        struct(8, width // 2, half, dtype=BF),
+        struct(8, width // 2 + SMALL, half, dtype=BF),
+        struct(8, width // 2 + SMALL, half, dtype=BF),
         struct(8, width),
     ]
     scratch = [
@@ -724,31 +725,6 @@
     )
 
 
-def cross_forward(x, low_x, keep, k, v, vec, wq, wo):
-    rows, width = x.shape
-    samples, patches = keep.shape
-    outs = [
-        struct(rows, width, dtype=BF),
-        struct(samples * (width // 128), patches, 128, dtype=BF),
-        struct(rows, width, dtype=BF),
-        struct(rows, width),
-        struct(rows, width, dtype=BF),
-        struct(rows, width, dtype=BF),
-        struct(rows, 1),
-    ]
-    q, a, o, y, low, n, r = call(
-        cross_forward_kernel,
-        outs,
-        [VMEM] * 8,
-        [],
-        21,
-        (x, low_x, keep, k, v, vec, wq, wo),
-        late=(3, 4, 7, 0),
-        early=(0, 1, 2),
-    )
-    return y, low, (low_x, k, v, q, a, o, n, r)
-
-
 def cross_backward(dy, saved, vec, wq, wo):
     low_x, k, v, q, a, o, n, r = saved
     rows, width = low_x.shape
@@ -783,7 +759,6 @@
         struct(8, 2 * hidden // 8, width // 2, dtype=BF),
         struct(8, 2 * hidden // 8, width // 2, dtype=BF),
         struct(8, width),
-        struct(1, hidden),
     ]
     scratch = [
         pltpu.VMEM((hidden, width), BF),
@@ -792,6 +767,7 @@
         pltpu.VMEM((width, rows), BF),
         pltpu.VMEM((rows, hidden), BF),
         pltpu.VMEM((rows, width), BF),
+        pltpu.VMEM((1, hidden), F32),
         copy_sems(count),
         copy_sems(count, hidden // width),
     ]
@@ -809,17 +785,24 @@
     )
 
 
-def feed_both(x, low_x, where, vec, bias, dy, weights, layer):
+def joining(x, low_x, where, keep, k, v, cross_vec, wq, wo, vec, bias, dy, weights):
     rows, width = x.shape
+    samples, patches = keep.shape
     hidden = bias.shape[1]
     count = len(weights)
+    low = struct(rows, width, dtype=BF)
+    pack = struct(8, 2 * hidden // 8, width // 2, dtype=BF)
     outs = [
+        low,
+        struct(samples * (width // 128), patches, 128, dtype=BF),
+        low,
+        low,
+        struct(rows, 1),
         struct(rows, width),
         struct(rows, width),
-        struct(8, 2 * hidden // 8, width // 2, dtype=BF),
-        struct(8, 2 * hidden // 8, width // 2, dtype=BF),
+        pack,
+        pack,
         struct(8, width),
-        struct(1, hidden),
     ]
     scratch = [
         pltpu.VMEM((hidden, width), BF),
@@ -828,26 +811,30 @@
         pltpu.VMEM((width, rows), BF),
         pltpu.VMEM((rows, hidden), BF),
         pltpu.VMEM((rows, width), BF),
+        pltpu.VMEM((1, hidden), F32),
         pltpu.VMEM((rows, hidden), BF),
         pltpu.VMEM((rows, hidden), BF),
+        pltpu.VMEM((rows, width), F32),
+        pltpu.VMEM((rows, width), BF),
         pltpu.VMEM((rows, width), BF),
         pltpu.VMEM((rows, width), BF),
         pltpu.VMEM((rows, 1), F32),
         copy_sems(count),
         copy_sems(count, hidden // width),
     ]
-    return call(
-        partial(feed_both_kernel, count, layer),
+    q, a, o, n, r, joined, dx, own, other, gv = call(
+        partial(joining_kernel, count),
         outs,
-        [SMEM] + [VMEM] * 5 + [ANYWHERE] * count,
+        [SMEM] + [VMEM] * 11 + [ANYWHERE] * count,
         scratch,
-        28,
-        (where, x, low_x, vec, bias, dy, *weights),
-        late=(1,),
-        early=(0,),
-        packs=(2, 3),
-        layer=layer,
+        48,
+        (where, x, low_x, keep, k, v, cross_vec, wq, wo, vec, bias, dy, *weights),
+        late=(4, 5, 8, 1),
+        early=(0, 1, 2, 3, 5),
+        packs=(7, 8),
+        layer=1,
     )
+    return (low_x, k, v, q, a, o, n, r), joined, dx, own, other, gv
 
 
 def lane_slices(a, lanes):
@@ -889,6 +876,11 @@
 
     def ring_z(self, a, step=1):
         return lax.ppermute(a, "dp", [(i, (i + 2 * step) % 8) for i in range(8)])
+
+    def by_distance(self, a):
+        for axis, place in ((0, self.x), (1, self.core), (3, self.y)):
+            a = jnp.where(place == 0, a, jnp.flip(a, axis))
+        return lax.dynamic_slice_in_dim(jnp.concatenate([a, a], axis=2), self.z, 4, 2)
 
     def turn(self, *moves, pre=(), compute=None, args=(), chain=False):
         tokens = (*self.arrived[-self.slack], *self.computed)
@@ -992,9 +984,6 @@
     def c(self):
         return self.step(self.grid.swap_core, self.grid.core, 1)
 
-    def x(self):
-        return self.step(self.grid.swap_x, self.grid.x, 0)
-
     def x0(self):
         self.halves = [dynamic(self.a, place, 0) for place in (self.grid.x, 1 - self.grid.x)]
         return self.x_half(0)
@@ -1022,13 +1011,8 @@
         value = dynamic(self.a, (self.grid.z + step) % 4, 0).astype(F32)
         return value + self.ring[-1].astype(F32) if self.ring else value
 
-    def z(self):
-        steps = [dynamic(self.a, (self.grid.z + k) % 4, 0) for k in range(4)]
-        self.ring = [steps[0]]
-        return [(partial(self.grid.ring_z, step=k), steps[k].astype(self.dtype), self.ring.append) for k in (1, 2, 3)]
-
     def total(self):
-        return self.block(0) if len(self.ring) == 3 else sum(a.astype(F32) for a in self.ring)
+        return self.block(0)
 
 
 def masks(caption_len, phrase_len, box_count, patch_mask, text_rows, patches):
@@ -1108,8 +1092,8 @@
         grads = [g_cq, g_co, dot(image, dk, TN).astype(BF), dot(image, dv, TN).astype(BF)]
         return jnp.concatenate([g.reshape(shards, -1, width) for g in grads], axis=1)
 
-    def vector_block(v_self, v_feed, v_up):
-        v = jnp.concatenate([v_self[:5], v_feed[:3], v_up.reshape(4, width)], axis=0)
+    def vector_block(v_self, v_feed):
+        v = jnp.concatenate([v_self[:5], v_feed[:7]], axis=0)
         return jnp.moveaxis(v.reshape(half, v_rows, n_dp, v_lanes), 2, 1)
 
     def pack_vectors(text, joining, v_cross):
@@ -1141,8 +1125,9 @@
         state, low, s_self, s_feed, s_self2 = text_forward(x, lengths, where, vecs, biases[0], weights)
         wq, wo, wk, wv = cross_weights(cross_whole)
         keys, values = keys_values(image, wk, wv, cvec)
-        state, low, s_cross = cross_forward(state, low, patch_keep, keys, values, cvec, wq, wo)
-        joined, grad, *g_feed2, v_feed2, v_up2 = feed_both(state, low, where, vecs[1], biases[1], seed, weights, 1)
+        s_cross, joined, grad, *g_feed2, v_feed2 = joining(
+            state, low, where, patch_keep, keys, values, cvec, wq, wo, vecs[1], biases[1], seed, weights
+        )
         grid.computed = (grad,)
 
         def fourth(grad):
@@ -1156,7 +1141,7 @@
             sum_cross.x0,
             compute=lambda grad: self_backward(grad, s_self2, where, vecs[1], weights, 1, BF), args=(grad,),
         )
-        grad, *g_feed, v_feed, v_up = turn(
+        grad, *g_feed, v_feed = turn(
             sum_cross.x1,
             compute=lambda grad: feed_backward(grad, s_feed, where, vecs[0], weights, 0, g_feed2), args=(grad,),
         )
@@ -1165,24 +1150,30 @@
             feed.c, sum_cross.y,
             compute=lambda grad: self_backward(grad, s_self, where, vecs[0], weights, 0, F32, g_self), args=(grad,),
         )
+        vectors = pack_vectors((v_self, v_feed), (v_self2, v_feed2), v_cross)
+        vectors = grid.by_distance(vectors.reshape(2, 2, 4, 2, SMALL, 128))
+        rows = g_self[0].shape[2] - SMALL
+        for k in range(2):
+            small = jnp.pad(vectors[:, k].reshape(2, 8, SMALL, 128), ((0, 0), (0, 0), (0, 0), (0, lanes - 128)))
+            g_self[k] = lax.dynamic_update_slice(g_self[k], small.astype(BF), (0, 0, rows, 0))
         attn = PairSum(grid, *g_self)
-        sum_vec = BlockSum(
-            grid,
-            pack_vectors((v_self, v_feed, v_up), (v_self2, v_feed2, v_up2), v_cross).reshape(2, 2, 4, 2, 16, 128),
-            F32,
-        )
         f0, f1, f2, f3, f4 = feed.steps()
         a0, a1, a2, a3, a4 = attn.steps()
         turn(*f0, attn.c, sum_cross.round)
-        turn(*f1, *a0, sum_vec.c, sum_cross.round)
-        turn(*f2, *a1, sum_vec.x, sum_cross.round)
-        turn(*f3, *a2, sum_vec.y)
-        turn(*f4, *a3)
-        turn(*a4, sum_vec.z)
+        turn(*f1)
+        grid.slack = 2
+        turn(*a0)
+        turn(*f2)
+        turn(*a1)
+        turn(*f3)
+        turn(*a2, sum_cross.round)
+        turn(*f4)
+        turn(*a3, sum_cross.round)
+        turn(*a4)
         attn_grads, feed_grads = attn.total(), feed.total()
         n_qkv, n_up = attn_qkv.shape[1], ffn_up.shape[1]
-        mine = [attn_grads[:n_qkv], attn_grads[n_qkv:], feed_grads[:n_up], feed_grads[n_up:]]
-        cross_grads, small = sum_cross.total(), sum_vec.total()
+        mine = [attn_grads[:n_qkv], attn_grads[n_qkv:rows], feed_grads[:n_up], feed_grads[n_up:]]
+        cross_grads, small = sum_cross.total(), attn_grads[rows:, :128]
     else:
         where = jnp.zeros((4,), jnp.int32)
         image = padded(image_feats)
@@ -1205,11 +1196,12 @@
             x, lengths, where, vecs, biases[0], [qkv1, out1, up1, down1, qkv2, out2]
         )
         keys, values = keys_values(image, wk, wv, cvec)
-        state, low, s_cross = cross_forward(state, low, patch_keep, keys, values, cvec, wq, wo)
-        joined, grad, *g_feed2, v_feed2, v_up2 = feed_both(state, low, where, vecs[1], biases[1], seed, [up2, down2], 1)
+        s_cross, joined, grad, *g_feed2, v_feed2 = joining(
+            state, low, where, patch_keep, keys, values, cvec, wq, wo, vecs[1], biases[1], seed, [up2, down2]
+        )
         grad, dk, dv, g_cq, g_co, v_cross = cross_backward(grad, s_cross, cvec, wq, wo)
         grad, *g_self, v_self2 = self_backward(grad, s_self2, where, vecs[1], [qkv2, out2], 1, BF)
-        grad, *g_feed, v_feed, v_up = feed_backward(grad, s_feed, where, vecs[0], [up1, down1], 0, g_feed2)
+        grad, *g_feed, v_feed = feed_backward(grad, s_feed, where, vecs[0], [up1, down1], 0, g_feed2)
         embed_grad, *g_self, v_self = self_backward(grad, s_self, where, vecs[0], [qkv1, out1], 0, F32, g_self)
         g_self1, g_self2 = ([g[k] for g in g_self] for k in range(2))
         g_feed1, g_feed2 = ([g[k] for g in g_feed] for k in range(2))
@@ -1240,7 +1232,7 @@
         mine = [packed[a:b] for a, b in zip(ends[:-1], ends[1:])]
         cross_grads = pack_cross(image, dk, dv, g_cq, g_co).reshape(-1, width)
         cross_grads = lax.psum_scatter(cross_grads, everyone, scatter_dimension=0, tiled=True).astype(F32)
-        small = pack_vectors((v_self, v_feed, v_up), (v_self2, v_feed2, v_up2), v_cross)
+        small = pack_vectors((v_self, v_feed), (v_self2, v_feed2), v_cross)
         small = lax.psum_scatter(small.reshape(-1, 128), everyone, scatter_dimension=0, tiled=True)
     mine[3] = lane_join(mine[3], hidden // width)
     return (

time: 526 us -> 517 us (0.983)
  waiting for transfers between devices: 198 us -> 187 us
  Pallas kernels: 163 us -> 157 us
  local copies, waits for them, and re-layouts: 32.6 us -> 37.9 us
    ppermute x18 -> x17, waiting for transfers between devices: 30.5 us -> 18.4 us  [swap_x(): return lax.ppermute(a, 'pipe', [(i, i ^ 2) for i in range(4)])]
    ppermute x17 -> x16, waiting for transfers between devices: 56.7 us -> 49.6 us  [swap_y(): return lax.ppermute(a, 'dp', [(i, i ^ 1) for i in range(8)])]
    ppermute x21 -> x18, starting transfers between devices: 14.3 us -> 7.61 us  [ring_z(): return lax.ppermute(a, 'dp', [(i, (i + 2 * step) % 8) for i in range(8)])]
    ppermute x21 -> x18, waiting for transfers between devices: 96.9 us -> 103 us  [ring_z(): return lax.ppermute(a, 'dp', [(i, (i + 2 * step) % 8) for i in range(8)])]
    ppermute x18 -> x17, starting transfers between devices: 15.7 us -> 21.3 us  [swap_x(): return lax.ppermute(a, 'pipe', [(i, i ^ 2) for i in range(4)])]
    pallas_call x7 -> x6, Pallas kernels: 160 us -> 155 us  [call(): pl.pallas_call(body, out_shape=outs, in_specs=specs, out_specs=[ANYWHERE...]
    unnamed x102 -> x115, local copies, waits for them, and re-layouts: 16.3 us -> 21.2 us
    ppermute x20 -> x19, waiting for transfers between devices: 10.5 us -> 12.9 us  [swap_core(): return lax.ppermute(a, 'pipe', [(i, i ^ 1) for i in range(4)])]
  transfers between devices with their start and end apart: 77 -> 71, of which waited for: 38 -> 32; matrix products, arithmetic and copies ran while one was open for 7% -> 8% of each run, Pallas kernels for 18% -> 18%
where the time goes in v7:
time: 517 us; the launch traced here: 508 us
  waiting for transfers between devices  187 us (36%)
  Pallas kernels  157 us (30%)
  starting transfers between devices  50.6 us (10%)
  other arithmetic  46.9 us (9%)
  local copies, waits for them, and re-layouts  37.9 us (7%)
  between operations  15.5 us (3%)
  matrix products  13.3 us (3%)
    pallas_call x6, Pallas kernels, call(): pl.pallas_call(body, out_shape=outs, in_specs=specs, out_specs=[ANYWHERE...  155 us
    ppermute x18, waiting for transfers between devices, ring_z(): return lax.ppermute(a, 'dp', [(i, (i + 2 * step) % 8) for i in range(8)])  103 us
    ppermute x16, waiting for transfers between devices, swap_y(): return lax.ppermute(a, 'dp', [(i, i ^ 1) for i in range(8)])  49.6 us
    convert_element_type x10, other arithmetic, ask(): self.block(own, y, z).astype(BF)  30.9 us
    ppermute x17, starting transfers between devices, swap_x(): return lax.ppermute(a, 'pipe', [(i, i ^ 2) for i in range(4)])  21.3 us
    unnamed x115, local copies, waits for them, and re-layouts  21.2 us
    ppermute x16, starting transfers between devices, swap_y(): return lax.ppermute(a, 'dp', [(i, i ^ 1) for i in range(8)])  18.8 us
    ppermute x17, waiting for transfers between devices, swap_x(): return lax.ppermute(a, 'pipe', [(i, i ^ 2) for i in range(4)])  18.4 us
  transfers between devices with their start and end apart: 71, of which 32 were waited for; matrix products, arithmetic and copies ran while one was open for 8% of the time, Pallas kernels for 18%

profile of v7, /device:TPU:0, one launch (start us, length us, event | category | flops | bytes accessed | tf_op | source)
XLA Modules:
  0.0 508.3 jit_solution(16840035320558879044)
XLA Ops:
  15.8 3.0 collective-permute-start.1
  21.9 16.8 %collective-permute-done.1.refs_5_.refs_10_.refs_16_.refs_13_.refs_12_ = bf16[1168,384]{1,0:T(8,128)(2,1)S(1)} collective-permute-done((bf16[1168,384]{1,0:T(8,128)(2,1)S(1)}, bf16[1168,384]{1,0:T(8,128)(2,1)S(1)}, u32[]{:S(2)}, u32[]{:S(2)}) %collective-permute-start.1) | collective-permute-done | bytes 897056 | tf_op jit(solution)/shard_map/ppermute | solution.py:875
  38.8 3.3 collective-permute-done.refs_2_.refs_7_.refs_13_.refs_10_.refs_9_
  48.4 16.1 %collective-permute-done.6.refs_18_.refs_23_.refs_29_.refs_26_.refs_25_ = bf16[1168,384]{1,0:T(8,128)(2,1)S(1)} collective-permute-done((bf16[1168,384]{1,0:T(8,128)(2,1)S(1)}, bf16[1168,384]{1,0:T(8,128)(2,1)S(1)}, u32[]{:S(2)}, u32[]{:S(2)}) %collective-permute-start.6) | collective-permute-done | bytes 897056 | tf_op jit(solution)/shard_map/ppermute | solution.py:869
  64.5 3.0 collective-permute-done.4.refs_3_.refs_8_.refs_14_.refs_11_.refs_10_
  70.2 21.6 %collective-permute-done.10.refs_4_.refs_9_.refs_15_.refs_12_.refs_11_ = bf16[1168,384]{1,0:T(8,128)(2,1)} collective-permute-done((bf16[1168,384]{1,0:T(8,128)(2,1)S(1)}, bf16[1168,384]{1,0:T(8,128)(2,1)}, u32[]{:S(2)}, u32[]{:S(2)}) %collective-permute-start.10) | collective-permute-done | bytes 897056 | tf_op jit(solution)/shard_map/ppermute | solution.py:878
  96.4 18.2 %collective-permute-done.16.refs_8_.refs_13_.refs_19_.refs_16_.refs_15_ = bf16[1168,384]{1,0:T(8,128)(2,1)} collective-permute-done((bf16[1168,384]{1,0:T(8,128)(2,1)}, bf16[1168,384]{1,0:T(8,128)(2,1)}, u32[]{:S(2)}, u32[]{:S(2)}) %collective-permute-start.16) | collective-permute-done | bytes 897056 | tf_op jit(solution)/shard_map/ppermute | solution.py:875
  115.2 2.1 collective-permute-done.20.refs_22_.refs_27_.refs_33_.refs_30_.refs_29_
  121.4 24.1 %collective-permute-done.23.refs_19_.refs_24_.refs_30_.refs_27_.refs_26_ = bf16[1168,384]{1,0:T(8,128)(2,1)} collective-permute-done((bf16[1168,384]{1,0:T(8,128)(2,1)}, bf16[1168,384]{1,0:T(8,128)(2,1)}, u32[]{:S(2)}, u32[]{:S(2)}) %collective-permute-start.23) | collective-permute-done | bytes 897056 | tf_op jit(solution)/shard_map/ppermute | solution.py:878
  151.0 2.5 shard_map.239
  154.3 32.9 %shard_map.240 = (bf16[512,2304]{1,0:T(8,128)(2,1)}, bf16[24,128,256]{2,1,0:T(8,128)(2,1)}, bf16[512,768]{1,0:T(8,128)(2,1)}, bf16[512,768]{1,0:T(8,128)(2,1)}, ...) custom-call(s32[8]{0:T(128)} %add_minimum_fusion.refs_0_, ...), custom_call_target="tpu_custom_call" | custom-call | flops 41799999488 | bytes 133000000 | tf_op jit(solution)/shard_map/pallas_call | solution.py:615
  187.2 3.0 all-gather.2.cloned.1.call-done
  190.2 2.1 fusion.59
  192.3 3.2 fusion.58
  195.5 3.5 convolution_convert_fusion.refs_4_.refs_2_
  199.0 3.5 add_convert_fusion.refs_5_.refs_3_
  202.5 45.7 %shard_map.241 = (bf16[512,768]{1,0:T(8,128)(2,1)}, bf16[48,160,128]{2,1,0:T(8,128)(2,1)}, bf16[512,768]{1,0:T(8,128)(2,1)}, bf16[512,768]{1,0:T(8,128)(2,1)}, f...) custom-call(s32[4]{0:T(128)} %pad_add_fusion.refs_0_.refs_1_, ...), custom_call_target="tpu_custom_call" | custom-call | flops 52800000000 | bytes 168000000 | tf_op jit(solution)/shard_map/pallas_call | solution.py:615
  248.2 19.9 %shard_map.242 = (f32[512,768]{1,0:T(8,128)}, bf16[1280,768]{1,0:T(8,128)(2,1)}, bf16[1280,768]{1,0:T(8,128)(2,1)}, bf16[768,768]{1,0:T(8,128)(2,1)}, bf16[768,768]{1,0:T(8,128)(2,1)}, /*index=5*/f32[8,768]{1,0:T(8,128)}) custom-call(f32[512,768]{1,0:T(8,128)} %get-tuple-element.178.refs_0_, bf16[512,768]{1,0:T(8,128)(2,1)} %get-tuple-element.173.refs_2_.refs_1_, ...), custom_call_target="tpu_custom_call" | custom-call | flops 28600000512 | bytes 91000000 | tf_op jit(solution)/shard_map/pallas_call | solution.py:615
  268.1 4.0 convolution_convert_fusion.2
  272.1 2.3 convolution_convert_fusion.1
  279.0 5.0 collective-permute-done.31
  285.6 3.4 convert_add_fusion
  291.5 18.1 %shard_map.243 = (bf16[512,768]{1,0:T(8,128)(2,1)}, bf16[2,8,400,384]{3,2,1,0:T(8,128)(2,1)}, bf16[2,8,400,384]{3,2,1,0:T(8,128)(2,1)}, f32[8,768]{1,0:T(8,128)}) custom-call(s32[4]{0:T(128)} %pad_add_fusion.refs_0_.refs_1_, f32[512,768]{1,0:T(8,128)} %get-tuple-element.191.refs_1_, bf16[512,768]{1,0:T(8,128)(2,1)} %get-tuple-element.192.refs_2_, ...), custom_call_target="tpu_custom_call" | custom-call | flops 24199999488 | bytes 77000000 | tf_op jit(solution)/shard_map/pallas_call | solution.py:615
  310.3 19.7 %shard_map.244 = (f32[512,768]{1,0:T(8,128)}, bf16[2,8,768,384]{3,2,1,0:T(8,128)(2,1)}, bf16[2,8,768,384]{3,2,1,0:T(8,128)(2,1)}, f32[8,768]{1,0:T(8,128)}) custom-call(s32[4]{0:T(128)} %pad_add_fusion.refs_0_.refs_1_, bf16[512,768]{1,0:T(8,128)(2,1)} %get-tuple-element.203.refs_1_, ...), custom_call_target="tpu_custom_call", output_to_operand_aliasing={{1}: (40, {}), {2}: (41, {})} | custom-call | flops 24199999488 | bytes 77000000 | tf_op jit(solution)/shard_map/pallas_call | solution.py:615
  335.1 18.4 %shard_map.245 = (f32[512,768]{1,0:T(8,128)}, bf16[2,8,400,384]{3,2,1,0:T(8,128)(2,1)}, bf16[2,8,400,384]{3,2,1,0:T(8,128)(2,1)}, f32[8,768]{1,0:T(8,128)}) custom-call(s32[4]{0:T(128)} %pad_add_fusion.refs_0_.refs_1_, f32[512,768]{1,0:T(8,128)} %get-tuple-element.217.refs_1_, ...), custom_call_target="tpu_custom_call", output_to_operand_aliasing={{1}: (41, {}), {2}: (42, {})} | custom-call | flops 24199999488 | bytes 77000000 | tf_op jit(solution)/shard_map/pallas_call | solution.py:615
  354.5 2.5 copy.71
  358.6 5.2 %fusion.42 = (bf16[768,384]{1,0:T(8,128)(2,1)S(1)}, bf16[768,384]{1,0:T(8,128)(2,1)S(1)}, bf16[768,384]{1,0:T(8,128)(2,1)}, bf16[768,384]{1,0:T(8,128)(2,1)S(1)}...) fusion(bf16[2,4,2,768,384]{4,3,2,1,0:T(8,128)(2,1)} %bitcast.37, ...), kind=kLoop, calls=%fused_computation.91 | loop fusion | flops 8257536 | bytes 12386304 | tf_op jit(solution)/shard_map/convert_element_type | solution.py:953
  364.1 2.0 collective-permute-start.37
  369.7 2.3 collective-permute-done.36
  372.0 4.5 fusion.51
  376.6 8.5 %collective-permute-done.40 = bf16[112,768]{1,0:T(8,128)(2,1)S(1)} collective-permute-done((bf16[112,768]{1,0:T(8,128)(2,1)S(1)}, bf16[112,768]{1,0:T(8,128)(2,1)S(1)}, u32[]{:S(2)}, u32[]{:S(2)}) %collective-permute-start.40) | collective-permute-done | bytes 172064 | tf_op jit(solution)/shard_map/ppermute | solution.py:878
  387.7 6.6 %collective-permute-done.41 = bf16[400,384]{1,0:T(8,128)(2,1)S(1)} collective-permute-done((bf16[400,384]{1,0:T(8,128)(2,1)S(1)}, bf16[400,384]{1,0:T(8,128)(2,1)S(1)}, u32[]{:S(2)}, u32[]{:S(2)}) %collective-permute-start.41) | collective-permute-done | bytes 307232 | tf_op jit(solution)/shard_map/ppermute | solution.py:875
  398.4 2.3 fusion.13
  402.9 3.8 collective-permute-done.44
  408.5 3.1 fusion.24
  412.7 4.1 collective-permute-done.54
  418.6 7.0 %collective-permute-done.56 = bf16[768,384]{1,0:T(8,128)(2,1)} collective-permute-done((bf16[768,384]{1,0:T(8,128)(2,1)S(1)}, bf16[768,384]{1,0:T(8,128)(2,1)}, u32[]{:S(2)}, u32[]{:S(2)}) %collective-permute-start.56) | collective-permute-done | bytes 589856 | tf_op jit(solution)/shard_map/ppermute | solution.py:878
  425.6 4.2 fusion.11
  431.2 4.7 collective-permute-done.47
  438.3 3.0 fusion.22
  441.3 3.5 collective-permute-done.57
  445.9 4.2 fusion.9
  454.0 11.9 %collective-permute-done.60 = bf16[768,384]{1,0:T(8,128)(2,1)S(1)} collective-permute-done((bf16[768,384]{1,0:T(8,128)(2,1)}, bf16[768,384]{1,0:T(8,128)(2,1)S(1)}, u32[]{:S(2)}, u32[]{:S(2)}) %collective-permute-start.60) | collective-permute-done | bytes 589856 | tf_op jit(solution)/shard_map/ppermute | solution.py:878
  465.9 3.3 collective-permute-start.53
  472.5 3.1 collective-permute-start.65
  478.2 7.8 %collective-permute-done.63 = bf16[768,384]{1,0:T(8,128)(2,1)S(1)} collective-permute-done((bf16[768,384]{1,0:T(8,128)(2,1)S(1)}, bf16[768,384]{1,0:T(8,128)(2,1)S(1)}, u32[]{:S(2)}, u32[]{:S(2)}) %collective-permute-start.63) | collective-permute-done | bytes 589856 | tf_op jit(solution)/shard_map/ppermute | solution.py:878
  489.4 2.0 collective-permute-start.68
  493.4 3.7 collective-permute-done.66
  (292 shorter events, 93.8 us)
Async XLA Ops:
  7.2 183.0 %all-gather.2.cloned.1.call-start = ((), (), s32[]{:S(2)}) async-start(), calls=%async_computation | async-start | bytes 5677056 | tf_op jit(solution)/shard_map/all_gather | solution.py:1122
  15.8 22.9 %collective-permute-start.1 = (bf16[1168,384]{1,0:T(8,128)(2,1)S(1)}, bf16[1168,384]{1,0:T(8,128)(2,1)S(1)}, u32[]{:S(2)}, u32[]{:S(2)}) collective-permute-start(bf16[1168,384]{1,0:T(8,128)(2,1)S(1)} %constant_dynamic-update-slice_fusion.refs_1_.refs_6_.refs_12_.refs_9_.refs_8_), channel_id=1, source_target_pairs={{0,1},{1,0},{2,3},{3,2},{4,5},{5,4},{6,7},{7,6},{8,9},{9,8},{10,11... | collective-permute-start | bytes 2691080 | tf_op jit(solution)/shard_map/ppermute | solution.py:875
  18.8 23.2 %collective-permute-start = (bf16[1168,384]{1,0:T(8,128)(2,1)S(1)}, bf16[1168,384]{1,0:T(8,128)(2,1)S(1)}, u32[]{:S(2)}, u32[]{:S(2)}) collective-permute-start(bf16[1168,384]{1,0:T(8,128)(2,1)S(1)} %constant_dynamic-update-slice_fusion.refs_1_.refs_6_.refs_12_.refs_9_.refs_8_), channel_id=1, source_target_pairs={{0,2},{1,3},{2,4},{3,5},{4,6},{5,7},{6,0},{7,1},{8,10},{9,11},{10,... | collective-permute-start | bytes 2691080 | tf_op jit(solution)/shard_map/ppermute | solution.py:878
  20.4 21.7 %collective-permute-start.2 = (bf16[1168,384]{1,0:T(8,128)(2,1)S(1)}, bf16[1168,384]{1,0:T(8,128)(2,1)S(1)}, u32[]{:S(2)}, u32[]{:S(2)}) collective-permute-start(bf16[1168,384]{1,0:T(8,128)(2,1)S(1)} %constant_dynamic-update-slice_fusion.refs_1_.refs_6_.refs_12_.refs_9_.refs_8_), channel_id=1, source_target_pairs={{0,16},{8,24},{16,0},{24,8},{1,17},{9,25},{17,1},{25,9},{2,18},{10... | collective-permute-start | bytes 2691080 | tf_op jit(solution)/shard_map/ppermute | solution.py:869
  21.9 20.2 %collective-permute-start.3 = (bf16[1168,384]{1,0:T(8,128)(2,1)S(1)}, bf16[1168,384]{1,0:T(8,128)(2,1)S(1)}, u32[]{:S(2)}, u32[]{:S(2)}) collective-permute-start(bf16[1168,384]{1,0:T(8,128)(2,1)S(1)} %constant_dynamic-update-slice_fusion.refs_1_.refs_6_.refs_12_.refs_9_.refs_8_), channel_id=1, source_target_pairs={{0,8},{8,0},{16,24},{24,16},{1,9},{9,1},{17,25},{25,17},{2,10},{10... | collective-permute-start | bytes 2691080 | tf_op jit(solution)/shard_map/ppermute | solution.py:872
  42.2 22.3 %collective-permute-start.6 = (bf16[1168,384]{1,0:T(8,128)(2,1)S(1)}, bf16[1168,384]{1,0:T(8,128)(2,1)S(1)}, u32[]{:S(2)}, u32[]{:S(2)}) collective-permute-start(bf16[1168,384]{1,0:T(8,128)(2,1)S(1)} %collective-permute-done.refs_2_.refs_7_.refs_13_.refs_10_.refs_9_), channel_id=1, source_target_pairs={{0,16},{8,24},{16,0},{24,8},{1,17},{9,25},{17,1},{25,9},{2,18},{10... | collective-permute-start | bytes 2691080 | tf_op jit(solution)/shard_map/ppermute | solution.py:869
  43.7 23.8 %collective-permute-start.4 = (bf16[1168,384]{1,0:T(8,128)(2,1)S(1)}, bf16[1168,384]{1,0:T(8,128)(2,1)S(1)}, u32[]{:S(2)}, u32[]{:S(2)}) collective-permute-start(bf16[1168,384]{1,0:T(8,128)(2,1)S(1)} %collective-permute-done.refs_2_.refs_7_.refs_13_.refs_10_.refs_9_), channel_id=1, source_target_pairs={{0,2},{1,3},{2,4},{3,5},{4,6},{5,7},{6,0},{7,1},{8,10},{9,11},{10,... | collective-permute-start | bytes 2691080 | tf_op jit(solution)/shard_map/ppermute | solution.py:878
  44.7 22.8 %collective-permute-start.5 = (bf16[1168,384]{1,0:T(8,128)(2,1)S(1)}, bf16[1168,384]{1,0:T(8,128)(2,1)S(1)}, u32[]{:S(2)}, u32[]{:S(2)}) collective-permute-start(bf16[1168,384]{1,0:T(8,128)(2,1)S(1)} %collective-permute-done.refs_2_.refs_7_.refs_13_.refs_10_.refs_9_), channel_id=1, source_target_pairs={{0,1},{1,0},{2,3},{3,2},{4,5},{5,4},{6,7},{7,6},{8,9},{9,8},{10,11... | collective-permute-start | bytes 2691080 | tf_op jit(solution)/shard_map/ppermute | solution.py:875
  45.2 22.3 %collective-permute-start.8 = (bf16[1168,384]{1,0:T(8,128)(2,1)S(1)}, bf16[1168,384]{1,0:T(8,128)(2,1)S(1)}, u32[]{:S(2)}, u32[]{:S(2)}) collective-permute-start(bf16[1168,384]{1,0:T(8,128)(2,1)S(1)} %collective-permute-done.1.refs_5_.refs_10_.refs_16_.refs_13_.refs_12_), channel_id=1, source_target_pairs={{0,8},{8,0},{16,24},{24,16},{1,9},{9,1},{17,25},{25,17},{2,10},{10... | collective-permute-start | bytes 2691080 | tf_op jit(solution)/shard_map/ppermute | solution.py:872
  46.2 21.4 %collective-permute-start.9 = (bf16[1168,384]{1,0:T(8,128)(2,1)S(1)}, bf16[1168,384]{1,0:T(8,128)(2,1)S(1)}, u32[]{:S(2)}, u32[]{:S(2)}) collective-permute-start(bf16[1168,384]{1,0:T(8,128)(2,1)S(1)} %collective-permute-done.2.refs_17_.refs_22_.refs_28_.refs_25_.refs_24_), channel_id=1, source_target_pairs={{0,8},{8,0},{16,24},{24,16},{1,9},{9,1},{17,25},{25,17},{2,10},{10... | collective-permute-start | bytes 2691080 | tf_op jit(solution)/shard_map/ppermute | solution.py:872
  67.6 24.2 %collective-permute-start.10 = (bf16[1168,384]{1,0:T(8,128)(2,1)S(1)}, bf16[1168,384]{1,0:T(8,128)(2,1)}, u32[]{:S(2)}, u32[]{:S(2)}) collective-permute-start(bf16[1168,384]{1,0:T(8,128)(2,1)S(1)} %collective-permute-done.4.refs_3_.refs_8_.refs_14_.refs_11_.refs_10_), channel_id=1, source_target_pairs={{0,2},{1,3},{2,4},{3,5},{4,6},{5,7},{6,0},{7,1},{8,10},{9,11},{10,... | collective-permute-start | bytes 2691080 | tf_op jit(solution)/shard_map/ppermute | solution.py:878
  68.2 23.7 %collective-permute-start.11 = (bf16[1168,384]{1,0:T(8,128)(2,1)S(1)}, bf16[1168,384]{1,0:T(8,128)(2,1)}, u32[]{:S(2)}, u32[]{:S(2)}) collective-permute-start(bf16[1168,384]{1,0:T(8,128)(2,1)S(1)} %collective-permute-done.4.refs_3_.refs_8_.refs_14_.refs_11_.refs_10_), channel_id=1, source_target_pairs={{0,1},{1,0},{2,3},{3,2},{4,5},{5,4},{6,7},{7,6},{8,9},{9,8},{10,11... | collective-permute-start | bytes 2691080 | tf_op jit(solution)/shard_map/ppermute | solution.py:875
  68.7 23.2 %collective-permute-start.12 = (bf16[1168,384]{1,0:T(8,128)(2,1)S(1)}, bf16[1168,384]{1,0:T(8,128)(2,1)}, u32[]{:S(2)}, u32[]{:S(2)}) collective-permute-start(bf16[1168,384]{1,0:T(8,128)(2,1)S(1)} %collective-permute-done.1.refs_5_.refs_10_.refs_16_.refs_13_.refs_12_), channel_id=1, source_target_pairs={{0,16},{8,24},{16,0},{24,8},{1,17},{9,25},{17,1},{25,9},{2,18},{10... | collective-permute-start | bytes 2691080 | tf_op jit(solution)/shard_map/ppermute | solution.py:869
  69.2 22.7 %collective-permute-start.14 = (bf16[1168,384]{1,0:T(8,128)(2,1)S(1)}, bf16[1168,384]{1,0:T(8,128)(2,1)S(1)}, u32[]{:S(2)}, u32[]{:S(2)}) collective-permute-start(bf16[1168,384]{1,0:T(8,128)(2,1)S(1)} %collective-permute-done.5.refs_6_.refs_11_.refs_17_.refs_14_.refs_13_), channel_id=1, source_target_pairs={{0,8},{8,0},{16,24},{24,16},{1,9},{9,1},{17,25},{25,17},{2,10},{10... | collective-permute-start | bytes 2691080 | tf_op jit(solution)/shard_map/ppermute | solution.py:872
  70.1 21.8 %collective-permute-start.15 = (bf16[1168,384]{1,0:T(8,128)(2,1)S(1)}, bf16[1168,384]{1,0:T(8,128)(2,1)S(1)}, u32[]{:S(2)}, u32[]{:S(2)}) collective-permute-start(bf16[1168,384]{1,0:T(8,128)(2,1)S(1)} %collective-permute-done.6.refs_18_.refs_23_.refs_29_.refs_26_.refs_25_), channel_id=1, source_target_pairs={{0,8},{8,0},{16,24},{24,16},{1,9},{9,1},{17,25},{25,17},{2,10},{10... | collective-permute-start | bytes 2691080 | tf_op jit(solution)/shard_map/ppermute | solution.py:872
  92.0 22.6 %collective-permute-start.16 = (bf16[1168,384]{1,0:T(8,128)(2,1)}, bf16[1168,384]{1,0:T(8,128)(2,1)}, u32[]{:S(2)}, u32[]{:S(2)}) collective-permute-start(bf16[1168,384]{1,0:T(8,128)(2,1)} %collective-permute-done.10.refs_4_.refs_9_.refs_15_.refs_12_.refs_11_), channel_id=1, source_target_pairs={{0,1},{1,0},{2,3},{3,2},{4,5},{5,4},{6,7},{7,6},{8,9},{9,8},{10,11... | collective-permute-start | bytes 2691080 | tf_op jit(solution)/shard_map/ppermute | solution.py:875
  92.6 22.1 %collective-permute-start.18 = (bf16[1168,384]{1,0:T(8,128)(2,1)}, bf16[1168,384]{1,0:T(8,128)(2,1)}, u32[]{:S(2)}, u32[]{:S(2)}) collective-permute-start(bf16[1168,384]{1,0:T(8,128)(2,1)} %collective-permute-done.11.refs_7_.refs_12_.refs_18_.refs_15_.refs_14_), channel_id=1, source_target_pairs={{0,8},{8,0},{16,24},{24,16},{1,9},{9,1},{17,25},{25,17},{2,10},{10... | collective-permute-start | bytes 2691080 | tf_op jit(solution)/shard_map/ppermute | solution.py:872
  92.7 22.5 %collective-permute-start.19 = (bf16[1168,384]{1,0:T(8,128)(2,1)}, bf16[1168,384]{1,0:T(8,128)(2,1)}, u32[]{:S(2)}, u32[]{:S(2)}) collective-permute-start(bf16[1168,384]{1,0:T(8,128)(2,1)} %collective-permute-done.10.refs_4_.refs_9_.refs_15_.refs_12_.refs_11_), channel_id=1, source_target_pairs={{0,16},{8,24},{16,0},{24,8},{1,17},{9,25},{17,1},{25,9},{2,18},{10... | collective-permute-start | bytes 2691080 | tf_op jit(solution)/shard_map/ppermute | solution.py:869
  93.3 24.0 %collective-permute-start.20 = (bf16[1168,384]{1,0:T(8,128)(2,1)}, bf16[1168,384]{1,0:T(8,128)(2,1)}, u32[]{:S(2)}, u32[]{:S(2)}) collective-permute-start(bf16[1168,384]{1,0:T(8,128)(2,1)} %collective-permute-done.12.refs_21_.refs_26_.refs_32_.refs_29_.refs_28_), channel_id=1, source_target_pairs={{0,2},{1,3},{2,4},{3,5},{4,6},{5,7},{6,0},{7,1},{8,10},{9,11},{10,... | collective-permute-start | bytes 2691080 | tf_op jit(solution)/shard_map/ppermute | solution.py:878
  95.6 21.7 %collective-permute-start.21 = (bf16[1168,384]{1,0:T(8,128)(2,1)}, bf16[1168,384]{1,0:T(8,128)(2,1)}, u32[]{:S(2)}, u32[]{:S(2)}) collective-permute-start(bf16[1168,384]{1,0:T(8,128)(2,1)} %collective-permute-done.12.refs_21_.refs_26_.refs_32_.refs_29_.refs_28_), channel_id=1, source_target_pairs={{0,8},{8,0},{16,24},{24,16},{1,9},{9,1},{17,25},{25,17},{2,10},{10... | collective-permute-start | bytes 2691080 | tf_op jit(solution)/shard_map/ppermute | solution.py:872
  117.9 27.7 %collective-permute-start.23 = (bf16[1168,384]{1,0:T(8,128)(2,1)}, bf16[1168,384]{1,0:T(8,128)(2,1)}, u32[]{:S(2)}, u32[]{:S(2)}) collective-permute-start(bf16[1168,384]{1,0:T(8,128)(2,1)} %copy-done.15), channel_id=1, source_target_pairs={{0,2},{1,3},{2,4},{3,5},{4,6},{5,7},{6,0},{7,1},{8,10},{9,11},{10,... | collective-permute-start | bytes 2691080 | tf_op jit(solution)/shard_map/ppermute | solution.py:878
  117.9 27.7 %collective-permute-start.24 = (bf16[1168,384]{1,0:T(8,128)(2,1)}, bf16[1168,384]{1,0:T(8,128)(2,1)}, u32[]{:S(2)}, u32[]{:S(2)}) collective-permute-start(bf16[1168,384]{1,0:T(8,128)(2,1)} %collective-permute-done.11.refs_7_.refs_12_.refs_18_.refs_15_.refs_14_), channel_id=1, source_target_pairs={{0,16},{8,24},{16,0},{24,8},{1,17},{9,25},{17,1},{25,9},{2,18},{10... | collective-permute-start | bytes 2691080 | tf_op jit(solution)/shard_map/ppermute | solution.py:869
  119.4 26.2 %collective-permute-start.25 = (bf16[1168,384]{1,0:T(8,128)(2,1)}, bf16[1168,384]{1,0:T(8,128)(2,1)}, u32[]{:S(2)}, u32[]{:S(2)}) collective-permute-start(bf16[1168,384]{1,0:T(8,128)(2,1)} %collective-permute-done.19.refs_20_.refs_25_.refs_31_.refs_28_.refs_27_), channel_id=1, source_target_pairs={{0,1},{1,0},{2,3},{3,2},{4,5},{5,4},{6,7},{7,6},{8,9},{9,8},{10,11... | collective-permute-start | bytes 2691080 | tf_op jit(solution)/shard_map/ppermute | solution.py:875
  120.9 24.7 %collective-permute-start.27 = (bf16[1168,384]{1,0:T(8,128)(2,1)}, bf16[1168,384]{1,0:T(8,128)(2,1)}, u32[]{:S(2)}, u32[]{:S(2)}) collective-permute-start(bf16[1168,384]{1,0:T(8,128)(2,1)} %collective-permute-done.19.refs_20_.refs_25_.refs_31_.refs_28_.refs_27_), channel_id=1, source_target_pairs={{0,8},{8,0},{16,24},{24,16},{1,9},{9,1},{17,25},{25,17},{2,10},{10... | collective-permute-start | bytes 2691080 | tf_op jit(solution)/shard_map/ppermute | solution.py:872
  290.0 19.5 %collective-permute-start.32 = (bf16[2,2,112,768]{3,2,0,1:T(8,128)(2,1)}, bf16[2,2,112,768]{3,2,0,1:T(8,128)(2,1)}, u32[]{:S(2)}, u32[]{:S(2)}) collective-permute-start(bf16[2,2,112,768]{3,2,0,1:T(8,128)(2,1)} %get-tuple-element.190), channel_id=1, source_target_pairs={{0,16},{8,24},{16,0},{24,8},{1,17},{9,25},{17,1},{25,9},{2,18},{10... | collective-permute-start | bytes 2064392 | tf_op jit(solution)/shard_map/ppermute | solution.py:869
  309.6 20.5 %collective-permute-start.33 = (bf16[2,2,112,768]{3,2,0,1:T(8,128)(2,1)S(1)}, bf16[2,2,112,768]{3,2,0,1:T(8,128)(2,1)}, u32[]{:S(2)}, u32[]{:S(2)}) collective-permute-start(bf16[2,2,112,768]{3,2,0,1:T(8,128)(2,1)S(1)} %get-tuple-element.202), channel_id=1, source_target_pairs={{0,16},{8,24},{16,0},{24,8},{1,17},{9,25},{17,1},{25,9},{2,18},{10... | collective-permute-start | bytes 2064392 | tf_op jit(solution)/shard_map/ppermute | solution.py:869
  333.2 25.5 %collective-permute-start.34 = (bf16[2,8,768,384]{3,2,1,0:T(8,128)(2,1)}, bf16[2,8,768,384]{3,2,1,0:T(8,128)(2,1)}, u32[]{:S(2)}, u32[]{:S(2)}) collective-permute-start(bf16[2,8,768,384]{3,2,1,0:T(8,128)(2,1)} %get-tuple-element.215), channel_id=1, source_target_pairs={{0,8},{8,0},{16,24},{24,16},{1,9},{9,1},{17,25},{25,17},{2,10},{10... | collective-permute-start | bytes 28311560 | tf_op jit(solution)/shard_map/ppermute | solution.py:872
  333.5 23.8 %collective-permute-start.35 = (bf16[4,112,768]{2,1,0:T(8,128)(2,1)S(1)}, bf16[4,112,768]{2,1,0:T(8,128)(2,1)S(1)}, u32[]{:S(2)}, u32[]{:S(2)}) collective-permute-start(bf16[4,112,768]{2,1,0:T(8,128)(2,1)S(1)} %fusion.21), channel_id=1, source_target_pairs={{0,1},{1,0},{2,3},{3,2},{4,5},{5,4},{6,7},{7,6},{8,9},{9,8},{10,11... | collective-permute-start | bytes 2064392 | tf_op jit(solution)/shard_map/ppermute | solution.py:875
  364.1 21.0 %collective-permute-start.37 = (bf16[768,384]{1,0:T(8,128)(2,1)S(1)}, bf16[768,384]{1,0:T(8,128)(2,1)S(1)}, u32[]{:S(2)}, u32[]{:S(2)}) collective-permute-start(bf16[768,384]{1,0:T(8,128)(2,1)S(1)} %get-tuple-element.230), channel_id=1, source_target_pairs={{0,2},{1,3},{2,4},{3,5},{4,6},{5,7},{6,0},{7,1},{8,10},{9,11},{10,... | collective-permute-start | bytes 1769480 | tf_op jit(solution)/shard_map/ppermute | solution.py:878
  366.1 19.0 %collective-permute-start.38 = (bf16[768,384]{1,0:T(8,128)(2,1)S(1)}, bf16[768,384]{1,0:T(8,128)(2,1)S(1)}, u32[]{:S(2)}, u32[]{:S(2)}) collective-permute-start(bf16[768,384]{1,0:T(8,128)(2,1)S(1)} %get-tuple-element.231), channel_id=1, source_target_pairs={{0,1},{1,0},{2,3},{3,2},{4,5},{5,4},{6,7},{7,6},{8,9},{9,8},{10,11... | collective-permute-start | bytes 1769480 | tf_op jit(solution)/shard_map/ppermute | solution.py:875
  366.6 18.5 %collective-permute-start.39 = (bf16[768,384]{1,0:T(8,128)(2,1)S(1)}, bf16[768,384]{1,0:T(8,128)(2,1)S(1)}, u32[]{:S(2)}, u32[]{:S(2)}) collective-permute-start(bf16[768,384]{1,0:T(8,128)(2,1)S(1)} %get-tuple-element.232), channel_id=1, source_target_pairs={{0,16},{8,24},{16,0},{24,8},{1,17},{9,25},{17,1},{25,9},{2,18},{10... | collective-permute-start | bytes 1769480 | tf_op jit(solution)/shard_map/ppermute | solution.py:869
  367.9 17.2 %collective-permute-start.40 = (bf16[112,768]{1,0:T(8,128)(2,1)S(1)}, bf16[112,768]{1,0:T(8,128)(2,1)S(1)}, u32[]{:S(2)}, u32[]{:S(2)}) collective-permute-start(bf16[112,768]{1,0:T(8,128)(2,1)S(1)} %fusion.54), channel_id=1, source_target_pairs={{0,2},{1,3},{2,4},{3,5},{4,6},{5,7},{6,0},{7,1},{8,10},{9,11},{10,... | collective-permute-start | bytes 516104 | tf_op jit(solution)/shard_map/ppermute | solution.py:878
  400.7 16.0 %collective-permute-start.54 = (bf16[768,384]{1,0:T(8,128)(2,1)}, bf16[768,384]{1,0:T(8,128)(2,1)}, u32[]{:S(2)}, u32[]{:S(2)}) collective-permute-start(bf16[768,384]{1,0:T(8,128)(2,1)} %get-tuple-element.247), channel_id=1, source_target_pairs={{0,1},{1,0},{2,3},{3,2},{4,5},{5,4},{6,7},{7,6},{8,9},{9,8},{10,11... | collective-permute-start | bytes 1769480 | tf_op jit(solution)/shard_map/ppermute | solution.py:875
  402.1 16.1 %collective-permute-start.55 = (bf16[768,384]{1,0:T(8,128)(2,1)}, bf16[768,384]{1,0:T(8,128)(2,1)}, u32[]{:S(2)}, u32[]{:S(2)}) collective-permute-start(bf16[768,384]{1,0:T(8,128)(2,1)} %fusion.13), channel_id=1, source_target_pairs={{0,16},{8,24},{16,0},{24,8},{1,17},{9,25},{17,1},{25,9},{2,18},{10... | collective-permute-start | bytes 1769480 | tf_op jit(solution)/shard_map/ppermute | solution.py:869
  407.5 18.2 %collective-permute-start.56 = (bf16[768,384]{1,0:T(8,128)(2,1)S(1)}, bf16[768,384]{1,0:T(8,128)(2,1)}, u32[]{:S(2)}, u32[]{:S(2)}) collective-permute-start(bf16[768,384]{1,0:T(8,128)(2,1)S(1)} %get-tuple-element.249), channel_id=1, source_target_pairs={{0,2},{1,3},{2,4},{3,5},{4,6},{5,7},{6,0},{7,1},{8,10},{9,11},{10,... | collective-permute-start | bytes 1769480 | tf_op jit(solution)/shard_map/ppermute | solution.py:878
  411.6 18.3 %collective-permute-start.49 = (bf16[112,768]{1,0:T(8,128)(2,1)S(1)}, bf16[112,768]{1,0:T(8,128)(2,1)S(1)}, u32[]{:S(2)}, u32[]{:S(2)}) collective-permute-start(bf16[112,768]{1,0:T(8,128)(2,1)S(1)} %fusion.44), channel_id=1, source_target_pairs={{0,2},{1,3},{2,4},{3,5},{4,6},{5,7},{6,0},{7,1},{8,10},{9,11},{10,... | collective-permute-start | bytes 516104 | tf_op jit(solution)/shard_map/ppermute | solution.py:878
  411.6 24.3 %collective-permute-start.47 = (bf16[400,384]{1,0:T(8,128)(2,1)S(1)}, bf16[400,384]{1,0:T(8,128)(2,1)}, u32[]{:S(2)}, u32[]{:S(2)}) collective-permute-start(bf16[400,384]{1,0:T(8,128)(2,1)S(1)} %get-tuple-element.240), channel_id=1, source_target_pairs={{0,2},{1,3},{2,4},{3,5},{4,6},{5,7},{6,0},{7,1},{8,10},{9,11},{10,... | collective-permute-start | bytes 921608 | tf_op jit(solution)/shard_map/ppermute | solution.py:878
  416.8 21.5 %collective-permute-start.48 = (bf16[400,384]{1,0:T(8,128)(2,1)}, bf16[400,384]{1,0:T(8,128)(2,1)}, u32[]{:S(2)}, u32[]{:S(2)}) collective-permute-start(bf16[400,384]{1,0:T(8,128)(2,1)} %get-tuple-element.241), channel_id=1, source_target_pairs={{0,1},{1,0},{2,3},{3,2},{4,5},{5,4},{6,7},{7,6},{8,9},{9,8},{10,11... | collective-permute-start | bytes 921608 | tf_op jit(solution)/shard_map/ppermute | solution.py:875
  418.2 20.1 %collective-permute-start.50 = (bf16[400,384]{1,0:T(8,128)(2,1)}, bf16[400,384]{1,0:T(8,128)(2,1)}, u32[]{:S(2)}, u32[]{:S(2)}) collective-permute-start(bf16[400,384]{1,0:T(8,128)(2,1)} %get-tuple-element.243), channel_id=1, source_target_pairs={{0,16},{8,24},{16,0},{24,8},{1,17},{9,25},{17,1},{25,9},{2,18},{10... | collective-permute-start | bytes 921608 | tf_op jit(solution)/shard_map/ppermute | solution.py:869
  429.9 14.9 %collective-permute-start.57 = (bf16[768,384]{1,0:T(8,128)(2,1)}, bf16[768,384]{1,0:T(8,128)(2,1)}, u32[]{:S(2)}, u32[]{:S(2)}) collective-permute-start(bf16[768,384]{1,0:T(8,128)(2,1)} %get-tuple-element.250), channel_id=1, source_target_pairs={{0,2},{1,3},{2,4},{3,5},{4,6},{5,7},{6,0},{7,1},{8,10},{9,11},{10,... | collective-permute-start | bytes 1769480 | tf_op jit(solution)/shard_map/ppermute | solution.py:878
  429.9 14.9 %collective-permute-start.58 = (bf16[768,384]{1,0:T(8,128)(2,1)}, bf16[768,384]{1,0:T(8,128)(2,1)}, u32[]{:S(2)}, u32[]{:S(2)}) collective-permute-start(bf16[768,384]{1,0:T(8,128)(2,1)} %get-tuple-element.251), channel_id=1, source_target_pairs={{0,1},{1,0},{2,3},{3,2},{4,5},{5,4},{6,7},{7,6},{8,9},{9,8},{10,11... | collective-permute-start | bytes 1769480 | tf_op jit(solution)/shard_map/ppermute | solution.py:875
  450.1 15.8 %collective-permute-start.60 = (bf16[768,384]{1,0:T(8,128)(2,1)}, bf16[768,384]{1,0:T(8,128)(2,1)S(1)}, u32[]{:S(2)}, u32[]{:S(2)}) collective-permute-start(bf16[768,384]{1,0:T(8,128)(2,1)} %get-tuple-element.253), channel_id=1, source_target_pairs={{0,2},{1,3},{2,4},{3,5},{4,6},{5,7},{6,0},{7,1},{8,10},{9,11},{10,... | collective-permute-start | bytes 1769480 | tf_op jit(solution)/shard_map/ppermute | solution.py:878
  450.1 19.0 %collective-permute-start.61 = (bf16[768,384]{1,0:T(8,128)(2,1)S(1)}, bf16[768,384]{1,0:T(8,128)(2,1)}, u32[]{:S(2)}, u32[]{:S(2)}) collective-permute-start(bf16[768,384]{1,0:T(8,128)(2,1)S(1)} %get-tuple-element.254), channel_id=1, source_target_pairs={{0,1},{1,0},{2,3},{3,2},{4,5},{5,4},{6,7},{7,6},{8,9},{9,8},{10,11... | collective-permute-start | bytes 1769480 | tf_op jit(solution)/shard_map/ppermute | solution.py:875
  451.4 17.7 %collective-permute-start.62 = (bf16[768,384]{1,0:T(8,128)(2,1)}, bf16[768,384]{1,0:T(8,128)(2,1)}, u32[]{:S(2)}, u32[]{:S(2)}) collective-permute-start(bf16[768,384]{1,0:T(8,128)(2,1)} %get-tuple-element.255), channel_id=1, source_target_pairs={{0,16},{8,24},{16,0},{24,8},{1,17},{9,25},{17,1},{25,9},{2,18},{10... | collective-permute-start | bytes 1769480 | tf_op jit(solution)/shard_map/ppermute | solution.py:869
  451.6 20.9 %collective-permute-start.51 = (bf16[400,384]{1,0:T(8,128)(2,1)}, bf16[400,384]{1,0:T(8,128)(2,1)S(1)}, u32[]{:S(2)}, u32[]{:S(2)}) collective-permute-start(bf16[400,384]{1,0:T(8,128)(2,1)} %get-tuple-element.244), channel_id=1, source_target_pairs={{0,2},{1,3},{2,4},{3,5},{4,6},{5,7},{6,0},{7,1},{8,10},{9,11},{10,... | collective-permute-start | bytes 921608 | tf_op jit(solution)/shard_map/ppermute | solution.py:878
  451.6 25.3 %collective-permute-start.52 = (bf16[400,384]{1,0:T(8,128)(2,1)S(1)}, bf16[400,384]{1,0:T(8,128)(2,1)S(1)}, u32[]{:S(2)}, u32[]{:S(2)}) collective-permute-start(bf16[400,384]{1,0:T(8,128)(2,1)S(1)} %copy-done.30), channel_id=1, source_target_pairs={{0,1},{1,0},{2,3},{3,2},{4,5},{5,4},{6,7},{7,6},{8,9},{9,8},{10,11... | collective-permute-start | bytes 921608 | tf_op jit(solution)/shard_map/ppermute | solution.py:875
  471.2 14.9 %collective-permute-start.63 = (bf16[768,384]{1,0:T(8,128)(2,1)S(1)}, bf16[768,384]{1,0:T(8,128)(2,1)S(1)}, u32[]{:S(2)}, u32[]{:S(2)}) collective-permute-start(bf16[768,384]{1,0:T(8,128)(2,1)S(1)} %fusion.20), channel_id=1, source_target_pairs={{0,2},{1,3},{2,4},{3,5},{4,6},{5,7},{6,0},{7,1},{8,10},{9,11},{10,... | collective-permute-start | bytes 1769480 | tf_op jit(solution)/shard_map/ppermute | solution.py:878
  471.2 14.8 %collective-permute-start.64 = (bf16[768,384]{1,0:T(8,128)(2,1)S(1)}, bf16[768,384]{1,0:T(8,128)(2,1)S(1)}, u32[]{:S(2)}, u32[]{:S(2)}) collective-permute-start(bf16[768,384]{1,0:T(8,128)(2,1)S(1)} %copy-done.28), channel_id=1, source_target_pairs={{0,1},{1,0},{2,3},{3,2},{4,5},{5,4},{6,7},{7,6},{8,9},{9,8},{10,11... | collective-permute-start | bytes 1769480 | tf_op jit(solution)/shard_map/ppermute | solution.py:875
  (75 other events, 1258.9 us)
Sparse Core Ops, SparseCore 0:
  117.4 72.7 all-gather.1

commit v8 on v7

--- a/solution.py
+++ b/solution.py
@@ -969,8 +969,8 @@
 
 
 class BlockSum:
-    def __init__(self, grid, a, dtype):
-        self.grid, self.a, self.dtype = grid, a, dtype
+    def __init__(self, grid, own, other, dtype):
+        self.grid, self.own, self.other, self.dtype = grid, own, other, dtype
         self.ring = []
 
     def step(self, swap, place, axis):
@@ -982,7 +982,10 @@
         return [(swap, dynamic(self.a, 1 - place, axis).astype(self.dtype), keep)]
 
     def c(self):
-        return self.step(self.grid.swap_core, self.grid.core, 1)
+        def keep(came):
+            self.a = self.own.astype(F32) + came.astype(F32)
+
+        return [(self.grid.swap_core, self.other, keep)]
 
     def x0(self):
         self.halves = [dynamic(self.a, place, 0) for place in (self.grid.x, 1 - self.grid.x)]
@@ -1090,7 +1093,7 @@
 
     def pack_cross(image, dk, dv, g_cq, g_co):
         grads = [g_cq, g_co, dot(image, dk, TN).astype(BF), dot(image, dv, TN).astype(BF)]
-        return jnp.concatenate([g.reshape(shards, -1, width) for g in grads], axis=1)
+        return [g.reshape(shards, -1, width) for g in grads]
 
     def vector_block(v_self, v_feed):
         v = jnp.concatenate([v_self[:5], v_feed[:7]], axis=0)
@@ -1135,7 +1138,9 @@
             return grad, v_cross, pack_cross(image, dk, dv, g_cq, g_co)
 
         grad, v_cross, cross_grads = fourth(grad)
-        sum_cross = BlockSum(grid, cross_grads.reshape(2, 2, 4, 2, -1, width), BF)
+        cross_grads = [g.reshape(2, 2, 4, 2, -1, width) for g in cross_grads]
+        halves = [jnp.concatenate([dynamic(g, c, 1) for g in cross_grads], axis=3) for c in (grid.core, 1 - grid.core)]
+        sum_cross = BlockSum(grid, *halves, BF)
         turn(sum_cross.c)
         grad, *g_self, v_self2 = turn(
             sum_cross.x0,
@@ -1230,7 +1235,7 @@
         packed = jnp.concatenate(parts, axis=2).reshape(-1, lanes)
         packed = lax.psum_scatter(packed, everyone, scatter_dimension=0, tiled=True).astype(F32)
         mine = [packed[a:b] for a, b in zip(ends[:-1], ends[1:])]
-        cross_grads = pack_cross(image, dk, dv, g_cq, g_co).reshape(-1, width)
+        cross_grads = jnp.concatenate(pack_cross(image, dk, dv, g_cq, g_co), axis=1).reshape(-1, width)
         cross_grads = lax.psum_scatter(cross_grads, everyone, scatter_dimension=0, tiled=True).astype(F32)
         small = pack_vectors((v_self, v_feed), (v_self2, v_feed2), v_cross)
         small = lax.psum_scatter(small.reshape(-1, 128), everyone, scatter_dimension=0, tiled=True)

time: 517 us -> 515 us (level)
    unnamed x115 -> x112, local copies, waits for them, and re-layouts: 21.2 us -> 19.5 us
where the time goes in v8:
time: 515 us; the launch traced here: 506 us
  waiting for transfers between devices  187 us (36%)
  Pallas kernels  157 us (30%)
  starting transfers between devices  50.3 us (10%)
  other arithmetic  46.8 us (9%)
  local copies, waits for them, and re-layouts  37.5 us (7%)
  between operations  15.6 us (3%)
  matrix products  11.6 us (2%)
    pallas_call x6, Pallas kernels, call(): pl.pallas_call(body, out_shape=outs, in_specs=specs, out_specs=[ANYWHERE...  155 us
    ppermute x18, waiting for transfers between devices, ring_z(): return lax.ppermute(a, 'dp', [(i, (i + 2 * step) % 8) for i in range(8)])  103 us
    ppermute x16, waiting for transfers between devices, swap_y(): return lax.ppermute(a, 'dp', [(i, i ^ 1) for i in range(8)])  49.4 us
    convert_element_type x10, other arithmetic, ask(): self.block(own, y, z).astype(BF)  30.9 us
    ppermute x17, starting transfers between devices, swap_x(): return lax.ppermute(a, 'pipe', [(i, i ^ 2) for i in range(4)])  20.1 us
    ppermute x16, starting transfers between devices, swap_y(): return lax.ppermute(a, 'dp', [(i, i ^ 1) for i in range(8)])  19.6 us
    unnamed x112, local copies, waits for them, and re-layouts  19.5 us
    ppermute x17, waiting for transfers between devices, swap_x(): return lax.ppermute(a, 'pipe', [(i, i ^ 2) for i in range(4)])  18.9 us
  transfers between devices with their start and end apart: 71, of which 32 were waited for; matrix products, arithmetic and copies ran while one was open for 8% of the time, Pallas kernels for 18%

profile of v8, /device:TPU:0, one launch (start us, length us, event | category | flops | bytes accessed | tf_op | source)
XLA Modules:
  0.0 505.9 jit_solution(4412262788353387073)
XLA Ops:
  15.8 3.0 collective-permute-start.1
  21.9 16.8 %collective-permute-done.1.refs_5_.refs_10_.refs_16_.refs_13_.refs_12_ = bf16[1168,384]{1,0:T(8,128)(2,1)S(1)} collective-permute-done((bf16[1168,384]{1,0:T(8,128)(2,1)S(1)}, bf16[1168,384]{1,0:T(8,128)(2,1)S(1)}, u32[]{:S(2)}, u32[]{:S(2)}) %collective-permute-start.1) | collective-permute-done | bytes 897056 | tf_op jit(solution)/shard_map/ppermute | solution.py:875
  38.8 3.3 collective-permute-done.refs_2_.refs_7_.refs_13_.refs_10_.refs_9_
  48.4 16.1 %collective-permute-done.6.refs_18_.refs_23_.refs_29_.refs_26_.refs_25_ = bf16[1168,384]{1,0:T(8,128)(2,1)S(1)} collective-permute-done((bf16[1168,384]{1,0:T(8,128)(2,1)S(1)}, bf16[1168,384]{1,0:T(8,128)(2,1)S(1)}, u32[]{:S(2)}, u32[]{:S(2)}) %collective-permute-start.6) | collective-permute-done | bytes 897056 | tf_op jit(solution)/shard_map/ppermute | solution.py:869
  64.5 3.0 collective-permute-done.4.refs_3_.refs_8_.refs_14_.refs_11_.refs_10_
  70.2 21.6 %collective-permute-done.10.refs_4_.refs_9_.refs_15_.refs_12_.refs_11_ = bf16[1168,384]{1,0:T(8,128)(2,1)} collective-permute-done((bf16[1168,384]{1,0:T(8,128)(2,1)S(1)}, bf16[1168,384]{1,0:T(8,128)(2,1)}, u32[]{:S(2)}, u32[]{:S(2)}) %collective-permute-start.10) | collective-permute-done | bytes 897056 | tf_op jit(solution)/shard_map/ppermute | solution.py:878
  96.4 18.2 %collective-permute-done.16.refs_8_.refs_13_.refs_19_.refs_16_.refs_15_ = bf16[1168,384]{1,0:T(8,128)(2,1)} collective-permute-done((bf16[1168,384]{1,0:T(8,128)(2,1)}, bf16[1168,384]{1,0:T(8,128)(2,1)}, u32[]{:S(2)}, u32[]{:S(2)}) %collective-permute-start.16) | collective-permute-done | bytes 897056 | tf_op jit(solution)/shard_map/ppermute | solution.py:875
  115.2 2.1 collective-permute-done.20.refs_22_.refs_27_.refs_33_.refs_30_.refs_29_
  121.4 24.1 %collective-permute-done.23.refs_19_.refs_24_.refs_30_.refs_27_.refs_26_ = bf16[1168,384]{1,0:T(8,128)(2,1)} collective-permute-done((bf16[1168,384]{1,0:T(8,128)(2,1)}, bf16[1168,384]{1,0:T(8,128)(2,1)}, u32[]{:S(2)}, u32[]{:S(2)}) %collective-permute-start.23) | collective-permute-done | bytes 897056 | tf_op jit(solution)/shard_map/ppermute | solution.py:878
  151.0 2.5 shard_map.239
  154.3 32.9 %shard_map.240 = (bf16[512,2304]{1,0:T(8,128)(2,1)}, bf16[24,128,256]{2,1,0:T(8,128)(2,1)}, bf16[512,768]{1,0:T(8,128)(2,1)}, bf16[512,768]{1,0:T(8,128)(2,1)}, ...) custom-call(s32[8]{0:T(128)} %add_minimum_fusion.refs_0_, ...), custom_call_target="tpu_custom_call" | custom-call | flops 41799999488 | bytes 133000000 | tf_op jit(solution)/shard_map/pallas_call | solution.py:615
  187.2 3.0 all-gather.2.cloned.1.call-done
  190.2 2.1 fusion.59
  192.3 3.2 fusion.58
  195.6 3.5 convolution_convert_fusion.refs_4_.refs_2_
  199.0 3.5 add_convert_fusion.refs_5_.refs_3_
  202.5 45.6 %shard_map.241 = (bf16[512,768]{1,0:T(8,128)(2,1)}, bf16[48,160,128]{2,1,0:T(8,128)(2,1)}, bf16[512,768]{1,0:T(8,128)(2,1)}, bf16[512,768]{1,0:T(8,128)(2,1)}, f...) custom-call(s32[4]{0:T(128)} %pad_add_fusion.refs_0_.refs_1_, ...), custom_call_target="tpu_custom_call" | custom-call | flops 52800000000 | bytes 168000000 | tf_op jit(solution)/shard_map/pallas_call | solution.py:615
  248.2 19.9 %shard_map.242 = (f32[512,768]{1,0:T(8,128)}, bf16[1280,768]{1,0:T(8,128)(2,1)}, bf16[1280,768]{1,0:T(8,128)(2,1)}, bf16[768,768]{1,0:T(8,128)(2,1)}, bf16[768,768]{1,0:T(8,128)(2,1)}, /*index=5*/f32[8,768]{1,0:T(8,128)}) custom-call(f32[512,768]{1,0:T(8,128)} %get-tuple-element.178.refs_0_, bf16[512,768]{1,0:T(8,128)(2,1)} %get-tuple-element.173.refs_2_.refs_1_, ...), custom_call_target="tpu_custom_call" | custom-call | flops 28600000512 | bytes 91000000 | tf_op jit(solution)/shard_map/pallas_call | solution.py:615
  268.1 2.6 constant_dynamic-slice_fusion.2
  272.3 2.3 convolution_convert_fusion.2
  274.6 2.3 convolution_convert_fusion.1
  279.6 5.0 collective-permute-done.31
  284.5 2.1 convert_add_fusion
  289.1 18.1 %shard_map.243 = (bf16[512,768]{1,0:T(8,128)(2,1)}, bf16[2,8,400,384]{3,2,1,0:T(8,128)(2,1)}, bf16[2,8,400,384]{3,2,1,0:T(8,128)(2,1)}, f32[8,768]{1,0:T(8,128)}) custom-call(s32[4]{0:T(128)} %pad_add_fusion.refs_0_.refs_1_, f32[512,768]{1,0:T(8,128)} %get-tuple-element.191.refs_1_, bf16[512,768]{1,0:T(8,128)(2,1)} %get-tuple-element.192.refs_2_, ...), custom_call_target="tpu_custom_call" | custom-call | flops 24199999488 | bytes 77000000 | tf_op jit(solution)/shard_map/pallas_call | solution.py:615
  308.0 19.7 %shard_map.244 = (f32[512,768]{1,0:T(8,128)}, bf16[2,8,768,384]{3,2,1,0:T(8,128)(2,1)}, bf16[2,8,768,384]{3,2,1,0:T(8,128)(2,1)}, f32[8,768]{1,0:T(8,128)}) custom-call(s32[4]{0:T(128)} %pad_add_fusion.refs_0_.refs_1_, bf16[512,768]{1,0:T(8,128)(2,1)} %get-tuple-element.203.refs_1_, ...), custom_call_target="tpu_custom_call", output_to_operand_aliasing={{1}: (40, {}), {2}: (41, {})} | custom-call | flops 24199999488 | bytes 77000000 | tf_op jit(solution)/shard_map/pallas_call | solution.py:615
  332.7 18.4 %shard_map.245 = (f32[512,768]{1,0:T(8,128)}, bf16[2,8,400,384]{3,2,1,0:T(8,128)(2,1)}, bf16[2,8,400,384]{3,2,1,0:T(8,128)(2,1)}, f32[8,768]{1,0:T(8,128)}) custom-call(s32[4]{0:T(128)} %pad_add_fusion.refs_0_.refs_1_, f32[512,768]{1,0:T(8,128)} %get-tuple-element.217.refs_1_, ...), custom_call_target="tpu_custom_call", output_to_operand_aliasing={{1}: (41, {}), {2}: (42, {})} | custom-call | flops 24199999488 | bytes 77000000 | tf_op jit(solution)/shard_map/pallas_call | solution.py:615
  352.2 2.5 copy.89
  356.3 5.2 %fusion.42 = (bf16[768,384]{1,0:T(8,128)(2,1)S(1)}, bf16[768,384]{1,0:T(8,128)(2,1)S(1)}, bf16[768,384]{1,0:T(8,128)(2,1)}, bf16[768,384]{1,0:T(8,128)(2,1)S(1)}...) fusion(bf16[2,4,2,768,384]{4,3,2,1,0:T(8,128)(2,1)} %bitcast.43, ...), kind=kLoop, calls=%fused_computation.93 | loop fusion | flops 8257536 | bytes 12386304 | tf_op jit(solution)/shard_map/convert_element_type | solution.py:953
  361.7 2.0 collective-permute-start.37
  367.4 2.3 collective-permute-done.36
  369.7 4.5 fusion.51
  374.2 8.5 %collective-permute-done.40 = bf16[112,768]{1,0:T(8,128)(2,1)S(1)} collective-permute-done((bf16[112,768]{1,0:T(8,128)(2,1)S(1)}, bf16[112,768]{1,0:T(8,128)(2,1)S(1)}, u32[]{:S(2)}, u32[]{:S(2)}) %collective-permute-start.40) | collective-permute-done | bytes 172064 | tf_op jit(solution)/shard_map/ppermute | solution.py:878
  385.5 6.6 %collective-permute-done.41 = bf16[400,384]{1,0:T(8,128)(2,1)S(1)} collective-permute-done((bf16[400,384]{1,0:T(8,128)(2,1)S(1)}, bf16[400,384]{1,0:T(8,128)(2,1)S(1)}, u32[]{:S(2)}, u32[]{:S(2)}) %collective-permute-start.41) | collective-permute-done | bytes 307232 | tf_op jit(solution)/shard_map/ppermute | solution.py:875
  396.1 2.3 fusion.13
  400.5 3.8 collective-permute-done.44
  406.0 3.1 fusion.24
  410.3 4.1 collective-permute-done.54
  416.3 6.9 %collective-permute-done.56 = bf16[768,384]{1,0:T(8,128)(2,1)} collective-permute-done((bf16[768,384]{1,0:T(8,128)(2,1)S(1)}, bf16[768,384]{1,0:T(8,128)(2,1)}, u32[]{:S(2)}, u32[]{:S(2)}) %collective-permute-start.56) | collective-permute-done | bytes 589856 | tf_op jit(solution)/shard_map/ppermute | solution.py:878
  423.2 4.2 fusion.11
  429.0 4.5 collective-permute-done.47
  436.1 3.0 fusion.22
  439.1 3.4 collective-permute-done.57
  443.4 4.2 fusion.9
  451.8 12.2 %collective-permute-done.60 = bf16[768,384]{1,0:T(8,128)(2,1)S(1)} collective-permute-done((bf16[768,384]{1,0:T(8,128)(2,1)}, bf16[768,384]{1,0:T(8,128)(2,1)S(1)}, u32[]{:S(2)}, u32[]{:S(2)}) %collective-permute-start.60) | collective-permute-done | bytes 589856 | tf_op jit(solution)/shard_map/ppermute | solution.py:878
  464.0 2.6 collective-permute-start.53
  470.6 2.5 collective-permute-start.65
  475.8 7.2 %collective-permute-done.63 = bf16[768,384]{1,0:T(8,128)(2,1)S(1)} collective-permute-done((bf16[768,384]{1,0:T(8,128)(2,1)S(1)}, bf16[768,384]{1,0:T(8,128)(2,1)S(1)}, u32[]{:S(2)}, u32[]{:S(2)}) %collective-permute-start.63) | collective-permute-done | bytes 589856 | tf_op jit(solution)/shard_map/ppermute | solution.py:878
  490.8 3.8 collective-permute-done.66
  (299 shorter events, 95.8 us)
Async XLA Ops:
  7.2 183.0 %all-gather.2.cloned.1.call-start = ((), (), s32[]{:S(2)}) async-start(), calls=%async_computation | async-start | bytes 5677056 | tf_op jit(solution)/shard_map/all_gather | solution.py:1125
  15.8 22.9 %collective-permute-start.1 = (bf16[1168,384]{1,0:T(8,128)(2,1)S(1)}, bf16[1168,384]{1,0:T(8,128)(2,1)S(1)}, u32[]{:S(2)}, u32[]{:S(2)}) collective-permute-start(bf16[1168,384]{1,0:T(8,128)(2,1)S(1)} %constant_dynamic-update-slice_fusion.refs_1_.refs_6_.refs_12_.refs_9_.refs_8_), channel_id=1, source_target_pairs={{0,1},{1,0},{2,3},{3,2},{4,5},{5,4},{6,7},{7,6},{8,9},{9,8},{10,11... | collective-permute-start | bytes 2691080 | tf_op jit(solution)/shard_map/ppermute | solution.py:875
  18.8 23.2 %collective-permute-start = (bf16[1168,384]{1,0:T(8,128)(2,1)S(1)}, bf16[1168,384]{1,0:T(8,128)(2,1)S(1)}, u32[]{:S(2)}, u32[]{:S(2)}) collective-permute-start(bf16[1168,384]{1,0:T(8,128)(2,1)S(1)} %constant_dynamic-update-slice_fusion.refs_1_.refs_6_.refs_12_.refs_9_.refs_8_), channel_id=1, source_target_pairs={{0,2},{1,3},{2,4},{3,5},{4,6},{5,7},{6,0},{7,1},{8,10},{9,11},{10,... | collective-permute-start | bytes 2691080 | tf_op jit(solution)/shard_map/ppermute | solution.py:878
  20.4 21.7 %collective-permute-start.2 = (bf16[1168,384]{1,0:T(8,128)(2,1)S(1)}, bf16[1168,384]{1,0:T(8,128)(2,1)S(1)}, u32[]{:S(2)}, u32[]{:S(2)}) collective-permute-start(bf16[1168,384]{1,0:T(8,128)(2,1)S(1)} %constant_dynamic-update-slice_fusion.refs_1_.refs_6_.refs_12_.refs_9_.refs_8_), channel_id=1, source_target_pairs={{0,16},{8,24},{16,0},{24,8},{1,17},{9,25},{17,1},{25,9},{2,18},{10... | collective-permute-start | bytes 2691080 | tf_op jit(solution)/shard_map/ppermute | solution.py:869
  21.9 20.2 %collective-permute-start.3 = (bf16[1168,384]{1,0:T(8,128)(2,1)S(1)}, bf16[1168,384]{1,0:T(8,128)(2,1)S(1)}, u32[]{:S(2)}, u32[]{:S(2)}) collective-permute-start(bf16[1168,384]{1,0:T(8,128)(2,1)S(1)} %constant_dynamic-update-slice_fusion.refs_1_.refs_6_.refs_12_.refs_9_.refs_8_), channel_id=1, source_target_pairs={{0,8},{8,0},{16,24},{24,16},{1,9},{9,1},{17,25},{25,17},{2,10},{10... | collective-permute-start | bytes 2691080 | tf_op jit(solution)/shard_map/ppermute | solution.py:872
  42.2 22.3 %collective-permute-start.6 = (bf16[1168,384]{1,0:T(8,128)(2,1)S(1)}, bf16[1168,384]{1,0:T(8,128)(2,1)S(1)}, u32[]{:S(2)}, u32[]{:S(2)}) collective-permute-start(bf16[1168,384]{1,0:T(8,128)(2,1)S(1)} %collective-permute-done.refs_2_.refs_7_.refs_13_.refs_10_.refs_9_), channel_id=1, source_target_pairs={{0,16},{8,24},{16,0},{24,8},{1,17},{9,25},{17,1},{25,9},{2,18},{10... | collective-permute-start | bytes 2691080 | tf_op jit(solution)/shard_map/ppermute | solution.py:869
  43.7 23.8 %collective-permute-start.4 = (bf16[1168,384]{1,0:T(8,128)(2,1)S(1)}, bf16[1168,384]{1,0:T(8,128)(2,1)S(1)}, u32[]{:S(2)}, u32[]{:S(2)}) collective-permute-start(bf16[1168,384]{1,0:T(8,128)(2,1)S(1)} %collective-permute-done.refs_2_.refs_7_.refs_13_.refs_10_.refs_9_), channel_id=1, source_target_pairs={{0,2},{1,3},{2,4},{3,5},{4,6},{5,7},{6,0},{7,1},{8,10},{9,11},{10,... | collective-permute-start | bytes 2691080 | tf_op jit(solution)/shard_map/ppermute | solution.py:878
  44.7 22.8 %collective-permute-start.5 = (bf16[1168,384]{1,0:T(8,128)(2,1)S(1)}, bf16[1168,384]{1,0:T(8,128)(2,1)S(1)}, u32[]{:S(2)}, u32[]{:S(2)}) collective-permute-start(bf16[1168,384]{1,0:T(8,128)(2,1)S(1)} %collective-permute-done.refs_2_.refs_7_.refs_13_.refs_10_.refs_9_), channel_id=1, source_target_pairs={{0,1},{1,0},{2,3},{3,2},{4,5},{5,4},{6,7},{7,6},{8,9},{9,8},{10,11... | collective-permute-start | bytes 2691080 | tf_op jit(solution)/shard_map/ppermute | solution.py:875
  45.2 22.3 %collective-permute-start.8 = (bf16[1168,384]{1,0:T(8,128)(2,1)S(1)}, bf16[1168,384]{1,0:T(8,128)(2,1)S(1)}, u32[]{:S(2)}, u32[]{:S(2)}) collective-permute-start(bf16[1168,384]{1,0:T(8,128)(2,1)S(1)} %collective-permute-done.1.refs_5_.refs_10_.refs_16_.refs_13_.refs_12_), channel_id=1, source_target_pairs={{0,8},{8,0},{16,24},{24,16},{1,9},{9,1},{17,25},{25,17},{2,10},{10... | collective-permute-start | bytes 2691080 | tf_op jit(solution)/shard_map/ppermute | solution.py:872
  46.2 21.4 %collective-permute-start.9 = (bf16[1168,384]{1,0:T(8,128)(2,1)S(1)}, bf16[1168,384]{1,0:T(8,128)(2,1)S(1)}, u32[]{:S(2)}, u32[]{:S(2)}) collective-permute-start(bf16[1168,384]{1,0:T(8,128)(2,1)S(1)} %collective-permute-done.2.refs_17_.refs_22_.refs_28_.refs_25_.refs_24_), channel_id=1, source_target_pairs={{0,8},{8,0},{16,24},{24,16},{1,9},{9,1},{17,25},{25,17},{2,10},{10... | collective-permute-start | bytes 2691080 | tf_op jit(solution)/shard_map/ppermute | solution.py:872
  67.6 24.2 %collective-permute-start.10 = (bf16[1168,384]{1,0:T(8,128)(2,1)S(1)}, bf16[1168,384]{1,0:T(8,128)(2,1)}, u32[]{:S(2)}, u32[]{:S(2)}) collective-permute-start(bf16[1168,384]{1,0:T(8,128)(2,1)S(1)} %collective-permute-done.4.refs_3_.refs_8_.refs_14_.refs_11_.refs_10_), channel_id=1, source_target_pairs={{0,2},{1,3},{2,4},{3,5},{4,6},{5,7},{6,0},{7,1},{8,10},{9,11},{10,... | collective-permute-start | bytes 2691080 | tf_op jit(solution)/shard_map/ppermute | solution.py:878
  68.2 23.7 %collective-permute-start.11 = (bf16[1168,384]{1,0:T(8,128)(2,1)S(1)}, bf16[1168,384]{1,0:T(8,128)(2,1)}, u32[]{:S(2)}, u32[]{:S(2)}) collective-permute-start(bf16[1168,384]{1,0:T(8,128)(2,1)S(1)} %collective-permute-done.4.refs_3_.refs_8_.refs_14_.refs_11_.refs_10_), channel_id=1, source_target_pairs={{0,1},{1,0},{2,3},{3,2},{4,5},{5,4},{6,7},{7,6},{8,9},{9,8},{10,11... | collective-permute-start | bytes 2691080 | tf_op jit(solution)/shard_map/ppermute | solution.py:875
  68.7 23.2 %collective-permute-start.12 = (bf16[1168,384]{1,0:T(8,128)(2,1)S(1)}, bf16[1168,384]{1,0:T(8,128)(2,1)}, u32[]{:S(2)}, u32[]{:S(2)}) collective-permute-start(bf16[1168,384]{1,0:T(8,128)(2,1)S(1)} %collective-permute-done.1.refs_5_.refs_10_.refs_16_.refs_13_.refs_12_), channel_id=1, source_target_pairs={{0,16},{8,24},{16,0},{24,8},{1,17},{9,25},{17,1},{25,9},{2,18},{10... | collective-permute-start | bytes 2691080 | tf_op jit(solution)/shard_map/ppermute | solution.py:869
  69.2 22.7 %collective-permute-start.14 = (bf16[1168,384]{1,0:T(8,128)(2,1)S(1)}, bf16[1168,384]{1,0:T(8,128)(2,1)S(1)}, u32[]{:S(2)}, u32[]{:S(2)}) collective-permute-start(bf16[1168,384]{1,0:T(8,128)(2,1)S(1)} %collective-permute-done.5.refs_6_.refs_11_.refs_17_.refs_14_.refs_13_), channel_id=1, source_target_pairs={{0,8},{8,0},{16,24},{24,16},{1,9},{9,1},{17,25},{25,17},{2,10},{10... | collective-permute-start | bytes 2691080 | tf_op jit(solution)/shard_map/ppermute | solution.py:872
  70.1 21.8 %collective-permute-start.15 = (bf16[1168,384]{1,0:T(8,128)(2,1)S(1)}, bf16[1168,384]{1,0:T(8,128)(2,1)S(1)}, u32[]{:S(2)}, u32[]{:S(2)}) collective-permute-start(bf16[1168,384]{1,0:T(8,128)(2,1)S(1)} %collective-permute-done.6.refs_18_.refs_23_.refs_29_.refs_26_.refs_25_), channel_id=1, source_target_pairs={{0,8},{8,0},{16,24},{24,16},{1,9},{9,1},{17,25},{25,17},{2,10},{10... | collective-permute-start | bytes 2691080 | tf_op jit(solution)/shard_map/ppermute | solution.py:872
  92.0 22.6 %collective-permute-start.16 = (bf16[1168,384]{1,0:T(8,128)(2,1)}, bf16[1168,384]{1,0:T(8,128)(2,1)}, u32[]{:S(2)}, u32[]{:S(2)}) collective-permute-start(bf16[1168,384]{1,0:T(8,128)(2,1)} %collective-permute-done.10.refs_4_.refs_9_.refs_15_.refs_12_.refs_11_), channel_id=1, source_target_pairs={{0,1},{1,0},{2,3},{3,2},{4,5},{5,4},{6,7},{7,6},{8,9},{9,8},{10,11... | collective-permute-start | bytes 2691080 | tf_op jit(solution)/shard_map/ppermute | solution.py:875
  92.6 22.1 %collective-permute-start.18 = (bf16[1168,384]{1,0:T(8,128)(2,1)}, bf16[1168,384]{1,0:T(8,128)(2,1)}, u32[]{:S(2)}, u32[]{:S(2)}) collective-permute-start(bf16[1168,384]{1,0:T(8,128)(2,1)} %collective-permute-done.11.refs_7_.refs_12_.refs_18_.refs_15_.refs_14_), channel_id=1, source_target_pairs={{0,8},{8,0},{16,24},{24,16},{1,9},{9,1},{17,25},{25,17},{2,10},{10... | collective-permute-start | bytes 2691080 | tf_op jit(solution)/shard_map/ppermute | solution.py:872
  92.7 22.5 %collective-permute-start.19 = (bf16[1168,384]{1,0:T(8,128)(2,1)}, bf16[1168,384]{1,0:T(8,128)(2,1)}, u32[]{:S(2)}, u32[]{:S(2)}) collective-permute-start(bf16[1168,384]{1,0:T(8,128)(2,1)} %collective-permute-done.10.refs_4_.refs_9_.refs_15_.refs_12_.refs_11_), channel_id=1, source_target_pairs={{0,16},{8,24},{16,0},{24,8},{1,17},{9,25},{17,1},{25,9},{2,18},{10... | collective-permute-start | bytes 2691080 | tf_op jit(solution)/shard_map/ppermute | solution.py:869
  93.3 24.0 %collective-permute-start.20 = (bf16[1168,384]{1,0:T(8,128)(2,1)}, bf16[1168,384]{1,0:T(8,128)(2,1)}, u32[]{:S(2)}, u32[]{:S(2)}) collective-permute-start(bf16[1168,384]{1,0:T(8,128)(2,1)} %collective-permute-done.12.refs_21_.refs_26_.refs_32_.refs_29_.refs_28_), channel_id=1, source_target_pairs={{0,2},{1,3},{2,4},{3,5},{4,6},{5,7},{6,0},{7,1},{8,10},{9,11},{10,... | collective-permute-start | bytes 2691080 | tf_op jit(solution)/shard_map/ppermute | solution.py:878
  95.6 21.7 %collective-permute-start.21 = (bf16[1168,384]{1,0:T(8,128)(2,1)}, bf16[1168,384]{1,0:T(8,128)(2,1)}, u32[]{:S(2)}, u32[]{:S(2)}) collective-permute-start(bf16[1168,384]{1,0:T(8,128)(2,1)} %collective-permute-done.12.refs_21_.refs_26_.refs_32_.refs_29_.refs_28_), channel_id=1, source_target_pairs={{0,8},{8,0},{16,24},{24,16},{1,9},{9,1},{17,25},{25,17},{2,10},{10... | collective-permute-start | bytes 2691080 | tf_op jit(solution)/shard_map/ppermute | solution.py:872
  117.9 27.7 %collective-permute-start.23 = (bf16[1168,384]{1,0:T(8,128)(2,1)}, bf16[1168,384]{1,0:T(8,128)(2,1)}, u32[]{:S(2)}, u32[]{:S(2)}) collective-permute-start(bf16[1168,384]{1,0:T(8,128)(2,1)} %copy-done.13), channel_id=1, source_target_pairs={{0,2},{1,3},{2,4},{3,5},{4,6},{5,7},{6,0},{7,1},{8,10},{9,11},{10,... | collective-permute-start | bytes 2691080 | tf_op jit(solution)/shard_map/ppermute | solution.py:878
  117.9 27.7 %collective-permute-start.24 = (bf16[1168,384]{1,0:T(8,128)(2,1)}, bf16[1168,384]{1,0:T(8,128)(2,1)}, u32[]{:S(2)}, u32[]{:S(2)}) collective-permute-start(bf16[1168,384]{1,0:T(8,128)(2,1)} %collective-permute-done.11.refs_7_.refs_12_.refs_18_.refs_15_.refs_14_), channel_id=1, source_target_pairs={{0,16},{8,24},{16,0},{24,8},{1,17},{9,25},{17,1},{25,9},{2,18},{10... | collective-permute-start | bytes 2691080 | tf_op jit(solution)/shard_map/ppermute | solution.py:869
  119.4 26.2 %collective-permute-start.25 = (bf16[1168,384]{1,0:T(8,128)(2,1)}, bf16[1168,384]{1,0:T(8,128)(2,1)}, u32[]{:S(2)}, u32[]{:S(2)}) collective-permute-start(bf16[1168,384]{1,0:T(8,128)(2,1)} %collective-permute-done.19.refs_20_.refs_25_.refs_31_.refs_28_.refs_27_), channel_id=1, source_target_pairs={{0,1},{1,0},{2,3},{3,2},{4,5},{5,4},{6,7},{7,6},{8,9},{9,8},{10,11... | collective-permute-start | bytes 2691080 | tf_op jit(solution)/shard_map/ppermute | solution.py:875
  120.9 24.7 %collective-permute-start.27 = (bf16[1168,384]{1,0:T(8,128)(2,1)}, bf16[1168,384]{1,0:T(8,128)(2,1)}, u32[]{:S(2)}, u32[]{:S(2)}) collective-permute-start(bf16[1168,384]{1,0:T(8,128)(2,1)} %collective-permute-done.19.refs_20_.refs_25_.refs_31_.refs_28_.refs_27_), channel_id=1, source_target_pairs={{0,8},{8,0},{16,24},{24,16},{1,9},{9,1},{17,25},{25,17},{2,10},{10... | collective-permute-start | bytes 2691080 | tf_op jit(solution)/shard_map/ppermute | solution.py:872
  287.7 19.5 %collective-permute-start.32 = (bf16[2,2,112,768]{3,2,0,1:T(8,128)(2,1)}, bf16[2,2,112,768]{3,2,0,1:T(8,128)(2,1)}, u32[]{:S(2)}, u32[]{:S(2)}) collective-permute-start(bf16[2,2,112,768]{3,2,0,1:T(8,128)(2,1)} %get-tuple-element.190), channel_id=1, source_target_pairs={{0,16},{8,24},{16,0},{24,8},{1,17},{9,25},{17,1},{25,9},{2,18},{10... | collective-permute-start | bytes 2064392 | tf_op jit(solution)/shard_map/ppermute | solution.py:869
  307.3 20.4 %collective-permute-start.33 = (bf16[2,2,112,768]{3,2,0,1:T(8,128)(2,1)S(1)}, bf16[2,2,112,768]{3,2,0,1:T(8,128)(2,1)}, u32[]{:S(2)}, u32[]{:S(2)}) collective-permute-start(bf16[2,2,112,768]{3,2,0,1:T(8,128)(2,1)S(1)} %get-tuple-element.202), channel_id=1, source_target_pairs={{0,16},{8,24},{16,0},{24,8},{1,17},{9,25},{17,1},{25,9},{2,18},{10... | collective-permute-start | bytes 2064392 | tf_op jit(solution)/shard_map/ppermute | solution.py:869
  330.8 25.4 %collective-permute-start.34 = (bf16[2,8,768,384]{3,2,1,0:T(8,128)(2,1)}, bf16[2,8,768,384]{3,2,1,0:T(8,128)(2,1)}, u32[]{:S(2)}, u32[]{:S(2)}) collective-permute-start(bf16[2,8,768,384]{3,2,1,0:T(8,128)(2,1)} %get-tuple-element.215), channel_id=1, source_target_pairs={{0,8},{8,0},{16,24},{24,16},{1,9},{9,1},{17,25},{25,17},{2,10},{10... | collective-permute-start | bytes 28311560 | tf_op jit(solution)/shard_map/ppermute | solution.py:872
  331.2 23.7 %collective-permute-start.35 = (bf16[4,112,768]{2,1,0:T(8,128)(2,1)S(1)}, bf16[4,112,768]{2,1,0:T(8,128)(2,1)S(1)}, u32[]{:S(2)}, u32[]{:S(2)}) collective-permute-start(bf16[4,112,768]{2,1,0:T(8,128)(2,1)S(1)} %fusion.21), channel_id=1, source_target_pairs={{0,1},{1,0},{2,3},{3,2},{4,5},{5,4},{6,7},{7,6},{8,9},{9,8},{10,11... | collective-permute-start | bytes 2064392 | tf_op jit(solution)/shard_map/ppermute | solution.py:875
  361.7 21.0 %collective-permute-start.37 = (bf16[768,384]{1,0:T(8,128)(2,1)S(1)}, bf16[768,384]{1,0:T(8,128)(2,1)S(1)}, u32[]{:S(2)}, u32[]{:S(2)}) collective-permute-start(bf16[768,384]{1,0:T(8,128)(2,1)S(1)} %get-tuple-element.230), channel_id=1, source_target_pairs={{0,2},{1,3},{2,4},{3,5},{4,6},{5,7},{6,0},{7,1},{8,10},{9,11},{10,... | collective-permute-start | bytes 1769480 | tf_op jit(solution)/shard_map/ppermute | solution.py:878
  363.7 19.0 %collective-permute-start.38 = (bf16[768,384]{1,0:T(8,128)(2,1)S(1)}, bf16[768,384]{1,0:T(8,128)(2,1)S(1)}, u32[]{:S(2)}, u32[]{:S(2)}) collective-permute-start(bf16[768,384]{1,0:T(8,128)(2,1)S(1)} %get-tuple-element.231), channel_id=1, source_target_pairs={{0,1},{1,0},{2,3},{3,2},{4,5},{5,4},{6,7},{7,6},{8,9},{9,8},{10,11... | collective-permute-start | bytes 1769480 | tf_op jit(solution)/shard_map/ppermute | solution.py:875
  364.2 18.5 %collective-permute-start.39 = (bf16[768,384]{1,0:T(8,128)(2,1)S(1)}, bf16[768,384]{1,0:T(8,128)(2,1)S(1)}, u32[]{:S(2)}, u32[]{:S(2)}) collective-permute-start(bf16[768,384]{1,0:T(8,128)(2,1)S(1)} %get-tuple-element.232), channel_id=1, source_target_pairs={{0,16},{8,24},{16,0},{24,8},{1,17},{9,25},{17,1},{25,9},{2,18},{10... | collective-permute-start | bytes 1769480 | tf_op jit(solution)/shard_map/ppermute | solution.py:869
  365.6 17.1 %collective-permute-start.40 = (bf16[112,768]{1,0:T(8,128)(2,1)S(1)}, bf16[112,768]{1,0:T(8,128)(2,1)S(1)}, u32[]{:S(2)}, u32[]{:S(2)}) collective-permute-start(bf16[112,768]{1,0:T(8,128)(2,1)S(1)} %fusion.54), channel_id=1, source_target_pairs={{0,2},{1,3},{2,4},{3,5},{4,6},{5,7},{6,0},{7,1},{8,10},{9,11},{10,... | collective-permute-start | bytes 516104 | tf_op jit(solution)/shard_map/ppermute | solution.py:878
  398.4 16.0 %collective-permute-start.54 = (bf16[768,384]{1,0:T(8,128)(2,1)}, bf16[768,384]{1,0:T(8,128)(2,1)}, u32[]{:S(2)}, u32[]{:S(2)}) collective-permute-start(bf16[768,384]{1,0:T(8,128)(2,1)} %get-tuple-element.247), channel_id=1, source_target_pairs={{0,1},{1,0},{2,3},{3,2},{4,5},{5,4},{6,7},{7,6},{8,9},{9,8},{10,11... | collective-permute-start | bytes 1769480 | tf_op jit(solution)/shard_map/ppermute | solution.py:875
  399.8 16.0 %collective-permute-start.55 = (bf16[768,384]{1,0:T(8,128)(2,1)}, bf16[768,384]{1,0:T(8,128)(2,1)}, u32[]{:S(2)}, u32[]{:S(2)}) collective-permute-start(bf16[768,384]{1,0:T(8,128)(2,1)} %fusion.13), channel_id=1, source_target_pairs={{0,16},{8,24},{16,0},{24,8},{1,17},{9,25},{17,1},{25,9},{2,18},{10... | collective-permute-start | bytes 1769480 | tf_op jit(solution)/shard_map/ppermute | solution.py:869
  405.0 18.2 %collective-permute-start.56 = (bf16[768,384]{1,0:T(8,128)(2,1)S(1)}, bf16[768,384]{1,0:T(8,128)(2,1)}, u32[]{:S(2)}, u32[]{:S(2)}) collective-permute-start(bf16[768,384]{1,0:T(8,128)(2,1)S(1)} %get-tuple-element.249), channel_id=1, source_target_pairs={{0,2},{1,3},{2,4},{3,5},{4,6},{5,7},{6,0},{7,1},{8,10},{9,11},{10,... | collective-permute-start | bytes 1769480 | tf_op jit(solution)/shard_map/ppermute | solution.py:878
  409.1 18.3 %collective-permute-start.49 = (bf16[112,768]{1,0:T(8,128)(2,1)S(1)}, bf16[112,768]{1,0:T(8,128)(2,1)S(1)}, u32[]{:S(2)}, u32[]{:S(2)}) collective-permute-start(bf16[112,768]{1,0:T(8,128)(2,1)S(1)} %fusion.44), channel_id=1, source_target_pairs={{0,2},{1,3},{2,4},{3,5},{4,6},{5,7},{6,0},{7,1},{8,10},{9,11},{10,... | collective-permute-start | bytes 516104 | tf_op jit(solution)/shard_map/ppermute | solution.py:878
  409.1 24.3 %collective-permute-start.47 = (bf16[400,384]{1,0:T(8,128)(2,1)S(1)}, bf16[400,384]{1,0:T(8,128)(2,1)}, u32[]{:S(2)}, u32[]{:S(2)}) collective-permute-start(bf16[400,384]{1,0:T(8,128)(2,1)S(1)} %get-tuple-element.240), channel_id=1, source_target_pairs={{0,2},{1,3},{2,4},{3,5},{4,6},{5,7},{6,0},{7,1},{8,10},{9,11},{10,... | collective-permute-start | bytes 921608 | tf_op jit(solution)/shard_map/ppermute | solution.py:878
  414.4 21.7 %collective-permute-start.48 = (bf16[400,384]{1,0:T(8,128)(2,1)}, bf16[400,384]{1,0:T(8,128)(2,1)}, u32[]{:S(2)}, u32[]{:S(2)}) collective-permute-start(bf16[400,384]{1,0:T(8,128)(2,1)} %get-tuple-element.241), channel_id=1, source_target_pairs={{0,1},{1,0},{2,3},{3,2},{4,5},{5,4},{6,7},{7,6},{8,9},{9,8},{10,11... | collective-permute-start | bytes 921608 | tf_op jit(solution)/shard_map/ppermute | solution.py:875
  415.9 20.2 %collective-permute-start.50 = (bf16[400,384]{1,0:T(8,128)(2,1)}, bf16[400,384]{1,0:T(8,128)(2,1)}, u32[]{:S(2)}, u32[]{:S(2)}) collective-permute-start(bf16[400,384]{1,0:T(8,128)(2,1)} %get-tuple-element.243), channel_id=1, source_target_pairs={{0,16},{8,24},{16,0},{24,8},{1,17},{9,25},{17,1},{25,9},{2,18},{10... | collective-permute-start | bytes 921608 | tf_op jit(solution)/shard_map/ppermute | solution.py:869
  427.4 15.1 %collective-permute-start.57 = (bf16[768,384]{1,0:T(8,128)(2,1)}, bf16[768,384]{1,0:T(8,128)(2,1)}, u32[]{:S(2)}, u32[]{:S(2)}) collective-permute-start(bf16[768,384]{1,0:T(8,128)(2,1)} %get-tuple-element.250), channel_id=1, source_target_pairs={{0,2},{1,3},{2,4},{3,5},{4,6},{5,7},{6,0},{7,1},{8,10},{9,11},{10,... | collective-permute-start | bytes 1769480 | tf_op jit(solution)/shard_map/ppermute | solution.py:878
  427.4 15.1 %collective-permute-start.58 = (bf16[768,384]{1,0:T(8,128)(2,1)}, bf16[768,384]{1,0:T(8,128)(2,1)}, u32[]{:S(2)}, u32[]{:S(2)}) collective-permute-start(bf16[768,384]{1,0:T(8,128)(2,1)} %get-tuple-element.251), channel_id=1, source_target_pairs={{0,1},{1,0},{2,3},{3,2},{4,5},{5,4},{6,7},{7,6},{8,9},{9,8},{10,11... | collective-permute-start | bytes 1769480 | tf_op jit(solution)/shard_map/ppermute | solution.py:875
  447.7 16.3 %collective-permute-start.60 = (bf16[768,384]{1,0:T(8,128)(2,1)}, bf16[768,384]{1,0:T(8,128)(2,1)S(1)}, u32[]{:S(2)}, u32[]{:S(2)}) collective-permute-start(bf16[768,384]{1,0:T(8,128)(2,1)} %get-tuple-element.253), channel_id=1, source_target_pairs={{0,2},{1,3},{2,4},{3,5},{4,6},{5,7},{6,0},{7,1},{8,10},{9,11},{10,... | collective-permute-start | bytes 1769480 | tf_op jit(solution)/shard_map/ppermute | solution.py:878
  447.7 18.9 %collective-permute-start.61 = (bf16[768,384]{1,0:T(8,128)(2,1)S(1)}, bf16[768,384]{1,0:T(8,128)(2,1)}, u32[]{:S(2)}, u32[]{:S(2)}) collective-permute-start(bf16[768,384]{1,0:T(8,128)(2,1)S(1)} %get-tuple-element.254), channel_id=1, source_target_pairs={{0,1},{1,0},{2,3},{3,2},{4,5},{5,4},{6,7},{7,6},{8,9},{9,8},{10,11... | collective-permute-start | bytes 1769480 | tf_op jit(solution)/shard_map/ppermute | solution.py:875
  449.4 17.2 %collective-permute-start.62 = (bf16[768,384]{1,0:T(8,128)(2,1)}, bf16[768,384]{1,0:T(8,128)(2,1)}, u32[]{:S(2)}, u32[]{:S(2)}) collective-permute-start(bf16[768,384]{1,0:T(8,128)(2,1)} %get-tuple-element.255), channel_id=1, source_target_pairs={{0,16},{8,24},{16,0},{24,8},{1,17},{9,25},{17,1},{25,9},{2,18},{10... | collective-permute-start | bytes 1769480 | tf_op jit(solution)/shard_map/ppermute | solution.py:869
  449.4 21.2 %collective-permute-start.51 = (bf16[400,384]{1,0:T(8,128)(2,1)}, bf16[400,384]{1,0:T(8,128)(2,1)S(1)}, u32[]{:S(2)}, u32[]{:S(2)}) collective-permute-start(bf16[400,384]{1,0:T(8,128)(2,1)} %get-tuple-element.244), channel_id=1, source_target_pairs={{0,2},{1,3},{2,4},{3,5},{4,6},{5,7},{6,0},{7,1},{8,10},{9,11},{10,... | collective-permute-start | bytes 921608 | tf_op jit(solution)/shard_map/ppermute | solution.py:878
  449.4 25.0 %collective-permute-start.52 = (bf16[400,384]{1,0:T(8,128)(2,1)S(1)}, bf16[400,384]{1,0:T(8,128)(2,1)S(1)}, u32[]{:S(2)}, u32[]{:S(2)}) collective-permute-start(bf16[400,384]{1,0:T(8,128)(2,1)S(1)} %copy-done.28), channel_id=1, source_target_pairs={{0,1},{1,0},{2,3},{3,2},{4,5},{5,4},{6,7},{7,6},{8,9},{9,8},{10,11... | collective-permute-start | bytes 921608 | tf_op jit(solution)/shard_map/ppermute | solution.py:875
  468.6 14.4 %collective-permute-start.63 = (bf16[768,384]{1,0:T(8,128)(2,1)S(1)}, bf16[768,384]{1,0:T(8,128)(2,1)S(1)}, u32[]{:S(2)}, u32[]{:S(2)}) collective-permute-start(bf16[768,384]{1,0:T(8,128)(2,1)S(1)} %fusion.20), channel_id=1, source_target_pairs={{0,2},{1,3},{2,4},{3,5},{4,6},{5,7},{6,0},{7,1},{8,10},{9,11},{10,... | collective-permute-start | bytes 1769480 | tf_op jit(solution)/shard_map/ppermute | solution.py:878
  468.6 14.4 %collective-permute-start.64 = (bf16[768,384]{1,0:T(8,128)(2,1)S(1)}, bf16[768,384]{1,0:T(8,128)(2,1)S(1)}, u32[]{:S(2)}, u32[]{:S(2)}) collective-permute-start(bf16[768,384]{1,0:T(8,128)(2,1)S(1)} %copy-done.26), channel_id=1, source_target_pairs={{0,1},{1,0},{2,3},{3,2},{4,5},{5,4},{6,7},{7,6},{8,9},{9,8},{10,11... | collective-permute-start | bytes 1769480 | tf_op jit(solution)/shard_map/ppermute | solution.py:875
  (74 other events, 1253.0 us)
Sparse Core Ops, SparseCore 0:
  117.4 72.7 all-gather.1

commit v9 on v8

--- a/solution.py
+++ b/solution.py
@@ -943,7 +943,7 @@
     def block(self, own, y, z):
         layer = 0 if own else 1
         parts = [self.own[layer, z, y], self.came[layer, z, y], *self.got.get((own, y, z), [])]
-        return sum(part.astype(F32) for part in parts)
+        return sum(parts[1:], parts[0])
 
     def move(self, over, own, y, z):
         to = {"z": (own, y, z - 1), "y": (own, 1 - y, z), "x": (True, y, z)}[over]
@@ -965,7 +965,7 @@
         ]
 
     def total(self):
-        return self.block(True, 0, 0)
+        return self.block(True, 0, 0).astype(F32)
 
 
 class BlockSum:
@@ -1114,6 +1114,7 @@
         gather = Gather(grid, jnp.concatenate([pack_attn, pack_feed, pad_to(small, 16, lanes)]))
         get = gather.get
         turn(get(0, 0, 1, "z"), get(0, 1, 0, "y"), get(1, 0, 0, "x"), gather.c3, chain=True)
+        grid.slack = 2
         image = turn(
             get(0, 0, 2, "z"), get(0, 1, 1, "y"), get(1, 0, 1, "x"), gather.c3, chain=True, compute=padded, args=(image_feats,)
         )
@@ -1121,6 +1122,7 @@
         turn(get(1, 1, 1, "z"), get(0, 1, 3, "y"), get(1, 0, 3, "x"), gather.c3, chain=True)
         turn(get(1, 0, 2, "z"), get(1, 1, 3, "y"), get(1, 1, 2, "x"), gather.c3, chain=True)
         turn(gather.c)
+        grid.slack = 1
         weights = gather.pieces()
         cross_whole = lax.all_gather(after(cross_pack, grid.arrived[-3]), everyone, axis=0, tiled=True)
         *vectors, cvec = gathered_vectors(weights, where, n_pack, v_rows, v_lanes, x_rows, c_rows)

time: 515 us -> 512 us (level)
    convert_element_type x10 -> x2, other arithmetic: 30.9 us -> 2.56 us  [total(): return self.block(True, 0, 0).astype(F32)]
    add x2 -> x10, other arithmetic: 2.87 us -> 28.2 us  [block(): return sum(parts[1:], parts[0])]
    ppermute x18, waiting for transfers between devices: 103 us -> 120 us  [ring_z(): return lax.ppermute(a, 'dp', [(i, (i + 2 * step) % 8) for i in range(8)])]
    ppermute x16, waiting for transfers between devices: 49.4 us -> 32.5 us  [swap_y(): return lax.ppermute(a, 'dp', [(i, i ^ 1) for i in range(8)])]
    unnamed x112 -> x102, local copies, waits for them, and re-layouts: 19.5 us -> 16.3 us
  transfers between devices with their start and end apart: 71 -> 71, of which waited for: 32 -> 34; matrix products, arithmetic and copies ran while one was open for 8% -> 8% of each run, Pallas kernels for 18% -> 18%
where the time goes in v9:
time: 512 us; the launch traced here: 503 us
  waiting for transfers between devices  191 us (37%)
  Pallas kernels  157 us (31%)
  starting transfers between devices  49.3 us (10%)
  other arithmetic  44.5 us (9%)
  local copies, waits for them, and re-layouts  34.5 us (7%)
  between operations  15.5 us (3%)
  matrix products  11.7 us (2%)
    pallas_call x6, Pallas kernels, call(): pl.pallas_call(body, out_shape=outs, in_specs=specs, out_specs=[ANYWHERE...  155 us
    ppermute x18, waiting for transfers between devices, ring_z(): return lax.ppermute(a, 'dp', [(i, (i + 2 * step) % 8) for i in range(8)])  120 us
    ppermute x16, waiting for transfers between devices, swap_y(): return lax.ppermute(a, 'dp', [(i, i ^ 1) for i in range(8)])  32.5 us
    add x10, other arithmetic, block(): return sum(parts[1:], parts[0])  28.2 us
    ppermute x16, starting transfers between devices, swap_y(): return lax.ppermute(a, 'dp', [(i, i ^ 1) for i in range(8)])  20.1 us
    ppermute x17, waiting for transfers between devices, swap_x(): return lax.ppermute(a, 'pipe', [(i, i ^ 2) for i in range(4)])  20 us
    ppermute x17, starting transfers between devices, swap_x(): return lax.ppermute(a, 'pipe', [(i, i ^ 2) for i in range(4)])  18.3 us
    unnamed x102, local copies, waits for them, and re-layouts  16.3 us
  transfers between devices with their start and end apart: 71, of which 34 were waited for; matrix products, arithmetic and copies ran while one was open for 8% of the time, Pallas kernels for 18%

profile of v9, /device:TPU:0, one launch (start us, length us, event | category | flops | bytes accessed | tf_op | source)
XLA Modules:
  0.0 503.5 jit_solution(11346975148393462245)
XLA Ops:
  16.4 3.1 collective-permute-start
  22.5 18.9 %collective-permute-done.refs_2_.refs_7_.refs_13_.refs_10_.refs_9_ = bf16[1168,384]{1,0:T(8,128)(2,1)S(1)} collective-permute-done((bf16[1168,384]{1,0:T(8,128)(2,1)S(1)}, bf16[1168,384]{1,0:T(8,128)(2,1)S(1)}, u32[]{:S(2)}, u32[]{:S(2)}) %collective-permute-start) | collective-permute-done | bytes 897056 | tf_op jit(solution)/shard_map/ppermute | solution.py:878
  46.9 15.7 %collective-permute-done.4.refs_18_.refs_23_.refs_29_.refs_26_.refs_25_ = bf16[1168,384]{1,0:T(8,128)(2,1)S(1)} collective-permute-done((bf16[1168,384]{1,0:T(8,128)(2,1)S(1)}, bf16[1168,384]{1,0:T(8,128)(2,1)S(1)}, u32[]{:S(2)}, u32[]{:S(2)}) %collective-permute-start.4) | collective-permute-done | bytes 897056 | tf_op jit(solution)/shard_map/ppermute | solution.py:869
  62.6 2.8 collective-permute-done.1.refs_3_.refs_8_.refs_14_.refs_11_.refs_10_
  67.6 19.3 %collective-permute-done.7.refs_4_.refs_9_.refs_15_.refs_12_.refs_11_ = bf16[1168,384]{1,0:T(8,128)(2,1)} collective-permute-done((bf16[1168,384]{1,0:T(8,128)(2,1)S(1)}, bf16[1168,384]{1,0:T(8,128)(2,1)}, u32[]{:S(2)}, u32[]{:S(2)}) %collective-permute-start.7) | collective-permute-done | bytes 897056 | tf_op jit(solution)/shard_map/ppermute | solution.py:878
  91.5 18.2 %collective-permute-done.13.refs_8_.refs_13_.refs_19_.refs_16_.refs_15_ = bf16[1168,384]{1,0:T(8,128)(2,1)} collective-permute-done((bf16[1168,384]{1,0:T(8,128)(2,1)}, bf16[1168,384]{1,0:T(8,128)(2,1)}, u32[]{:S(2)}, u32[]{:S(2)}) %collective-permute-start.13) | collective-permute-done | bytes 897056 | tf_op jit(solution)/shard_map/ppermute | solution.py:875
  111.3 2.1 collective-permute-done.19.refs_22_.refs_27_.refs_33_.refs_30_.refs_29_
  114.0 2.3 collective-permute-done.14.refs_11_.refs_16_.refs_22_.refs_19_.refs_18_
  121.9 25.2 %collective-permute-done.22.refs_19_.refs_24_.refs_30_.refs_27_.refs_26_ = bf16[1168,384]{1,0:T(8,128)(2,1)} collective-permute-done((bf16[1168,384]{1,0:T(8,128)(2,1)}, bf16[1168,384]{1,0:T(8,128)(2,1)}, u32[]{:S(2)}, u32[]{:S(2)}) %collective-permute-start.22) | collective-permute-done | bytes 897056 | tf_op jit(solution)/shard_map/ppermute | solution.py:878
  152.5 2.5 shard_map.239
  155.8 32.9 %shard_map.240 = (bf16[512,2304]{1,0:T(8,128)(2,1)}, bf16[24,128,256]{2,1,0:T(8,128)(2,1)}, bf16[512,768]{1,0:T(8,128)(2,1)}, bf16[512,768]{1,0:T(8,128)(2,1)}, ...) custom-call(s32[8]{0:T(128)} %add_minimum_fusion.refs_0_, ...), custom_call_target="tpu_custom_call" | custom-call | flops 41799999488 | bytes 133000000 | tf_op jit(solution)/shard_map/pallas_call | solution.py:615
  188.7 2.1 all-gather.2.cloned.1.call-done
  190.8 2.1 fusion.81
  192.9 3.2 fusion.80
  196.1 3.5 convolution_convert_fusion.refs_4_.refs_2_
  199.6 3.5 add_convert_fusion.refs_5_.refs_3_
  203.1 45.6 %shard_map.241 = (bf16[512,768]{1,0:T(8,128)(2,1)}, bf16[48,160,128]{2,1,0:T(8,128)(2,1)}, bf16[512,768]{1,0:T(8,128)(2,1)}, bf16[512,768]{1,0:T(8,128)(2,1)}, f...) custom-call(s32[4]{0:T(128)} %pad_add_fusion.refs_0_.refs_1_, ...), custom_call_target="tpu_custom_call" | custom-call | flops 52800000000 | bytes 168000000 | tf_op jit(solution)/shard_map/pallas_call | solution.py:615
  248.7 19.9 %shard_map.242 = (f32[512,768]{1,0:T(8,128)}, bf16[1280,768]{1,0:T(8,128)(2,1)}, bf16[1280,768]{1,0:T(8,128)(2,1)}, bf16[768,768]{1,0:T(8,128)(2,1)}, bf16[768,768]{1,0:T(8,128)(2,1)}, /*index=5*/f32[8,768]{1,0:T(8,128)}) custom-call(f32[512,768]{1,0:T(8,128)} %get-tuple-element.166.refs_0_, bf16[512,768]{1,0:T(8,128)(2,1)} %get-tuple-element.161.refs_2_.refs_1_, ...), custom_call_target="tpu_custom_call" | custom-call | flops 28600000512 | bytes 91000000 | tf_op jit(solution)/shard_map/pallas_call | solution.py:615
  268.7 2.8 constant_dynamic-slice_fusion.2
  271.5 2.3 convolution_convert_fusion.2
  273.9 2.3 convolution_convert_fusion.1
  278.8 5.0 collective-permute-done.31
  283.8 2.1 convert_add_fusion
  288.4 18.1 %shard_map.243 = (bf16[512,768]{1,0:T(8,128)(2,1)}, bf16[2,8,400,384]{3,2,1,0:T(8,128)(2,1)}, bf16[2,8,400,384]{3,2,1,0:T(8,128)(2,1)}, f32[8,768]{1,0:T(8,128)}) custom-call(s32[4]{0:T(128)} %pad_add_fusion.refs_0_.refs_1_, f32[512,768]{1,0:T(8,128)} %get-tuple-element.179.refs_1_, bf16[512,768]{1,0:T(8,128)(2,1)} %get-tuple-element.180.refs_2_, ...), custom_call_target="tpu_custom_call" | custom-call | flops 24199999488 | bytes 77000000 | tf_op jit(solution)/shard_map/pallas_call | solution.py:615
  307.2 19.7 %shard_map.244 = (f32[512,768]{1,0:T(8,128)}, bf16[2,8,768,384]{3,2,1,0:T(8,128)(2,1)}, bf16[2,8,768,384]{3,2,1,0:T(8,128)(2,1)}, f32[8,768]{1,0:T(8,128)}) custom-call(s32[4]{0:T(128)} %pad_add_fusion.refs_0_.refs_1_, bf16[512,768]{1,0:T(8,128)(2,1)} %get-tuple-element.191.refs_1_, ...), custom_call_target="tpu_custom_call", output_to_operand_aliasing={{1}: (40, {}), {2}: (41, {})} | custom-call | flops 24199999488 | bytes 77000000 | tf_op jit(solution)/shard_map/pallas_call | solution.py:615
  332.0 18.4 %shard_map.245 = (f32[512,768]{1,0:T(8,128)}, bf16[2,8,400,384]{3,2,1,0:T(8,128)(2,1)}, bf16[2,8,400,384]{3,2,1,0:T(8,128)(2,1)}, f32[8,768]{1,0:T(8,128)}) custom-call(s32[4]{0:T(128)} %pad_add_fusion.refs_0_.refs_1_, f32[512,768]{1,0:T(8,128)} %get-tuple-element.205.refs_1_, ...), custom_call_target="tpu_custom_call", output_to_operand_aliasing={{1}: (41, {}), {2}: (42, {})} | custom-call | flops 24199999488 | bytes 77000000 | tf_op jit(solution)/shard_map/pallas_call | solution.py:615
  351.5 2.5 copy.89
  354.9 4.6 fusion.13
  359.7 2.0 collective-permute-start.37
  365.1 2.6 collective-permute-done.36
  367.7 4.2 fusion.42
  371.9 8.8 %collective-permute-done.40 = bf16[112,768]{1,0:T(8,128)(2,1)S(1)} collective-permute-done((bf16[112,768]{1,0:T(8,128)(2,1)S(1)}, bf16[112,768]{1,0:T(8,128)(2,1)S(1)}, u32[]{:S(2)}, u32[]{:S(2)}) %collective-permute-start.40) | collective-permute-done | bytes 172064 | tf_op jit(solution)/shard_map/ppermute | solution.py:878
  383.4 6.7 %collective-permute-done.41 = bf16[400,384]{1,0:T(8,128)(2,1)S(1)} collective-permute-done((bf16[400,384]{1,0:T(8,128)(2,1)S(1)}, bf16[400,384]{1,0:T(8,128)(2,1)S(1)}, u32[]{:S(2)}, u32[]{:S(2)}) %collective-permute-start.41) | collective-permute-done | bytes 307232 | tf_op jit(solution)/shard_map/ppermute | solution.py:875
  394.3 2.2 fusion.24
  398.7 3.5 collective-permute-done.44
  404.3 2.8 fusion.49
  408.3 4.1 collective-permute-done.54
  414.2 7.0 %collective-permute-done.56 = bf16[768,384]{1,0:T(8,128)(2,1)} collective-permute-done((bf16[768,384]{1,0:T(8,128)(2,1)S(1)}, bf16[768,384]{1,0:T(8,128)(2,1)}, u32[]{:S(2)}, u32[]{:S(2)}) %collective-permute-start.56) | collective-permute-done | bytes 589856 | tf_op jit(solution)/shard_map/ppermute | solution.py:878
  421.2 3.8 fusion.20
  426.5 4.9 collective-permute-done.47
  433.9 2.8 fusion.44
  436.7 4.0 collective-permute-done.57
  441.6 3.8 fusion.15
  449.4 13.0 %collective-permute-done.60 = bf16[768,384]{1,0:T(8,128)(2,1)S(1)} collective-permute-done((bf16[768,384]{1,0:T(8,128)(2,1)}, bf16[768,384]{1,0:T(8,128)(2,1)S(1)}, u32[]{:S(2)}, u32[]{:S(2)}) %collective-permute-start.60) | collective-permute-done | bytes 589856 | tf_op jit(solution)/shard_map/ppermute | solution.py:878
  462.4 2.0 collective-permute-start.53
  473.4 7.0 %collective-permute-done.63 = bf16[768,384]{1,0:T(8,128)(2,1)S(1)} collective-permute-done((bf16[768,384]{1,0:T(8,128)(2,1)S(1)}, bf16[768,384]{1,0:T(8,128)(2,1)S(1)}, u32[]{:S(2)}, u32[]{:S(2)}) %collective-permute-start.63) | collective-permute-done | bytes 589856 | tf_op jit(solution)/shard_map/ppermute | solution.py:878
  484.5 2.0 collective-permute-start.68
  488.5 3.8 collective-permute-done.66
  (289 shorter events, 96.3 us)
Async XLA Ops:
  7.2 183.6 %all-gather.2.cloned.1.call-start = ((), (), s32[]{:S(2)}) async-start(), calls=%async_computation | async-start | bytes 5677056 | tf_op jit(solution)/shard_map/all_gather | solution.py:1127
  16.4 25.0 %collective-permute-start = (bf16[1168,384]{1,0:T(8,128)(2,1)S(1)}, bf16[1168,384]{1,0:T(8,128)(2,1)S(1)}, u32[]{:S(2)}, u32[]{:S(2)}) collective-permute-start(bf16[1168,384]{1,0:T(8,128)(2,1)S(1)} %constant_dynamic-update-slice_fusion.refs_1_.refs_6_.refs_12_.refs_9_.refs_8_), channel_id=1, source_target_pairs={{0,2},{1,3},{2,4},{3,5},{4,6},{5,7},{6,0},{7,1},{8,10},{9,11},{10,... | collective-permute-start | bytes 2691080 | tf_op jit(solution)/shard_map/ppermute | solution.py:878
  19.5 23.4 %collective-permute-start.2 = (bf16[1168,384]{1,0:T(8,128)(2,1)S(1)}, bf16[1168,384]{1,0:T(8,128)(2,1)S(1)}, u32[]{:S(2)}, u32[]{:S(2)}) collective-permute-start(bf16[1168,384]{1,0:T(8,128)(2,1)S(1)} %constant_dynamic-update-slice_fusion.refs_1_.refs_6_.refs_12_.refs_9_.refs_8_), channel_id=1, source_target_pairs={{0,1},{1,0},{2,3},{3,2},{4,5},{5,4},{6,7},{7,6},{8,9},{9,8},{10,11... | collective-permute-start | bytes 2691080 | tf_op jit(solution)/shard_map/ppermute | solution.py:875
  21.0 23.5 %collective-permute-start.5 = (bf16[1168,384]{1,0:T(8,128)(2,1)S(1)}, bf16[1168,384]{1,0:T(8,128)(2,1)S(1)}, u32[]{:S(2)}, u32[]{:S(2)}) collective-permute-start(bf16[1168,384]{1,0:T(8,128)(2,1)S(1)} %constant_dynamic-update-slice_fusion.refs_1_.refs_6_.refs_12_.refs_9_.refs_8_), channel_id=1, source_target_pairs={{0,16},{8,24},{16,0},{24,8},{1,17},{9,25},{17,1},{25,9},{2,18},{10... | collective-permute-start | bytes 2691080 | tf_op jit(solution)/shard_map/ppermute | solution.py:869
  22.5 23.8 %collective-permute-start.6 = (bf16[1168,384]{1,0:T(8,128)(2,1)S(1)}, bf16[1168,384]{1,0:T(8,128)(2,1)S(1)}, u32[]{:S(2)}, u32[]{:S(2)}) collective-permute-start(bf16[1168,384]{1,0:T(8,128)(2,1)S(1)} %constant_dynamic-update-slice_fusion.refs_1_.refs_6_.refs_12_.refs_9_.refs_8_), channel_id=1, source_target_pairs={{0,8},{8,0},{16,24},{24,16},{1,9},{9,1},{17,25},{25,17},{2,10},{10... | collective-permute-start | bytes 2691080 | tf_op jit(solution)/shard_map/ppermute | solution.py:872
  41.5 21.1 %collective-permute-start.4 = (bf16[1168,384]{1,0:T(8,128)(2,1)S(1)}, bf16[1168,384]{1,0:T(8,128)(2,1)S(1)}, u32[]{:S(2)}, u32[]{:S(2)}) collective-permute-start(bf16[1168,384]{1,0:T(8,128)(2,1)S(1)} %collective-permute-done.refs_2_.refs_7_.refs_13_.refs_10_.refs_9_), channel_id=1, source_target_pairs={{0,16},{8,24},{16,0},{24,8},{1,17},{9,25},{17,1},{25,9},{2,18},{10... | collective-permute-start | bytes 2691080 | tf_op jit(solution)/shard_map/ppermute | solution.py:869
  43.0 22.4 %collective-permute-start.1 = (bf16[1168,384]{1,0:T(8,128)(2,1)S(1)}, bf16[1168,384]{1,0:T(8,128)(2,1)S(1)}, u32[]{:S(2)}, u32[]{:S(2)}) collective-permute-start(bf16[1168,384]{1,0:T(8,128)(2,1)S(1)} %collective-permute-done.refs_2_.refs_7_.refs_13_.refs_10_.refs_9_), channel_id=1, source_target_pairs={{0,2},{1,3},{2,4},{3,5},{4,6},{5,7},{6,0},{7,1},{8,10},{9,11},{10,... | collective-permute-start | bytes 2691080 | tf_op jit(solution)/shard_map/ppermute | solution.py:878
  43.0 22.4 %collective-permute-start.3 = (bf16[1168,384]{1,0:T(8,128)(2,1)S(1)}, bf16[1168,384]{1,0:T(8,128)(2,1)S(1)}, u32[]{:S(2)}, u32[]{:S(2)}) collective-permute-start(bf16[1168,384]{1,0:T(8,128)(2,1)S(1)} %collective-permute-done.refs_2_.refs_7_.refs_13_.refs_10_.refs_9_), channel_id=1, source_target_pairs={{0,1},{1,0},{2,3},{3,2},{4,5},{5,4},{6,7},{7,6},{8,9},{9,8},{10,11... | collective-permute-start | bytes 2691080 | tf_op jit(solution)/shard_map/ppermute | solution.py:875
  44.6 23.0 %collective-permute-start.10 = (bf16[1168,384]{1,0:T(8,128)(2,1)S(1)}, bf16[1168,384]{1,0:T(8,128)(2,1)S(1)}, u32[]{:S(2)}, u32[]{:S(2)}) collective-permute-start(bf16[1168,384]{1,0:T(8,128)(2,1)S(1)} %collective-permute-done.refs_2_.refs_7_.refs_13_.refs_10_.refs_9_), channel_id=1, source_target_pairs={{0,8},{8,0},{16,24},{24,16},{1,9},{9,1},{17,25},{25,17},{2,10},{10... | collective-permute-start | bytes 2691080 | tf_op jit(solution)/shard_map/ppermute | solution.py:872
  46.3 21.3 %collective-permute-start.11 = (bf16[1168,384]{1,0:T(8,128)(2,1)S(1)}, bf16[1168,384]{1,0:T(8,128)(2,1)S(1)}, u32[]{:S(2)}, u32[]{:S(2)}) collective-permute-start(bf16[1168,384]{1,0:T(8,128)(2,1)S(1)} %collective-permute-done.2.refs_5_.refs_10_.refs_16_.refs_13_.refs_12_), channel_id=1, source_target_pairs={{0,8},{8,0},{16,24},{24,16},{1,9},{9,1},{17,25},{25,17},{2,10},{10... | collective-permute-start | bytes 2691080 | tf_op jit(solution)/shard_map/ppermute | solution.py:872
  65.3 21.6 %collective-permute-start.7 = (bf16[1168,384]{1,0:T(8,128)(2,1)S(1)}, bf16[1168,384]{1,0:T(8,128)(2,1)}, u32[]{:S(2)}, u32[]{:S(2)}) collective-permute-start(bf16[1168,384]{1,0:T(8,128)(2,1)S(1)} %collective-permute-done.1.refs_3_.refs_8_.refs_14_.refs_11_.refs_10_), channel_id=1, source_target_pairs={{0,2},{1,3},{2,4},{3,5},{4,6},{5,7},{6,0},{7,1},{8,10},{9,11},{10,... | collective-permute-start | bytes 2691080 | tf_op jit(solution)/shard_map/ppermute | solution.py:878
  65.4 21.5 %collective-permute-start.8 = (bf16[1168,384]{1,0:T(8,128)(2,1)S(1)}, bf16[1168,384]{1,0:T(8,128)(2,1)}, u32[]{:S(2)}, u32[]{:S(2)}) collective-permute-start(bf16[1168,384]{1,0:T(8,128)(2,1)S(1)} %collective-permute-done.1.refs_3_.refs_8_.refs_14_.refs_11_.refs_10_), channel_id=1, source_target_pairs={{0,1},{1,0},{2,3},{3,2},{4,5},{5,4},{6,7},{7,6},{8,9},{9,8},{10,11... | collective-permute-start | bytes 2691080 | tf_op jit(solution)/shard_map/ppermute | solution.py:875
  67.0 20.0 %collective-permute-start.9 = (bf16[1168,384]{1,0:T(8,128)(2,1)S(1)}, bf16[1168,384]{1,0:T(8,128)(2,1)}, u32[]{:S(2)}, u32[]{:S(2)}) collective-permute-start(bf16[1168,384]{1,0:T(8,128)(2,1)S(1)} %collective-permute-done.2.refs_5_.refs_10_.refs_16_.refs_13_.refs_12_), channel_id=1, source_target_pairs={{0,16},{8,24},{16,0},{24,8},{1,17},{9,25},{17,1},{25,9},{2,18},{10... | collective-permute-start | bytes 2691080 | tf_op jit(solution)/shard_map/ppermute | solution.py:869
  67.5 19.4 %collective-permute-start.12 = (bf16[1168,384]{1,0:T(8,128)(2,1)S(1)}, bf16[1168,384]{1,0:T(8,128)(2,1)S(1)}, u32[]{:S(2)}, u32[]{:S(2)}) collective-permute-start(bf16[1168,384]{1,0:T(8,128)(2,1)S(1)} %collective-permute-done.5.refs_17_.refs_22_.refs_28_.refs_25_.refs_24_), channel_id=1, source_target_pairs={{0,8},{8,0},{16,24},{24,16},{1,9},{9,1},{17,25},{25,17},{2,10},{10... | collective-permute-start | bytes 2691080 | tf_op jit(solution)/shard_map/ppermute | solution.py:872
  87.1 22.6 %collective-permute-start.13 = (bf16[1168,384]{1,0:T(8,128)(2,1)}, bf16[1168,384]{1,0:T(8,128)(2,1)}, u32[]{:S(2)}, u32[]{:S(2)}) collective-permute-start(bf16[1168,384]{1,0:T(8,128)(2,1)} %collective-permute-done.7.refs_4_.refs_9_.refs_15_.refs_12_.refs_11_), channel_id=1, source_target_pairs={{0,1},{1,0},{2,3},{3,2},{4,5},{5,4},{6,7},{7,6},{8,9},{9,8},{10,11... | collective-permute-start | bytes 2691080 | tf_op jit(solution)/shard_map/ppermute | solution.py:875
  88.6 21.1 %collective-permute-start.17 = (bf16[1168,384]{1,0:T(8,128)(2,1)}, bf16[1168,384]{1,0:T(8,128)(2,1)}, u32[]{:S(2)}, u32[]{:S(2)}) collective-permute-start(bf16[1168,384]{1,0:T(8,128)(2,1)} %collective-permute-done.8.refs_7_.refs_12_.refs_18_.refs_15_.refs_14_), channel_id=1, source_target_pairs={{0,8},{8,0},{16,24},{24,16},{1,9},{9,1},{17,25},{25,17},{2,10},{10... | collective-permute-start | bytes 2691080 | tf_op jit(solution)/shard_map/ppermute | solution.py:872
  88.8 22.5 %collective-permute-start.18 = (bf16[1168,384]{1,0:T(8,128)(2,1)}, bf16[1168,384]{1,0:T(8,128)(2,1)}, u32[]{:S(2)}, u32[]{:S(2)}) collective-permute-start(bf16[1168,384]{1,0:T(8,128)(2,1)} %collective-permute-done.7.refs_4_.refs_9_.refs_15_.refs_12_.refs_11_), channel_id=1, source_target_pairs={{0,16},{8,24},{16,0},{24,8},{1,17},{9,25},{17,1},{25,9},{2,18},{10... | collective-permute-start | bytes 2691080 | tf_op jit(solution)/shard_map/ppermute | solution.py:869
  89.3 24.0 %collective-permute-start.19 = (bf16[1168,384]{1,0:T(8,128)(2,1)}, bf16[1168,384]{1,0:T(8,128)(2,1)}, u32[]{:S(2)}, u32[]{:S(2)}) collective-permute-start(bf16[1168,384]{1,0:T(8,128)(2,1)} %collective-permute-done.9.refs_21_.refs_26_.refs_32_.refs_29_.refs_28_), channel_id=1, source_target_pairs={{0,2},{1,3},{2,4},{3,5},{4,6},{5,7},{6,0},{7,1},{8,10},{9,11},{10,... | collective-permute-start | bytes 2691080 | tf_op jit(solution)/shard_map/ppermute | solution.py:878
  90.6 22.7 %collective-permute-start.25 = (bf16[1168,384]{1,0:T(8,128)(2,1)}, bf16[1168,384]{1,0:T(8,128)(2,1)}, u32[]{:S(2)}, u32[]{:S(2)}) collective-permute-start(bf16[1168,384]{1,0:T(8,128)(2,1)} %collective-permute-done.9.refs_21_.refs_26_.refs_32_.refs_29_.refs_28_), channel_id=1, source_target_pairs={{0,8},{8,0},{16,24},{24,16},{1,9},{9,1},{17,25},{25,17},{2,10},{10... | collective-permute-start | bytes 2691080 | tf_op jit(solution)/shard_map/ppermute | solution.py:872
  119.1 28.0 %collective-permute-start.22 = (bf16[1168,384]{1,0:T(8,128)(2,1)}, bf16[1168,384]{1,0:T(8,128)(2,1)}, u32[]{:S(2)}, u32[]{:S(2)}) collective-permute-start(bf16[1168,384]{1,0:T(8,128)(2,1)} %copy-done.12), channel_id=1, source_target_pairs={{0,2},{1,3},{2,4},{3,5},{4,6},{5,7},{6,0},{7,1},{8,10},{9,11},{10,... | collective-permute-start | bytes 2691080 | tf_op jit(solution)/shard_map/ppermute | solution.py:878
  119.2 28.0 %collective-permute-start.23 = (bf16[1168,384]{1,0:T(8,128)(2,1)}, bf16[1168,384]{1,0:T(8,128)(2,1)}, u32[]{:S(2)}, u32[]{:S(2)}) collective-permute-start(bf16[1168,384]{1,0:T(8,128)(2,1)} %collective-permute-done.8.refs_7_.refs_12_.refs_18_.refs_15_.refs_14_), channel_id=1, source_target_pairs={{0,16},{8,24},{16,0},{24,8},{1,17},{9,25},{17,1},{25,9},{2,18},{10... | collective-permute-start | bytes 2691080 | tf_op jit(solution)/shard_map/ppermute | solution.py:869
  120.7 26.5 %collective-permute-start.24 = (bf16[1168,384]{1,0:T(8,128)(2,1)}, bf16[1168,384]{1,0:T(8,128)(2,1)}, u32[]{:S(2)}, u32[]{:S(2)}) collective-permute-start(bf16[1168,384]{1,0:T(8,128)(2,1)} %collective-permute-done.18.refs_20_.refs_25_.refs_31_.refs_28_.refs_27_), channel_id=1, source_target_pairs={{0,1},{1,0},{2,3},{3,2},{4,5},{5,4},{6,7},{7,6},{8,9},{9,8},{10,11... | collective-permute-start | bytes 2691080 | tf_op jit(solution)/shard_map/ppermute | solution.py:875
  121.2 28.6 %collective-permute-start.21 = (bf16[1168,384]{1,0:T(8,128)(2,1)}, bf16[1168,384]{1,0:T(8,128)(2,1)}, u32[]{:S(2)}, u32[]{:S(2)}) collective-permute-start(bf16[1168,384]{1,0:T(8,128)(2,1)} %collective-permute-done.13.refs_8_.refs_13_.refs_19_.refs_16_.refs_15_), channel_id=1, source_target_pairs={{0,8},{8,0},{16,24},{24,16},{1,9},{9,1},{17,25},{25,17},{2,10},{10... | collective-permute-start | bytes 2691080 | tf_op jit(solution)/shard_map/ppermute | solution.py:872
  121.8 27.9 %collective-permute-start.28 = (bf16[1168,384]{1,0:T(8,128)(2,1)}, bf16[1168,384]{1,0:T(8,128)(2,1)}, u32[]{:S(2)}, u32[]{:S(2)}) collective-permute-start(bf16[1168,384]{1,0:T(8,128)(2,1)} %collective-permute-done.18.refs_20_.refs_25_.refs_31_.refs_28_.refs_27_), channel_id=1, source_target_pairs={{0,8},{8,0},{16,24},{24,16},{1,9},{9,1},{17,25},{25,17},{2,10},{10... | collective-permute-start | bytes 2691080 | tf_op jit(solution)/shard_map/ppermute | solution.py:872
  286.9 19.5 %collective-permute-start.32 = (bf16[2,2,112,768]{3,2,0,1:T(8,128)(2,1)}, bf16[2,2,112,768]{3,2,0,1:T(8,128)(2,1)}, u32[]{:S(2)}, u32[]{:S(2)}) collective-permute-start(bf16[2,2,112,768]{3,2,0,1:T(8,128)(2,1)} %get-tuple-element.178), channel_id=1, source_target_pairs={{0,16},{8,24},{16,0},{24,8},{1,17},{9,25},{17,1},{25,9},{2,18},{10... | collective-permute-start | bytes 2064392 | tf_op jit(solution)/shard_map/ppermute | solution.py:869
  306.5 20.5 %collective-permute-start.33 = (bf16[2,2,112,768]{3,2,0,1:T(8,128)(2,1)S(1)}, bf16[2,2,112,768]{3,2,0,1:T(8,128)(2,1)}, u32[]{:S(2)}, u32[]{:S(2)}) collective-permute-start(bf16[2,2,112,768]{3,2,0,1:T(8,128)(2,1)S(1)} %get-tuple-element.190), channel_id=1, source_target_pairs={{0,16},{8,24},{16,0},{24,8},{1,17},{9,25},{17,1},{25,9},{2,18},{10... | collective-permute-start | bytes 2064392 | tf_op jit(solution)/shard_map/ppermute | solution.py:869
  330.1 24.8 %collective-permute-start.34 = (bf16[2,8,768,384]{3,2,1,0:T(8,128)(2,1)}, bf16[2,8,768,384]{3,2,1,0:T(8,128)(2,1)}, u32[]{:S(2)}, u32[]{:S(2)}) collective-permute-start(bf16[2,8,768,384]{3,2,1,0:T(8,128)(2,1)} %get-tuple-element.203), channel_id=1, source_target_pairs={{0,8},{8,0},{16,24},{24,16},{1,9},{9,1},{17,25},{25,17},{2,10},{10... | collective-permute-start | bytes 28311560 | tf_op jit(solution)/shard_map/ppermute | solution.py:872
  330.5 23.8 %collective-permute-start.35 = (bf16[4,112,768]{2,1,0:T(8,128)(2,1)S(1)}, bf16[4,112,768]{2,1,0:T(8,128)(2,1)S(1)}, u32[]{:S(2)}, u32[]{:S(2)}) collective-permute-start(bf16[4,112,768]{2,1,0:T(8,128)(2,1)S(1)} %fusion.7), channel_id=1, source_target_pairs={{0,1},{1,0},{2,3},{3,2},{4,5},{5,4},{6,7},{7,6},{8,9},{9,8},{10,11... | collective-permute-start | bytes 2064392 | tf_op jit(solution)/shard_map/ppermute | solution.py:875
  359.7 21.0 %collective-permute-start.37 = (bf16[768,384]{1,0:T(8,128)(2,1)S(1)}, bf16[768,384]{1,0:T(8,128)(2,1)S(1)}, u32[]{:S(2)}, u32[]{:S(2)}) collective-permute-start(bf16[768,384]{1,0:T(8,128)(2,1)S(1)} %get-tuple-element.218), channel_id=1, source_target_pairs={{0,2},{1,3},{2,4},{3,5},{4,6},{5,7},{6,0},{7,1},{8,10},{9,11},{10,... | collective-permute-start | bytes 1769480 | tf_op jit(solution)/shard_map/ppermute | solution.py:878
  361.7 19.0 %collective-permute-start.38 = (bf16[768,384]{1,0:T(8,128)(2,1)S(1)}, bf16[768,384]{1,0:T(8,128)(2,1)S(1)}, u32[]{:S(2)}, u32[]{:S(2)}) collective-permute-start(bf16[768,384]{1,0:T(8,128)(2,1)S(1)} %get-tuple-element.219), channel_id=1, source_target_pairs={{0,1},{1,0},{2,3},{3,2},{4,5},{5,4},{6,7},{7,6},{8,9},{9,8},{10,11... | collective-permute-start | bytes 1769480 | tf_op jit(solution)/shard_map/ppermute | solution.py:875
  362.3 18.5 %collective-permute-start.39 = (bf16[768,384]{1,0:T(8,128)(2,1)S(1)}, bf16[768,384]{1,0:T(8,128)(2,1)S(1)}, u32[]{:S(2)}, u32[]{:S(2)}) collective-permute-start(bf16[768,384]{1,0:T(8,128)(2,1)S(1)} %get-tuple-element.220), channel_id=1, source_target_pairs={{0,16},{8,24},{16,0},{24,8},{1,17},{9,25},{17,1},{25,9},{2,18},{10... | collective-permute-start | bytes 1769480 | tf_op jit(solution)/shard_map/ppermute | solution.py:869
  363.5 17.2 %collective-permute-start.40 = (bf16[112,768]{1,0:T(8,128)(2,1)S(1)}, bf16[112,768]{1,0:T(8,128)(2,1)S(1)}, u32[]{:S(2)}, u32[]{:S(2)}) collective-permute-start(bf16[112,768]{1,0:T(8,128)(2,1)S(1)} %fusion.76), channel_id=1, source_target_pairs={{0,2},{1,3},{2,4},{3,5},{4,6},{5,7},{6,0},{7,1},{8,10},{9,11},{10,... | collective-permute-start | bytes 516104 | tf_op jit(solution)/shard_map/ppermute | solution.py:878
  396.5 15.9 %collective-permute-start.54 = (bf16[768,384]{1,0:T(8,128)(2,1)}, bf16[768,384]{1,0:T(8,128)(2,1)}, u32[]{:S(2)}, u32[]{:S(2)}) collective-permute-start(bf16[768,384]{1,0:T(8,128)(2,1)} %get-tuple-element.235), channel_id=1, source_target_pairs={{0,1},{1,0},{2,3},{3,2},{4,5},{5,4},{6,7},{7,6},{8,9},{9,8},{10,11... | collective-permute-start | bytes 1769480 | tf_op jit(solution)/shard_map/ppermute | solution.py:875
  397.9 15.9 %collective-permute-start.55 = (bf16[768,384]{1,0:T(8,128)(2,1)}, bf16[768,384]{1,0:T(8,128)(2,1)}, u32[]{:S(2)}, u32[]{:S(2)}) collective-permute-start(bf16[768,384]{1,0:T(8,128)(2,1)} %fusion.24), channel_id=1, source_target_pairs={{0,16},{8,24},{16,0},{24,8},{1,17},{9,25},{17,1},{25,9},{2,18},{10... | collective-permute-start | bytes 1769480 | tf_op jit(solution)/shard_map/ppermute | solution.py:869
  403.0 18.2 %collective-permute-start.56 = (bf16[768,384]{1,0:T(8,128)(2,1)S(1)}, bf16[768,384]{1,0:T(8,128)(2,1)}, u32[]{:S(2)}, u32[]{:S(2)}) collective-permute-start(bf16[768,384]{1,0:T(8,128)(2,1)S(1)} %get-tuple-element.237), channel_id=1, source_target_pairs={{0,2},{1,3},{2,4},{3,5},{4,6},{5,7},{6,0},{7,1},{8,10},{9,11},{10,... | collective-permute-start | bytes 1769480 | tf_op jit(solution)/shard_map/ppermute | solution.py:878
  407.1 17.9 %collective-permute-start.49 = (bf16[112,768]{1,0:T(8,128)(2,1)S(1)}, bf16[112,768]{1,0:T(8,128)(2,1)S(1)}, u32[]{:S(2)}, u32[]{:S(2)}) collective-permute-start(bf16[112,768]{1,0:T(8,128)(2,1)S(1)} %fusion.41), channel_id=1, source_target_pairs={{0,2},{1,3},{2,4},{3,5},{4,6},{5,7},{6,0},{7,1},{8,10},{9,11},{10,... | collective-permute-start | bytes 516104 | tf_op jit(solution)/shard_map/ppermute | solution.py:878
  407.1 24.3 %collective-permute-start.47 = (bf16[400,384]{1,0:T(8,128)(2,1)S(1)}, bf16[400,384]{1,0:T(8,128)(2,1)}, u32[]{:S(2)}, u32[]{:S(2)}) collective-permute-start(bf16[400,384]{1,0:T(8,128)(2,1)S(1)} %get-tuple-element.228), channel_id=1, source_target_pairs={{0,2},{1,3},{2,4},{3,5},{4,6},{5,7},{6,0},{7,1},{8,10},{9,11},{10,... | collective-permute-start | bytes 921608 | tf_op jit(solution)/shard_map/ppermute | solution.py:878
  412.4 21.5 %collective-permute-start.48 = (bf16[400,384]{1,0:T(8,128)(2,1)}, bf16[400,384]{1,0:T(8,128)(2,1)}, u32[]{:S(2)}, u32[]{:S(2)}) collective-permute-start(bf16[400,384]{1,0:T(8,128)(2,1)} %get-tuple-element.229), channel_id=1, source_target_pairs={{0,1},{1,0},{2,3},{3,2},{4,5},{5,4},{6,7},{7,6},{8,9},{9,8},{10,11... | collective-permute-start | bytes 921608 | tf_op jit(solution)/shard_map/ppermute | solution.py:875
  413.9 20.0 %collective-permute-start.50 = (bf16[400,384]{1,0:T(8,128)(2,1)}, bf16[400,384]{1,0:T(8,128)(2,1)}, u32[]{:S(2)}, u32[]{:S(2)}) collective-permute-start(bf16[400,384]{1,0:T(8,128)(2,1)} %get-tuple-element.231), channel_id=1, source_target_pairs={{0,16},{8,24},{16,0},{24,8},{1,17},{9,25},{17,1},{25,9},{2,18},{10... | collective-permute-start | bytes 921608 | tf_op jit(solution)/shard_map/ppermute | solution.py:869
  425.0 15.7 %collective-permute-start.57 = (bf16[768,384]{1,0:T(8,128)(2,1)}, bf16[768,384]{1,0:T(8,128)(2,1)}, u32[]{:S(2)}, u32[]{:S(2)}) collective-permute-start(bf16[768,384]{1,0:T(8,128)(2,1)} %get-tuple-element.238), channel_id=1, source_target_pairs={{0,2},{1,3},{2,4},{3,5},{4,6},{5,7},{6,0},{7,1},{8,10},{9,11},{10,... | collective-permute-start | bytes 1769480 | tf_op jit(solution)/shard_map/ppermute | solution.py:878
  425.0 15.7 %collective-permute-start.58 = (bf16[768,384]{1,0:T(8,128)(2,1)}, bf16[768,384]{1,0:T(8,128)(2,1)}, u32[]{:S(2)}, u32[]{:S(2)}) collective-permute-start(bf16[768,384]{1,0:T(8,128)(2,1)} %get-tuple-element.239), channel_id=1, source_target_pairs={{0,1},{1,0},{2,3},{3,2},{4,5},{5,4},{6,7},{7,6},{8,9},{9,8},{10,11... | collective-permute-start | bytes 1769480 | tf_op jit(solution)/shard_map/ppermute | solution.py:875
  445.5 16.9 %collective-permute-start.60 = (bf16[768,384]{1,0:T(8,128)(2,1)}, bf16[768,384]{1,0:T(8,128)(2,1)S(1)}, u32[]{:S(2)}, u32[]{:S(2)}) collective-permute-start(bf16[768,384]{1,0:T(8,128)(2,1)} %get-tuple-element.241), channel_id=1, source_target_pairs={{0,2},{1,3},{2,4},{3,5},{4,6},{5,7},{6,0},{7,1},{8,10},{9,11},{10,... | collective-permute-start | bytes 1769480 | tf_op jit(solution)/shard_map/ppermute | solution.py:878
  445.5 18.9 %collective-permute-start.61 = (bf16[768,384]{1,0:T(8,128)(2,1)S(1)}, bf16[768,384]{1,0:T(8,128)(2,1)}, u32[]{:S(2)}, u32[]{:S(2)}) collective-permute-start(bf16[768,384]{1,0:T(8,128)(2,1)S(1)} %get-tuple-element.242), channel_id=1, source_target_pairs={{0,1},{1,0},{2,3},{3,2},{4,5},{5,4},{6,7},{7,6},{8,9},{9,8},{10,11... | collective-permute-start | bytes 1769480 | tf_op jit(solution)/shard_map/ppermute | solution.py:875
  447.0 17.4 %collective-permute-start.62 = (bf16[768,384]{1,0:T(8,128)(2,1)}, bf16[768,384]{1,0:T(8,128)(2,1)}, u32[]{:S(2)}, u32[]{:S(2)}) collective-permute-start(bf16[768,384]{1,0:T(8,128)(2,1)} %get-tuple-element.243), channel_id=1, source_target_pairs={{0,16},{8,24},{16,0},{24,8},{1,17},{9,25},{17,1},{25,9},{2,18},{10... | collective-permute-start | bytes 1769480 | tf_op jit(solution)/shard_map/ppermute | solution.py:869
  447.0 22.0 %collective-permute-start.51 = (bf16[400,384]{1,0:T(8,128)(2,1)}, bf16[400,384]{1,0:T(8,128)(2,1)S(1)}, u32[]{:S(2)}, u32[]{:S(2)}) collective-permute-start(bf16[400,384]{1,0:T(8,128)(2,1)} %get-tuple-element.232), channel_id=1, source_target_pairs={{0,2},{1,3},{2,4},{3,5},{4,6},{5,7},{6,0},{7,1},{8,10},{9,11},{10,... | collective-permute-start | bytes 921608 | tf_op jit(solution)/shard_map/ppermute | solution.py:878
  447.0 25.2 %collective-permute-start.52 = (bf16[400,384]{1,0:T(8,128)(2,1)S(1)}, bf16[400,384]{1,0:T(8,128)(2,1)S(1)}, u32[]{:S(2)}, u32[]{:S(2)}) collective-permute-start(bf16[400,384]{1,0:T(8,128)(2,1)S(1)} %copy-done.25), channel_id=1, source_target_pairs={{0,1},{1,0},{2,3},{3,2},{4,5},{5,4},{6,7},{7,6},{8,9},{9,8},{10,11... | collective-permute-start | bytes 921608 | tf_op jit(solution)/shard_map/ppermute | solution.py:875
  466.1 14.3 %collective-permute-start.63 = (bf16[768,384]{1,0:T(8,128)(2,1)S(1)}, bf16[768,384]{1,0:T(8,128)(2,1)S(1)}, u32[]{:S(2)}, u32[]{:S(2)}) collective-permute-start(bf16[768,384]{1,0:T(8,128)(2,1)S(1)} %fusion.36), channel_id=1, source_target_pairs={{0,2},{1,3},{2,4},{3,5},{4,6},{5,7},{6,0},{7,1},{8,10},{9,11},{10,... | collective-permute-start | bytes 1769480 | tf_op jit(solution)/shard_map/ppermute | solution.py:878
  466.2 14.2 %collective-permute-start.64 = (bf16[768,384]{1,0:T(8,128)(2,1)S(1)}, bf16[768,384]{1,0:T(8,128)(2,1)S(1)}, u32[]{:S(2)}, u32[]{:S(2)}) collective-permute-start(bf16[768,384]{1,0:T(8,128)(2,1)S(1)} %copy-done.23), channel_id=1, source_target_pairs={{0,1},{1,0},{2,3},{3,2},{4,5},{5,4},{6,7},{7,6},{8,9},{9,8},{10,11... | collective-permute-start | bytes 1769480 | tf_op jit(solution)/shard_map/ppermute | solution.py:875
  (69 other events, 1280.3 us)
Sparse Core Ops, SparseCore 0:
  113.5 77.2 all-gather.1
